TPU v7x, 512 devices: a whole 4x4x16 slice. The times are simulated.
512 devices in a mesh: phase: 8 (over y, x_hi), blk: 64 (over x_lo, z, core).
Axes of the slice: x: 4 (x_hi: 2, x_lo: 2; x = x_hi * 2 + x_lo), y: 4, z: 16, core: 2. Of those that a mesh axis runs over, the one named last changes fastest.
Arguments:
- layer_input: bfloat16 [1024, 8192], P(None, 'blk'), may hold values from -40 to 40
- norm_gain: bfloat16 [8192], P('blk'), may hold values from 0.099609375 to 1.8984375
- gate_weight: bfloat16 [26624, 8192], P(('phase', 'blk')), may hold values from -0.0625 to 0.0625
- up_weight: bfloat16 [26624, 8192], P(('phase', 'blk')), may hold values from -0.0625 to 0.0625
- down_weight: bfloat16 [26624, 8192], P('phase', 'blk'), may hold values from -0.0390625 to 0.0390625
Outputs:
- layer_output: bfloat16 [1024, 8192], P('phase', 'blk')
All inputs are finite; a program needn't handle non-finite values.
Results may differ from a plain program's by a relative error of at most 0.0056.
Values may be sent and summed in bfloat16 or wider, within the bound.
No kernel may reach another device: no remote copies, remote signals or barrier semaphores. Data moves between devices by JAX's collectives and lax.ppermute only.
A program may use at most 64 MiB of HBM per device.

v0:
```python
import jax
import jax.numpy as jnp
from jax import lax
from jax.sharding import PartitionSpec as P

FEAT = 8192


epsilon = 1e-05


def times_rows(left, weight):
    return lax.dot_general(
        left, weight, (((1,), (1,)), ((), ())), preferred_element_type=jnp.float32
    )


def local(layer_input, norm_gain, gate_weight, up_weight, down_weight):
    row_count = layer_input.shape[0]
    phase_rows = row_count // lax.axis_size("phase")
    row_start = lax.axis_index("phase") * phase_rows
    local_vals = layer_input.astype(jnp.float32)
    sq_total = lax.psum(jnp.sum(local_vals * local_vals, axis=1), "blk")
    inv_rms = lax.rsqrt(sq_total / FEAT + epsilon)[:, None]
    normed = (local_vals * inv_rms * norm_gain.astype(jnp.float32)).astype(jnp.bfloat16)
    segment = lax.all_gather(normed, "blk", axis=1, tiled=True)
    gate_sum = times_rows(segment, gate_weight)
    up_sum = times_rows(segment, up_weight)
    activated = (jax.nn.silu(gate_sum) * up_sum).astype(jnp.bfloat16)
    partials = jnp.dot(
        lax.all_gather(activated, "blk", axis=1, tiled=True),
        down_weight,
        preferred_element_type=jnp.float32,
    )
    ffn_out = lax.psum_scatter(partials, "phase", scatter_dimension=0, tiled=True)
    residual = lax.dynamic_slice_in_dim(layer_input, row_start, phase_rows, 0)
    return (residual.astype(jnp.float32) + ffn_out).astype(jnp.bfloat16)


def solution(mesh):
    return jax.shard_map(
        local,
        mesh=mesh,
        in_specs=(
            P(None, "blk"),
            P("blk"),
            P(("phase", "blk"), None),
            P(("phase", "blk"), None),
            P("phase", "blk"),
        ),
        out_specs=P("phase", "blk"),
        check_vma=False,
    )
```

profile of v0, /device:TPU:1, one launch (start us, length us, event | category | flops | bytes accessed | tf_op | source)
XLA Modules:
  0.0 537.3 jit_solution(10507351979427872239)
XLA Ops:
  6.5 0.0 copy-start
  6.5 0.0 copy-start.2
  6.5 0.0 all-gather.4.cloned.1.call-start
  6.5 0.8 convert_element_type.20
  7.3 1.2 fusion.2
  8.5 112.2 %psum.7 = f32[1024]{0:T(1024)S(1)} all-reduce(f32[1024]{0:T(1024)S(1)} %fusion.2), channel_id=1, replica_groups=mesh['phase'=8,'blk'=64] {'blk'}, use_global_device_ids=true, to_apply=%region_1.0 | all-reduce | flops 1024 | bytes 8192 | tf_op jit(solution)/shard_map/psum | solution.py:23
  120.7 1.9 fusion.4
  122.6 0.0 all-gather.4.cloned.1.call-update
  122.6 0.0 all-gather.6.cloned.1.call-start
  122.7 169.4 %all-gather.4.cloned.1.call-done = bf16[1024,8192]{1,0:T(8,128)(2,1)} async-done(((bf16[1024,128]{1,0:T(8,128)(2,1)}), bf16[1024,8192]{1,0:T(8,128)(2,1)}) %all-gather.4.cloned.1.call-update) | async-done | bytes 16777232 | tf_op jit(solution)/shard_map/all_gather | solution.py:26
  292.1 0.0 copy-done
  292.1 0.0 copy-start.1
  292.1 11.1 %fusion.5 = f32[1024,52]{0,1:T(8,128)S(1)} fusion(bf16[1024,8192]{1,0:T(8,128)(2,1)} %all-gather.4.cloned.1.call-done, bf16[52,8192]{1,0:T(8,128)(2,1)S(1)} %copy-done), kind=kOutput, calls=%fused_computation.10 | convolution fusion | flops 872415232 | bytes 17842176 | tf_op jit(solution)/shard_map/dot_general | solution.py:13
  303.2 0.0 copy-done.2
  303.2 0.0 copy-done.1
  303.2 0.0 copy-start.3
  303.2 5.9 %fusion.1 = bf16[1,52,1024]{2,1,0:T(8,128)(2,1)} fusion(bf16[1024,8192]{1,0:T(8,128)(2,1)S(1)} %copy-done.1, bf16[52,8192]{1,0:T(8,128)(2,1)S(1)} %copy-done.2, f32[1024,52]{0,1:T(8,128)S(1)} %fusion.5), kind=kOutput, calls=%fused_computation.2 | convolution fusion | flops 872734720 | bytes 17948672 | tf_op jit(solution)/shard_map/dot_general | solution.py:13
  309.1 0.0 all-gather.6.cloned.1.call-update
  309.2 0.0 reduce-scatter.2.cloned.1.call-start
  309.2 125.3 %all-gather.6.cloned.1.call-done = bf16[64,52,1024]{2,1,0:T(8,128)(2,1)} async-done(((bf16[1,52,1024]{2,1,0:T(8,128)(2,1)}), bf16[64,52,1024]{2,1,0:T(8,128)(2,1)}) %all-gather.6.cloned.1.call-update) | async-done | bytes 6815760 | tf_op jit(solution)/shard_map/all_gather | solution.py:31
  434.5 9.8 %reshape.3 = bf16[3328,1024]{1,0:T(8,128)(2,1)} reshape(bf16[64,52,1024]{2,1,0:T(8,128)(2,1)} %all-gather.6.cloned.1.call-done) | data formatting | bytes 13631488
  444.2 0.0 copy-done.3
  444.2 5.7 %fusion.6 = f32[1024,128]{1,0:T(8,128)} fusion(bf16[3328,1024]{1,0:T(8,128)(2,1)} %reshape.3, bf16[3328,128]{1,0:T(8,128)(2,1)S(1)} %copy-done.3), kind=kOutput, calls=%fused_computation.11 | convolution fusion | flops 872415232 | bytes 8192000 | tf_op jit(solution)/shard_map/dot_general | solution.py:30
  449.9 0.0 reduce-scatter.2.cloned.1.call-update
  450.0 79.4 %reduce-scatter.2.cloned.1.call-done = f32[128,128]{1,0:T(8,128)} async-done(((f32[1024,128]{1,0:T(8,128)}), f32[128,128]{1,0:T(8,128)}) %reduce-scatter.2.cloned.1.call-update) | async-done | bytes 65552 | tf_op jit(solution)/shard_map/reduce_scatter | solution.py:35
  529.3 1.5 add_convert_fusion
  (1 shorter events, 0.0 us)
Async XLA Ops:
  6.5 285.5 %copy-start = (bf16[52,8192]{1,0:T(8,128)(2,1)S(1)}, bf16[52,8192]{1,0:T(8,128)(2,1)}, u32[]{:S(2)}) copy-start(bf16[52,8192]{1,0:T(8,128)(2,1)} %param.7) | copy-start | bytes 2555908
  6.5 296.7 %copy-start.2 = (bf16[52,8192]{1,0:T(8,128)(2,1)S(1)}, bf16[52,8192]{1,0:T(8,128)(2,1)}, u32[]{:S(2)}) copy-start(bf16[52,8192]{1,0:T(8,128)(2,1)} %param.8) | copy-start | bytes 2555908
  6.5 285.5 %all-gather.4.cloned.1.call-start = ((), (), s32[]{:S(2)}) async-start(), calls=%async_computation.1 | async-start | bytes 17039360 | tf_op jit(solution)/shard_map/all_gather | solution.py:26
  122.6 311.8 %all-gather.6.cloned.1.call-start = ((), (), s32[]{:S(2)}) async-start(), calls=%async_computation.3 | async-start | bytes 7454720 | tf_op jit(solution)/shard_map/all_gather | solution.py:31
  292.1 11.2 %copy-start.1 = (bf16[1024,8192]{1,0:T(8,128)(2,1)S(1)}, bf16[1024,8192]{1,0:T(8,128)(2,1)}, u32[]{:S(2)}) copy-start(bf16[1024,8192]{1,0:T(8,128)(2,1)} %all-gather.4.cloned.1.call-done) | copy-start | bytes 50331652
  303.2 141.0 %copy-start.3 = (bf16[3328,128]{1,0:T(8,128)(2,1)S(1)}, bf16[3328,128]{1,0:T(8,128)(2,1)}, u32[]{:S(2)}) copy-start(bf16[3328,128]{1,0:T(8,128)(2,1)} %param.9) | copy-start | bytes 2555908
  309.2 220.1 %reduce-scatter.2.cloned.1.call-start = ((), (), s32[]{:S(2)}) async-start(), calls=%async_computation.2 | async-start | bytes 589824 | tf_op jit(solution)/shard_map/reduce_scatter | solution.py:35
Sparse Core Ops, SparseCore 0:
  122.7 169.2 all-gather.3
  309.3 125.1 all-gather.5
  450.1 79.1 reduce-scatter.1
where the time goes:
time: 538 us; the launch traced here: 537 us
  waiting for transfers between devices  374 us (70%)
  blocking collectives  112 us (21%)
  matrix products  22.7 us (4%)
  between operations  13.1 us (2%)
  local copies, waits for them, and re-layouts  9.79 us (2%)
    all_gather x1, waiting for transfers between devices, local(): segment = lax.all_gather(normed, 'blk', axis=1, tiled=True)  169 us
    all_gather x1, waiting for transfers between devices, local(): lax.all_gather(activated, 'blk', axis=1, tiled=True)  125 us
    psum x1, blocking collectives, local(): sq_total = lax.psum(jnp.sum(local_vals * local_vals, axis=1), 'blk')  112 us
    reduce_scatter x1, waiting for transfers between devices, local(): lax.psum_scatter(partials, 'phase', scatter_dimension=0, tiled=True)  79.4 us
    dot_general x2, matrix products, times_rows(): lax.dot_general(left, weight, (((1,), (1,)), ((), ())), preferred_element...  17 us
  transfers between devices with their start and end apart: 3, of which 3 were waited for; matrix products, arithmetic and copies ran while one was open for 0% of the time, Pallas kernels for 0%

commit v1 on v0

v1 whole, which is shorter than its diff:
```python
import jax
import jax.numpy as jnp
from jax import lax
from jax.sharding import Mesh, PartitionSpec as P

FEAT = 8192
EPS = 1e-05
LANES = 128

AXES = ("y", "xh", "xl", "zh", "zm", "z0", "core")
SIZES = (4, 2, 2, 4, 2, 2, 2)
PHASE = ("y", "xh")
BLK = ("xl", "zh", "zm", "z0", "core")
GROUP = ("zh", "zm")
MEMBER = ("xl", "z0")
NEAR = ("xl", "zm", "z0")
FAR = "zh"

f32, bf16 = jnp.float32, jnp.bfloat16


def swap_cores(value):
    return lax.ppermute(value, "core", ((0, 1), (1, 0)))


def exchange(value, axes):
    return lax.all_to_all(value, axes, 0, 0, tiled=True)


def copies(value, count):
    return jnp.broadcast_to(value[None], (count, *value.shape))


def by_core(own, other, axis):
    first = lax.axis_index("core") == 0
    return jnp.stack((jnp.where(first, own, other), jnp.where(first, other, own)), axis)


def local(layer_input, norm_gain, gate_weight, up_weight, down_weight):
    phase = lax.axis_index(PHASE)
    units = gate_weight.shape[0]
    rows = layer_input.shape[0] // 16

    both = jnp.concatenate((gate_weight, up_weight), 0)
    both = both.reshape(2 * units, 2, 8, 512).transpose(2, 0, 1, 3)
    own_w = exchange(both.reshape(8, 2 * units, 1024), PHASE)
    other_w = swap_cores(own_w)
    down = down_weight.reshape(2, 4, 8 * units, LANES).transpose(1, 0, 2, 3)
    down = exchange(down.reshape(4, 16 * units, LANES), FAR)
    other_down = swap_cores(down)

    mine = lax.dynamic_slice_in_dim(layer_input, phase * 2 * rows, 2 * rows, 0)
    gain = jnp.broadcast_to(norm_gain[None, None], (2, 8, LANES))
    mine = jnp.concatenate((mine.reshape(2, rows, LANES), gain), 1)
    sent = jnp.broadcast_to(mine[None], (8, 2, rows + 8, LANES))
    got = exchange(sent.reshape(16, rows + 8, LANES), (*GROUP, "core"))
    got = exchange(got.reshape(8, 2, rows + 8, LANES), PHASE)
    got = exchange(copies(got, 4), MEMBER)
    gains = got[:, :1, :, rows : rows + 1].astype(f32)
    vals = got[:, :, :, :rows].astype(f32)
    sq = jnp.sum(vals * vals, axis=(0, 2, 4)).reshape(8 * rows)
    scaled = (vals * gains).astype(bf16).transpose(1, 3, 0, 2, 4).reshape(8 * rows, 1024)

    def times(weight):
        return lax.dot_general(
            weight.reshape(16 * units, 1024),
            scaled,
            (((1,), (1,)), ((), ())),
            preferred_element_type=f32,
        ).astype(bf16).reshape(8, 2 * units, 8 * rows)

    sq_hi = sq.astype(bf16)
    sq_rest = sq - sq_hi.astype(f32)
    sq_mid = sq_rest.astype(bf16)
    sq_lo = (sq_rest - sq_mid.astype(f32)).astype(bf16)
    zero = jnp.zeros_like(sq_hi)
    sq_rows = jnp.stack((sq_hi, sq_mid, sq_lo, zero, zero, zero, zero, zero))
    sums = jnp.concatenate((times(own_w), times(other_w), copies(sq_rows, 8)), 1)
    sums = jnp.sum(exchange(sums, PHASE).astype(f32), 0)
    sq_total = jnp.sum(sums[4 * units : 4 * units + 3], 0)
    inv_rms = lax.rsqrt(sq_total / FEAT + EPS)
    sums = sums[: 4 * units].reshape(2, 2, units, 8 * rows) * inv_rms
    acts = (jax.nn.silu(sums[:, 0]) * sums[:, 1]).astype(bf16)
    acts = by_core(acts[0], acts[1], 0).reshape(2 * units, 8 * rows)

    acts = exchange(copies(acts, 8), NEAR).reshape(16 * units, 8 * rows)
    weights = by_core(down, other_down, 1).transpose(2, 0, 1, 3).reshape(16 * units, 1024)
    partials = lax.dot_general(
        acts, weights, (((0,), (0,)), ((), ())), preferred_element_type=f32
    ).astype(bf16)
    partials = exchange(partials.reshape(8, rows, 1024), PHASE)
    partials = jnp.sum(partials.astype(f32), 0).astype(bf16)
    partials = partials.reshape(rows, 8, LANES).transpose(1, 0, 2)
    partials = exchange(partials, (FAR, "core")).astype(f32)
    ffn_out = jnp.sum(partials.reshape(4, 2 * rows, LANES), 0)
    residual = lax.dynamic_slice_in_dim(layer_input, phase * 2 * rows, 2 * rows, 0)
    return (residual.astype(f32) + ffn_out).astype(bf16)


def solution(mesh):
    fine = Mesh(mesh.devices.reshape(SIZES), AXES)
    return jax.shard_map(
        local,
        mesh=fine,
        in_specs=(
            P(None, BLK),
            P(BLK),
            P((*PHASE, *BLK), None),
            P((*PHASE, *BLK), None),
            P(PHASE, BLK),
        ),
        out_specs=P(PHASE, BLK),
        check_vma=False,
    )
```

time: 538 us -> 261 us (0.49)
  waiting for transfers between devices: 374 us -> 117 us
  starting transfers between devices: 0.09 us -> 32.7 us
  blocking collectives: 112 us -> 79.8 us
  matrix products: 22.7 us -> 7.49 us
  between operations: 13.1 us -> 0.29 us
    all_gather x2 -> x0, waiting for transfers between devices: 295 us -> none  [the longest x1 169 us: local(): segment = lax.all_gather(normed, 'blk', axis=1, tiled=True)]
    all_to_all x0 -> x6, waiting for transfers between devices: none -> 115 us  [exchange(): return lax.all_to_all(value, axes, 0, 0, tiled=True)]
    psum x1 -> x0, blocking collectives: 112 us -> none  [local(): sq_total = lax.psum(jnp.sum(local_vals * local_vals, axis=1), 'blk')]
    all_to_all x0 -> x3, blocking collectives: none -> 79.8 us  [exchange(): return lax.all_to_all(value, axes, 0, 0, tiled=True)]
    reduce_scatter x1 -> x0, waiting for transfers between devices: 79.4 us -> none  [local(): lax.psum_scatter(partials, 'phase', scatter_dimension=0, tiled=True)]
    all_to_all x0 -> x6, starting transfers between devices: none -> 26 us  [exchange(): return lax.all_to_all(value, axes, 0, 0, tiled=True)]
    dot_general x3, matrix products: 22.7 us -> 7.49 us  [the longest x2 5.07 us: times(): lax.dot_general(weight.reshape(16 * units, 1024), scaled, (((1,), (1,)),...]
    unnamed x9 -> x6, local copies, waits for them, and re-layouts: 9.79 us -> 0.67 us
  transfers between devices with their start and end apart: 3 -> 8, of which waited for: 3 -> 7; matrix products, arithmetic and copies ran while one was open for 0% -> 6% of each run, Pallas kernels for 0% -> 0%
where the time goes in v1:
time: 261 us; the launch traced here: 260 us
  waiting for transfers between devices  117 us (45%)
  blocking collectives  79.8 us (31%)
  starting transfers between devices  32.7 us (13%)
  local copies, waits for them, and re-layouts  14.2 us (5%)
  other arithmetic  8.26 us (3%)
  matrix products  7.49 us (3%)
    all_to_all x6, waiting for transfers between devices, exchange(): return lax.all_to_all(value, axes, 0, 0, tiled=True)  115 us
    all_to_all x3, blocking collectives, exchange(): return lax.all_to_all(value, axes, 0, 0, tiled=True)  79.8 us
    all_to_all x6, starting transfers between devices, exchange(): return lax.all_to_all(value, axes, 0, 0, tiled=True)  26 us
    ppermute x2, starting transfers between devices, swap_cores(): return lax.ppermute(value, 'core', ((0, 1), (1, 0)))  6.75 us
  transfers between devices with their start and end apart: 8, of which 7 were waited for; matrix products, arithmetic and copies ran while one was open for 6% of the time, Pallas kernels for 0%

profile of v1, /device:TPU:1, one launch (start us, length us, event | category | flops | bytes accessed | tf_op | source)
XLA Modules:
  0.0 259.6 jit_solution(12725997703775486474)
XLA Ops:
  0.0 0.0 copy-start
  0.0 0.8 constant_dynamic-slice_fusion
  0.8 0.7 broadcast_in_dim.12
  1.6 38.4 %all_to_all.45 = bf16[16,72,128]{2,1,0:T(8,128)(2,1)} all-to-all(bf16[16,72,128]{2,1,0:T(8,128)(2,1)S(1)} %bitcast.61), channel_id=1, replica_groups=mesh['y'=4,'xh'=2,'xl'=2,'zh'=4,'zm'=2,'z0'=2,'core'=2] {'zh','zm','core'}, dimensions={0} | all-to-all | bytes 589824 | tf_op jit(solution)/shard_map/all_to_all | solution.py:27
  40.0 6.7 %all-to-all-start.2 = ((bf16[8,2,72,128]{3,2,1,0:T(8,128)(2,1)}), bf16[8,2,72,128]{3,2,1,0:T(8,128)(2,1)S(1)}, u32[]{:S(2)}, u32[]{:S(2)}) async-start(bf16[8,2,72,128]{3,2,1,0:T(8,128)(2,1)} %bitcast.4), calls=%async_computation.2 | async-start | bytes 589824 | tf_op jit(solution)/shard_map/all_to_all | solution.py:27
  46.6 0.0 copy-done
  46.6 1.4 pad_maximum_fusion.1
  48.0 0.6 copy.23
  48.7 1.3 copy.26
  50.0 2.1 reshape.116
  52.2 3.2 %all-to-all-done.2 = bf16[8,2,72,128]{3,2,1,0:T(8,128)(2,1)S(1)} async-done(((bf16[8,2,72,128]{3,2,1,0:T(8,128)(2,1)}), bf16[8,2,72,128]{3,2,1,0:T(8,128)(2,1)S(1)}, u32[]{:S(2)}, u32[]{:S(2)}) %all-to-all-start.2) | async-done | bytes 294944 | tf_op jit(solution)/shard_map/all_to_all | solution.py:27
  55.4 4.3 %all-to-all-start = ((bf16[8,104,1024]{2,1,0:T(8,128)(2,1)}), bf16[8,104,1024]{2,1,0:T(8,128)(2,1)}, u32[]{:S(2)}, u32[]{:S(2)}) async-start(bf16[8,104,1024]{2,1,0:T(8,128)(2,1)} %reshape.116), calls=%async_computation | async-start | bytes 3407872 | tf_op jit(solution)/shard_map/all_to_all | solution.py:27
  59.7 0.2 copy.16
  59.9 24.0 %all-to-all-done = bf16[8,104,1024]{2,1,0:T(8,128)(2,1)} async-done(((bf16[8,104,1024]{2,1,0:T(8,128)(2,1)}), bf16[8,104,1024]{2,1,0:T(8,128)(2,1)}, u32[]{:S(2)}, u32[]{:S(2)}) %all-to-all-start) | async-done | bytes 1703968 | tf_op jit(solution)/shard_map/all_to_all | solution.py:27
  83.9 1.6 broadcast_in_dim.14
  85.5 3.5 %all-to-all-start.3 = ((bf16[4,8,2,72,128]{4,2,3,1,0:T(2,128)(2,1)}), bf16[4,8,2,72,128]{4,2,3,1,0:T(2,128)(2,1)S(1)}, u32[]{:S(2)}, u32[]{:S(2)}) async-start(bf16[4,8,2,72,128]{4,2,3,1,0:T(2,128)(2,1)} %broadcast_in_dim.14), calls=%async_computation.3 | async-start | bytes 2359296 | tf_op jit(solution)/shard_map/all_to_all | solution.py:27
  89.1 2.9 %collective-permute-start = (bf16[8,104,1024]{2,1,0:T(8,128)(2,1)}, bf16[8,104,1024]{2,1,0:T(8,128)(2,1)}, u32[]{:S(2)}, u32[]{:S(2)}) collective-permute-start(bf16[8,104,1024]{2,1,0:T(8,128)(2,1)} %all-to-all-done), channel_id=1, source_target_pairs={{0,1},{1,0},{2,3},{3,2},{4,5},{5,4},{6,7},{7,6},{8,9},{9,8},{10,11... | collective-permute-start | bytes 5111816 | tf_op jit(solution)/shard_map/ppermute | solution.py:23
  92.0 11.5 %all-to-all-done.3 = bf16[4,8,2,72,128]{4,2,3,1,0:T(2,128)(2,1)S(1)} async-done(((bf16[4,8,2,72,128]{4,2,3,1,0:T(2,128)(2,1)}), bf16[4,8,2,72,128]{4,2,3,1,0:T(2,128)(2,1)S(1)}, u32[]{:S(2)}, u32[]{:S(2)}) %all-to-all-start.3) | async-done | bytes 1179680 | tf_op jit(solution)/shard_map/all_to_all | solution.py:27
  103.5 3.2 %fusion.2 = (bf16[8,64,4,2,128]{4,3,1,0,2:T(2,128)(2,1)S(1)}, f32[8,64]{1,0:T(8,128)S(1)}) fusion(f32[4,2,128]{2,1,0:T(2,128)S(1)} %fusion.5, bf16[4,8,2,72,128]{4,2,3,1,0:T(2,128)(2,1)S(1)} %all-to-all-done.3), kind=kLoop, calls=%fused_computation.12 | loop fusion | flops 2620928 | bytes 2103296 | tf_op jit(solution)/shard_map/transpose | solution.py:62
  106.7 0.1 reshape.125
  106.8 0.7 copy.17
  107.5 0.8 reshape.121
  108.3 0.0 collective-permute-done
  108.3 2.5 convolution_convert_fusion.1
  110.9 2.5 convolution_convert_fusion.2
  113.5 1.4 pad_maximum_fusion
  114.8 0.0 copy-start.1
  114.8 3.7 %all-to-all-start.4 = ((bf16[8,216,512]{2,1,0:T(8,128)(2,1)}), bf16[8,216,512]{2,1,0:T(8,128)(2,1)S(1)}, u32[]{:S(2)}, u32[]{:S(2)}) async-start(bf16[8,216,512]{2,1,0:T(8,128)(2,1)} %pad_maximum_fusion), calls=%async_computation.4 | async-start | bytes 3538944 | tf_op jit(solution)/shard_map/all_to_all | solution.py:27
  118.6 0.0 copy-done.1
  118.6 1.0 copy.19
  119.6 22.4 %all-to-all-done.4 = bf16[8,216,512]{2,1,0:T(8,128)(2,1)S(1)} async-done(((bf16[8,216,512]{2,1,0:T(8,128)(2,1)}), bf16[8,216,512]{2,1,0:T(8,128)(2,1)S(1)}, u32[]{:S(2)}, u32[]{:S(2)}) %all-to-all-start.4) | async-done | bytes 1769504 | tf_op jit(solution)/shard_map/all_to_all | solution.py:27
  142.0 3.5 %all-to-all-start.6 = ((bf16[4,832,128]{2,1,0:T(8,128)(2,1)}), bf16[4,832,128]{2,1,0:T(8,128)(2,1)S(1)}, u32[]{:S(2)}, u32[]{:S(2)}) async-start(bf16[4,832,128]{2,1,0:T(8,128)(2,1)} %bitcast.15), calls=%async_computation.6 | async-start | bytes 1703936 | tf_op jit(solution)/shard_map/all_to_all | solution.py:27
  145.5 0.2 convert_reduce_fusion
  145.9 0.1 fusion.4
  146.1 42.6 %all-to-all-done.6 = bf16[4,832,128]{2,1,0:T(8,128)(2,1)S(1)} async-done(((bf16[4,832,128]{2,1,0:T(8,128)(2,1)}), bf16[4,832,128]{2,1,0:T(8,128)(2,1)S(1)}, u32[]{:S(2)}, u32[]{:S(2)}) %all-to-all-start.6) | async-done | bytes 852000 | tf_op jit(solution)/shard_map/all_to_all | solution.py:27
  188.7 1.0 broadcast_in_dim.17
  189.6 4.2 %all-to-all-start.5 = ((bf16[8,104,512]{2,1,0:T(8,128)(2,1)}), bf16[8,104,512]{2,1,0:T(8,128)(2,1)}, u32[]{:S(2)}, u32[]{:S(2)}) async-start(bf16[8,104,512]{2,1,0:T(8,128)(2,1)} %broadcast_in_dim.17), calls=%async_computation.5 | async-start | bytes 1703936 | tf_op jit(solution)/shard_map/all_to_all | solution.py:27
  193.9 3.8 %collective-permute-start.1 = (bf16[4,832,128]{2,1,0:T(8,128)(2,1)S(1)}, bf16[4,832,128]{2,1,0:T(8,128)(2,1)S(1)}, u32[]{:S(2)}, u32[]{:S(2)}) collective-permute-start(bf16[4,832,128]{2,1,0:T(8,128)(2,1)S(1)} %all-to-all-done.6), channel_id=1, source_target_pairs={{0,1},{1,0},{2,3},{3,2},{4,5},{5,4},{6,7},{7,6},{8,9},{9,8},{10,11... | collective-permute-start | bytes 2555912 | tf_op jit(solution)/shard_map/ppermute | solution.py:23
  197.7 1.8 collective-permute-done.1
  199.5 0.1 select_bitcast_fusion.1
  199.6 0.2 maximum_bitcast_fusion
  199.8 1.8 copy.20
  201.6 1.2 reshape.130
  202.8 11.3 %all-to-all-done.5 = bf16[8,104,512]{2,1,0:T(8,128)(2,1)} async-done(((bf16[8,104,512]{2,1,0:T(8,128)(2,1)}), bf16[8,104,512]{2,1,0:T(8,128)(2,1)}, u32[]{:S(2)}, u32[]{:S(2)}) %all-to-all-start.5) | async-done | bytes 852000 | tf_op jit(solution)/shard_map/all_to_all | solution.py:27
  214.2 2.4 convolution_convert_fusion
  216.6 15.8 %all_to_all.46 = bf16[8,64,1024]{2,1,0:T(8,128)(2,1)S(1)} all-to-all(bf16[8,64,1024]{2,1,0:T(8,128)(2,1)S(1)} %bitcast.62), channel_id=1, replica_groups=mesh['y'=4,'xh'=2,'xl'=2,'zh'=4,'zm'=2,'z0'=2,'core'=2] {'y','xh'}, dimensions={0} | all-to-all | bytes 2097152 | tf_op jit(solution)/shard_map/all_to_all | solution.py:27
  232.4 0.2 reduce_sum.51
  232.6 25.6 %all_to_all.47 = bf16[8,64,128]{2,1,0:T(8,128)(2,1)S(1)} all-to-all(bf16[8,64,128]{2,1,0:T(8,128)(2,1)S(1)} %copy.21), channel_id=1, replica_groups=mesh['y'=4,'xh'=2,'xl'=2,'zh'=4,'zm'=2,'z0'=2,'core'=2] {'zh','core'}, dimensions={0} | all-to-all | bytes 262144 | tf_op jit(solution)/shard_map/all_to_all | solution.py:27
  258.2 1.4 add_convert_fusion
  (19 shorter events, 0.4 us)
Async XLA Ops:
  0.0 46.6 %copy-start = (bf16[52,8192]{1,0:T(8,128)(2,1)S(1)}, bf16[52,8192]{1,0:T(8,128)(2,1)}, u32[]{:S(2)}) copy-start(bf16[52,8192]{1,0:T(8,128)(2,1)} %param.8) | copy-start | bytes 2555908
  40.0 15.4 %all-to-all-start.2 = ((bf16[8,2,72,128]{3,2,1,0:T(8,128)(2,1)}), bf16[8,2,72,128]{3,2,1,0:T(8,128)(2,1)S(1)}, u32[]{:S(2)}, u32[]{:S(2)}) async-start(bf16[8,2,72,128]{3,2,1,0:T(8,128)(2,1)} %bitcast.4), calls=%async_computation.2 | async-start | bytes 589824 | tf_op jit(solution)/shard_map/all_to_all | solution.py:27
  55.4 28.6 %all-to-all-start = ((bf16[8,104,1024]{2,1,0:T(8,128)(2,1)}), bf16[8,104,1024]{2,1,0:T(8,128)(2,1)}, u32[]{:S(2)}, u32[]{:S(2)}) async-start(bf16[8,104,1024]{2,1,0:T(8,128)(2,1)} %reshape.116), calls=%async_computation | async-start | bytes 3407872 | tf_op jit(solution)/shard_map/all_to_all | solution.py:27
  85.5 18.0 %all-to-all-start.3 = ((bf16[4,8,2,72,128]{4,2,3,1,0:T(2,128)(2,1)}), bf16[4,8,2,72,128]{4,2,3,1,0:T(2,128)(2,1)S(1)}, u32[]{:S(2)}, u32[]{:S(2)}) async-start(bf16[4,8,2,72,128]{4,2,3,1,0:T(2,128)(2,1)} %broadcast_in_dim.14), calls=%async_computation.3 | async-start | bytes 2359296 | tf_op jit(solution)/shard_map/all_to_all | solution.py:27
  89.1 19.2 %collective-permute-start = (bf16[8,104,1024]{2,1,0:T(8,128)(2,1)}, bf16[8,104,1024]{2,1,0:T(8,128)(2,1)}, u32[]{:S(2)}, u32[]{:S(2)}) collective-permute-start(bf16[8,104,1024]{2,1,0:T(8,128)(2,1)} %all-to-all-done), channel_id=1, source_target_pairs={{0,1},{1,0},{2,3},{3,2},{4,5},{5,4},{6,7},{7,6},{8,9},{9,8},{10,11... | collective-permute-start | bytes 5111816 | tf_op jit(solution)/shard_map/ppermute | solution.py:23
  114.8 3.7 %copy-start.1 = (bf16[3328,128]{1,0:T(8,128)(2,1)S(1)}, bf16[3328,128]{1,0:T(8,128)(2,1)}, u32[]{:S(2)}) copy-start(bf16[3328,128]{1,0:T(8,128)(2,1)} %param.9) | copy-start | bytes 2555908
  114.8 27.1 %all-to-all-start.4 = ((bf16[8,216,512]{2,1,0:T(8,128)(2,1)}), bf16[8,216,512]{2,1,0:T(8,128)(2,1)S(1)}, u32[]{:S(2)}, u32[]{:S(2)}) async-start(bf16[8,216,512]{2,1,0:T(8,128)(2,1)} %pad_maximum_fusion), calls=%async_computation.4 | async-start | bytes 3538944 | tf_op jit(solution)/shard_map/all_to_all | solution.py:27
  142.0 46.7 %all-to-all-start.6 = ((bf16[4,832,128]{2,1,0:T(8,128)(2,1)}), bf16[4,832,128]{2,1,0:T(8,128)(2,1)S(1)}, u32[]{:S(2)}, u32[]{:S(2)}) async-start(bf16[4,832,128]{2,1,0:T(8,128)(2,1)} %bitcast.15), calls=%async_computation.6 | async-start | bytes 1703936 | tf_op jit(solution)/shard_map/all_to_all | solution.py:27
  189.6 24.5 %all-to-all-start.5 = ((bf16[8,104,512]{2,1,0:T(8,128)(2,1)}), bf16[8,104,512]{2,1,0:T(8,128)(2,1)}, u32[]{:S(2)}, u32[]{:S(2)}) async-start(bf16[8,104,512]{2,1,0:T(8,128)(2,1)} %broadcast_in_dim.17), calls=%async_computation.5 | async-start | bytes 1703936 | tf_op jit(solution)/shard_map/all_to_all | solution.py:27
  193.9 5.7 %collective-permute-start.1 = (bf16[4,832,128]{2,1,0:T(8,128)(2,1)S(1)}, bf16[4,832,128]{2,1,0:T(8,128)(2,1)S(1)}, u32[]{:S(2)}, u32[]{:S(2)}) collective-permute-start(bf16[4,832,128]{2,1,0:T(8,128)(2,1)S(1)} %all-to-all-done.6), channel_id=1, source_target_pairs={{0,1},{1,0},{2,3},{3,2},{4,5},{5,4},{6,7},{7,6},{8,9},{9,8},{10,11... | collective-permute-start | bytes 2555912 | tf_op jit(solution)/shard_map/ppermute | solution.py:23

commit v2 on v0

v2 whole, which is shorter than its diff:
```python
import jax
import jax.numpy as jnp
import numpy as np
from jax import lax
from jax.experimental import pallas as pl
from jax.experimental.pallas import tpu as pltpu
from jax.sharding import Mesh, PartitionSpec as P

FEAT = 8192
EPS = 1e-05
LANES = 128
PAD = 16

AXES = ("y", "xh", "xl", "zh", "zm", "z0", "core")
SIZES = (4, 2, 2, 4, 2, 2, 2)
PHASE = ("y", "xh")
BLK = ("xl", "zh", "zm", "z0", "core")
NEAR = ("xl", "zm", "z0")
FAR = "zh"

f32, bf16 = jnp.float32, jnp.bfloat16


def exchange(value, axes):
    return lax.all_to_all(value, axes, 0, 0, tiled=True)


def route(move):
    pairs = []
    for at in np.ndindex(*SIZES):
        to = dict(zip(AXES, at))
        move(to)
        to = tuple(to[a] % n for a, n in zip(AXES, SIZES))
        pairs.append([int(np.ravel_multi_index(i, SIZES)) for i in (at, to)])
    return pairs


def send(value, move):
    return lax.ppermute(value, AXES, route(move))


def spread(turn, cross):
    def move(to):
        part, group = to["y"] * 2 + to["xh"], to["zh"] * 2 + to["zm"]
        to["y"], to["xh"] = divmod(group, 2)
        to["zh"], to["zm"] = divmod((part + turn - group) % 8, 2)
        to["core"] += cross

    return move


def shift(**by):
    def move(to):
        for axis, count in by.items():
            to[axis] += count

    return move


def sums_kernel(at, x0, x1, x2, x3, w_own, w_other, out, scaled):
    rows = scaled.shape[0]
    squares = jnp.zeros((rows, LANES), f32)
    for chip, block in enumerate((x0, x1, x2, x3)):
        for core in (0, 1):
            vals = block[core, :rows].astype(f32)
            gain = block[core, rows:].astype(f32)[:1]
            squares += vals * vals
            place = (jnp.bitwise_xor(at[1], chip) * 2 + jnp.bitwise_xor(at[0], core)) * LANES
            scaled[:, pl.ds(pl.multiple_of(place, LANES), LANES)] = (vals * gain).astype(bf16)
    total = lax.dot_general(
        jnp.ones((8, LANES), f32),
        squares,
        (((1,), (1,)), ((), ())),
        precision=lax.Precision.HIGHEST,
        preferred_element_type=f32,
    )
    hi = total.astype(bf16).astype(f32)
    mid = (total - hi).astype(bf16).astype(f32)
    row = lax.broadcasted_iota(jnp.int32, (8, rows), 0)
    extra = jnp.where(row == 4, hi, jnp.where(row == 5, mid, jnp.where(row == 6, total - hi - mid, 0.0)))
    extra = jnp.concatenate((jnp.zeros((48, rows), f32), extra, jnp.zeros((56, rows), f32)))
    right = scaled[...]
    for side, weight in enumerate((w_own, w_other)):
        part = lax.dot_general(
            weight[...].reshape(8 * 112, 1024),
            right,
            (((1,), (1,)), ((), ())),
            preferred_element_type=f32,
        ).reshape(8, 112, rows)
        if side == 0:
            part = part + extra[None]
        out[:, side] = part.astype(bf16)


def acts_kernel(at, sums, out):
    rows = sums.shape[-1]
    own = sums[0, 0].astype(f32)
    other = sums[0, 1].astype(f32)
    for part in range(1, 8):
        own += sums[part, 0].astype(f32)
        other += sums[part, 1].astype(f32)
    row = lax.broadcasted_iota(jnp.int32, (8, rows), 0)
    squares = jnp.where((row >= 4) & (row < 7), own[48:56], 0.0)
    inv_rms = lax.rsqrt(jnp.sum(squares, 0, keepdims=True) / FEAT + EPS)
    unit = lax.broadcasted_iota(jnp.int32, (56, rows), 0)
    for side, total in enumerate((own, other)):
        gate = total[:56] * inv_rms
        acts = gate / (1.0 + jnp.exp(-gate)) * (total[56:] * inv_rms)
        acts = jnp.where(unit < 52, acts, 0.0).astype(bf16)
        for copy in range(8):
            out[copy, jnp.bitwise_xor(at[0], side)] = acts


def place_kernel(at, parts, out):
    total = parts[0].astype(f32)
    for part in range(1, 8):
        total += parts[part].astype(f32)
    for far in range(4):
        for core in (0, 1):
            to = jnp.bitwise_and(at[2] - far, 3) * 2 + jnp.bitwise_xor(at[0], core)
            column = (far * 2 + core) * LANES
            out[to] = total[:, column : column + LANES].astype(bf16)


def run(kernel, out_shape, operands, scratch=(), flops=0):
    moved = sum(o.size * o.dtype.itemsize for o in operands) + int(np.prod(out_shape)) * 2
    return pl.pallas_call(
        kernel,
        out_shape=jax.ShapeDtypeStruct(out_shape, bf16),
        in_specs=[pl.BlockSpec(memory_space=pltpu.SMEM)]
        + [pl.BlockSpec(memory_space=pltpu.VMEM)] * (len(operands) - 1),
        out_specs=pl.BlockSpec(memory_space=pltpu.VMEM),
        scratch_shapes=list(scratch),
        compiler_params=pltpu.CompilerParams(vmem_limit_bytes=40 * 2**20),
        cost_estimate=pl.CostEstimate(flops=flops, bytes_accessed=moved, transcendentals=0),
    )(*operands)


def local(layer_input, norm_gain, gate_weight, up_weight, down_weight):
    phase, core, far = (lax.axis_index(a) for a in (PHASE, "core", FAR))
    at = jnp.stack((core, lax.axis_index(("xl", "z0")), far)).astype(jnp.int32)
    units = gate_weight.shape[0]
    rows = layer_input.shape[0] // 2

    halves = layer_input.reshape(8, 2, rows // 8, LANES)
    gain = jnp.broadcast_to(norm_gain[None], (PAD, LANES))

    def half(index):
        part = lax.dynamic_slice_in_dim(halves, index, 1, 1).reshape(rows, LANES)
        return jnp.concatenate((part, gain))

    mine, yours, gate_weight, up_weight = lax.optimization_barrier(
        (half(core), half(1 - core), gate_weight, up_weight)
    )
    both = jnp.stack((gate_weight, up_weight))
    both = jnp.pad(both, ((0, 0), (0, 56 - units), (0, 0))).reshape(112, 2, 8, 512)
    own_w = exchange(both.transpose(2, 0, 1, 3).reshape(8, 112, 1024), PHASE)
    first = send(mine, spread(0, 0))
    second = send(yours, spread(4, 1))
    first, second, own_w = lax.optimization_barrier((first, second, own_w))
    other_w = send(own_w, shift(core=1))
    held = jnp.stack((first, second))
    blocks = [held] + [send(held, shift(xl=i, z0=j)) for i, j in ((0, 1), (1, 0), (1, 1))]

    down, _ = lax.optimization_barrier((down_weight, held))
    down = down.reshape(2, 4, 8, units, LANES)
    down = jnp.pad(down, ((0, 0), (0, 0), (0, 0), (0, 56 - units), (0, 0)))

    def quarter(count):
        part = lax.dynamic_slice_in_dim(down, (far + count) % 4, 1, 1).reshape(896, LANES)
        return send(part, shift(zh=count)) if count else part

    own_d = jnp.stack([quarter(count) for count in range(4)])
    sums = run(
        sums_kernel,
        (8, 2, 112, rows),
        (at, *blocks, own_w, other_w),
        (pltpu.VMEM((rows, 1024), bf16),),
        flops=2 * 1792 * 1024 * rows,
    )
    sums, own_d = lax.optimization_barrier((exchange(sums, PHASE), own_d))
    other_d = send(own_d, shift(core=1))
    d_all = jnp.stack((own_d, other_d), 1).transpose(2, 0, 1, 3).reshape(896, 1024)

    acts = run(acts_kernel, (8, 2, 56, rows), (at, sums))
    acts = exchange(acts.reshape(8, 112, rows), NEAR).reshape(896, rows)
    partials = lax.dot_general(
        acts, d_all, (((0,), (0,)), ((), ())), preferred_element_type=f32
    ).astype(bf16)
    partials = exchange(partials.reshape(8, rows // 8, 1024), PHASE)
    partials = run(place_kernel, (8, rows // 8, LANES), (at, partials))
    partials = exchange(partials, (FAR, "core")).astype(f32)
    ffn_out = jnp.sum(partials.reshape(4, rows // 4, LANES), 0)
    residual = lax.dynamic_slice_in_dim(layer_input, phase * (rows // 4), rows // 4, 0)
    return (residual.astype(f32) + ffn_out).astype(bf16)


def solution(mesh):
    fine = Mesh(mesh.devices.reshape(SIZES), AXES)
    return jax.shard_map(
        local,
        mesh=fine,
        in_specs=(
            P(None, BLK),
            P(BLK),
            P((*PHASE, *BLK), None),
            P((*PHASE, *BLK), None),
            P(PHASE, BLK),
        ),
        out_specs=P(PHASE, BLK),
        check_vma=False,
    )
```

time: 538 us -> 220 us (0.41)
  waiting for transfers between devices: 374 us -> 59.8 us
  starting transfers between devices: 0.09 us -> 112 us
  blocking collectives: 112 us -> 21.8 us
  matrix products: 22.7 us -> 3.08 us
  between operations: 13.1 us -> 0.2 us
  Pallas kernels: 0 us -> 7.44 us
    all_gather x2 -> x0, waiting for transfers between devices: 295 us -> none  [the longest x1 169 us: local(): segment = lax.all_gather(normed, 'blk', axis=1, tiled=True)]
    psum x1 -> x0, blocking collectives: 112 us -> none  [local(): sq_total = lax.psum(jnp.sum(local_vals * local_vals, axis=1), 'blk')]
    reduce_scatter x1 -> x0, waiting for transfers between devices: 79.4 us -> none  [local(): lax.psum_scatter(partials, 'phase', scatter_dimension=0, tiled=True)]
    all_to_all x0 -> x4, starting transfers between devices: none -> 61 us  [exchange(): return lax.all_to_all(value, axes, 0, 0, tiled=True)]
    ppermute x0 -> x10, starting transfers between devices: none -> 50.8 us  [send(): return lax.ppermute(value, AXES, route(move))]
    ppermute x0 -> x10, waiting for transfers between devices: none -> 31 us  [send(): return lax.ppermute(value, AXES, route(move))]
    all_to_all x0 -> x4, waiting for transfers between devices: none -> 28.8 us  [exchange(): return lax.all_to_all(value, axes, 0, 0, tiled=True)]
    all_to_all x0 -> x1, blocking collectives: none -> 21.8 us  [exchange(): return lax.all_to_all(value, axes, 0, 0, tiled=True)]
  transfers between devices with their start and end apart: 3 -> 14, of which waited for: 3 -> 9; matrix products, arithmetic and copies ran while one was open for 0% -> 2% of each run, Pallas kernels for 0% -> 0%
where the time goes in v2:
time: 220 us; the launch traced here: 219 us
  starting transfers between devices  112 us (51%)
  waiting for transfers between devices  59.8 us (27%)
  blocking collectives  21.8 us (10%)
  local copies, waits for them, and re-layouts  11.2 us (5%)
  Pallas kernels  7.44 us (3%)
  other arithmetic  3.44 us (2%)
  matrix products  3.08 us (1%)
    all_to_all x4, starting transfers between devices, exchange(): return lax.all_to_all(value, axes, 0, 0, tiled=True)  61 us
    ppermute x10, starting transfers between devices, send(): return lax.ppermute(value, AXES, route(move))  50.8 us
    ppermute x10, waiting for transfers between devices, send(): return lax.ppermute(value, AXES, route(move))  31 us
    all_to_all x4, waiting for transfers between devices, exchange(): return lax.all_to_all(value, axes, 0, 0, tiled=True)  28.8 us
    all_to_all x1, blocking collectives, exchange(): return lax.all_to_all(value, axes, 0, 0, tiled=True)  21.8 us
    pallas_call x3, Pallas kernels, run(): pl.pallas_call(kernel, out_shape=jax.ShapeDtypeStruct(out_shape, bf16), i...  7.44 us
  transfers between devices with their start and end apart: 14, of which 9 were waited for; matrix products, arithmetic and copies ran while one was open for 2% of the time, Pallas kernels for 0%

profile of v2, /device:TPU:1, one launch (start us, length us, event | category | flops | bytes accessed | tf_op | source)
XLA Modules:
  0.0 218.8 jit_solution(8480690150850612803)
XLA Ops:
  0.0 1.0 constant_dynamic-slice_fusion
  1.0 0.7 broadcast_in_dim.2
  1.7 1.6 fusion.2
  3.3 0.7 copy.19
  4.0 1.4 copy.21
  5.4 2.3 %reshape.50 = bf16[8,112,1024]{2,1,0:T(8,128)(2,1)} reshape(bf16[8,112,2,512]{3,2,1,0:T(2,128)(2,1)S(1)} %bitcast.43) | data formatting | bytes 3670016 | tf_op jit(solution)/shard_map/reshape | solution.py:157
  7.7 7.5 %all-to-all-start = ((bf16[8,112,1024]{2,1,0:T(8,128)(2,1)}), bf16[8,112,1024]{2,1,0:T(8,128)(2,1)S(1)}, u32[]{:S(2)}, u32[]{:S(2)}) async-start(bf16[8,112,1024]{2,1,0:T(8,128)(2,1)} %reshape.50), calls=%async_computation | async-start | bytes 3670016 | tf_op jit(solution)/shard_map/all_to_all | solution.py:25
  15.2 0.7 collective-permute-start
  15.9 21.0 %collective-permute-start.1 = (bf16[528,128]{1,0:T(8,128)(2,1)S(1)}, bf16[528,128]{1,0:T(8,128)(2,1)S(1)}, u32[]{:S(2)}, u32[]{:S(2)}) collective-permute-start(bf16[528,128]{1,0:T(8,128)(2,1)S(1)} %get-tuple-element.16), channel_id=1, source_target_pairs={{0,17},{1,16},{2,19},{3,18},{4,77},{5,76},{6,79},{7,78},{8,137},{9... | collective-permute-start | bytes 405512 | tf_op jit(solution)/shard_map/ppermute | solution.py:39
  36.9 0.0 collective-permute-done
  37.0 5.5 %collective-permute-done.1 = bf16[528,128]{1,0:T(8,128)(2,1)S(1)} collective-permute-done((bf16[528,128]{1,0:T(8,128)(2,1)S(1)}, bf16[528,128]{1,0:T(8,128)(2,1)S(1)}, u32[]{:S(2)}, u32[]{:S(2)}) %collective-permute-start.1) | collective-permute-done | bytes 135200 | tf_op jit(solution)/shard_map/ppermute | solution.py:39
  42.4 0.0 all-to-all-done.w_own
  42.4 1.9 collective-permute-start.5
  44.4 4.2 %collective-permute-start.2 = (bf16[2,528,128]{2,1,0:T(8,128)(2,1)S(1)}, bf16[2,528,128]{2,1,0:T(8,128)(2,1)S(1)}, u32[]{:S(2)}, u32[]{:S(2)}) collective-permute-start(bf16[2,528,128]{2,1,0:T(8,128)(2,1)S(1)} %pad_maximum_fusion.1.x0), channel_id=1, source_target_pairs={{0,2},{1,3},{2,0},{3,1},{4,6},{5,7},{6,4},{7,5},{8,10},{9,11},{10,... | collective-permute-start | bytes 811016 | tf_op jit(solution)/shard_map/ppermute | solution.py:39
  48.6 2.3 %collective-permute-start.3 = (bf16[2,528,128]{2,1,0:T(8,128)(2,1)S(1)}, bf16[2,528,128]{2,1,0:T(8,128)(2,1)S(1)}, u32[]{:S(2)}, u32[]{:S(2)}) collective-permute-start(bf16[2,528,128]{2,1,0:T(8,128)(2,1)S(1)} %pad_maximum_fusion.1.x0), channel_id=1, source_target_pairs={{0,32},{1,33},{2,34},{3,35},{4,36},{5,37},{6,38},{7,39},{8,40},{9,... | collective-permute-start | bytes 811016 | tf_op jit(solution)/shard_map/ppermute | solution.py:39
  50.9 2.7 %collective-permute-start.4 = (bf16[2,528,128]{2,1,0:T(8,128)(2,1)S(1)}, bf16[2,528,128]{2,1,0:T(8,128)(2,1)S(1)}, u32[]{:S(2)}, u32[]{:S(2)}) collective-permute-start(bf16[2,528,128]{2,1,0:T(8,128)(2,1)S(1)} %pad_maximum_fusion.1.x0), channel_id=1, source_target_pairs={{0,34},{1,35},{2,32},{3,33},{4,38},{5,39},{6,36},{7,37},{8,42},{9,... | collective-permute-start | bytes 811016 | tf_op jit(solution)/shard_map/ppermute | solution.py:39
  53.6 0.1 pad_add_fusion.at
  53.7 1.3 collective-permute-done.2.x1
  55.0 8.5 %collective-permute-done.3.x2 = bf16[2,528,128]{2,1,0:T(8,128)(2,1)S(1)} collective-permute-done((bf16[2,528,128]{2,1,0:T(8,128)(2,1)S(1)}, bf16[2,528,128]{2,1,0:T(8,128)(2,1)S(1)}, u32[]{:S(2)}, u32[]{:S(2)}) %collective-permute-start.3) | collective-permute-done | bytes 270368 | tf_op jit(solution)/shard_map/ppermute | solution.py:39
  63.5 0.0 collective-permute-done.4.x3
  63.5 0.0 collective-permute-done.5.w_other
  63.5 4.3 %shard_map.55 = bf16[8,2,112,512]{3,2,1,0:T(8,128)(2,1)S(1)} custom-call(s32[3]{0:T(128)S(1)} %pad_add_fusion.at, bf16[2,528,128]{2,1,0:T(8,128)(2,1)S(1)} %pad_maximum_fusion.1.x0, bf16[2,528,128]{2,1,0:T(8,128)(2,1)S(1)} %collective-permute-done.2.x1, bf16[2,528,128]{2,1,0:T(8,128)(2,1)S(1)} %collective-permute-done.3.x2, ...), custom_call_target="tpu_custom_call" | custom-call | flops 1879048192 | bytes 6586380 | tf_op jit(solution)/shard_map/pallas_call | solution.py:127
  67.8 0.0 copy-start
  67.8 1.2 copy-done
  69.0 14.1 %all-to-all-start.1 = ((bf16[8,2,112,512]{3,2,1,0:T(8,128)(2,1)}), bf16[8,2,112,512]{3,2,1,0:T(8,128)(2,1)S(1)}, u32[]{:S(2)}, u32[]{:S(2)}) async-start(bf16[8,2,112,512]{3,2,1,0:T(8,128)(2,1)} %copy-done), calls=%async_computation.1 | async-start | bytes 3670016 | tf_op jit(solution)/shard_map/all_to_all | solution.py:25
  83.1 1.2 reshape.51
  84.3 0.1 pad_dynamic-slice_fusion.3
  84.4 4.0 %collective-permute-start.8 = (bf16[896,128]{1,0:T(8,128)(2,1)S(1)}, bf16[896,128]{1,0:T(8,128)(2,1)S(1)}, u32[]{:S(2)}, u32[]{:S(2)}) collective-permute-start(bf16[896,128]{1,0:T(8,128)(2,1)S(1)} %bitcast.61), channel_id=1, source_target_pairs={{0,24},{1,25},{2,26},{3,27},{4,28},{5,29},{6,30},{7,31},{8,0},{9,1... | collective-permute-start | bytes 688136 | tf_op jit(solution)/shard_map/ppermute | solution.py:39
  88.4 6.0 %collective-permute-start.7 = (bf16[896,128]{1,0:T(8,128)(2,1)S(1)}, bf16[896,128]{1,0:T(8,128)(2,1)S(1)}, u32[]{:S(2)}, u32[]{:S(2)}) collective-permute-start(bf16[896,128]{1,0:T(8,128)(2,1)S(1)} %bitcast.60), channel_id=1, source_target_pairs={{0,16},{1,17},{2,18},{3,19},{4,20},{5,21},{6,22},{7,23},{8,24},{9,... | collective-permute-start | bytes 688136 | tf_op jit(solution)/shard_map/ppermute | solution.py:39
  94.4 5.3 %collective-permute-start.6 = (bf16[896,128]{1,0:T(8,128)(2,1)S(1)}, bf16[896,128]{1,0:T(8,128)(2,1)S(1)}, u32[]{:S(2)}, u32[]{:S(2)}) collective-permute-start(bf16[896,128]{1,0:T(8,128)(2,1)S(1)} %bitcast.59), channel_id=1, source_target_pairs={{0,8},{1,9},{2,10},{3,11},{4,12},{5,13},{6,14},{7,15},{8,16},{9,17... | collective-permute-start | bytes 688136 | tf_op jit(solution)/shard_map/ppermute | solution.py:39
  99.7 4.4 %collective-permute-done.8 = bf16[896,128]{1,0:T(8,128)(2,1)S(1)} collective-permute-done((bf16[896,128]{1,0:T(8,128)(2,1)S(1)}, bf16[896,128]{1,0:T(8,128)(2,1)S(1)}, u32[]{:S(2)}, u32[]{:S(2)}) %collective-permute-start.8) | collective-permute-done | bytes 229408 | tf_op jit(solution)/shard_map/ppermute | solution.py:39
  104.2 2.2 %collective-permute-done.7 = bf16[896,128]{1,0:T(8,128)(2,1)S(1)} collective-permute-done((bf16[896,128]{1,0:T(8,128)(2,1)S(1)}, bf16[896,128]{1,0:T(8,128)(2,1)S(1)}, u32[]{:S(2)}, u32[]{:S(2)}) %collective-permute-start.7) | collective-permute-done | bytes 229408 | tf_op jit(solution)/shard_map/ppermute | solution.py:39
  106.4 7.0 %collective-permute-done.6 = bf16[896,128]{1,0:T(8,128)(2,1)S(1)} collective-permute-done((bf16[896,128]{1,0:T(8,128)(2,1)S(1)}, bf16[896,128]{1,0:T(8,128)(2,1)S(1)}, u32[]{:S(2)}, u32[]{:S(2)}) %collective-permute-start.6) | collective-permute-done | bytes 229408 | tf_op jit(solution)/shard_map/ppermute | solution.py:39
  113.4 0.1 pad_maximum_fusion
  113.5 0.0 all-to-all-done.1.sums
  113.5 1.8 shard_map.56
  115.3 30.1 %all-to-all-start.2 = ((bf16[8,112,512]{2,1,0:T(8,128)(2,1)}), bf16[8,112,512]{2,1,0:T(8,128)(2,1)}, u32[]{:S(2)}, u32[]{:S(2)}) async-start(bf16[8,112,512]{2,1,0:T(8,128)(2,1)} %bitcast.18), calls=%async_computation.2 | async-start | bytes 1835008 | tf_op jit(solution)/shard_map/all_to_all | solution.py:25
  145.4 2.8 %collective-permute-start.9 = (bf16[4,896,128]{2,1,0:T(8,128)(2,1)S(1)}, bf16[4,896,128]{2,1,0:T(8,128)(2,1)S(1)}, u32[]{:S(2)}, u32[]{:S(2)}) collective-permute-start(bf16[4,896,128]{2,1,0:T(8,128)(2,1)S(1)} %pad_maximum_fusion), channel_id=1, source_target_pairs={{0,1},{1,0},{2,3},{3,2},{4,5},{5,4},{6,7},{7,6},{8,9},{9,8},{10,11... | collective-permute-start | bytes 2752520 | tf_op jit(solution)/shard_map/ppermute | solution.py:39
  148.2 2.1 collective-permute-done.9
  150.2 0.2 maximum_bitcast_fusion
  150.4 2.6 %copy.16 = bf16[896,4,2,128]{0,3,2,1:T(8,128)(2,1)} copy(bf16[896,4,2,128]{3,0,1,2:T(8,128)(2,1)S(1)} %maximum_bitcast_fusion) | data formatting | bytes 3670016 | tf_op jit(solution)/shard_map/transpose | solution.py:183
  153.0 15.2 %all-to-all-done.2 = bf16[8,112,512]{2,1,0:T(8,128)(2,1)} async-done(((bf16[8,112,512]{2,1,0:T(8,128)(2,1)}), bf16[8,112,512]{2,1,0:T(8,128)(2,1)}, u32[]{:S(2)}, u32[]{:S(2)}) %all-to-all-start.2) | async-done | bytes 917536 | tf_op jit(solution)/shard_map/all_to_all | solution.py:25
  168.2 3.1 %convolution_convert_fusion = bf16[512,1024]{1,0:T(8,128)(2,1)S(1)} fusion(bf16[896,512]{1,0:T(8,128)(2,1)} %bitcast.19, bf16[896,1024]{0,1:T(8,128)(2,1)} %bitcast.46), kind=kOutput, calls=%fused_computation.6 | convolution fusion | flops 940048384 | bytes 3801088 | tf_op jit(solution)/shard_map/dot_general | solution.py:187
  171.3 21.8 %all_to_all.25.parts = bf16[8,64,1024]{2,1,0:T(8,128)(2,1)S(1)} all-to-all(bf16[8,64,1024]{2,1,0:T(8,128)(2,1)S(1)} %bitcast.47), channel_id=1, replica_groups=mesh['y'=4,'xh'=2,'xl'=2,'zh'=4,'zm'=2,'z0'=2,'core'=2] {'y','xh'}, dimensions={0} | all-to-all | bytes 2097152 | tf_op jit(solution)/shard_map/all_to_all | solution.py:25
  193.1 1.3 shard_map.57
  194.4 9.4 %all-to-all-start.4 = ((bf16[8,64,128]{2,1,0:T(8,128)(2,1)}), bf16[8,64,128]{2,1,0:T(8,128)(2,1)S(1)}, u32[]{:S(2)}, u32[]{:S(2)}) async-start(bf16[8,64,128]{2,1,0:T(8,128)(2,1)} %shard_map.57), calls=%async_computation.4 | async-start | bytes 262144 | tf_op jit(solution)/shard_map/all_to_all | solution.py:25
  203.8 13.6 %all-to-all-done.4 = bf16[8,64,128]{2,1,0:T(8,128)(2,1)S(1)} async-done(((bf16[8,64,128]{2,1,0:T(8,128)(2,1)}), bf16[8,64,128]{2,1,0:T(8,128)(2,1)S(1)}, u32[]{:S(2)}, u32[]{:S(2)}) %all-to-all-start.4) | async-done | bytes 131104 | tf_op jit(solution)/shard_map/all_to_all | solution.py:25
  217.4 1.4 add_convert_fusion
  (3 shorter events, 0.1 us)
Async XLA Ops:
  7.7 34.7 %all-to-all-start = ((bf16[8,112,1024]{2,1,0:T(8,128)(2,1)}), bf16[8,112,1024]{2,1,0:T(8,128)(2,1)S(1)}, u32[]{:S(2)}, u32[]{:S(2)}) async-start(bf16[8,112,1024]{2,1,0:T(8,128)(2,1)} %reshape.50), calls=%async_computation | async-start | bytes 3670016 | tf_op jit(solution)/shard_map/all_to_all | solution.py:25
  15.2 21.7 %collective-permute-start = (bf16[528,128]{1,0:T(8,128)(2,1)S(1)}, bf16[528,128]{1,0:T(8,128)(2,1)S(1)}, u32[]{:S(2)}, u32[]{:S(2)}) collective-permute-start(bf16[528,128]{1,0:T(8,128)(2,1)S(1)} %get-tuple-element.15), channel_id=1, source_target_pairs={{0,0},{1,1},{2,2},{3,3},{4,92},{5,93},{6,94},{7,95},{8,152},{9,153... | collective-permute-start | bytes 405512 | tf_op jit(solution)/shard_map/ppermute | solution.py:39
  15.9 26.5 %collective-permute-start.1 = (bf16[528,128]{1,0:T(8,128)(2,1)S(1)}, bf16[528,128]{1,0:T(8,128)(2,1)S(1)}, u32[]{:S(2)}, u32[]{:S(2)}) collective-permute-start(bf16[528,128]{1,0:T(8,128)(2,1)S(1)} %get-tuple-element.16), channel_id=1, source_target_pairs={{0,17},{1,16},{2,19},{3,18},{4,77},{5,76},{6,79},{7,78},{8,137},{9... | collective-permute-start | bytes 405512 | tf_op jit(solution)/shard_map/ppermute | solution.py:39
  42.4 21.0 %collective-permute-start.5 = (bf16[8,112,1024]{2,1,0:T(8,128)(2,1)S(1)}, bf16[8,112,1024]{2,1,0:T(8,128)(2,1)}, u32[]{:S(2)}, u32[]{:S(2)}) collective-permute-start(bf16[8,112,1024]{2,1,0:T(8,128)(2,1)S(1)} %all-to-all-done.w_own), channel_id=1, source_target_pairs={{0,1},{1,0},{2,3},{3,2},{4,5},{5,4},{6,7},{7,6},{8,9},{9,8},{10,11... | collective-permute-start | bytes 5505032 | tf_op jit(solution)/shard_map/ppermute | solution.py:39
  44.4 10.6 %collective-permute-start.2 = (bf16[2,528,128]{2,1,0:T(8,128)(2,1)S(1)}, bf16[2,528,128]{2,1,0:T(8,128)(2,1)S(1)}, u32[]{:S(2)}, u32[]{:S(2)}) collective-permute-start(bf16[2,528,128]{2,1,0:T(8,128)(2,1)S(1)} %pad_maximum_fusion.1.x0), channel_id=1, source_target_pairs={{0,2},{1,3},{2,0},{3,1},{4,6},{5,7},{6,4},{7,5},{8,10},{9,11},{10,... | collective-permute-start | bytes 811016 | tf_op jit(solution)/shard_map/ppermute | solution.py:39
  48.6 14.9 %collective-permute-start.3 = (bf16[2,528,128]{2,1,0:T(8,128)(2,1)S(1)}, bf16[2,528,128]{2,1,0:T(8,128)(2,1)S(1)}, u32[]{:S(2)}, u32[]{:S(2)}) collective-permute-start(bf16[2,528,128]{2,1,0:T(8,128)(2,1)S(1)} %pad_maximum_fusion.1.x0), channel_id=1, source_target_pairs={{0,32},{1,33},{2,34},{3,35},{4,36},{5,37},{6,38},{7,39},{8,40},{9,... | collective-permute-start | bytes 811016 | tf_op jit(solution)/shard_map/ppermute | solution.py:39
  50.9 12.6 %collective-permute-start.4 = (bf16[2,528,128]{2,1,0:T(8,128)(2,1)S(1)}, bf16[2,528,128]{2,1,0:T(8,128)(2,1)S(1)}, u32[]{:S(2)}, u32[]{:S(2)}) collective-permute-start(bf16[2,528,128]{2,1,0:T(8,128)(2,1)S(1)} %pad_maximum_fusion.1.x0), channel_id=1, source_target_pairs={{0,34},{1,35},{2,32},{3,33},{4,38},{5,39},{6,36},{7,37},{8,42},{9,... | collective-permute-start | bytes 811016 | tf_op jit(solution)/shard_map/ppermute | solution.py:39
  67.8 1.3 copy-start
  69.0 44.5 %all-to-all-start.1 = ((bf16[8,2,112,512]{3,2,1,0:T(8,128)(2,1)}), bf16[8,2,112,512]{3,2,1,0:T(8,128)(2,1)S(1)}, u32[]{:S(2)}, u32[]{:S(2)}) async-start(bf16[8,2,112,512]{3,2,1,0:T(8,128)(2,1)} %copy-done), calls=%async_computation.1 | async-start | bytes 3670016 | tf_op jit(solution)/shard_map/all_to_all | solution.py:25
  84.4 19.7 %collective-permute-start.8 = (bf16[896,128]{1,0:T(8,128)(2,1)S(1)}, bf16[896,128]{1,0:T(8,128)(2,1)S(1)}, u32[]{:S(2)}, u32[]{:S(2)}) collective-permute-start(bf16[896,128]{1,0:T(8,128)(2,1)S(1)} %bitcast.61), channel_id=1, source_target_pairs={{0,24},{1,25},{2,26},{3,27},{4,28},{5,29},{6,30},{7,31},{8,0},{9,1... | collective-permute-start | bytes 688136 | tf_op jit(solution)/shard_map/ppermute | solution.py:39
  88.4 18.0 %collective-permute-start.7 = (bf16[896,128]{1,0:T(8,128)(2,1)S(1)}, bf16[896,128]{1,0:T(8,128)(2,1)S(1)}, u32[]{:S(2)}, u32[]{:S(2)}) collective-permute-start(bf16[896,128]{1,0:T(8,128)(2,1)S(1)} %bitcast.60), channel_id=1, source_target_pairs={{0,16},{1,17},{2,18},{3,19},{4,20},{5,21},{6,22},{7,23},{8,24},{9,... | collective-permute-start | bytes 688136 | tf_op jit(solution)/shard_map/ppermute | solution.py:39
  94.4 19.0 %collective-permute-start.6 = (bf16[896,128]{1,0:T(8,128)(2,1)S(1)}, bf16[896,128]{1,0:T(8,128)(2,1)S(1)}, u32[]{:S(2)}, u32[]{:S(2)}) collective-permute-start(bf16[896,128]{1,0:T(8,128)(2,1)S(1)} %bitcast.59), channel_id=1, source_target_pairs={{0,8},{1,9},{2,10},{3,11},{4,12},{5,13},{6,14},{7,15},{8,16},{9,17... | collective-permute-start | bytes 688136 | tf_op jit(solution)/shard_map/ppermute | solution.py:39
  115.3 52.9 %all-to-all-start.2 = ((bf16[8,112,512]{2,1,0:T(8,128)(2,1)}), bf16[8,112,512]{2,1,0:T(8,128)(2,1)}, u32[]{:S(2)}, u32[]{:S(2)}) async-start(bf16[8,112,512]{2,1,0:T(8,128)(2,1)} %bitcast.18), calls=%async_computation.2 | async-start | bytes 1835008 | tf_op jit(solution)/shard_map/all_to_all | solution.py:25
  145.4 4.8 %collective-permute-start.9 = (bf16[4,896,128]{2,1,0:T(8,128)(2,1)S(1)}, bf16[4,896,128]{2,1,0:T(8,128)(2,1)S(1)}, u32[]{:S(2)}, u32[]{:S(2)}) collective-permute-start(bf16[4,896,128]{2,1,0:T(8,128)(2,1)S(1)} %pad_maximum_fusion), channel_id=1, source_target_pairs={{0,1},{1,0},{2,3},{3,2},{4,5},{5,4},{6,7},{7,6},{8,9},{9,8},{10,11... | collective-permute-start | bytes 2752520 | tf_op jit(solution)/shard_map/ppermute | solution.py:39
  194.4 22.9 %all-to-all-start.4 = ((bf16[8,64,128]{2,1,0:T(8,128)(2,1)}), bf16[8,64,128]{2,1,0:T(8,128)(2,1)S(1)}, u32[]{:S(2)}, u32[]{:S(2)}) async-start(bf16[8,64,128]{2,1,0:T(8,128)(2,1)} %shard_map.57), calls=%async_computation.4 | async-start | bytes 262144 | tf_op jit(solution)/shard_map/all_to_all | solution.py:25

commit v3 on v2

--- a/solution.py
+++ b/solution.py
@@ -152,15 +152,17 @@
     mine, yours, gate_weight, up_weight = lax.optimization_barrier(
         (half(core), half(1 - core), gate_weight, up_weight)
     )
+    first = send(mine, spread(0, 0))
+    second = send(yours, spread(4, 1))
     both = jnp.stack((gate_weight, up_weight))
     both = jnp.pad(both, ((0, 0), (0, 56 - units), (0, 0))).reshape(112, 2, 8, 512)
-    own_w = exchange(both.transpose(2, 0, 1, 3).reshape(8, 112, 1024), PHASE)
-    first = send(mine, spread(0, 0))
-    second = send(yours, spread(4, 1))
-    first, second, own_w = lax.optimization_barrier((first, second, own_w))
-    other_w = send(own_w, shift(core=1))
+    both = both.transpose(2, 0, 1, 3).reshape(8, 112, 1024)
+    first, second, both = lax.optimization_barrier((first, second, both))
+    own_w = exchange(both, PHASE)
     held = jnp.stack((first, second))
     blocks = [held] + [send(held, shift(xl=i, z0=j)) for i, j in ((0, 1), (1, 0), (1, 1))]
+    *blocks, own_w = lax.optimization_barrier((*blocks, own_w))
+    other_w = send(own_w, shift(core=1))
 
     down, _ = lax.optimization_barrier((down_weight, held))
     down = down.reshape(2, 4, 8, units, LANES)
@@ -170,7 +172,7 @@
         part = lax.dynamic_slice_in_dim(down, (far + count) % 4, 1, 1).reshape(896, LANES)
         return send(part, shift(zh=count)) if count else part
 
-    own_d = jnp.stack([quarter(count) for count in range(4)])
+    quarters = [quarter(count) for count in range(4)]
     sums = run(
         sums_kernel,
         (8, 2, 112, rows),
@@ -178,7 +180,9 @@
         (pltpu.VMEM((rows, 1024), bf16),),
         flops=2 * 1792 * 1024 * rows,
     )
-    sums, own_d = lax.optimization_barrier((exchange(sums, PHASE), own_d))
+    sums, quarters[1], quarters[3] = lax.optimization_barrier((sums, quarters[1], quarters[3]))
+    sums, quarters[2] = lax.optimization_barrier((exchange(sums, PHASE), quarters[2]))
+    own_d = jnp.stack(quarters)
     other_d = send(own_d, shift(core=1))
     d_all = jnp.stack((own_d, other_d), 1).transpose(2, 0, 1, 3).reshape(896, 1024)
 

time: 220 us -> 226 us (1.027)
  waiting for transfers between devices: 59.8 us -> 89 us
  starting transfers between devices: 112 us -> 84.5 us
  local copies, waits for them, and re-layouts: 11.2 us -> 14.7 us
    ppermute x10, waiting for transfers between devices: 31 us -> 57.3 us  [send(): return lax.ppermute(value, AXES, route(move))]
    all_to_all x4, starting transfers between devices: 61 us -> 36.9 us  [exchange(): return lax.all_to_all(value, axes, 0, 0, tiled=True)]
    ppermute x10, starting transfers between devices: 50.8 us -> 47.6 us  [send(): return lax.ppermute(value, AXES, route(move))]
    all_to_all x4, waiting for transfers between devices: 28.8 us -> 31.7 us  [exchange(): return lax.all_to_all(value, axes, 0, 0, tiled=True)]
  transfers between devices with their start and end apart: 14 -> 14, of which waited for: 9 -> 8; matrix products, arithmetic and copies ran while one was open for 2% -> 6% of each run, Pallas kernels for 0% -> 2%
where the time goes in v3:
time: 226 us; the launch traced here: 225 us
  waiting for transfers between devices  89 us (39%)
  starting transfers between devices  84.5 us (37%)
  blocking collectives  22 us (10%)
  local copies, waits for them, and re-layouts  14.7 us (7%)
  Pallas kernels  7.45 us (3%)
  other arithmetic  4.42 us (2%)
  matrix products  3.08 us (1%)
    ppermute x10, waiting for transfers between devices, send(): return lax.ppermute(value, AXES, route(move))  57.3 us
    ppermute x10, starting transfers between devices, send(): return lax.ppermute(value, AXES, route(move))  47.6 us
    all_to_all x4, starting transfers between devices, exchange(): return lax.all_to_all(value, axes, 0, 0, tiled=True)  36.9 us
    all_to_all x4, waiting for transfers between devices, exchange(): return lax.all_to_all(value, axes, 0, 0, tiled=True)  31.7 us
    all_to_all x1, blocking collectives, exchange(): return lax.all_to_all(value, axes, 0, 0, tiled=True)  22 us
    pallas_call x3, Pallas kernels, run(): pl.pallas_call(kernel, out_shape=jax.ShapeDtypeStruct(out_shape, bf16), i...  7.45 us
  transfers between devices with their start and end apart: 14, of which 8 were waited for; matrix products, arithmetic and copies ran while one was open for 6% of the time, Pallas kernels for 2%

profile of v3, /device:TPU:1, one launch (start us, length us, event | category | flops | bytes accessed | tf_op | source)
XLA Modules:
  0.0 225.4 jit_solution(4780403630157618625)
XLA Ops:
  0.0 1.0 constant_dynamic-slice_fusion
  1.0 0.7 broadcast_in_dim.2
  1.7 0.7 collective-permute-start
  2.4 21.3 %collective-permute-start.1 = (bf16[528,128]{1,0:T(8,128)(2,1)S(1)}, bf16[528,128]{1,0:T(8,128)(2,1)S(1)}, u32[]{:S(2)}, u32[]{:S(2)}) collective-permute-start(bf16[528,128]{1,0:T(8,128)(2,1)S(1)} %get-tuple-element.24), channel_id=1, source_target_pairs={{0,17},{1,16},{2,19},{3,18},{4,77},{5,76},{6,79},{7,78},{8,137},{9... | collective-permute-start | bytes 405512 | tf_op jit(solution)/shard_map/ppermute | solution.py:39
  23.6 1.6 fusion.2
  25.3 0.7 copy.19
  26.0 1.4 copy.21
  27.4 2.3 %reshape.50 = bf16[8,112,1024]{2,1,0:T(8,128)(2,1)} reshape(bf16[8,112,2,512]{3,2,1,0:T(2,128)(2,1)S(1)} %bitcast.44) | data formatting | bytes 3670016 | tf_op jit(solution)/shard_map/reshape | solution.py:159
  29.6 0.0 collective-permute-done
  29.6 0.0 collective-permute-done.1
  29.7 13.3 %all-to-all-start = ((bf16[8,112,1024]{2,1,0:T(8,128)(2,1)}), bf16[8,112,1024]{2,1,0:T(8,128)(2,1)S(1)}, u32[]{:S(2)}, u32[]{:S(2)}) async-start(bf16[8,112,1024]{2,1,0:T(8,128)(2,1)} %reshape.50), calls=%async_computation | async-start | bytes 3670016 | tf_op jit(solution)/shard_map/all_to_all | solution.py:25
  43.0 1.9 collective-permute-start.2
  44.9 3.1 %collective-permute-start.3 = (bf16[2,528,128]{2,1,0:T(8,128)(2,1)S(1)}, bf16[2,528,128]{2,1,0:T(8,128)(2,1)S(1)}, u32[]{:S(2)}, u32[]{:S(2)}) collective-permute-start(bf16[2,528,128]{2,1,0:T(8,128)(2,1)S(1)} %pad_maximum_fusion.1.x0), channel_id=1, source_target_pairs={{0,32},{1,33},{2,34},{3,35},{4,36},{5,37},{6,38},{7,39},{8,40},{9,... | collective-permute-start | bytes 811016 | tf_op jit(solution)/shard_map/ppermute | solution.py:39
  48.0 3.3 %collective-permute-start.4 = (bf16[2,528,128]{2,1,0:T(8,128)(2,1)S(1)}, bf16[2,528,128]{2,1,0:T(8,128)(2,1)S(1)}, u32[]{:S(2)}, u32[]{:S(2)}) collective-permute-start(bf16[2,528,128]{2,1,0:T(8,128)(2,1)S(1)} %pad_maximum_fusion.1.x0), channel_id=1, source_target_pairs={{0,34},{1,35},{2,32},{3,33},{4,38},{5,39},{6,36},{7,37},{8,42},{9,... | collective-permute-start | bytes 811016 | tf_op jit(solution)/shard_map/ppermute | solution.py:39
  51.4 0.5 collective-permute-done.2.x1
  51.9 23.8 %collective-permute-done.3.x2 = bf16[2,528,128]{2,1,0:T(8,128)(2,1)S(1)} collective-permute-done((bf16[2,528,128]{2,1,0:T(8,128)(2,1)S(1)}, bf16[2,528,128]{2,1,0:T(8,128)(2,1)S(1)}, u32[]{:S(2)}, u32[]{:S(2)}) %collective-permute-start.3) | collective-permute-done | bytes 270368 | tf_op jit(solution)/shard_map/ppermute | solution.py:39
  75.7 0.0 collective-permute-done.4.x3
  75.7 0.0 all-to-all-done.w_own
  75.7 3.5 %collective-permute-start.5 = (bf16[8,112,1024]{2,1,0:T(8,128)(2,1)S(1)}, bf16[8,112,1024]{2,1,0:T(8,128)(2,1)}, u32[]{:S(2)}, u32[]{:S(2)}) collective-permute-start(bf16[8,112,1024]{2,1,0:T(8,128)(2,1)S(1)} %all-to-all-done.w_own), channel_id=1, source_target_pairs={{0,1},{1,0},{2,3},{3,2},{4,5},{5,4},{6,7},{7,6},{8,9},{9,8},{10,11... | collective-permute-start | bytes 5505032 | tf_op jit(solution)/shard_map/ppermute | solution.py:39
  79.2 2.1 reshape.51
  81.3 2.1 pad_dynamic-slice_fusion
  83.4 2.2 collective-permute-start.6
  85.6 7.0 %collective-permute-start.7 = (bf16[896,128]{1,0:T(8,128)(2,1)S(1)}, bf16[896,128]{1,0:T(8,128)(2,1)}, u32[]{:S(2)}, u32[]{:S(2)}) collective-permute-start(bf16[896,128]{1,0:T(8,128)(2,1)S(1)} %bitcast.58), channel_id=1, source_target_pairs={{0,24},{1,25},{2,26},{3,27},{4,28},{5,29},{6,30},{7,31},{8,0},{9,1... | collective-permute-start | bytes 688136 | tf_op jit(solution)/shard_map/ppermute | solution.py:39
  92.6 0.1 pad_add_fusion.at
  92.7 0.0 collective-permute-done.5.w_other
  92.7 4.3 %shard_map.55 = bf16[8,2,112,512]{3,2,1,0:T(8,128)(2,1)S(1)} custom-call(s32[3]{0:T(128)S(1)} %pad_add_fusion.at, bf16[2,528,128]{2,1,0:T(8,128)(2,1)S(1)} %pad_maximum_fusion.1.x0, bf16[2,528,128]{2,1,0:T(8,128)(2,1)S(1)} %collective-permute-done.2.x1, bf16[2,528,128]{2,1,0:T(8,128)(2,1)S(1)} %collective-permute-done.3.x2, ...), custom_call_target="tpu_custom_call" | custom-call | flops 1879048192 | bytes 6586380 | tf_op jit(solution)/shard_map/pallas_call | solution.py:127
  97.0 0.0 copy-start
  97.0 1.2 copy-done
  98.2 0.0 copy-start.1
  98.2 13.0 %collective-permute-done.6 = bf16[896,128]{1,0:T(8,128)(2,1)S(1)} collective-permute-done((bf16[896,128]{1,0:T(8,128)(2,1)S(1)}, bf16[896,128]{1,0:T(8,128)(2,1)S(1)}, u32[]{:S(2)}, u32[]{:S(2)}) %collective-permute-start.6) | collective-permute-done | bytes 229408 | tf_op jit(solution)/shard_map/ppermute | solution.py:39
  111.2 0.0 collective-permute-done.7
  111.2 7.4 %all-to-all-start.1 = ((bf16[8,2,112,512]{3,2,1,0:T(8,128)(2,1)}), bf16[8,2,112,512]{3,2,1,0:T(8,128)(2,1)S(1)}, u32[]{:S(2)}, u32[]{:S(2)}) async-start(bf16[8,2,112,512]{3,2,1,0:T(8,128)(2,1)} %copy-done), calls=%async_computation.1 | async-start | bytes 3670016 | tf_op jit(solution)/shard_map/all_to_all | solution.py:25
  118.6 0.0 copy-done.1
  118.6 1.9 collective-permute-start.8
  120.5 18.0 %collective-permute-done.8 = bf16[896,128]{1,0:T(8,128)(2,1)S(1)} collective-permute-done((bf16[896,128]{1,0:T(8,128)(2,1)S(1)}, bf16[896,128]{1,0:T(8,128)(2,1)S(1)}, u32[]{:S(2)}, u32[]{:S(2)}) %collective-permute-start.8) | collective-permute-done | bytes 229408 | tf_op jit(solution)/shard_map/ppermute | solution.py:39
  138.5 0.0 copy-start.2
  138.5 0.7 copy-done.2
  139.2 4.0 %all-to-all-done.1.sums = bf16[8,2,112,512]{3,2,1,0:T(8,128)(2,1)S(1)} async-done(((bf16[8,2,112,512]{3,2,1,0:T(8,128)(2,1)}), bf16[8,2,112,512]{3,2,1,0:T(8,128)(2,1)S(1)}, u32[]{:S(2)}, u32[]{:S(2)}) %all-to-all-start.1) | async-done | bytes 1835040 | tf_op jit(solution)/shard_map/all_to_all | solution.py:25
  143.2 1.8 shard_map.56
  145.0 0.0 copy-start.3
  145.0 9.7 %all-to-all-start.2 = ((bf16[8,112,512]{2,1,0:T(8,128)(2,1)}), bf16[8,112,512]{2,1,0:T(8,128)(2,1)}, u32[]{:S(2)}, u32[]{:S(2)}) async-start(bf16[8,112,512]{2,1,0:T(8,128)(2,1)} %bitcast.14), calls=%async_computation.2 | async-start | bytes 1835008 | tf_op jit(solution)/shard_map/all_to_all | solution.py:25
  154.7 0.0 copy-done.3
  154.7 1.1 fusion.3
  155.8 2.7 %collective-permute-start.9 = (bf16[4,896,128]{2,1,0:T(8,128)(2,1)S(1)}, bf16[4,896,128]{2,1,0:T(8,128)(2,1)S(1)}, u32[]{:S(2)}, u32[]{:S(2)}) collective-permute-start(bf16[4,896,128]{2,1,0:T(8,128)(2,1)S(1)} %get-tuple-element.42), channel_id=1, source_target_pairs={{0,1},{1,0},{2,3},{3,2},{4,5},{5,4},{6,7},{7,6},{8,9},{9,8},{10,11... | collective-permute-start | bytes 2752520 | tf_op jit(solution)/shard_map/ppermute | solution.py:39
  158.5 2.1 collective-permute-done.9
  160.6 0.2 maximum_bitcast_fusion
  160.8 2.6 %copy.16 = bf16[896,4,2,128]{0,3,2,1:T(8,128)(2,1)} copy(bf16[896,4,2,128]{3,0,1,2:T(8,128)(2,1)S(1)} %maximum_bitcast_fusion) | data formatting | bytes 3670016 | tf_op jit(solution)/shard_map/transpose | solution.py:187
  163.4 14.2 %all-to-all-done.2 = bf16[8,112,512]{2,1,0:T(8,128)(2,1)} async-done(((bf16[8,112,512]{2,1,0:T(8,128)(2,1)}), bf16[8,112,512]{2,1,0:T(8,128)(2,1)}, u32[]{:S(2)}, u32[]{:S(2)}) %all-to-all-start.2) | async-done | bytes 917536 | tf_op jit(solution)/shard_map/all_to_all | solution.py:25
  177.6 3.1 %convolution_convert_fusion = bf16[512,1024]{1,0:T(8,128)(2,1)S(1)} fusion(bf16[896,512]{1,0:T(8,128)(2,1)} %bitcast.15, bf16[896,1024]{0,1:T(8,128)(2,1)} %bitcast.46), kind=kOutput, calls=%fused_computation.6 | convolution fusion | flops 940048384 | bytes 3801088 | tf_op jit(solution)/shard_map/dot_general | solution.py:191
  180.7 22.0 %all_to_all.25.parts = bf16[8,64,1024]{2,1,0:T(8,128)(2,1)S(1)} all-to-all(bf16[8,64,1024]{2,1,0:T(8,128)(2,1)S(1)} %bitcast.47), channel_id=1, replica_groups=mesh['y'=4,'xh'=2,'xl'=2,'zh'=4,'zm'=2,'z0'=2,'core'=2] {'y','xh'}, dimensions={0} | all-to-all | bytes 2097152 | tf_op jit(solution)/shard_map/all_to_all | solution.py:25
  202.6 1.3 shard_map.57
  204.0 6.5 %all-to-all-start.4 = ((bf16[8,64,128]{2,1,0:T(8,128)(2,1)}), bf16[8,64,128]{2,1,0:T(8,128)(2,1)S(1)}, u32[]{:S(2)}, u32[]{:S(2)}) async-start(bf16[8,64,128]{2,1,0:T(8,128)(2,1)} %shard_map.57), calls=%async_computation.4 | async-start | bytes 262144 | tf_op jit(solution)/shard_map/all_to_all | solution.py:25
  210.4 13.5 %all-to-all-done.4 = bf16[8,64,128]{2,1,0:T(8,128)(2,1)S(1)} async-done(((bf16[8,64,128]{2,1,0:T(8,128)(2,1)}), bf16[8,64,128]{2,1,0:T(8,128)(2,1)S(1)}, u32[]{:S(2)}, u32[]{:S(2)}) %all-to-all-start.4) | async-done | bytes 131104 | tf_op jit(solution)/shard_map/all_to_all | solution.py:25
  224.0 1.4 add_convert_fusion
  (3 shorter events, 0.1 us)
Async XLA Ops:
  1.7 28.0 %collective-permute-start = (bf16[528,128]{1,0:T(8,128)(2,1)S(1)}, bf16[528,128]{1,0:T(8,128)(2,1)S(1)}, u32[]{:S(2)}, u32[]{:S(2)}) collective-permute-start(bf16[528,128]{1,0:T(8,128)(2,1)S(1)} %get-tuple-element.23), channel_id=1, source_target_pairs={{0,0},{1,1},{2,2},{3,3},{4,92},{5,93},{6,94},{7,95},{8,152},{9,153... | collective-permute-start | bytes 405512 | tf_op jit(solution)/shard_map/ppermute | solution.py:39
  2.4 27.3 %collective-permute-start.1 = (bf16[528,128]{1,0:T(8,128)(2,1)S(1)}, bf16[528,128]{1,0:T(8,128)(2,1)S(1)}, u32[]{:S(2)}, u32[]{:S(2)}) collective-permute-start(bf16[528,128]{1,0:T(8,128)(2,1)S(1)} %get-tuple-element.24), channel_id=1, source_target_pairs={{0,17},{1,16},{2,19},{3,18},{4,77},{5,76},{6,79},{7,78},{8,137},{9... | collective-permute-start | bytes 405512 | tf_op jit(solution)/shard_map/ppermute | solution.py:39
  29.7 46.0 %all-to-all-start = ((bf16[8,112,1024]{2,1,0:T(8,128)(2,1)}), bf16[8,112,1024]{2,1,0:T(8,128)(2,1)S(1)}, u32[]{:S(2)}, u32[]{:S(2)}) async-start(bf16[8,112,1024]{2,1,0:T(8,128)(2,1)} %reshape.50), calls=%async_computation | async-start | bytes 3670016 | tf_op jit(solution)/shard_map/all_to_all | solution.py:25
  43.0 8.9 %collective-permute-start.2 = (bf16[2,528,128]{2,1,0:T(8,128)(2,1)S(1)}, bf16[2,528,128]{2,1,0:T(8,128)(2,1)S(1)}, u32[]{:S(2)}, u32[]{:S(2)}) collective-permute-start(bf16[2,528,128]{2,1,0:T(8,128)(2,1)S(1)} %pad_maximum_fusion.1.x0), channel_id=1, source_target_pairs={{0,2},{1,3},{2,0},{3,1},{4,6},{5,7},{6,4},{7,5},{8,10},{9,11},{10,... | collective-permute-start | bytes 811016 | tf_op jit(solution)/shard_map/ppermute | solution.py:39
  44.9 30.8 %collective-permute-start.3 = (bf16[2,528,128]{2,1,0:T(8,128)(2,1)S(1)}, bf16[2,528,128]{2,1,0:T(8,128)(2,1)S(1)}, u32[]{:S(2)}, u32[]{:S(2)}) collective-permute-start(bf16[2,528,128]{2,1,0:T(8,128)(2,1)S(1)} %pad_maximum_fusion.1.x0), channel_id=1, source_target_pairs={{0,32},{1,33},{2,34},{3,35},{4,36},{5,37},{6,38},{7,39},{8,40},{9,... | collective-permute-start | bytes 811016 | tf_op jit(solution)/shard_map/ppermute | solution.py:39
  48.0 27.6 %collective-permute-start.4 = (bf16[2,528,128]{2,1,0:T(8,128)(2,1)S(1)}, bf16[2,528,128]{2,1,0:T(8,128)(2,1)S(1)}, u32[]{:S(2)}, u32[]{:S(2)}) collective-permute-start(bf16[2,528,128]{2,1,0:T(8,128)(2,1)S(1)} %pad_maximum_fusion.1.x0), channel_id=1, source_target_pairs={{0,34},{1,35},{2,32},{3,33},{4,38},{5,39},{6,36},{7,37},{8,42},{9,... | collective-permute-start | bytes 811016 | tf_op jit(solution)/shard_map/ppermute | solution.py:39
  75.7 17.0 %collective-permute-start.5 = (bf16[8,112,1024]{2,1,0:T(8,128)(2,1)S(1)}, bf16[8,112,1024]{2,1,0:T(8,128)(2,1)}, u32[]{:S(2)}, u32[]{:S(2)}) collective-permute-start(bf16[8,112,1024]{2,1,0:T(8,128)(2,1)S(1)} %all-to-all-done.w_own), channel_id=1, source_target_pairs={{0,1},{1,0},{2,3},{3,2},{4,5},{5,4},{6,7},{7,6},{8,9},{9,8},{10,11... | collective-permute-start | bytes 5505032 | tf_op jit(solution)/shard_map/ppermute | solution.py:39
  83.4 27.8 %collective-permute-start.6 = (bf16[896,128]{1,0:T(8,128)(2,1)S(1)}, bf16[896,128]{1,0:T(8,128)(2,1)S(1)}, u32[]{:S(2)}, u32[]{:S(2)}) collective-permute-start(bf16[896,128]{1,0:T(8,128)(2,1)S(1)} %bitcast.59), channel_id=1, source_target_pairs={{0,8},{1,9},{2,10},{3,11},{4,12},{5,13},{6,14},{7,15},{8,16},{9,17... | collective-permute-start | bytes 688136 | tf_op jit(solution)/shard_map/ppermute | solution.py:39
  85.6 25.6 %collective-permute-start.7 = (bf16[896,128]{1,0:T(8,128)(2,1)S(1)}, bf16[896,128]{1,0:T(8,128)(2,1)}, u32[]{:S(2)}, u32[]{:S(2)}) collective-permute-start(bf16[896,128]{1,0:T(8,128)(2,1)S(1)} %bitcast.58), channel_id=1, source_target_pairs={{0,24},{1,25},{2,26},{3,27},{4,28},{5,29},{6,30},{7,31},{8,0},{9,1... | collective-permute-start | bytes 688136 | tf_op jit(solution)/shard_map/ppermute | solution.py:39
  97.0 1.2 copy-start
  98.2 20.4 %copy-start.1 = (bf16[2,1,8,56,128]{4,3,2,1,0:T(8,128)(2,1)S(1)}, bf16[2,1,8,56,128]{4,3,2,1,0:T(8,128)(2,1)}, u32[]{:S(2)}) copy-start(bf16[2,1,8,56,128]{4,3,2,1,0:T(8,128)(2,1)} %get-tuple-element.45) | copy-start | bytes 688132
  111.2 32.0 %all-to-all-start.1 = ((bf16[8,2,112,512]{3,2,1,0:T(8,128)(2,1)}), bf16[8,2,112,512]{3,2,1,0:T(8,128)(2,1)S(1)}, u32[]{:S(2)}, u32[]{:S(2)}) async-start(bf16[8,2,112,512]{3,2,1,0:T(8,128)(2,1)} %copy-done), calls=%async_computation.1 | async-start | bytes 3670016 | tf_op jit(solution)/shard_map/all_to_all | solution.py:25
  118.6 19.9 %collective-permute-start.8 = (bf16[896,128]{1,0:T(8,128)(2,1)S(1)}, bf16[896,128]{1,0:T(8,128)(2,1)S(1)}, u32[]{:S(2)}, u32[]{:S(2)}) collective-permute-start(bf16[896,128]{1,0:T(8,128)(2,1)S(1)} %bitcast.57), channel_id=1, source_target_pairs={{0,16},{1,17},{2,18},{3,19},{4,20},{5,21},{6,22},{7,23},{8,24},{9,... | collective-permute-start | bytes 688136 | tf_op jit(solution)/shard_map/ppermute | solution.py:39
  138.5 0.7 copy-start.2
  145.0 9.7 %copy-start.3 = (bf16[896,128]{1,0:T(8,128)(2,1)S(1)}, bf16[896,128]{1,0:T(8,128)(2,1)}, u32[]{:S(2)}) copy-start(bf16[896,128]{1,0:T(8,128)(2,1)} %copy-done.2) | copy-start | bytes 688132
  145.0 32.5 %all-to-all-start.2 = ((bf16[8,112,512]{2,1,0:T(8,128)(2,1)}), bf16[8,112,512]{2,1,0:T(8,128)(2,1)}, u32[]{:S(2)}, u32[]{:S(2)}) async-start(bf16[8,112,512]{2,1,0:T(8,128)(2,1)} %bitcast.14), calls=%async_computation.2 | async-start | bytes 1835008 | tf_op jit(solution)/shard_map/all_to_all | solution.py:25
  155.8 4.8 %collective-permute-start.9 = (bf16[4,896,128]{2,1,0:T(8,128)(2,1)S(1)}, bf16[4,896,128]{2,1,0:T(8,128)(2,1)S(1)}, u32[]{:S(2)}, u32[]{:S(2)}) collective-permute-start(bf16[4,896,128]{2,1,0:T(8,128)(2,1)S(1)} %get-tuple-element.42), channel_id=1, source_target_pairs={{0,1},{1,0},{2,3},{3,2},{4,5},{5,4},{6,7},{7,6},{8,9},{9,8},{10,11... | collective-permute-start | bytes 2752520 | tf_op jit(solution)/shard_map/ppermute | solution.py:39
  204.0 20.0 %all-to-all-start.4 = ((bf16[8,64,128]{2,1,0:T(8,128)(2,1)}), bf16[8,64,128]{2,1,0:T(8,128)(2,1)S(1)}, u32[]{:S(2)}, u32[]{:S(2)}) async-start(bf16[8,64,128]{2,1,0:T(8,128)(2,1)} %shard_map.57), calls=%async_computation.4 | async-start | bytes 262144 | tf_op jit(solution)/shard_map/all_to_all | solution.py:25

commit v4 on v2

--- a/solution.py
+++ b/solution.py
@@ -55,6 +55,14 @@
             to[axis] += count
 
     return move
+
+
+def cut_kernel(at, both, out):
+    del at
+    for group in range(8):
+        for side in (0, 1):
+            start = side * FEAT // 2 + group * 512
+            out[group, :, side * 512 : side * 512 + 512] = both[:, start : start + 512]
 
 
 def sums_kernel(at, x0, x1, x2, x3, w_own, w_other, out, scaled):
@@ -149,14 +157,11 @@
         part = lax.dynamic_slice_in_dim(halves, index, 1, 1).reshape(rows, LANES)
         return jnp.concatenate((part, gain))
 
-    mine, yours, gate_weight, up_weight = lax.optimization_barrier(
-        (half(core), half(1 - core), gate_weight, up_weight)
-    )
     both = jnp.stack((gate_weight, up_weight))
-    both = jnp.pad(both, ((0, 0), (0, 56 - units), (0, 0))).reshape(112, 2, 8, 512)
-    own_w = exchange(both.transpose(2, 0, 1, 3).reshape(8, 112, 1024), PHASE)
-    first = send(mine, spread(0, 0))
-    second = send(yours, spread(4, 1))
+    both = jnp.pad(both, ((0, 0), (0, 56 - units), (0, 0))).reshape(112, FEAT)
+    own_w = exchange(run(cut_kernel, (8, 112, 1024), (at, both)), PHASE)
+    first = send(half(core), spread(0, 0))
+    second = send(half(1 - core), spread(4, 1))
     first, second, own_w = lax.optimization_barrier((first, second, own_w))
     other_w = send(own_w, shift(core=1))
     held = jnp.stack((first, second))
@@ -170,7 +175,7 @@
         part = lax.dynamic_slice_in_dim(down, (far + count) % 4, 1, 1).reshape(896, LANES)
         return send(part, shift(zh=count)) if count else part
 
-    own_d = jnp.stack([quarter(count) for count in range(4)])
+    quarters = [quarter(count) for count in range(4)]
     sums = run(
         sums_kernel,
         (8, 2, 112, rows),
@@ -178,7 +183,10 @@
         (pltpu.VMEM((rows, 1024), bf16),),
         flops=2 * 1792 * 1024 * rows,
     )
-    sums, own_d = lax.optimization_barrier((exchange(sums, PHASE), own_d))
+    sums, quarters[1], quarters[3] = lax.optimization_barrier(
+        (exchange(sums, PHASE), quarters[1], quarters[3])
+    )
+    own_d = jnp.stack(quarters)
     other_d = send(own_d, shift(core=1))
     d_all = jnp.stack((own_d, other_d), 1).transpose(2, 0, 1, 3).reshape(896, 1024)
 

time: 220 us -> 217 us (0.986)
  the two profiles are of different devices: /device:TPU:1 before, /device:TPU:64 now
where the time goes in v4:
time: 217 us; the launch traced here: 216 us
  waiting for transfers between devices  94.5 us (44%)
  starting transfers between devices  76.2 us (35%)
  blocking collectives  24.7 us (11%)
  Pallas kernels  8.44 us (4%)
  local copies, waits for them, and re-layouts  5.24 us (2%)
  other arithmetic  3.78 us (2%)
  matrix products  2.82 us (1%)
    ppermute x10, waiting for transfers between devices, send(): return lax.ppermute(value, AXES, route(move))  77.3 us
    ppermute x10, starting transfers between devices, send(): return lax.ppermute(value, AXES, route(move))  52.4 us
    all_to_all x1, blocking collectives, exchange(): return lax.all_to_all(value, axes, 0, 0, tiled=True)  24.7 us
    all_to_all x4, starting transfers between devices, exchange(): return lax.all_to_all(value, axes, 0, 0, tiled=True)  23.8 us
    all_to_all x4, waiting for transfers between devices, exchange(): return lax.all_to_all(value, axes, 0, 0, tiled=True)  17.3 us
    pallas_call x4, Pallas kernels, run(): pl.pallas_call(kernel, out_shape=jax.ShapeDtypeStruct(out_shape, bf16), i...  8.44 us
  transfers between devices with their start and end apart: 14, of which 10 were waited for; matrix products, arithmetic and copies ran while one was open for 2% of the time, Pallas kernels for 0%

profile of v4, /device:TPU:64, one launch (start us, length us, event | category | flops | bytes accessed | tf_op | source)
XLA Modules:
  0.0 215.9 jit_solution(13935571903690546559)
XLA Ops:
  0.0 1.6 fusion.2
  1.6 0.1 pad_add_fusion.at
  1.7 1.9 shard_map.55
  3.7 0.0 copy-start.1
  3.7 0.0 copy-start.4
  3.7 7.1 %all-to-all-start = ((bf16[8,112,1024]{2,1,0:T(8,128)(2,1)}), bf16[8,112,1024]{2,1,0:T(8,128)(2,1)S(1)}, u32[]{:S(2)}, u32[]{:S(2)}) async-start(bf16[8,112,1024]{2,1,0:T(8,128)(2,1)} %shard_map.55), calls=%async_computation | async-start | bytes 3670016 | tf_op jit(solution)/shard_map/all_to_all | solution.py:25
  10.7 0.0 copy-done.1
  10.8 0.0 copy-done.4
  10.8 13.9 %collective-permute-start = (bf16[528,128]{1,0:T(8,128)(2,1)S(1)}, bf16[528,128]{1,0:T(8,128)(2,1)S(1)}, u32[]{:S(2)}, u32[]{:S(2)}) collective-permute-start(bf16[528,128]{1,0:T(8,128)(2,1)S(1)} %get-tuple-element.28), channel_id=1, source_target_pairs={{0,0},{1,1},{2,2},{3,3},{4,92},{5,93},{6,94},{7,95},{8,152},{9,153... | collective-permute-start | bytes 405512 | tf_op jit(solution)/shard_map/ppermute | solution.py:39
  24.7 5.9 %collective-permute-start.1 = (bf16[528,128]{1,0:T(8,128)(2,1)S(1)}, bf16[528,128]{1,0:T(8,128)(2,1)S(1)}, u32[]{:S(2)}, u32[]{:S(2)}) collective-permute-start(bf16[528,128]{1,0:T(8,128)(2,1)S(1)} %get-tuple-element.27), channel_id=1, source_target_pairs={{0,17},{1,16},{2,19},{3,18},{4,77},{5,76},{6,79},{7,78},{8,137},{9... | collective-permute-start | bytes 405512 | tf_op jit(solution)/shard_map/ppermute | solution.py:39
  30.6 2.2 %collective-permute-done = bf16[528,128]{1,0:T(8,128)(2,1)S(1)} collective-permute-done((bf16[528,128]{1,0:T(8,128)(2,1)S(1)}, bf16[528,128]{1,0:T(8,128)(2,1)S(1)}, u32[]{:S(2)}, u32[]{:S(2)}) %collective-permute-start) | collective-permute-done | bytes 135200 | tf_op jit(solution)/shard_map/ppermute | solution.py:39
  32.8 7.8 %collective-permute-done.1 = bf16[528,128]{1,0:T(8,128)(2,1)S(1)} collective-permute-done((bf16[528,128]{1,0:T(8,128)(2,1)S(1)}, bf16[528,128]{1,0:T(8,128)(2,1)S(1)}, u32[]{:S(2)}, u32[]{:S(2)}) %collective-permute-start.1) | collective-permute-done | bytes 135200 | tf_op jit(solution)/shard_map/ppermute | solution.py:39
  40.6 2.5 %all-to-all-done.w_own = bf16[8,112,1024]{2,1,0:T(8,128)(2,1)S(1)} async-done(((bf16[8,112,1024]{2,1,0:T(8,128)(2,1)}), bf16[8,112,1024]{2,1,0:T(8,128)(2,1)S(1)}, u32[]{:S(2)}, u32[]{:S(2)}) %all-to-all-start) | async-done | bytes 1835040 | tf_op jit(solution)/shard_map/all_to_all | solution.py:25
  43.1 1.9 collective-permute-start.5
  45.0 5.9 %collective-permute-start.2 = (bf16[2,528,128]{2,1,0:T(8,128)(2,1)S(1)}, bf16[2,528,128]{2,1,0:T(8,128)(2,1)S(1)}, u32[]{:S(2)}, u32[]{:S(2)}) collective-permute-start(bf16[2,528,128]{2,1,0:T(8,128)(2,1)S(1)} %pad_maximum_fusion.1.x0), channel_id=1, source_target_pairs={{0,2},{1,3},{2,0},{3,1},{4,6},{5,7},{6,4},{7,5},{8,10},{9,11},{10,... | collective-permute-start | bytes 811016 | tf_op jit(solution)/shard_map/ppermute | solution.py:39
  51.0 2.5 %collective-permute-start.3 = (bf16[2,528,128]{2,1,0:T(8,128)(2,1)S(1)}, bf16[2,528,128]{2,1,0:T(8,128)(2,1)S(1)}, u32[]{:S(2)}, u32[]{:S(2)}) collective-permute-start(bf16[2,528,128]{2,1,0:T(8,128)(2,1)S(1)} %pad_maximum_fusion.1.x0), channel_id=1, source_target_pairs={{0,32},{1,33},{2,34},{3,35},{4,36},{5,37},{6,38},{7,39},{8,40},{9,... | collective-permute-start | bytes 811016 | tf_op jit(solution)/shard_map/ppermute | solution.py:39
  53.5 2.8 %collective-permute-start.4 = (bf16[2,528,128]{2,1,0:T(8,128)(2,1)S(1)}, bf16[2,528,128]{2,1,0:T(8,128)(2,1)S(1)}, u32[]{:S(2)}, u32[]{:S(2)}) collective-permute-start(bf16[2,528,128]{2,1,0:T(8,128)(2,1)S(1)} %pad_maximum_fusion.1.x0), channel_id=1, source_target_pairs={{0,34},{1,35},{2,32},{3,33},{4,38},{5,39},{6,36},{7,37},{8,42},{9,... | collective-permute-start | bytes 811016 | tf_op jit(solution)/shard_map/ppermute | solution.py:39
  56.3 1.8 collective-permute-done.2.x1
  58.1 9.2 %collective-permute-done.3.x2 = bf16[2,528,128]{2,1,0:T(8,128)(2,1)S(1)} collective-permute-done((bf16[2,528,128]{2,1,0:T(8,128)(2,1)S(1)}, bf16[2,528,128]{2,1,0:T(8,128)(2,1)S(1)}, u32[]{:S(2)}, u32[]{:S(2)}) %collective-permute-start.3) | collective-permute-done | bytes 270368 | tf_op jit(solution)/shard_map/ppermute | solution.py:39
  67.2 0.0 collective-permute-done.4.x3
  67.2 0.0 collective-permute-done.5.w_other
  67.2 3.3 %shard_map.56 = bf16[8,2,112,512]{3,2,1,0:T(8,128)(2,1)S(1)} custom-call(s32[3]{0:T(128)S(1)} %pad_add_fusion.at, bf16[2,528,128]{2,1,0:T(8,128)(2,1)S(1)} %pad_maximum_fusion.1.x0, bf16[2,528,128]{2,1,0:T(8,128)(2,1)S(1)} %collective-permute-done.2.x1, bf16[2,528,128]{2,1,0:T(8,128)(2,1)S(1)} %collective-permute-done.3.x2, ...), custom_call_target="tpu_custom_call" | custom-call | flops 1879048192 | bytes 6586380 | tf_op jit(solution)/shard_map/pallas_call | solution.py:135
  70.6 0.0 copy-start
  70.6 1.3 copy-done
  71.8 6.0 %all-to-all-start.1 = ((bf16[8,2,112,512]{3,2,1,0:T(8,128)(2,1)}), bf16[8,2,112,512]{3,2,1,0:T(8,128)(2,1)S(1)}, u32[]{:S(2)}, u32[]{:S(2)}) async-start(bf16[8,2,112,512]{3,2,1,0:T(8,128)(2,1)} %copy-done), calls=%async_computation.1 | async-start | bytes 3670016 | tf_op jit(solution)/shard_map/all_to_all | solution.py:25
  77.8 1.2 reshape.47
  79.0 0.1 pad_dynamic-slice_fusion.1
  79.1 5.5 %collective-permute-start.6 = (bf16[896,128]{1,0:T(8,128)(2,1)S(1)}, bf16[896,128]{1,0:T(8,128)(2,1)S(1)}, u32[]{:S(2)}, u32[]{:S(2)}) collective-permute-start(bf16[896,128]{1,0:T(8,128)(2,1)S(1)} %bitcast.53), channel_id=1, source_target_pairs={{0,8},{1,9},{2,10},{3,11},{4,12},{5,13},{6,14},{7,15},{8,16},{9,17... | collective-permute-start | bytes 688136 | tf_op jit(solution)/shard_map/ppermute | solution.py:39
  84.6 4.3 %collective-permute-start.7 = (bf16[896,128]{1,0:T(8,128)(2,1)S(1)}, bf16[896,128]{1,0:T(8,128)(2,1)S(1)}, u32[]{:S(2)}, u32[]{:S(2)}) collective-permute-start(bf16[896,128]{1,0:T(8,128)(2,1)S(1)} %bitcast.52), channel_id=1, source_target_pairs={{0,24},{1,25},{2,26},{3,27},{4,28},{5,29},{6,30},{7,31},{8,0},{9,1... | collective-permute-start | bytes 688136 | tf_op jit(solution)/shard_map/ppermute | solution.py:39
  88.9 11.4 %collective-permute-done.6 = bf16[896,128]{1,0:T(8,128)(2,1)S(1)} collective-permute-done((bf16[896,128]{1,0:T(8,128)(2,1)S(1)}, bf16[896,128]{1,0:T(8,128)(2,1)S(1)}, u32[]{:S(2)}, u32[]{:S(2)}) %collective-permute-start.6) | collective-permute-done | bytes 229408 | tf_op jit(solution)/shard_map/ppermute | solution.py:39
  100.4 0.0 copy-start.2
  100.4 9.6 %collective-permute-done.7 = bf16[896,128]{1,0:T(8,128)(2,1)S(1)} collective-permute-done((bf16[896,128]{1,0:T(8,128)(2,1)S(1)}, bf16[896,128]{1,0:T(8,128)(2,1)S(1)}, u32[]{:S(2)}, u32[]{:S(2)}) %collective-permute-start.7) | collective-permute-done | bytes 229408 | tf_op jit(solution)/shard_map/ppermute | solution.py:39
  109.9 0.0 copy-start.3
  109.9 0.0 all-to-all-done.1.sums
  110.0 1.9 shard_map.57
  111.8 0.0 copy-done.2
  111.8 0.0 copy-done.3
  111.8 4.7 %all-to-all-start.2 = ((bf16[8,112,512]{2,1,0:T(8,128)(2,1)}), bf16[8,112,512]{2,1,0:T(8,128)(2,1)S(1)}, u32[]{:S(2)}, u32[]{:S(2)}) async-start(bf16[8,112,512]{2,1,0:T(8,128)(2,1)} %bitcast.13), calls=%async_computation.2 | async-start | bytes 1835008 | tf_op jit(solution)/shard_map/all_to_all | solution.py:25
  116.5 7.8 %collective-permute-start.8 = (bf16[896,128]{1,0:T(8,128)(2,1)S(1)}, bf16[896,128]{1,0:T(8,128)(2,1)S(1)}, u32[]{:S(2)}, u32[]{:S(2)}) collective-permute-start(bf16[896,128]{1,0:T(8,128)(2,1)S(1)} %bitcast.49), channel_id=1, source_target_pairs={{0,16},{1,17},{2,18},{3,19},{4,20},{5,21},{6,22},{7,23},{8,24},{9,... | collective-permute-start | bytes 688136 | tf_op jit(solution)/shard_map/ppermute | solution.py:39
  124.4 32.8 %collective-permute-done.8 = bf16[896,128]{1,0:T(8,128)(2,1)S(1)} collective-permute-done((bf16[896,128]{1,0:T(8,128)(2,1)S(1)}, bf16[896,128]{1,0:T(8,128)(2,1)S(1)}, u32[]{:S(2)}, u32[]{:S(2)}) %collective-permute-start.8) | collective-permute-done | bytes 229408 | tf_op jit(solution)/shard_map/ppermute | solution.py:39
  157.2 1.2 fusion.3
  158.4 1.9 collective-permute-start.9
  160.3 2.4 %collective-permute-done.9 = bf16[4,896,128]{2,1,0:T(8,128)(2,1)S(1)} collective-permute-done((bf16[4,896,128]{2,1,0:T(8,128)(2,1)S(1)}, bf16[4,896,128]{2,1,0:T(8,128)(2,1)S(1)}, u32[]{:S(2)}, u32[]{:S(2)}) %collective-permute-start.9) | collective-permute-done | bytes 917536 | tf_op jit(solution)/shard_map/ppermute | solution.py:39
  162.7 0.2 maximum_bitcast_fusion
  162.9 2.6 %copy.13 = bf16[896,4,2,128]{0,3,2,1:T(8,128)(2,1)} copy(bf16[896,4,2,128]{3,0,1,2:T(8,128)(2,1)S(1)} %maximum_bitcast_fusion) | data formatting | bytes 3670016 | tf_op jit(solution)/shard_map/transpose | solution.py:191
  165.5 0.0 all-to-all-done.2
  165.5 2.8 %convolution_convert_fusion = bf16[512,1024]{1,0:T(8,128)(2,1)S(1)} fusion(bf16[896,512]{1,0:T(8,128)(2,1)S(1)} %bitcast.43, bf16[896,1024]{0,1:T(8,128)(2,1)} %bitcast.38), kind=kOutput, calls=%fused_computation.5 | convolution fusion | flops 940048384 | bytes 3801088 | tf_op jit(solution)/shard_map/dot_general | solution.py:195
  168.3 24.7 %all_to_all.25.parts = bf16[8,64,1024]{2,1,0:T(8,128)(2,1)S(1)} all-to-all(bf16[8,64,1024]{2,1,0:T(8,128)(2,1)S(1)} %bitcast.39), channel_id=1, replica_groups=mesh['y'=4,'xh'=2,'xl'=2,'zh'=4,'zm'=2,'z0'=2,'core'=2] {'y','xh'}, dimensions={0} | all-to-all | bytes 2097152 | tf_op jit(solution)/shard_map/all_to_all | solution.py:25
  193.1 1.3 shard_map.58
  194.4 6.1 %all-to-all-start.4 = ((bf16[8,64,128]{2,1,0:T(8,128)(2,1)}), bf16[8,64,128]{2,1,0:T(8,128)(2,1)S(1)}, u32[]{:S(2)}, u32[]{:S(2)}) async-start(bf16[8,64,128]{2,1,0:T(8,128)(2,1)} %shard_map.58), calls=%async_computation.4 | async-start | bytes 262144 | tf_op jit(solution)/shard_map/all_to_all | solution.py:25
  200.5 14.7 %all-to-all-done.4 = bf16[8,64,128]{2,1,0:T(8,128)(2,1)S(1)} async-done(((bf16[8,64,128]{2,1,0:T(8,128)(2,1)}), bf16[8,64,128]{2,1,0:T(8,128)(2,1)S(1)}, u32[]{:S(2)}, u32[]{:S(2)}) %all-to-all-start.4) | async-done | bytes 131104 | tf_op jit(solution)/shard_map/all_to_all | solution.py:25
  215.3 0.6 add_convert_fusion
  (5 shorter events, 0.1 us)
Async XLA Ops:
  3.7 7.1 %copy-start.1 = (bf16[1024,128]{1,0:T(8,128)(2,1)S(1)}, bf16[1024,128]{1,0:T(8,128)(2,1)}, u32[]{:S(2)}) copy-start(bf16[1024,128]{1,0:T(8,128)(2,1)} %param.5) | copy-start | bytes 786436
  3.7 7.1 %copy-start.4 = (bf16[128]{0:T(256)(128)(2,1)S(1)}, bf16[128]{0:T(256)(128)(2,1)}, u32[]{:S(2)}) copy-start(bf16[128]{0:T(256)(128)(2,1)} %param.6) | copy-start | bytes 772
  3.7 39.4 %all-to-all-start = ((bf16[8,112,1024]{2,1,0:T(8,128)(2,1)}), bf16[8,112,1024]{2,1,0:T(8,128)(2,1)S(1)}, u32[]{:S(2)}, u32[]{:S(2)}) async-start(bf16[8,112,1024]{2,1,0:T(8,128)(2,1)} %shard_map.55), calls=%async_computation | async-start | bytes 3670016 | tf_op jit(solution)/shard_map/all_to_all | solution.py:25
  10.8 22.0 %collective-permute-start = (bf16[528,128]{1,0:T(8,128)(2,1)S(1)}, bf16[528,128]{1,0:T(8,128)(2,1)S(1)}, u32[]{:S(2)}, u32[]{:S(2)}) collective-permute-start(bf16[528,128]{1,0:T(8,128)(2,1)S(1)} %get-tuple-element.28), channel_id=1, source_target_pairs={{0,0},{1,1},{2,2},{3,3},{4,92},{5,93},{6,94},{7,95},{8,152},{9,153... | collective-permute-start | bytes 405512 | tf_op jit(solution)/shard_map/ppermute | solution.py:39
  24.7 15.9 %collective-permute-start.1 = (bf16[528,128]{1,0:T(8,128)(2,1)S(1)}, bf16[528,128]{1,0:T(8,128)(2,1)S(1)}, u32[]{:S(2)}, u32[]{:S(2)}) collective-permute-start(bf16[528,128]{1,0:T(8,128)(2,1)S(1)} %get-tuple-element.27), channel_id=1, source_target_pairs={{0,17},{1,16},{2,19},{3,18},{4,77},{5,76},{6,79},{7,78},{8,137},{9... | collective-permute-start | bytes 405512 | tf_op jit(solution)/shard_map/ppermute | solution.py:39
  43.1 24.2 %collective-permute-start.5 = (bf16[8,112,1024]{2,1,0:T(8,128)(2,1)S(1)}, bf16[8,112,1024]{2,1,0:T(8,128)(2,1)S(1)}, u32[]{:S(2)}, u32[]{:S(2)}) collective-permute-start(bf16[8,112,1024]{2,1,0:T(8,128)(2,1)S(1)} %all-to-all-done.w_own), channel_id=1, source_target_pairs={{0,1},{1,0},{2,3},{3,2},{4,5},{5,4},{6,7},{7,6},{8,9},{9,8},{10,11... | collective-permute-start | bytes 5505032 | tf_op jit(solution)/shard_map/ppermute | solution.py:39
  45.0 13.0 %collective-permute-start.2 = (bf16[2,528,128]{2,1,0:T(8,128)(2,1)S(1)}, bf16[2,528,128]{2,1,0:T(8,128)(2,1)S(1)}, u32[]{:S(2)}, u32[]{:S(2)}) collective-permute-start(bf16[2,528,128]{2,1,0:T(8,128)(2,1)S(1)} %pad_maximum_fusion.1.x0), channel_id=1, source_target_pairs={{0,2},{1,3},{2,0},{3,1},{4,6},{5,7},{6,4},{7,5},{8,10},{9,11},{10,... | collective-permute-start | bytes 811016 | tf_op jit(solution)/shard_map/ppermute | solution.py:39
  51.0 16.3 %collective-permute-start.3 = (bf16[2,528,128]{2,1,0:T(8,128)(2,1)S(1)}, bf16[2,528,128]{2,1,0:T(8,128)(2,1)S(1)}, u32[]{:S(2)}, u32[]{:S(2)}) collective-permute-start(bf16[2,528,128]{2,1,0:T(8,128)(2,1)S(1)} %pad_maximum_fusion.1.x0), channel_id=1, source_target_pairs={{0,32},{1,33},{2,34},{3,35},{4,36},{5,37},{6,38},{7,39},{8,40},{9,... | collective-permute-start | bytes 811016 | tf_op jit(solution)/shard_map/ppermute | solution.py:39
  53.5 13.8 %collective-permute-start.4 = (bf16[2,528,128]{2,1,0:T(8,128)(2,1)S(1)}, bf16[2,528,128]{2,1,0:T(8,128)(2,1)S(1)}, u32[]{:S(2)}, u32[]{:S(2)}) collective-permute-start(bf16[2,528,128]{2,1,0:T(8,128)(2,1)S(1)} %pad_maximum_fusion.1.x0), channel_id=1, source_target_pairs={{0,34},{1,35},{2,32},{3,33},{4,38},{5,39},{6,36},{7,37},{8,42},{9,... | collective-permute-start | bytes 811016 | tf_op jit(solution)/shard_map/ppermute | solution.py:39
  70.6 1.3 copy-start
  71.8 38.1 %all-to-all-start.1 = ((bf16[8,2,112,512]{3,2,1,0:T(8,128)(2,1)}), bf16[8,2,112,512]{3,2,1,0:T(8,128)(2,1)S(1)}, u32[]{:S(2)}, u32[]{:S(2)}) async-start(bf16[8,2,112,512]{3,2,1,0:T(8,128)(2,1)} %copy-done), calls=%async_computation.1 | async-start | bytes 3670016 | tf_op jit(solution)/shard_map/all_to_all | solution.py:25
  79.1 21.2 %collective-permute-start.6 = (bf16[896,128]{1,0:T(8,128)(2,1)S(1)}, bf16[896,128]{1,0:T(8,128)(2,1)S(1)}, u32[]{:S(2)}, u32[]{:S(2)}) collective-permute-start(bf16[896,128]{1,0:T(8,128)(2,1)S(1)} %bitcast.53), channel_id=1, source_target_pairs={{0,8},{1,9},{2,10},{3,11},{4,12},{5,13},{6,14},{7,15},{8,16},{9,17... | collective-permute-start | bytes 688136 | tf_op jit(solution)/shard_map/ppermute | solution.py:39
  84.6 25.3 %collective-permute-start.7 = (bf16[896,128]{1,0:T(8,128)(2,1)S(1)}, bf16[896,128]{1,0:T(8,128)(2,1)S(1)}, u32[]{:S(2)}, u32[]{:S(2)}) collective-permute-start(bf16[896,128]{1,0:T(8,128)(2,1)S(1)} %bitcast.52), channel_id=1, source_target_pairs={{0,24},{1,25},{2,26},{3,27},{4,28},{5,29},{6,30},{7,31},{8,0},{9,1... | collective-permute-start | bytes 688136 | tf_op jit(solution)/shard_map/ppermute | solution.py:39
  100.4 11.5 %copy-start.2 = (bf16[896,128]{1,0:T(8,128)(2,1)}, bf16[896,128]{1,0:T(8,128)(2,1)S(1)}, u32[]{:S(2)}) copy-start(bf16[896,128]{1,0:T(8,128)(2,1)S(1)} %collective-permute-done.6) | copy-start | bytes 688132
  109.9 1.9 copy-start.3
  111.8 53.7 %all-to-all-start.2 = ((bf16[8,112,512]{2,1,0:T(8,128)(2,1)}), bf16[8,112,512]{2,1,0:T(8,128)(2,1)S(1)}, u32[]{:S(2)}, u32[]{:S(2)}) async-start(bf16[8,112,512]{2,1,0:T(8,128)(2,1)} %bitcast.13), calls=%async_computation.2 | async-start | bytes 1835008 | tf_op jit(solution)/shard_map/all_to_all | solution.py:25
  116.5 40.6 %collective-permute-start.8 = (bf16[896,128]{1,0:T(8,128)(2,1)S(1)}, bf16[896,128]{1,0:T(8,128)(2,1)S(1)}, u32[]{:S(2)}, u32[]{:S(2)}) collective-permute-start(bf16[896,128]{1,0:T(8,128)(2,1)S(1)} %bitcast.49), channel_id=1, source_target_pairs={{0,16},{1,17},{2,18},{3,19},{4,20},{5,21},{6,22},{7,23},{8,24},{9,... | collective-permute-start | bytes 688136 | tf_op jit(solution)/shard_map/ppermute | solution.py:39
  158.4 4.4 %collective-permute-start.9 = (bf16[4,896,128]{2,1,0:T(8,128)(2,1)S(1)}, bf16[4,896,128]{2,1,0:T(8,128)(2,1)S(1)}, u32[]{:S(2)}, u32[]{:S(2)}) collective-permute-start(bf16[4,896,128]{2,1,0:T(8,128)(2,1)S(1)} %get-tuple-element.20), channel_id=1, source_target_pairs={{0,1},{1,0},{2,3},{3,2},{4,5},{5,4},{6,7},{7,6},{8,9},{9,8},{10,11... | collective-permute-start | bytes 2752520 | tf_op jit(solution)/shard_map/ppermute | solution.py:39
  194.4 20.9 %all-to-all-start.4 = ((bf16[8,64,128]{2,1,0:T(8,128)(2,1)}), bf16[8,64,128]{2,1,0:T(8,128)(2,1)S(1)}, u32[]{:S(2)}, u32[]{:S(2)}) async-start(bf16[8,64,128]{2,1,0:T(8,128)(2,1)} %shard_map.58), calls=%async_computation.4 | async-start | bytes 262144 | tf_op jit(solution)/shard_map/all_to_all | solution.py:25

commit v5 on v4

--- a/solution.py
+++ b/solution.py
@@ -15,8 +15,8 @@
 SIZES = (4, 2, 2, 4, 2, 2, 2)
 PHASE = ("y", "xh")
 BLK = ("xl", "zh", "zm", "z0", "core")
-NEAR = ("xl", "zm", "z0")
 FAR = "zh"
+BLOCK = ("xl", "zm", "z0")
 
 f32, bf16 = jnp.float32, jnp.bfloat16
 
@@ -115,7 +115,7 @@
         gate = total[:56] * inv_rms
         acts = gate / (1.0 + jnp.exp(-gate)) * (total[56:] * inv_rms)
         acts = jnp.where(unit < 52, acts, 0.0).astype(bf16)
-        for copy in range(8):
+        for copy in range(4):
             out[copy, jnp.bitwise_xor(at[0], side)] = acts
 
 
@@ -123,11 +123,9 @@
     total = parts[0].astype(f32)
     for part in range(1, 8):
         total += parts[part].astype(f32)
-    for far in range(4):
-        for core in (0, 1):
-            to = jnp.bitwise_and(at[2] - far, 3) * 2 + jnp.bitwise_xor(at[0], core)
-            column = (far * 2 + core) * LANES
-            out[to] = total[:, column : column + LANES].astype(bf16)
+    for piece in range(16):
+        column = piece * LANES
+        out[jnp.bitwise_xor(at[2], piece)] = total[:, column : column + LANES].astype(bf16)
 
 
 def run(kernel, out_shape, operands, scratch=(), flops=0):
@@ -145,8 +143,9 @@
 
 
 def local(layer_input, norm_gain, gate_weight, up_weight, down_weight):
-    phase, core, far = (lax.axis_index(a) for a in (PHASE, "core", FAR))
-    at = jnp.stack((core, lax.axis_index(("xl", "z0")), far)).astype(jnp.int32)
+    phase, core = lax.axis_index(PHASE), lax.axis_index("core")
+    at = (core, lax.axis_index(("xl", "z0")), lax.axis_index((*BLOCK, "core")))
+    at = jnp.stack(at).astype(jnp.int32)
     units = gate_weight.shape[0]
     rows = layer_input.shape[0] // 2
 
@@ -168,14 +167,19 @@
     blocks = [held] + [send(held, shift(xl=i, z0=j)) for i, j in ((0, 1), (1, 0), (1, 1))]
 
     down, _ = lax.optimization_barrier((down_weight, held))
-    down = down.reshape(2, 4, 8, units, LANES)
-    down = jnp.pad(down, ((0, 0), (0, 0), (0, 0), (0, 56 - units), (0, 0)))
-
-    def quarter(count):
-        part = lax.dynamic_slice_in_dim(down, (far + count) % 4, 1, 1).reshape(896, LANES)
-        return send(part, shift(zh=count)) if count else part
-
-    quarters = [quarter(count) for count in range(4)]
+    down = jnp.pad(down.reshape(64, units, LANES), ((0, 0), (0, 56 - units), (0, 0)))
+    down = down.reshape(2, 4, 2, 2, 112, LANES).transpose(3, 2, 0, 1, 4, 5).reshape(2, 2, 2, 448, LANES)
+
+    def halve(value, axis):
+        place = lax.axis_index(axis)
+        kept, sent = (
+            lax.dynamic_index_in_dim(value, i, 0, keepdims=False) for i in (place, 1 - place)
+        )
+        return kept, send(sent, shift(**{axis: 1}))
+
+    down = jnp.stack(halve(down, "z0"), 2)
+    down = jnp.stack(halve(down, "zm"), 1)
+
     sums = run(
         sums_kernel,
         (8, 2, 112, rows),
@@ -183,22 +187,19 @@
         (pltpu.VMEM((rows, 1024), bf16),),
         flops=2 * 1792 * 1024 * rows,
     )
-    sums, quarters[1], quarters[3] = lax.optimization_barrier(
-        (exchange(sums, PHASE), quarters[1], quarters[3])
-    )
-    own_d = jnp.stack(quarters)
-    other_d = send(own_d, shift(core=1))
-    d_all = jnp.stack((own_d, other_d), 1).transpose(2, 0, 1, 3).reshape(896, 1024)
-
-    acts = run(acts_kernel, (8, 2, 56, rows), (at, sums))
-    acts = exchange(acts.reshape(8, 112, rows), NEAR).reshape(896, rows)
+    sums, down = lax.optimization_barrier((exchange(sums, PHASE), down))
+    down = jnp.stack(halve(down, "xl")).reshape(8, 448, LANES)
+    down = jnp.stack((down, send(down, shift(core=1))), 1)
+    down = down.transpose(2, 0, 1, 3).reshape(448, 2048)
+    acts = run(acts_kernel, (4, 2, 56, rows), (at, sums))
+    acts = exchange(acts.reshape(4, 112, rows), FAR).reshape(448, rows)
     partials = lax.dot_general(
-        acts, d_all, (((0,), (0,)), ((), ())), preferred_element_type=f32
+        acts, down, (((0,), (0,)), ((), ())), preferred_element_type=f32
     ).astype(bf16)
-    partials = exchange(partials.reshape(8, rows // 8, 1024), PHASE)
-    partials = run(place_kernel, (8, rows // 8, LANES), (at, partials))
-    partials = exchange(partials, (FAR, "core")).astype(f32)
-    ffn_out = jnp.sum(partials.reshape(4, rows // 4, LANES), 0)
+    partials = exchange(partials.reshape(8, rows // 8, 2048), PHASE)
+    partials = run(place_kernel, (16, rows // 8, LANES), (at, partials))
+    partials = exchange(partials, (*BLOCK, "core")).astype(f32)
+    ffn_out = jnp.sum(partials.reshape(8, rows // 4, LANES), 0)
     residual = lax.dynamic_slice_in_dim(layer_input, phase * (rows // 4), rows // 4, 0)
     return (residual.astype(f32) + ffn_out).astype(bf16)
 

time: 217 us -> 211 us (0.972)
  the two profiles are of different devices: /device:TPU:64 before, /device:TPU:1 now
where the time goes in v5:
time: 211 us; the launch traced here: 210 us
  starting transfers between devices  83.2 us (39%)
  waiting for transfers between devices  69.7 us (33%)
  blocking collectives  32.9 us (16%)
  local copies, waits for them, and re-layouts  8.67 us (4%)
  Pallas kernels  8.42 us (4%)
  other arithmetic  3.87 us (2%)
  matrix products  2.79 us (1%)
    ppermute x10, waiting for transfers between devices, send(): return lax.ppermute(value, AXES, route(move))  50 us
    ppermute x10, starting transfers between devices, send(): return lax.ppermute(value, AXES, route(move))  45.4 us
    all_to_all x4, starting transfers between devices, exchange(): return lax.all_to_all(value, axes, 0, 0, tiled=True)  37.8 us
    all_to_all x1, blocking collectives, exchange(): return lax.all_to_all(value, axes, 0, 0, tiled=True)  32.9 us
    all_to_all x4, waiting for transfers between devices, exchange(): return lax.all_to_all(value, axes, 0, 0, tiled=True)  19.7 us
    pallas_call x4, Pallas kernels, run(): pl.pallas_call(kernel, out_shape=jax.ShapeDtypeStruct(out_shape, bf16), i...  8.42 us
  transfers between devices with their start and end apart: 14, of which 9 were waited for; matrix products, arithmetic and copies ran while one was open for 3% of the time, Pallas kernels for 1%

profile of v5, /device:TPU:1, one launch (start us, length us, event | category | flops | bytes accessed | tf_op | source)
XLA Modules:
  0.0 209.8 jit_solution(11648514103657866399)
XLA Ops:
  0.0 1.6 fusion.2
  1.6 0.1 pad_add_fusion.at
  1.7 1.9 shard_map.55
  3.7 0.0 copy-start.2
  3.7 0.0 copy-start.3
  3.7 7.6 %all-to-all-start = ((bf16[8,112,1024]{2,1,0:T(8,128)(2,1)}), bf16[8,112,1024]{2,1,0:T(8,128)(2,1)S(1)}, u32[]{:S(2)}, u32[]{:S(2)}) async-start(bf16[8,112,1024]{2,1,0:T(8,128)(2,1)} %shard_map.55), calls=%async_computation | async-start | bytes 3670016 | tf_op jit(solution)/shard_map/all_to_all | solution.py:25
  11.3 0.0 copy-done.2
  11.3 0.0 copy-done.3
  11.4 0.7 collective-permute-start
  12.0 21.0 %collective-permute-start.1 = (bf16[528,128]{1,0:T(8,128)(2,1)S(1)}, bf16[528,128]{1,0:T(8,128)(2,1)S(1)}, u32[]{:S(2)}, u32[]{:S(2)}) collective-permute-start(bf16[528,128]{1,0:T(8,128)(2,1)S(1)} %get-tuple-element.25), channel_id=1, source_target_pairs={{0,17},{1,16},{2,19},{3,18},{4,77},{5,76},{6,79},{7,78},{8,137},{9... | collective-permute-start | bytes 405512 | tf_op jit(solution)/shard_map/ppermute | solution.py:39
  33.1 0.0 collective-permute-done
  33.1 5.4 %collective-permute-done.1 = bf16[528,128]{1,0:T(8,128)(2,1)S(1)} collective-permute-done((bf16[528,128]{1,0:T(8,128)(2,1)S(1)}, bf16[528,128]{1,0:T(8,128)(2,1)S(1)}, u32[]{:S(2)}, u32[]{:S(2)}) %collective-permute-start.1) | collective-permute-done | bytes 135200 | tf_op jit(solution)/shard_map/ppermute | solution.py:39
  38.5 0.0 all-to-all-done.w_own
  38.5 1.9 collective-permute-start.5
  40.5 4.2 %collective-permute-start.2 = (bf16[2,528,128]{2,1,0:T(8,128)(2,1)S(1)}, bf16[2,528,128]{2,1,0:T(8,128)(2,1)S(1)}, u32[]{:S(2)}, u32[]{:S(2)}) collective-permute-start(bf16[2,528,128]{2,1,0:T(8,128)(2,1)S(1)} %pad_maximum_fusion.2.x0), channel_id=1, source_target_pairs={{0,2},{1,3},{2,0},{3,1},{4,6},{5,7},{6,4},{7,5},{8,10},{9,11},{10,... | collective-permute-start | bytes 811016 | tf_op jit(solution)/shard_map/ppermute | solution.py:39
  44.7 2.3 %collective-permute-start.3 = (bf16[2,528,128]{2,1,0:T(8,128)(2,1)S(1)}, bf16[2,528,128]{2,1,0:T(8,128)(2,1)S(1)}, u32[]{:S(2)}, u32[]{:S(2)}) collective-permute-start(bf16[2,528,128]{2,1,0:T(8,128)(2,1)S(1)} %pad_maximum_fusion.2.x0), channel_id=1, source_target_pairs={{0,32},{1,33},{2,34},{3,35},{4,36},{5,37},{6,38},{7,39},{8,40},{9,... | collective-permute-start | bytes 811016 | tf_op jit(solution)/shard_map/ppermute | solution.py:39
  47.0 2.7 %collective-permute-start.4 = (bf16[2,528,128]{2,1,0:T(8,128)(2,1)S(1)}, bf16[2,528,128]{2,1,0:T(8,128)(2,1)S(1)}, u32[]{:S(2)}, u32[]{:S(2)}) collective-permute-start(bf16[2,528,128]{2,1,0:T(8,128)(2,1)S(1)} %pad_maximum_fusion.2.x0), channel_id=1, source_target_pairs={{0,34},{1,35},{2,32},{3,33},{4,38},{5,39},{6,36},{7,37},{8,42},{9,... | collective-permute-start | bytes 811016 | tf_op jit(solution)/shard_map/ppermute | solution.py:39
  49.7 1.4 collective-permute-done.2.x1
  51.1 8.5 %collective-permute-done.3.x2 = bf16[2,528,128]{2,1,0:T(8,128)(2,1)S(1)} collective-permute-done((bf16[2,528,128]{2,1,0:T(8,128)(2,1)S(1)}, bf16[2,528,128]{2,1,0:T(8,128)(2,1)S(1)}, u32[]{:S(2)}, u32[]{:S(2)}) %collective-permute-start.3) | collective-permute-done | bytes 270368 | tf_op jit(solution)/shard_map/ppermute | solution.py:39
  59.6 0.0 collective-permute-done.4.x3
  59.6 0.0 collective-permute-done.5.w_other
  59.6 3.3 %shard_map.56 = bf16[8,2,112,512]{3,2,1,0:T(8,128)(2,1)S(1)} custom-call(s32[3]{0:T(128)S(1)} %pad_add_fusion.at, bf16[2,528,128]{2,1,0:T(8,128)(2,1)S(1)} %pad_maximum_fusion.2.x0, bf16[2,528,128]{2,1,0:T(8,128)(2,1)S(1)} %collective-permute-done.2.x1, bf16[2,528,128]{2,1,0:T(8,128)(2,1)S(1)} %collective-permute-done.3.x2, ...), custom_call_target="tpu_custom_call" | custom-call | flops 1879048192 | bytes 6586380 | tf_op jit(solution)/shard_map/pallas_call | solution.py:133
  62.9 0.0 copy-start
  62.9 1.3 copy-done
  64.2 14.1 %all-to-all-start.1 = ((bf16[8,2,112,512]{3,2,1,0:T(8,128)(2,1)}), bf16[8,2,112,512]{3,2,1,0:T(8,128)(2,1)S(1)}, u32[]{:S(2)}, u32[]{:S(2)}) async-start(bf16[8,2,112,512]{3,2,1,0:T(8,128)(2,1)} %copy-done), calls=%async_computation.1 | async-start | bytes 3670016 | tf_op jit(solution)/shard_map/all_to_all | solution.py:25
  78.3 1.2 reshape.49
  79.6 0.1 pad.9
  79.6 0.1 copy.11
  79.7 0.1 dynamic-slice_bitcast_fusion.1
  79.8 2.2 %collective-permute-start.6 = (bf16[2,2,448,128]{3,2,1,0:T(8,128)(2,1)S(1)}, bf16[2,2,448,128]{3,2,1,0:T(8,128)(2,1)S(1)}, u32[]{:S(2)}, u32[]{:S(2)}) collective-permute-start(bf16[2,2,448,128]{3,2,1,0:T(8,128)(2,1)S(1)} %get-tuple-element.21), channel_id=1, source_target_pairs={{0,2},{1,3},{2,0},{3,1},{4,6},{5,7},{6,4},{7,5},{8,10},{9,11},{10,... | collective-permute-start | bytes 1376264 | tf_op jit(solution)/shard_map/ppermute | solution.py:39
  82.1 10.3 %collective-permute-done.6 = bf16[2,2,448,128]{3,2,1,0:T(8,128)(2,1)S(1)} collective-permute-done((bf16[2,2,448,128]{3,2,1,0:T(8,128)(2,1)S(1)}, bf16[2,2,448,128]{3,2,1,0:T(8,128)(2,1)S(1)}, u32[]{:S(2)}, u32[]{:S(2)}) %collective-permute-start.6) | collective-permute-done | bytes 458784 | tf_op jit(solution)/shard_map/ppermute | solution.py:39
  92.3 0.1 fusion.4
  92.4 4.5 %collective-permute-start.7 = (bf16[2,2,448,128]{3,2,1,0:T(8,128)(2,1)S(1)}, bf16[2,2,448,128]{3,2,1,0:T(8,128)(2,1)S(1)}, u32[]{:S(2)}, u32[]{:S(2)}) collective-permute-start(bf16[2,2,448,128]{3,2,1,0:T(8,128)(2,1)S(1)} %bitcast.64), channel_id=1, source_target_pairs={{0,4},{1,5},{2,6},{3,7},{4,0},{5,1},{6,2},{7,3},{8,12},{9,13},{10,... | collective-permute-start | bytes 1376264 | tf_op jit(solution)/shard_map/ppermute | solution.py:39
  97.0 20.3 %collective-permute-done.7 = bf16[2,2,448,128]{3,2,1,0:T(8,128)(2,1)S(1)} collective-permute-done((bf16[2,2,448,128]{3,2,1,0:T(8,128)(2,1)S(1)}, bf16[2,2,448,128]{3,2,1,0:T(8,128)(2,1)S(1)}, u32[]{:S(2)}, u32[]{:S(2)}) %collective-permute-start.7) | collective-permute-done | bytes 458784 | tf_op jit(solution)/shard_map/ppermute | solution.py:39
  117.3 0.0 copy-start.1
  117.3 0.8 copy-done.1
  118.1 1.1 pad_maximum_fusion
  119.2 0.0 all-to-all-done.1.sums
  119.2 0.8 constant_dynamic-slice_fusion
  120.0 2.2 %collective-permute-start.8 = (bf16[2,2,448,128]{3,2,1,0:T(8,128)(2,1)}, bf16[2,2,448,128]{3,2,1,0:T(8,128)(2,1)S(1)}, u32[]{:S(2)}, u32[]{:S(2)}) collective-permute-start(bf16[2,2,448,128]{3,2,1,0:T(8,128)(2,1)} %get-tuple-element.18), channel_id=1, source_target_pairs={{0,32},{1,33},{2,34},{3,35},{4,36},{5,37},{6,38},{7,39},{8,40},{9,... | collective-permute-start | bytes 1376264 | tf_op jit(solution)/shard_map/ppermute | solution.py:39
  122.2 1.6 shard_map.57
  123.8 7.4 %all-to-all-start.2 = ((bf16[4,112,512]{2,1,0:T(8,128)(2,1)}), bf16[4,112,512]{2,1,0:T(8,128)(2,1)S(1)}, u32[]{:S(2)}, u32[]{:S(2)}) async-start(bf16[4,112,512]{2,1,0:T(8,128)(2,1)} %bitcast.21), calls=%async_computation.2 | async-start | bytes 917504 | tf_op jit(solution)/shard_map/all_to_all | solution.py:25
  131.2 2.0 collective-permute-done.8
  133.2 0.1 pad_maximum_fusion.1
  133.3 3.8 %collective-permute-start.9 = (bf16[8,448,128]{2,1,0:T(8,128)(2,1)S(1)}, bf16[8,448,128]{2,1,0:T(8,128)(2,1)S(1)}, u32[]{:S(2)}, u32[]{:S(2)}) collective-permute-start(bf16[8,448,128]{2,1,0:T(8,128)(2,1)S(1)} %bitcast.49), channel_id=1, source_target_pairs={{0,1},{1,0},{2,3},{3,2},{4,5},{5,4},{6,7},{7,6},{8,9},{9,8},{10,11... | collective-permute-start | bytes 2752520 | tf_op jit(solution)/shard_map/ppermute | solution.py:39
  137.1 2.1 collective-permute-done.9
  139.1 0.2 maximum_bitcast_fusion
  139.3 1.9 copy.14
  141.2 2.4 %reshape.55 = bf16[448,2048]{1,0:T(8,128)(2,1)} reshape(bf16[448,8,2,128]{3,2,1,0:T(2,128)(2,1)S(1)} %copy.14) | data formatting | bytes 3670016 | tf_op jit(solution)/shard_map/reshape | solution.py:193
  143.6 10.2 %all-to-all-done.2 = bf16[4,112,512]{2,1,0:T(8,128)(2,1)S(1)} async-done(((bf16[4,112,512]{2,1,0:T(8,128)(2,1)}), bf16[4,112,512]{2,1,0:T(8,128)(2,1)S(1)}, u32[]{:S(2)}, u32[]{:S(2)}) %all-to-all-start.2) | async-done | bytes 458784 | tf_op jit(solution)/shard_map/all_to_all | solution.py:25
  153.8 2.8 %convolution_convert_fusion = bf16[512,2048]{1,0:T(8,128)(2,1)S(1)} fusion(bf16[448,512]{1,0:T(8,128)(2,1)S(1)} %bitcast.63, bf16[448,2048]{1,0:T(8,128)(2,1)} %reshape.55), kind=kOutput, calls=%fused_computation.3 | convolution fusion | flops 940572672 | bytes 4390912 | tf_op jit(solution)/shard_map/dot_general | solution.py:196
  156.6 32.9 %all_to_all.25.parts = bf16[8,64,2048]{2,1,0:T(8,128)(2,1)S(1)} all-to-all(bf16[8,64,2048]{2,1,0:T(8,128)(2,1)S(1)} %bitcast.53), channel_id=1, replica_groups=mesh['y'=4,'xh'=2,'xl'=2,'zh'=4,'zm'=2,'z0'=2,'core'=2] {'y','xh'}, dimensions={0} | all-to-all | bytes 4194304 | tf_op jit(solution)/shard_map/all_to_all | solution.py:25
  189.5 1.5 shard_map.58
  191.0 8.6 %all-to-all-start.4 = ((bf16[16,64,128]{2,1,0:T(8,128)(2,1)}), bf16[16,64,128]{2,1,0:T(8,128)(2,1)S(1)}, u32[]{:S(2)}, u32[]{:S(2)}) async-start(bf16[16,64,128]{2,1,0:T(8,128)(2,1)} %shard_map.58), calls=%async_computation.4 | async-start | bytes 524288 | tf_op jit(solution)/shard_map/all_to_all | solution.py:25
  199.6 9.5 %all-to-all-done.4 = bf16[16,64,128]{2,1,0:T(8,128)(2,1)S(1)} async-done(((bf16[16,64,128]{2,1,0:T(8,128)(2,1)}), bf16[16,64,128]{2,1,0:T(8,128)(2,1)S(1)}, u32[]{:S(2)}, u32[]{:S(2)}) %all-to-all-start.4) | async-done | bytes 262176 | tf_op jit(solution)/shard_map/all_to_all | solution.py:25
  209.2 0.6 add_convert_fusion
  (7 shorter events, 0.2 us)
Async XLA Ops:
  3.7 7.6 %copy-start.2 = (bf16[1024,128]{1,0:T(8,128)(2,1)S(1)}, bf16[1024,128]{1,0:T(8,128)(2,1)}, u32[]{:S(2)}) copy-start(bf16[1024,128]{1,0:T(8,128)(2,1)} %param.5) | copy-start | bytes 786436
  3.7 7.7 %copy-start.3 = (bf16[128]{0:T(256)(128)(2,1)S(1)}, bf16[128]{0:T(256)(128)(2,1)}, u32[]{:S(2)}) copy-start(bf16[128]{0:T(256)(128)(2,1)} %param.6) | copy-start | bytes 772
  3.7 34.9 %all-to-all-start = ((bf16[8,112,1024]{2,1,0:T(8,128)(2,1)}), bf16[8,112,1024]{2,1,0:T(8,128)(2,1)S(1)}, u32[]{:S(2)}, u32[]{:S(2)}) async-start(bf16[8,112,1024]{2,1,0:T(8,128)(2,1)} %shard_map.55), calls=%async_computation | async-start | bytes 3670016 | tf_op jit(solution)/shard_map/all_to_all | solution.py:25
  11.4 21.7 %collective-permute-start = (bf16[528,128]{1,0:T(8,128)(2,1)S(1)}, bf16[528,128]{1,0:T(8,128)(2,1)S(1)}, u32[]{:S(2)}, u32[]{:S(2)}) collective-permute-start(bf16[528,128]{1,0:T(8,128)(2,1)S(1)} %get-tuple-element.26), channel_id=1, source_target_pairs={{0,0},{1,1},{2,2},{3,3},{4,92},{5,93},{6,94},{7,95},{8,152},{9,153... | collective-permute-start | bytes 405512 | tf_op jit(solution)/shard_map/ppermute | solution.py:39
  12.0 26.5 %collective-permute-start.1 = (bf16[528,128]{1,0:T(8,128)(2,1)S(1)}, bf16[528,128]{1,0:T(8,128)(2,1)S(1)}, u32[]{:S(2)}, u32[]{:S(2)}) collective-permute-start(bf16[528,128]{1,0:T(8,128)(2,1)S(1)} %get-tuple-element.25), channel_id=1, source_target_pairs={{0,17},{1,16},{2,19},{3,18},{4,77},{5,76},{6,79},{7,78},{8,137},{9... | collective-permute-start | bytes 405512 | tf_op jit(solution)/shard_map/ppermute | solution.py:39
  38.5 21.0 %collective-permute-start.5 = (bf16[8,112,1024]{2,1,0:T(8,128)(2,1)S(1)}, bf16[8,112,1024]{2,1,0:T(8,128)(2,1)S(1)}, u32[]{:S(2)}, u32[]{:S(2)}) collective-permute-start(bf16[8,112,1024]{2,1,0:T(8,128)(2,1)S(1)} %all-to-all-done.w_own), channel_id=1, source_target_pairs={{0,1},{1,0},{2,3},{3,2},{4,5},{5,4},{6,7},{7,6},{8,9},{9,8},{10,11... | collective-permute-start | bytes 5505032 | tf_op jit(solution)/shard_map/ppermute | solution.py:39
  40.5 10.6 %collective-permute-start.2 = (bf16[2,528,128]{2,1,0:T(8,128)(2,1)S(1)}, bf16[2,528,128]{2,1,0:T(8,128)(2,1)S(1)}, u32[]{:S(2)}, u32[]{:S(2)}) collective-permute-start(bf16[2,528,128]{2,1,0:T(8,128)(2,1)S(1)} %pad_maximum_fusion.2.x0), channel_id=1, source_target_pairs={{0,2},{1,3},{2,0},{3,1},{4,6},{5,7},{6,4},{7,5},{8,10},{9,11},{10,... | collective-permute-start | bytes 811016 | tf_op jit(solution)/shard_map/ppermute | solution.py:39
  44.7 14.9 %collective-permute-start.3 = (bf16[2,528,128]{2,1,0:T(8,128)(2,1)S(1)}, bf16[2,528,128]{2,1,0:T(8,128)(2,1)S(1)}, u32[]{:S(2)}, u32[]{:S(2)}) collective-permute-start(bf16[2,528,128]{2,1,0:T(8,128)(2,1)S(1)} %pad_maximum_fusion.2.x0), channel_id=1, source_target_pairs={{0,32},{1,33},{2,34},{3,35},{4,36},{5,37},{6,38},{7,39},{8,40},{9,... | collective-permute-start | bytes 811016 | tf_op jit(solution)/shard_map/ppermute | solution.py:39
  47.0 12.6 %collective-permute-start.4 = (bf16[2,528,128]{2,1,0:T(8,128)(2,1)S(1)}, bf16[2,528,128]{2,1,0:T(8,128)(2,1)S(1)}, u32[]{:S(2)}, u32[]{:S(2)}) collective-permute-start(bf16[2,528,128]{2,1,0:T(8,128)(2,1)S(1)} %pad_maximum_fusion.2.x0), channel_id=1, source_target_pairs={{0,34},{1,35},{2,32},{3,33},{4,38},{5,39},{6,36},{7,37},{8,42},{9,... | collective-permute-start | bytes 811016 | tf_op jit(solution)/shard_map/ppermute | solution.py:39
  62.9 1.3 copy-start
  64.2 55.0 %all-to-all-start.1 = ((bf16[8,2,112,512]{3,2,1,0:T(8,128)(2,1)}), bf16[8,2,112,512]{3,2,1,0:T(8,128)(2,1)S(1)}, u32[]{:S(2)}, u32[]{:S(2)}) async-start(bf16[8,2,112,512]{3,2,1,0:T(8,128)(2,1)} %copy-done), calls=%async_computation.1 | async-start | bytes 3670016 | tf_op jit(solution)/shard_map/all_to_all | solution.py:25
  79.8 12.5 %collective-permute-start.6 = (bf16[2,2,448,128]{3,2,1,0:T(8,128)(2,1)S(1)}, bf16[2,2,448,128]{3,2,1,0:T(8,128)(2,1)S(1)}, u32[]{:S(2)}, u32[]{:S(2)}) collective-permute-start(bf16[2,2,448,128]{3,2,1,0:T(8,128)(2,1)S(1)} %get-tuple-element.21), channel_id=1, source_target_pairs={{0,2},{1,3},{2,0},{3,1},{4,6},{5,7},{6,4},{7,5},{8,10},{9,11},{10,... | collective-permute-start | bytes 1376264 | tf_op jit(solution)/shard_map/ppermute | solution.py:39
  92.4 24.9 %collective-permute-start.7 = (bf16[2,2,448,128]{3,2,1,0:T(8,128)(2,1)S(1)}, bf16[2,2,448,128]{3,2,1,0:T(8,128)(2,1)S(1)}, u32[]{:S(2)}, u32[]{:S(2)}) collective-permute-start(bf16[2,2,448,128]{3,2,1,0:T(8,128)(2,1)S(1)} %bitcast.64), channel_id=1, source_target_pairs={{0,4},{1,5},{2,6},{3,7},{4,0},{5,1},{6,2},{7,3},{8,12},{9,13},{10,... | collective-permute-start | bytes 1376264 | tf_op jit(solution)/shard_map/ppermute | solution.py:39
  117.3 0.8 copy-start.1
  120.0 13.2 %collective-permute-start.8 = (bf16[2,2,448,128]{3,2,1,0:T(8,128)(2,1)}, bf16[2,2,448,128]{3,2,1,0:T(8,128)(2,1)S(1)}, u32[]{:S(2)}, u32[]{:S(2)}) collective-permute-start(bf16[2,2,448,128]{3,2,1,0:T(8,128)(2,1)} %get-tuple-element.18), channel_id=1, source_target_pairs={{0,32},{1,33},{2,34},{3,35},{4,36},{5,37},{6,38},{7,39},{8,40},{9,... | collective-permute-start | bytes 1376264 | tf_op jit(solution)/shard_map/ppermute | solution.py:39
  123.8 29.9 %all-to-all-start.2 = ((bf16[4,112,512]{2,1,0:T(8,128)(2,1)}), bf16[4,112,512]{2,1,0:T(8,128)(2,1)S(1)}, u32[]{:S(2)}, u32[]{:S(2)}) async-start(bf16[4,112,512]{2,1,0:T(8,128)(2,1)} %bitcast.21), calls=%async_computation.2 | async-start | bytes 917504 | tf_op jit(solution)/shard_map/all_to_all | solution.py:25
  133.3 5.8 %collective-permute-start.9 = (bf16[8,448,128]{2,1,0:T(8,128)(2,1)S(1)}, bf16[8,448,128]{2,1,0:T(8,128)(2,1)S(1)}, u32[]{:S(2)}, u32[]{:S(2)}) collective-permute-start(bf16[8,448,128]{2,1,0:T(8,128)(2,1)S(1)} %bitcast.49), channel_id=1, source_target_pairs={{0,1},{1,0},{2,3},{3,2},{4,5},{5,4},{6,7},{7,6},{8,9},{9,8},{10,11... | collective-permute-start | bytes 2752520 | tf_op jit(solution)/shard_map/ppermute | solution.py:39
  191.0 18.1 %all-to-all-start.4 = ((bf16[16,64,128]{2,1,0:T(8,128)(2,1)}), bf16[16,64,128]{2,1,0:T(8,128)(2,1)S(1)}, u32[]{:S(2)}, u32[]{:S(2)}) async-start(bf16[16,64,128]{2,1,0:T(8,128)(2,1)} %shard_map.58), calls=%async_computation.4 | async-start | bytes 524288 | tf_op jit(solution)/shard_map/all_to_all | solution.py:25

commit v6 on v5

--- a/solution.py
+++ b/solution.py
@@ -156,19 +156,18 @@
         part = lax.dynamic_slice_in_dim(halves, index, 1, 1).reshape(rows, LANES)
         return jnp.concatenate((part, gain))
 
+    down = jnp.pad(down_weight.reshape(64, units, LANES), ((0, 0), (0, 56 - units), (0, 0)))
+    down = down.reshape(2, 4, 2, 2, 112, LANES).transpose(3, 2, 0, 1, 4, 5).reshape(2, 2, 2, 448, LANES)
+
     both = jnp.stack((gate_weight, up_weight))
     both = jnp.pad(both, ((0, 0), (0, 56 - units), (0, 0))).reshape(112, FEAT)
     own_w = exchange(run(cut_kernel, (8, 112, 1024), (at, both)), PHASE)
     first = send(half(core), spread(0, 0))
     second = send(half(1 - core), spread(4, 1))
-    first, second, own_w = lax.optimization_barrier((first, second, own_w))
+    first, second, own_w, down = lax.optimization_barrier((first, second, own_w, down))
     other_w = send(own_w, shift(core=1))
     held = jnp.stack((first, second))
     blocks = [held] + [send(held, shift(xl=i, z0=j)) for i, j in ((0, 1), (1, 0), (1, 1))]
-
-    down, _ = lax.optimization_barrier((down_weight, held))
-    down = jnp.pad(down.reshape(64, units, LANES), ((0, 0), (0, 56 - units), (0, 0)))
-    down = down.reshape(2, 4, 2, 2, 112, LANES).transpose(3, 2, 0, 1, 4, 5).reshape(2, 2, 2, 448, LANES)
 
     def halve(value, axis):
         place = lax.axis_index(axis)
@@ -178,8 +177,6 @@
         return kept, send(sent, shift(**{axis: 1}))
 
     down = jnp.stack(halve(down, "z0"), 2)
-    down = jnp.stack(halve(down, "zm"), 1)
-
     sums = run(
         sums_kernel,
         (8, 2, 112, rows),
@@ -187,6 +184,8 @@
         (pltpu.VMEM((rows, 1024), bf16),),
         flops=2 * 1792 * 1024 * rows,
     )
+    sums, down = lax.optimization_barrier((sums, down))
+    down = jnp.stack(halve(down, "zm"), 1)
     sums, down = lax.optimization_barrier((exchange(sums, PHASE), down))
     down = jnp.stack(halve(down, "xl")).reshape(8, 448, LANES)
     down = jnp.stack((down, send(down, shift(core=1))), 1)

time: 211 us -> 210 us (level)
  starting transfers between devices: 83.2 us -> 99.7 us
  waiting for transfers between devices: 69.7 us -> 57 us
  blocking collectives: 32.9 us -> 26.5 us
    all_to_all x4, starting transfers between devices: 37.8 us -> 52 us  [exchange(): return lax.all_to_all(value, axes, 0, 0, tiled=True)]
    ppermute x10, waiting for transfers between devices: 50 us -> 40.4 us  [send(): return lax.ppermute(value, AXES, route(move))]
    all_to_all x1, blocking collectives: 32.9 us -> 26.5 us  [exchange(): return lax.all_to_all(value, axes, 0, 0, tiled=True)]
    all_to_all x4, waiting for transfers between devices: 19.7 us -> 16.6 us  [exchange(): return lax.all_to_all(value, axes, 0, 0, tiled=True)]
    ppermute x10, starting transfers between devices: 45.4 us -> 47.7 us  [send(): return lax.ppermute(value, AXES, route(move))]
  transfers between devices with their start and end apart: 14 -> 14, of which waited for: 9 -> 9; matrix products, arithmetic and copies ran while one was open for 3% -> 4% of each run, Pallas kernels for 1% -> 1%
where the time goes in v6:
time: 210 us
  starting transfers between devices  99.7 us (47%)
  waiting for transfers between devices  57 us (27%)
  blocking collectives  26.5 us (13%)
  local copies, waits for them, and re-layouts  9.49 us (5%)
  Pallas kernels  9.39 us (4%)
  other arithmetic  4.52 us (2%)
  matrix products  2.79 us (1%)
    all_to_all x4, starting transfers between devices, exchange(): return lax.all_to_all(value, axes, 0, 0, tiled=True)  52 us
    ppermute x10, starting transfers between devices, send(): return lax.ppermute(value, AXES, route(move))  47.7 us
    ppermute x10, waiting for transfers between devices, send(): return lax.ppermute(value, AXES, route(move))  40.4 us
    all_to_all x1, blocking collectives, exchange(): return lax.all_to_all(value, axes, 0, 0, tiled=True)  26.5 us
    all_to_all x4, waiting for transfers between devices, exchange(): return lax.all_to_all(value, axes, 0, 0, tiled=True)  16.6 us
    pallas_call x4, Pallas kernels, run(): pl.pallas_call(kernel, out_shape=jax.ShapeDtypeStruct(out_shape, bf16), i...  9.39 us
  transfers between devices with their start and end apart: 14, of which 9 were waited for; matrix products, arithmetic and copies ran while one was open for 4% of the time, Pallas kernels for 1%

profile of v6, /device:TPU:1, one launch (start us, length us, event | category | flops | bytes accessed | tf_op | source)
XLA Modules:
  0.0 209.6 jit_solution(12241338728390937974)
XLA Ops:
  0.0 1.6 fusion.2
  1.6 0.1 pad_add_fusion.at
  1.7 1.9 shard_map.55
  3.7 0.0 copy-start.2
  3.7 0.0 copy-start.3
  3.7 7.6 %all-to-all-start = ((bf16[8,112,1024]{2,1,0:T(8,128)(2,1)}), bf16[8,112,1024]{2,1,0:T(8,128)(2,1)S(1)}, u32[]{:S(2)}, u32[]{:S(2)}) async-start(bf16[8,112,1024]{2,1,0:T(8,128)(2,1)} %shard_map.55), calls=%async_computation | async-start | bytes 3670016 | tf_op jit(solution)/shard_map/all_to_all | solution.py:25
  11.3 0.0 copy-done.2
  11.3 0.0 copy-done.3
  11.3 0.7 pad_maximum_fusion.4
  12.0 1.6 collective-permute-start
  13.6 20.1 %collective-permute-start.1 = (bf16[528,128]{1,0:T(8,128)(2,1)S(1)}, bf16[528,128]{1,0:T(8,128)(2,1)S(1)}, u32[]{:S(2)}, u32[]{:S(2)}) collective-permute-start(bf16[528,128]{1,0:T(8,128)(2,1)S(1)} %get-tuple-element.29), channel_id=1, source_target_pairs={{0,17},{1,16},{2,19},{3,18},{4,77},{5,76},{6,79},{7,78},{8,137},{9... | collective-permute-start | bytes 405512 | tf_op jit(solution)/shard_map/ppermute | solution.py:39
  33.7 1.2 reshape.49
  35.0 0.1 pad.9
  35.1 0.1 copy.11
  35.1 0.0 collective-permute-done
  35.1 3.7 %collective-permute-done.1 = bf16[528,128]{1,0:T(8,128)(2,1)S(1)} collective-permute-done((bf16[528,128]{1,0:T(8,128)(2,1)S(1)}, bf16[528,128]{1,0:T(8,128)(2,1)S(1)}, u32[]{:S(2)}, u32[]{:S(2)}) %collective-permute-start.1) | collective-permute-done | bytes 135200 | tf_op jit(solution)/shard_map/ppermute | solution.py:39
  38.9 0.0 all-to-all-done.w_own
  38.9 1.9 collective-permute-start.5
  40.8 0.1 dynamic-slice_bitcast_fusion.2
  40.9 4.2 %collective-permute-start.6 = (bf16[2,2,448,128]{3,2,1,0:T(8,128)(2,1)S(1)}, bf16[2,2,448,128]{3,2,1,0:T(8,128)(2,1)S(1)}, u32[]{:S(2)}, u32[]{:S(2)}) collective-permute-start(bf16[2,2,448,128]{3,2,1,0:T(8,128)(2,1)S(1)} %get-tuple-element.26), channel_id=1, source_target_pairs={{0,2},{1,3},{2,0},{3,1},{4,6},{5,7},{6,4},{7,5},{8,10},{9,11},{10,... | collective-permute-start | bytes 1376264 | tf_op jit(solution)/shard_map/ppermute | solution.py:39
  45.1 1.9 collective-permute-start.2
  47.0 2.7 %collective-permute-start.3 = (bf16[2,528,128]{2,1,0:T(8,128)(2,1)S(1)}, bf16[2,528,128]{2,1,0:T(8,128)(2,1)S(1)}, u32[]{:S(2)}, u32[]{:S(2)}) collective-permute-start(bf16[2,528,128]{2,1,0:T(8,128)(2,1)S(1)} %pad_maximum_fusion.3.x0), channel_id=1, source_target_pairs={{0,32},{1,33},{2,34},{3,35},{4,36},{5,37},{6,38},{7,39},{8,40},{9,... | collective-permute-start | bytes 811016 | tf_op jit(solution)/shard_map/ppermute | solution.py:39
  49.7 3.7 %collective-permute-start.4 = (bf16[2,528,128]{2,1,0:T(8,128)(2,1)S(1)}, bf16[2,528,128]{2,1,0:T(8,128)(2,1)S(1)}, u32[]{:S(2)}, u32[]{:S(2)}) collective-permute-start(bf16[2,528,128]{2,1,0:T(8,128)(2,1)S(1)} %pad_maximum_fusion.3.x0), channel_id=1, source_target_pairs={{0,34},{1,35},{2,32},{3,33},{4,38},{5,39},{6,36},{7,37},{8,42},{9,... | collective-permute-start | bytes 811016 | tf_op jit(solution)/shard_map/ppermute | solution.py:39
  53.5 2.0 collective-permute-done.6
  55.5 0.1 pad_maximum_fusion
  55.5 5.7 %collective-permute-done.2.x1 = bf16[2,528,128]{2,1,0:T(8,128)(2,1)S(1)} collective-permute-done((bf16[2,528,128]{2,1,0:T(8,128)(2,1)S(1)}, bf16[2,528,128]{2,1,0:T(8,128)(2,1)S(1)}, u32[]{:S(2)}, u32[]{:S(2)}) %collective-permute-start.2) | collective-permute-done | bytes 270368 | tf_op jit(solution)/shard_map/ppermute | solution.py:39
  61.2 0.0 collective-permute-done.3.x2
  61.2 6.0 %collective-permute-done.4.x3 = bf16[2,528,128]{2,1,0:T(8,128)(2,1)S(1)} collective-permute-done((bf16[2,528,128]{2,1,0:T(8,128)(2,1)S(1)}, bf16[2,528,128]{2,1,0:T(8,128)(2,1)S(1)}, u32[]{:S(2)}, u32[]{:S(2)}) %collective-permute-start.4) | collective-permute-done | bytes 270368 | tf_op jit(solution)/shard_map/ppermute | solution.py:39
  67.3 0.0 collective-permute-done.5.w_other
  67.3 4.3 %shard_map.56 = bf16[8,2,112,512]{3,2,1,0:T(8,128)(2,1)S(1)} custom-call(s32[3]{0:T(128)S(1)} %pad_add_fusion.at, bf16[2,528,128]{2,1,0:T(8,128)(2,1)S(1)} %pad_maximum_fusion.3.x0, bf16[2,528,128]{2,1,0:T(8,128)(2,1)S(1)} %collective-permute-done.2.x1, bf16[2,528,128]{2,1,0:T(8,128)(2,1)S(1)} %collective-permute-done.3.x2, ...), custom_call_target="tpu_custom_call" | custom-call | flops 1879048192 | bytes 6586380 | tf_op jit(solution)/shard_map/pallas_call | solution.py:133
  71.6 0.0 copy-start
  71.6 1.3 copy-done
  72.8 14.4 %all-to-all-start.1 = ((bf16[8,2,112,512]{3,2,1,0:T(8,128)(2,1)}), bf16[8,2,112,512]{3,2,1,0:T(8,128)(2,1)S(1)}, u32[]{:S(2)}, u32[]{:S(2)}) async-start(bf16[8,2,112,512]{3,2,1,0:T(8,128)(2,1)} %copy-done), calls=%async_computation.1 | async-start | bytes 3670016 | tf_op jit(solution)/shard_map/all_to_all | solution.py:25
  87.2 0.1 constant_dynamic-slice_fusion.2
  87.3 0.8 copy.19
  88.1 4.2 %collective-permute-start.7 = (bf16[2,2,448,128]{3,2,1,0:T(8,128)(2,1)}, bf16[2,2,448,128]{3,2,1,0:T(8,128)(2,1)S(1)}, u32[]{:S(2)}, u32[]{:S(2)}) collective-permute-start(bf16[2,2,448,128]{3,2,1,0:T(8,128)(2,1)} %bitcast.45), channel_id=1, source_target_pairs={{0,4},{1,5},{2,6},{3,7},{4,0},{5,1},{6,2},{7,3},{8,12},{9,13},{10,... | collective-permute-start | bytes 1376264 | tf_op jit(solution)/shard_map/ppermute | solution.py:39
  92.3 20.0 %collective-permute-done.7 = bf16[2,2,448,128]{3,2,1,0:T(8,128)(2,1)S(1)} collective-permute-done((bf16[2,2,448,128]{3,2,1,0:T(8,128)(2,1)}, bf16[2,2,448,128]{3,2,1,0:T(8,128)(2,1)S(1)}, u32[]{:S(2)}, u32[]{:S(2)}) %collective-permute-start.7) | collective-permute-done | bytes 458784 | tf_op jit(solution)/shard_map/ppermute | solution.py:39
  112.4 0.0 copy-start.1
  112.4 0.8 copy-done.1
  113.1 1.1 pad_maximum_fusion.1
  114.2 0.0 all-to-all-done.1.sums
  114.2 0.8 constant_dynamic-slice_fusion
  115.1 3.0 %collective-permute-start.8 = (bf16[2,2,448,128]{3,2,1,0:T(8,128)(2,1)}, bf16[2,2,448,128]{3,2,1,0:T(8,128)(2,1)S(1)}, u32[]{:S(2)}, u32[]{:S(2)}) collective-permute-start(bf16[2,2,448,128]{3,2,1,0:T(8,128)(2,1)} %get-tuple-element.22), channel_id=1, source_target_pairs={{0,32},{1,33},{2,34},{3,35},{4,36},{5,37},{6,38},{7,39},{8,40},{9,... | collective-permute-start | bytes 1376264 | tf_op jit(solution)/shard_map/ppermute | solution.py:39
  118.1 1.6 shard_map.57
  119.8 7.1 %all-to-all-start.2 = ((bf16[4,112,512]{2,1,0:T(8,128)(2,1)}), bf16[4,112,512]{2,1,0:T(8,128)(2,1)S(1)}, u32[]{:S(2)}, u32[]{:S(2)}) async-start(bf16[4,112,512]{2,1,0:T(8,128)(2,1)} %bitcast.20), calls=%async_computation.2 | async-start | bytes 917504 | tf_op jit(solution)/shard_map/all_to_all | solution.py:25
  126.9 0.8 collective-permute-done.8
  127.7 0.1 pad_maximum_fusion.2
  127.8 4.3 %collective-permute-start.9 = (bf16[8,448,128]{2,1,0:T(8,128)(2,1)S(1)}, bf16[8,448,128]{2,1,0:T(8,128)(2,1)S(1)}, u32[]{:S(2)}, u32[]{:S(2)}) collective-permute-start(bf16[8,448,128]{2,1,0:T(8,128)(2,1)S(1)} %bitcast.49), channel_id=1, source_target_pairs={{0,1},{1,0},{2,3},{3,2},{4,5},{5,4},{6,7},{7,6},{8,9},{9,8},{10,11... | collective-permute-start | bytes 2752520 | tf_op jit(solution)/shard_map/ppermute | solution.py:39
  132.1 2.1 collective-permute-done.9
  134.2 0.2 maximum_bitcast_fusion
  134.4 1.9 copy.14
  136.3 2.4 %reshape.55 = bf16[448,2048]{1,0:T(8,128)(2,1)} reshape(bf16[448,8,2,128]{3,2,1,0:T(2,128)(2,1)S(1)} %copy.14) | data formatting | bytes 3670016 | tf_op jit(solution)/shard_map/reshape | solution.py:192
  138.6 7.1 %all-to-all-done.2 = bf16[4,112,512]{2,1,0:T(8,128)(2,1)S(1)} async-done(((bf16[4,112,512]{2,1,0:T(8,128)(2,1)}), bf16[4,112,512]{2,1,0:T(8,128)(2,1)S(1)}, u32[]{:S(2)}, u32[]{:S(2)}) %all-to-all-start.2) | async-done | bytes 458784 | tf_op jit(solution)/shard_map/all_to_all | solution.py:25
  145.7 2.8 %convolution_convert_fusion = bf16[512,2048]{1,0:T(8,128)(2,1)S(1)} fusion(bf16[448,512]{1,0:T(8,128)(2,1)S(1)} %bitcast.64, bf16[448,2048]{1,0:T(8,128)(2,1)} %reshape.55), kind=kOutput, calls=%fused_computation.3 | convolution fusion | flops 940572672 | bytes 4390912 | tf_op jit(solution)/shard_map/dot_general | solution.py:195
  148.5 26.5 %all_to_all.25.parts = bf16[8,64,2048]{2,1,0:T(8,128)(2,1)S(1)} all-to-all(bf16[8,64,2048]{2,1,0:T(8,128)(2,1)S(1)} %bitcast.53), channel_id=1, replica_groups=mesh['y'=4,'xh'=2,'xl'=2,'zh'=4,'zm'=2,'z0'=2,'core'=2] {'y','xh'}, dimensions={0} | all-to-all | bytes 4194304 | tf_op jit(solution)/shard_map/all_to_all | solution.py:25
  175.0 1.5 shard_map.58
  176.6 22.9 %all-to-all-start.4 = ((bf16[16,64,128]{2,1,0:T(8,128)(2,1)}), bf16[16,64,128]{2,1,0:T(8,128)(2,1)S(1)}, u32[]{:S(2)}, u32[]{:S(2)}) async-start(bf16[16,64,128]{2,1,0:T(8,128)(2,1)} %shard_map.58), calls=%async_computation.4 | async-start | bytes 524288 | tf_op jit(solution)/shard_map/all_to_all | solution.py:25
  199.4 9.5 %all-to-all-done.4 = bf16[16,64,128]{2,1,0:T(8,128)(2,1)S(1)} async-done(((bf16[16,64,128]{2,1,0:T(8,128)(2,1)}), bf16[16,64,128]{2,1,0:T(8,128)(2,1)S(1)}, u32[]{:S(2)}, u32[]{:S(2)}) %all-to-all-start.4) | async-done | bytes 262176 | tf_op jit(solution)/shard_map/all_to_all | solution.py:25
  209.0 0.6 add_convert_fusion
  (5 shorter events, 0.1 us)
Async XLA Ops:
  3.7 7.6 %copy-start.2 = (bf16[1024,128]{1,0:T(8,128)(2,1)S(1)}, bf16[1024,128]{1,0:T(8,128)(2,1)}, u32[]{:S(2)}) copy-start(bf16[1024,128]{1,0:T(8,128)(2,1)} %param.5) | copy-start | bytes 786436
  3.7 7.7 %copy-start.3 = (bf16[128]{0:T(256)(128)(2,1)S(1)}, bf16[128]{0:T(256)(128)(2,1)}, u32[]{:S(2)}) copy-start(bf16[128]{0:T(256)(128)(2,1)} %param.6) | copy-start | bytes 772
  3.7 35.2 %all-to-all-start = ((bf16[8,112,1024]{2,1,0:T(8,128)(2,1)}), bf16[8,112,1024]{2,1,0:T(8,128)(2,1)S(1)}, u32[]{:S(2)}, u32[]{:S(2)}) async-start(bf16[8,112,1024]{2,1,0:T(8,128)(2,1)} %shard_map.55), calls=%async_computation | async-start | bytes 3670016 | tf_op jit(solution)/shard_map/all_to_all | solution.py:25
  12.0 23.1 %collective-permute-start = (bf16[528,128]{1,0:T(8,128)(2,1)}, bf16[528,128]{1,0:T(8,128)(2,1)S(1)}, u32[]{:S(2)}, u32[]{:S(2)}) collective-permute-start(bf16[528,128]{1,0:T(8,128)(2,1)} %get-tuple-element.30), channel_id=1, source_target_pairs={{0,0},{1,1},{2,2},{3,3},{4,92},{5,93},{6,94},{7,95},{8,152},{9,153... | collective-permute-start | bytes 405512 | tf_op jit(solution)/shard_map/ppermute | solution.py:39
  13.6 25.3 %collective-permute-start.1 = (bf16[528,128]{1,0:T(8,128)(2,1)S(1)}, bf16[528,128]{1,0:T(8,128)(2,1)S(1)}, u32[]{:S(2)}, u32[]{:S(2)}) collective-permute-start(bf16[528,128]{1,0:T(8,128)(2,1)S(1)} %get-tuple-element.29), channel_id=1, source_target_pairs={{0,17},{1,16},{2,19},{3,18},{4,77},{5,76},{6,79},{7,78},{8,137},{9... | collective-permute-start | bytes 405512 | tf_op jit(solution)/shard_map/ppermute | solution.py:39
  38.9 28.4 %collective-permute-start.5 = (bf16[8,112,1024]{2,1,0:T(8,128)(2,1)S(1)}, bf16[8,112,1024]{2,1,0:T(8,128)(2,1)}, u32[]{:S(2)}, u32[]{:S(2)}) collective-permute-start(bf16[8,112,1024]{2,1,0:T(8,128)(2,1)S(1)} %all-to-all-done.w_own), channel_id=1, source_target_pairs={{0,1},{1,0},{2,3},{3,2},{4,5},{5,4},{6,7},{7,6},{8,9},{9,8},{10,11... | collective-permute-start | bytes 5505032 | tf_op jit(solution)/shard_map/ppermute | solution.py:39
  40.9 14.6 %collective-permute-start.6 = (bf16[2,2,448,128]{3,2,1,0:T(8,128)(2,1)S(1)}, bf16[2,2,448,128]{3,2,1,0:T(8,128)(2,1)S(1)}, u32[]{:S(2)}, u32[]{:S(2)}) collective-permute-start(bf16[2,2,448,128]{3,2,1,0:T(8,128)(2,1)S(1)} %get-tuple-element.26), channel_id=1, source_target_pairs={{0,2},{1,3},{2,0},{3,1},{4,6},{5,7},{6,4},{7,5},{8,10},{9,11},{10,... | collective-permute-start | bytes 1376264 | tf_op jit(solution)/shard_map/ppermute | solution.py:39
  45.1 16.2 %collective-permute-start.2 = (bf16[2,528,128]{2,1,0:T(8,128)(2,1)S(1)}, bf16[2,528,128]{2,1,0:T(8,128)(2,1)S(1)}, u32[]{:S(2)}, u32[]{:S(2)}) collective-permute-start(bf16[2,528,128]{2,1,0:T(8,128)(2,1)S(1)} %pad_maximum_fusion.3.x0), channel_id=1, source_target_pairs={{0,2},{1,3},{2,0},{3,1},{4,6},{5,7},{6,4},{7,5},{8,10},{9,11},{10,... | collective-permute-start | bytes 811016 | tf_op jit(solution)/shard_map/ppermute | solution.py:39
  47.0 14.3 %collective-permute-start.3 = (bf16[2,528,128]{2,1,0:T(8,128)(2,1)S(1)}, bf16[2,528,128]{2,1,0:T(8,128)(2,1)S(1)}, u32[]{:S(2)}, u32[]{:S(2)}) collective-permute-start(bf16[2,528,128]{2,1,0:T(8,128)(2,1)S(1)} %pad_maximum_fusion.3.x0), channel_id=1, source_target_pairs={{0,32},{1,33},{2,34},{3,35},{4,36},{5,37},{6,38},{7,39},{8,40},{9,... | collective-permute-start | bytes 811016 | tf_op jit(solution)/shard_map/ppermute | solution.py:39
  49.7 17.5 %collective-permute-start.4 = (bf16[2,528,128]{2,1,0:T(8,128)(2,1)S(1)}, bf16[2,528,128]{2,1,0:T(8,128)(2,1)S(1)}, u32[]{:S(2)}, u32[]{:S(2)}) collective-permute-start(bf16[2,528,128]{2,1,0:T(8,128)(2,1)S(1)} %pad_maximum_fusion.3.x0), channel_id=1, source_target_pairs={{0,34},{1,35},{2,32},{3,33},{4,38},{5,39},{6,36},{7,37},{8,42},{9,... | collective-permute-start | bytes 811016 | tf_op jit(solution)/shard_map/ppermute | solution.py:39
  71.6 1.3 copy-start
  72.8 41.4 %all-to-all-start.1 = ((bf16[8,2,112,512]{3,2,1,0:T(8,128)(2,1)}), bf16[8,2,112,512]{3,2,1,0:T(8,128)(2,1)S(1)}, u32[]{:S(2)}, u32[]{:S(2)}) async-start(bf16[8,2,112,512]{3,2,1,0:T(8,128)(2,1)} %copy-done), calls=%async_computation.1 | async-start | bytes 3670016 | tf_op jit(solution)/shard_map/all_to_all | solution.py:25
  88.1 24.3 %collective-permute-start.7 = (bf16[2,2,448,128]{3,2,1,0:T(8,128)(2,1)}, bf16[2,2,448,128]{3,2,1,0:T(8,128)(2,1)S(1)}, u32[]{:S(2)}, u32[]{:S(2)}) collective-permute-start(bf16[2,2,448,128]{3,2,1,0:T(8,128)(2,1)} %bitcast.45), channel_id=1, source_target_pairs={{0,4},{1,5},{2,6},{3,7},{4,0},{5,1},{6,2},{7,3},{8,12},{9,13},{10,... | collective-permute-start | bytes 1376264 | tf_op jit(solution)/shard_map/ppermute | solution.py:39
  112.4 0.8 copy-start.1
  115.1 12.6 %collective-permute-start.8 = (bf16[2,2,448,128]{3,2,1,0:T(8,128)(2,1)}, bf16[2,2,448,128]{3,2,1,0:T(8,128)(2,1)S(1)}, u32[]{:S(2)}, u32[]{:S(2)}) collective-permute-start(bf16[2,2,448,128]{3,2,1,0:T(8,128)(2,1)} %get-tuple-element.22), channel_id=1, source_target_pairs={{0,32},{1,33},{2,34},{3,35},{4,36},{5,37},{6,38},{7,39},{8,40},{9,... | collective-permute-start | bytes 1376264 | tf_op jit(solution)/shard_map/ppermute | solution.py:39
  119.8 26.0 %all-to-all-start.2 = ((bf16[4,112,512]{2,1,0:T(8,128)(2,1)}), bf16[4,112,512]{2,1,0:T(8,128)(2,1)S(1)}, u32[]{:S(2)}, u32[]{:S(2)}) async-start(bf16[4,112,512]{2,1,0:T(8,128)(2,1)} %bitcast.20), calls=%async_computation.2 | async-start | bytes 917504 | tf_op jit(solution)/shard_map/all_to_all | solution.py:25
  127.8 6.4 %collective-permute-start.9 = (bf16[8,448,128]{2,1,0:T(8,128)(2,1)S(1)}, bf16[8,448,128]{2,1,0:T(8,128)(2,1)S(1)}, u32[]{:S(2)}, u32[]{:S(2)}) collective-permute-start(bf16[8,448,128]{2,1,0:T(8,128)(2,1)S(1)} %bitcast.49), channel_id=1, source_target_pairs={{0,1},{1,0},{2,3},{3,2},{4,5},{5,4},{6,7},{7,6},{8,9},{9,8},{10,11... | collective-permute-start | bytes 2752520 | tf_op jit(solution)/shard_map/ppermute | solution.py:39
  176.6 32.4 %all-to-all-start.4 = ((bf16[16,64,128]{2,1,0:T(8,128)(2,1)}), bf16[16,64,128]{2,1,0:T(8,128)(2,1)S(1)}, u32[]{:S(2)}, u32[]{:S(2)}) async-start(bf16[16,64,128]{2,1,0:T(8,128)(2,1)} %shard_map.58), calls=%async_computation.4 | async-start | bytes 524288 | tf_op jit(solution)/shard_map/all_to_all | solution.py:25

commit v7 on v6

--- a/solution.py
+++ b/solution.py
@@ -156,8 +156,16 @@
         part = lax.dynamic_slice_in_dim(halves, index, 1, 1).reshape(rows, LANES)
         return jnp.concatenate((part, gain))
 
+    def halve(value, axis):
+        place = lax.axis_index(axis)
+        kept, sent = (
+            lax.dynamic_index_in_dim(value, i, 0, keepdims=False) for i in (place, 1 - place)
+        )
+        return kept, send(sent, shift(**{axis: 1}))
+
     down = jnp.pad(down_weight.reshape(64, units, LANES), ((0, 0), (0, 56 - units), (0, 0)))
     down = down.reshape(2, 4, 2, 2, 112, LANES).transpose(3, 2, 0, 1, 4, 5).reshape(2, 2, 2, 448, LANES)
+    down = jnp.stack(halve(down, "z0"), 2)
 
     both = jnp.stack((gate_weight, up_weight))
     both = jnp.pad(both, ((0, 0), (0, 56 - units), (0, 0))).reshape(112, FEAT)
@@ -169,14 +177,6 @@
     held = jnp.stack((first, second))
     blocks = [held] + [send(held, shift(xl=i, z0=j)) for i, j in ((0, 1), (1, 0), (1, 1))]
 
-    def halve(value, axis):
-        place = lax.axis_index(axis)
-        kept, sent = (
-            lax.dynamic_index_in_dim(value, i, 0, keepdims=False) for i in (place, 1 - place)
-        )
-        return kept, send(sent, shift(**{axis: 1}))
-
-    down = jnp.stack(halve(down, "z0"), 2)
     sums = run(
         sums_kernel,
         (8, 2, 112, rows),

time: 210 us -> 202 us (0.962)
  starting transfers between devices: 99.7 us -> 82.9 us
  blocking collectives: 26.5 us -> 32.5 us
  local copies, waits for them, and re-layouts: 9.49 us -> 11.7 us
    all_to_all x4, starting transfers between devices: 52 us -> 35.1 us  [exchange(): return lax.all_to_all(value, axes, 0, 0, tiled=True)]
    all_to_all x1, blocking collectives: 26.5 us -> 32.5 us  [exchange(): return lax.all_to_all(value, axes, 0, 0, tiled=True)]
  transfers between devices with their start and end apart: 14 -> 14, of which waited for: 9 -> 8; matrix products, arithmetic and copies ran while one was open for 4% -> 5% of each run, Pallas kernels for 1% -> 1%
where the time goes in v7:
time: 202 us; the launch traced here: 201 us
  starting transfers between devices  82.9 us (41%)
  waiting for transfers between devices  57 us (28%)
  blocking collectives  32.5 us (16%)
  local copies, waits for them, and re-layouts  11.7 us (6%)
  Pallas kernels  8.43 us (4%)
  other arithmetic  5.86 us (3%)
  matrix products  2.79 us (1%)
    ppermute x10, starting transfers between devices, send(): return lax.ppermute(value, AXES, route(move))  47.8 us
    ppermute x10, waiting for transfers between devices, send(): return lax.ppermute(value, AXES, route(move))  41.9 us
    all_to_all x4, starting transfers between devices, exchange(): return lax.all_to_all(value, axes, 0, 0, tiled=True)  35.1 us
    all_to_all x1, blocking collectives, exchange(): return lax.all_to_all(value, axes, 0, 0, tiled=True)  32.5 us
    all_to_all x4, waiting for transfers between devices, exchange(): return lax.all_to_all(value, axes, 0, 0, tiled=True)  15.1 us
    pallas_call x4, Pallas kernels, run(): pl.pallas_call(kernel, out_shape=jax.ShapeDtypeStruct(out_shape, bf16), i...  8.43 us
  transfers between devices with their start and end apart: 14, of which 8 were waited for; matrix products, arithmetic and copies ran while one was open for 5% of the time, Pallas kernels for 1%

profile of v7, /device:TPU:1, one launch (start us, length us, event | category | flops | bytes accessed | tf_op | source)
XLA Modules:
  0.0 201.5 jit_solution(7783643170938390166)
XLA Ops:
  0.0 1.6 fusion.2
  1.6 0.1 pad_add_fusion.at
  1.7 1.9 shard_map.55
  3.7 7.5 %all-to-all-start = ((bf16[8,112,1024]{2,1,0:T(8,128)(2,1)}), bf16[8,112,1024]{2,1,0:T(8,128)(2,1)S(1)}, u32[]{:S(2)}, u32[]{:S(2)}) async-start(bf16[8,112,1024]{2,1,0:T(8,128)(2,1)} %shard_map.55), calls=%async_computation | async-start | bytes 3670016 | tf_op jit(solution)/shard_map/all_to_all | solution.py:25
  11.1 1.2 reshape.49
  12.4 0.1 pad.9
  12.5 0.0 copy-start.3
  12.5 0.0 copy-start.5
  12.5 0.1 copy.11
  12.6 0.9 dynamic-slice_bitcast_fusion.2
  13.4 3.5 %collective-permute-start.2 = (bf16[2,2,448,128]{3,2,1,0:T(8,128)(2,1)}, bf16[2,2,448,128]{3,2,1,0:T(8,128)(2,1)S(1)}, u32[]{:S(2)}, u32[]{:S(2)}) collective-permute-start(bf16[2,2,448,128]{3,2,1,0:T(8,128)(2,1)} %get-tuple-element.26), channel_id=1, source_target_pairs={{0,2},{1,3},{2,0},{3,1},{4,6},{5,7},{6,4},{7,5},{8,10},{9,11},{10,... | collective-permute-start | bytes 1376264 | tf_op jit(solution)/shard_map/ppermute | solution.py:39
  17.0 0.0 copy-done.3
  17.0 0.0 copy-done.5
  17.1 0.7 collective-permute-start
  17.7 20.4 %collective-permute-start.1 = (bf16[528,128]{1,0:T(8,128)(2,1)S(1)}, bf16[528,128]{1,0:T(8,128)(2,1)}, u32[]{:S(2)}, u32[]{:S(2)}) collective-permute-start(bf16[528,128]{1,0:T(8,128)(2,1)S(1)} %get-tuple-element.29), channel_id=1, source_target_pairs={{0,17},{1,16},{2,19},{3,18},{4,77},{5,76},{6,79},{7,78},{8,137},{9... | collective-permute-start | bytes 405512 | tf_op jit(solution)/shard_map/ppermute | solution.py:39
  38.2 0.0 collective-permute-done.2
  38.2 0.0 copy-start.1
  38.2 0.8 copy-done.1
  39.0 1.1 pad_maximum_fusion
  40.1 0.0 collective-permute-done
  40.1 0.0 copy-start.4
  40.1 0.6 copy-done.4
  40.7 3.5 %collective-permute-done.1 = bf16[528,128]{1,0:T(8,128)(2,1)} collective-permute-done((bf16[528,128]{1,0:T(8,128)(2,1)S(1)}, bf16[528,128]{1,0:T(8,128)(2,1)}, u32[]{:S(2)}, u32[]{:S(2)}) %collective-permute-start.1) | collective-permute-done | bytes 135200 | tf_op jit(solution)/shard_map/ppermute | solution.py:39
  44.2 0.0 all-to-all-done.w_own
  44.2 2.0 %collective-permute-start.6 = (bf16[8,112,1024]{2,1,0:T(8,128)(2,1)S(1)}, bf16[8,112,1024]{2,1,0:T(8,128)(2,1)S(1)}, u32[]{:S(2)}, u32[]{:S(2)}) collective-permute-start(bf16[8,112,1024]{2,1,0:T(8,128)(2,1)S(1)} %all-to-all-done.w_own), channel_id=1, source_target_pairs={{0,1},{1,0},{2,3},{3,2},{4,5},{5,4},{6,7},{7,6},{8,9},{9,8},{10,11... | collective-permute-start | bytes 5505032 | tf_op jit(solution)/shard_map/ppermute | solution.py:39
  46.3 1.0 pad_maximum_fusion.3.x0
  47.3 2.4 %collective-permute-start.3 = (bf16[2,528,128]{2,1,0:T(8,128)(2,1)S(1)}, bf16[2,528,128]{2,1,0:T(8,128)(2,1)S(1)}, u32[]{:S(2)}, u32[]{:S(2)}) collective-permute-start(bf16[2,528,128]{2,1,0:T(8,128)(2,1)S(1)} %pad_maximum_fusion.3.x0), channel_id=1, source_target_pairs={{0,2},{1,3},{2,0},{3,1},{4,6},{5,7},{6,4},{7,5},{8,10},{9,11},{10,... | collective-permute-start | bytes 811016 | tf_op jit(solution)/shard_map/ppermute | solution.py:39
  49.7 2.2 %collective-permute-start.4 = (bf16[2,528,128]{2,1,0:T(8,128)(2,1)S(1)}, bf16[2,528,128]{2,1,0:T(8,128)(2,1)S(1)}, u32[]{:S(2)}, u32[]{:S(2)}) collective-permute-start(bf16[2,528,128]{2,1,0:T(8,128)(2,1)S(1)} %pad_maximum_fusion.3.x0), channel_id=1, source_target_pairs={{0,32},{1,33},{2,34},{3,35},{4,36},{5,37},{6,38},{7,39},{8,40},{9,... | collective-permute-start | bytes 811016 | tf_op jit(solution)/shard_map/ppermute | solution.py:39
  51.9 3.8 %collective-permute-start.5 = (bf16[2,528,128]{2,1,0:T(8,128)(2,1)S(1)}, bf16[2,528,128]{2,1,0:T(8,128)(2,1)S(1)}, u32[]{:S(2)}, u32[]{:S(2)}) collective-permute-start(bf16[2,528,128]{2,1,0:T(8,128)(2,1)S(1)} %pad_maximum_fusion.3.x0), channel_id=1, source_target_pairs={{0,34},{1,35},{2,32},{3,33},{4,38},{5,39},{6,36},{7,37},{8,42},{9,... | collective-permute-start | bytes 811016 | tf_op jit(solution)/shard_map/ppermute | solution.py:39
  55.7 1.2 collective-permute-done.3.x1
  56.9 7.9 %collective-permute-done.4.x2 = bf16[2,528,128]{2,1,0:T(8,128)(2,1)S(1)} collective-permute-done((bf16[2,528,128]{2,1,0:T(8,128)(2,1)S(1)}, bf16[2,528,128]{2,1,0:T(8,128)(2,1)S(1)}, u32[]{:S(2)}, u32[]{:S(2)}) %collective-permute-start.4) | collective-permute-done | bytes 270368 | tf_op jit(solution)/shard_map/ppermute | solution.py:39
  64.8 0.0 collective-permute-done.5.x3
  64.8 0.0 collective-permute-done.6.w_other
  64.8 3.3 %shard_map.56 = bf16[8,2,112,512]{3,2,1,0:T(8,128)(2,1)S(1)} custom-call(s32[3]{0:T(128)S(1)} %pad_add_fusion.at, bf16[2,528,128]{2,1,0:T(8,128)(2,1)S(1)} %pad_maximum_fusion.3.x0, bf16[2,528,128]{2,1,0:T(8,128)(2,1)S(1)} %collective-permute-done.3.x1, bf16[2,528,128]{2,1,0:T(8,128)(2,1)S(1)} %collective-permute-done.4.x2, ...), custom_call_target="tpu_custom_call" | custom-call | flops 1879048192 | bytes 6586380 | tf_op jit(solution)/shard_map/pallas_call | solution.py:133
  68.2 0.0 copy-start
  68.2 1.2 copy-done
  69.4 13.3 %all-to-all-start.1 = ((bf16[8,2,112,512]{3,2,1,0:T(8,128)(2,1)}), bf16[8,2,112,512]{3,2,1,0:T(8,128)(2,1)S(1)}, u32[]{:S(2)}, u32[]{:S(2)}) async-start(bf16[8,2,112,512]{3,2,1,0:T(8,128)(2,1)} %copy-done), calls=%async_computation.1 | async-start | bytes 3670016 | tf_op jit(solution)/shard_map/all_to_all | solution.py:25
  82.7 0.1 constant_dynamic-slice_fusion.2
  82.8 0.8 copy.19
  83.6 7.2 %collective-permute-start.7 = (bf16[2,2,448,128]{3,2,1,0:T(8,128)(2,1)}, bf16[2,2,448,128]{3,2,1,0:T(8,128)(2,1)S(1)}, u32[]{:S(2)}, u32[]{:S(2)}) collective-permute-start(bf16[2,2,448,128]{3,2,1,0:T(8,128)(2,1)} %bitcast.45), channel_id=1, source_target_pairs={{0,4},{1,5},{2,6},{3,7},{4,0},{5,1},{6,2},{7,3},{8,12},{9,13},{10,... | collective-permute-start | bytes 1376264 | tf_op jit(solution)/shard_map/ppermute | solution.py:39
  90.8 20.9 %collective-permute-done.7 = bf16[2,2,448,128]{3,2,1,0:T(8,128)(2,1)S(1)} collective-permute-done((bf16[2,2,448,128]{3,2,1,0:T(8,128)(2,1)}, bf16[2,2,448,128]{3,2,1,0:T(8,128)(2,1)S(1)}, u32[]{:S(2)}, u32[]{:S(2)}) %collective-permute-start.7) | collective-permute-done | bytes 458784 | tf_op jit(solution)/shard_map/ppermute | solution.py:39
  111.8 0.0 copy-start.2
  111.8 0.8 copy-done.2
  112.6 1.1 pad_maximum_fusion.1
  113.7 0.0 all-to-all-done.1.sums
  113.7 0.9 constant_dynamic-slice_fusion
  114.5 2.2 %collective-permute-start.8 = (bf16[2,2,448,128]{3,2,1,0:T(8,128)(2,1)}, bf16[2,2,448,128]{3,2,1,0:T(8,128)(2,1)S(1)}, u32[]{:S(2)}, u32[]{:S(2)}) collective-permute-start(bf16[2,2,448,128]{3,2,1,0:T(8,128)(2,1)} %get-tuple-element.22), channel_id=1, source_target_pairs={{0,32},{1,33},{2,34},{3,35},{4,36},{5,37},{6,38},{7,39},{8,40},{9,... | collective-permute-start | bytes 1376264 | tf_op jit(solution)/shard_map/ppermute | solution.py:39
  116.7 1.7 shard_map.57
  118.4 3.5 %all-to-all-start.2 = ((bf16[4,112,512]{2,1,0:T(8,128)(2,1)}), bf16[4,112,512]{2,1,0:T(8,128)(2,1)S(1)}, u32[]{:S(2)}, u32[]{:S(2)}) async-start(bf16[4,112,512]{2,1,0:T(8,128)(2,1)} %bitcast.21), calls=%async_computation.2 | async-start | bytes 917504 | tf_op jit(solution)/shard_map/all_to_all | solution.py:25
  121.9 6.3 %collective-permute-done.8 = bf16[2,2,448,128]{3,2,1,0:T(8,128)(2,1)S(1)} collective-permute-done((bf16[2,2,448,128]{3,2,1,0:T(8,128)(2,1)}, bf16[2,2,448,128]{3,2,1,0:T(8,128)(2,1)S(1)}, u32[]{:S(2)}, u32[]{:S(2)}) %collective-permute-start.8) | collective-permute-done | bytes 458784 | tf_op jit(solution)/shard_map/ppermute | solution.py:39
  128.2 0.1 pad_maximum_fusion.2
  128.2 3.3 %collective-permute-start.9 = (bf16[8,448,128]{2,1,0:T(8,128)(2,1)S(1)}, bf16[8,448,128]{2,1,0:T(8,128)(2,1)S(1)}, u32[]{:S(2)}, u32[]{:S(2)}) collective-permute-start(bf16[8,448,128]{2,1,0:T(8,128)(2,1)S(1)} %bitcast.49), channel_id=1, source_target_pairs={{0,1},{1,0},{2,3},{3,2},{4,5},{5,4},{6,7},{7,6},{8,9},{9,8},{10,11... | collective-permute-start | bytes 2752520 | tf_op jit(solution)/shard_map/ppermute | solution.py:39
  131.6 2.1 %collective-permute-done.9 = bf16[8,448,128]{2,1,0:T(8,128)(2,1)S(1)} collective-permute-done((bf16[8,448,128]{2,1,0:T(8,128)(2,1)S(1)}, bf16[8,448,128]{2,1,0:T(8,128)(2,1)S(1)}, u32[]{:S(2)}, u32[]{:S(2)}) %collective-permute-start.9) | collective-permute-done | bytes 917536 | tf_op jit(solution)/shard_map/ppermute | solution.py:39
  133.6 0.2 maximum_bitcast_fusion
  133.8 1.9 copy.14
  135.7 2.4 %reshape.55 = bf16[448,2048]{1,0:T(8,128)(2,1)} reshape(bf16[448,8,2,128]{3,2,1,0:T(2,128)(2,1)S(1)} %copy.14) | data formatting | bytes 3670016 | tf_op jit(solution)/shard_map/reshape | solution.py:192
  138.1 5.6 %all-to-all-done.2 = bf16[4,112,512]{2,1,0:T(8,128)(2,1)S(1)} async-done(((bf16[4,112,512]{2,1,0:T(8,128)(2,1)}), bf16[4,112,512]{2,1,0:T(8,128)(2,1)S(1)}, u32[]{:S(2)}, u32[]{:S(2)}) %all-to-all-start.2) | async-done | bytes 458784 | tf_op jit(solution)/shard_map/all_to_all | solution.py:25
  143.6 2.8 %convolution_convert_fusion = bf16[512,2048]{1,0:T(8,128)(2,1)S(1)} fusion(bf16[448,512]{1,0:T(8,128)(2,1)S(1)} %bitcast.64, bf16[448,2048]{1,0:T(8,128)(2,1)} %reshape.55), kind=kOutput, calls=%fused_computation.3 | convolution fusion | flops 940572672 | bytes 4390912 | tf_op jit(solution)/shard_map/dot_general | solution.py:195
  146.4 32.5 %all_to_all.25.parts = bf16[8,64,2048]{2,1,0:T(8,128)(2,1)S(1)} all-to-all(bf16[8,64,2048]{2,1,0:T(8,128)(2,1)S(1)} %bitcast.53), channel_id=1, replica_groups=mesh['y'=4,'xh'=2,'xl'=2,'zh'=4,'zm'=2,'z0'=2,'core'=2] {'y','xh'}, dimensions={0} | all-to-all | bytes 4194304 | tf_op jit(solution)/shard_map/all_to_all | solution.py:25
  178.9 1.5 shard_map.58
  180.4 10.9 %all-to-all-start.4 = ((bf16[16,64,128]{2,1,0:T(8,128)(2,1)}), bf16[16,64,128]{2,1,0:T(8,128)(2,1)S(1)}, u32[]{:S(2)}, u32[]{:S(2)}) async-start(bf16[16,64,128]{2,1,0:T(8,128)(2,1)} %shard_map.58), calls=%async_computation.4 | async-start | bytes 524288 | tf_op jit(solution)/shard_map/all_to_all | solution.py:25
  191.3 9.5 %all-to-all-done.4 = bf16[16,64,128]{2,1,0:T(8,128)(2,1)S(1)} async-done(((bf16[16,64,128]{2,1,0:T(8,128)(2,1)}), bf16[16,64,128]{2,1,0:T(8,128)(2,1)S(1)}, u32[]{:S(2)}, u32[]{:S(2)}) %all-to-all-start.4) | async-done | bytes 262176 | tf_op jit(solution)/shard_map/all_to_all | solution.py:25
  200.8 0.6 add_convert_fusion
  (5 shorter events, 0.1 us)
Async XLA Ops:
  3.7 40.6 %all-to-all-start = ((bf16[8,112,1024]{2,1,0:T(8,128)(2,1)}), bf16[8,112,1024]{2,1,0:T(8,128)(2,1)S(1)}, u32[]{:S(2)}, u32[]{:S(2)}) async-start(bf16[8,112,1024]{2,1,0:T(8,128)(2,1)} %shard_map.55), calls=%async_computation | async-start | bytes 3670016 | tf_op jit(solution)/shard_map/all_to_all | solution.py:25
  12.5 4.5 %copy-start.3 = (bf16[1024,128]{1,0:T(8,128)(2,1)S(1)}, bf16[1024,128]{1,0:T(8,128)(2,1)}, u32[]{:S(2)}) copy-start(bf16[1024,128]{1,0:T(8,128)(2,1)} %param.5) | copy-start | bytes 786436
  12.5 4.5 %copy-start.5 = (bf16[128]{0:T(256)(128)(2,1)S(1)}, bf16[128]{0:T(256)(128)(2,1)}, u32[]{:S(2)}) copy-start(bf16[128]{0:T(256)(128)(2,1)} %param.6) | copy-start | bytes 772
  13.4 24.8 %collective-permute-start.2 = (bf16[2,2,448,128]{3,2,1,0:T(8,128)(2,1)}, bf16[2,2,448,128]{3,2,1,0:T(8,128)(2,1)S(1)}, u32[]{:S(2)}, u32[]{:S(2)}) collective-permute-start(bf16[2,2,448,128]{3,2,1,0:T(8,128)(2,1)} %get-tuple-element.26), channel_id=1, source_target_pairs={{0,2},{1,3},{2,0},{3,1},{4,6},{5,7},{6,4},{7,5},{8,10},{9,11},{10,... | collective-permute-start | bytes 1376264 | tf_op jit(solution)/shard_map/ppermute | solution.py:39
  17.1 23.0 %collective-permute-start = (bf16[528,128]{1,0:T(8,128)(2,1)S(1)}, bf16[528,128]{1,0:T(8,128)(2,1)S(1)}, u32[]{:S(2)}, u32[]{:S(2)}) collective-permute-start(bf16[528,128]{1,0:T(8,128)(2,1)S(1)} %get-tuple-element.30), channel_id=1, source_target_pairs={{0,0},{1,1},{2,2},{3,3},{4,92},{5,93},{6,94},{7,95},{8,152},{9,153... | collective-permute-start | bytes 405512 | tf_op jit(solution)/shard_map/ppermute | solution.py:39
  17.7 26.5 %collective-permute-start.1 = (bf16[528,128]{1,0:T(8,128)(2,1)S(1)}, bf16[528,128]{1,0:T(8,128)(2,1)}, u32[]{:S(2)}, u32[]{:S(2)}) collective-permute-start(bf16[528,128]{1,0:T(8,128)(2,1)S(1)} %get-tuple-element.29), channel_id=1, source_target_pairs={{0,17},{1,16},{2,19},{3,18},{4,77},{5,76},{6,79},{7,78},{8,137},{9... | collective-permute-start | bytes 405512 | tf_op jit(solution)/shard_map/ppermute | solution.py:39
  38.2 0.8 copy-start.1
  40.1 0.7 copy-start.4
  44.2 20.6 %collective-permute-start.6 = (bf16[8,112,1024]{2,1,0:T(8,128)(2,1)S(1)}, bf16[8,112,1024]{2,1,0:T(8,128)(2,1)S(1)}, u32[]{:S(2)}, u32[]{:S(2)}) collective-permute-start(bf16[8,112,1024]{2,1,0:T(8,128)(2,1)S(1)} %all-to-all-done.w_own), channel_id=1, source_target_pairs={{0,1},{1,0},{2,3},{3,2},{4,5},{5,4},{6,7},{7,6},{8,9},{9,8},{10,11... | collective-permute-start | bytes 5505032 | tf_op jit(solution)/shard_map/ppermute | solution.py:39
  47.3 9.6 %collective-permute-start.3 = (bf16[2,528,128]{2,1,0:T(8,128)(2,1)S(1)}, bf16[2,528,128]{2,1,0:T(8,128)(2,1)S(1)}, u32[]{:S(2)}, u32[]{:S(2)}) collective-permute-start(bf16[2,528,128]{2,1,0:T(8,128)(2,1)S(1)} %pad_maximum_fusion.3.x0), channel_id=1, source_target_pairs={{0,2},{1,3},{2,0},{3,1},{4,6},{5,7},{6,4},{7,5},{8,10},{9,11},{10,... | collective-permute-start | bytes 811016 | tf_op jit(solution)/shard_map/ppermute | solution.py:39
  49.7 15.1 %collective-permute-start.4 = (bf16[2,528,128]{2,1,0:T(8,128)(2,1)S(1)}, bf16[2,528,128]{2,1,0:T(8,128)(2,1)S(1)}, u32[]{:S(2)}, u32[]{:S(2)}) collective-permute-start(bf16[2,528,128]{2,1,0:T(8,128)(2,1)S(1)} %pad_maximum_fusion.3.x0), channel_id=1, source_target_pairs={{0,32},{1,33},{2,34},{3,35},{4,36},{5,37},{6,38},{7,39},{8,40},{9,... | collective-permute-start | bytes 811016 | tf_op jit(solution)/shard_map/ppermute | solution.py:39
  51.9 12.9 %collective-permute-start.5 = (bf16[2,528,128]{2,1,0:T(8,128)(2,1)S(1)}, bf16[2,528,128]{2,1,0:T(8,128)(2,1)S(1)}, u32[]{:S(2)}, u32[]{:S(2)}) collective-permute-start(bf16[2,528,128]{2,1,0:T(8,128)(2,1)S(1)} %pad_maximum_fusion.3.x0), channel_id=1, source_target_pairs={{0,34},{1,35},{2,32},{3,33},{4,38},{5,39},{6,36},{7,37},{8,42},{9,... | collective-permute-start | bytes 811016 | tf_op jit(solution)/shard_map/ppermute | solution.py:39
  68.2 1.3 copy-start
  69.4 44.2 %all-to-all-start.1 = ((bf16[8,2,112,512]{3,2,1,0:T(8,128)(2,1)}), bf16[8,2,112,512]{3,2,1,0:T(8,128)(2,1)S(1)}, u32[]{:S(2)}, u32[]{:S(2)}) async-start(bf16[8,2,112,512]{3,2,1,0:T(8,128)(2,1)} %copy-done), calls=%async_computation.1 | async-start | bytes 3670016 | tf_op jit(solution)/shard_map/all_to_all | solution.py:25
  83.6 28.2 %collective-permute-start.7 = (bf16[2,2,448,128]{3,2,1,0:T(8,128)(2,1)}, bf16[2,2,448,128]{3,2,1,0:T(8,128)(2,1)S(1)}, u32[]{:S(2)}, u32[]{:S(2)}) collective-permute-start(bf16[2,2,448,128]{3,2,1,0:T(8,128)(2,1)} %bitcast.45), channel_id=1, source_target_pairs={{0,4},{1,5},{2,6},{3,7},{4,0},{5,1},{6,2},{7,3},{8,12},{9,13},{10,... | collective-permute-start | bytes 1376264 | tf_op jit(solution)/shard_map/ppermute | solution.py:39
  111.8 0.8 copy-start.2
  114.5 13.6 %collective-permute-start.8 = (bf16[2,2,448,128]{3,2,1,0:T(8,128)(2,1)}, bf16[2,2,448,128]{3,2,1,0:T(8,128)(2,1)S(1)}, u32[]{:S(2)}, u32[]{:S(2)}) collective-permute-start(bf16[2,2,448,128]{3,2,1,0:T(8,128)(2,1)} %get-tuple-element.22), channel_id=1, source_target_pairs={{0,32},{1,33},{2,34},{3,35},{4,36},{5,37},{6,38},{7,39},{8,40},{9,... | collective-permute-start | bytes 1376264 | tf_op jit(solution)/shard_map/ppermute | solution.py:39
  118.4 25.2 %all-to-all-start.2 = ((bf16[4,112,512]{2,1,0:T(8,128)(2,1)}), bf16[4,112,512]{2,1,0:T(8,128)(2,1)S(1)}, u32[]{:S(2)}, u32[]{:S(2)}) async-start(bf16[4,112,512]{2,1,0:T(8,128)(2,1)} %bitcast.21), calls=%async_computation.2 | async-start | bytes 917504 | tf_op jit(solution)/shard_map/all_to_all | solution.py:25
  128.2 5.4 %collective-permute-start.9 = (bf16[8,448,128]{2,1,0:T(8,128)(2,1)S(1)}, bf16[8,448,128]{2,1,0:T(8,128)(2,1)S(1)}, u32[]{:S(2)}, u32[]{:S(2)}) collective-permute-start(bf16[8,448,128]{2,1,0:T(8,128)(2,1)S(1)} %bitcast.49), channel_id=1, source_target_pairs={{0,1},{1,0},{2,3},{3,2},{4,5},{5,4},{6,7},{7,6},{8,9},{9,8},{10,11... | collective-permute-start | bytes 2752520 | tf_op jit(solution)/shard_map/ppermute | solution.py:39
  180.4 20.4 %all-to-all-start.4 = ((bf16[16,64,128]{2,1,0:T(8,128)(2,1)}), bf16[16,64,128]{2,1,0:T(8,128)(2,1)S(1)}, u32[]{:S(2)}, u32[]{:S(2)}) async-start(bf16[16,64,128]{2,1,0:T(8,128)(2,1)} %shard_map.58), calls=%async_computation.4 | async-start | bytes 524288 | tf_op jit(solution)/shard_map/all_to_all | solution.py:25

commit v8 on v7

--- a/solution.py
+++ b/solution.py
@@ -57,12 +57,14 @@
     return move
 
 
-def cut_kernel(at, both, out):
+def cut_kernel(at, gate, up, out):
     del at
+    zero = jnp.zeros((56 - gate.shape[0], 512), f32)
     for group in range(8):
         for side in (0, 1):
             start = side * FEAT // 2 + group * 512
-            out[group, :, side * 512 : side * 512 + 512] = both[:, start : start + 512]
+            parts = (gate[:, start : start + 512].astype(f32), zero, up[:, start : start + 512].astype(f32), zero)
+            out[group, :, side * 512 : side * 512 + 512] = jnp.concatenate(parts).astype(bf16)
 
 
 def sums_kernel(at, x0, x1, x2, x3, w_own, w_other, out, scaled):
@@ -167,9 +169,7 @@
     down = down.reshape(2, 4, 2, 2, 112, LANES).transpose(3, 2, 0, 1, 4, 5).reshape(2, 2, 2, 448, LANES)
     down = jnp.stack(halve(down, "z0"), 2)
 
-    both = jnp.stack((gate_weight, up_weight))
-    both = jnp.pad(both, ((0, 0), (0, 56 - units), (0, 0))).reshape(112, FEAT)
-    own_w = exchange(run(cut_kernel, (8, 112, 1024), (at, both)), PHASE)
+    own_w = exchange(run(cut_kernel, (8, 112, 1024), (at, gate_weight, up_weight)), PHASE)
     first = send(half(core), spread(0, 0))
     second = send(half(1 - core), spread(4, 1))
     first, second, own_w, down = lax.optimization_barrier((first, second, own_w, down))
@@ -184,13 +184,13 @@
         (pltpu.VMEM((rows, 1024), bf16),),
         flops=2 * 1792 * 1024 * rows,
     )
-    sums, down = lax.optimization_barrier((sums, down))
-    down = jnp.stack(halve(down, "zm"), 1)
-    sums, down = lax.optimization_barrier((exchange(sums, PHASE), down))
-    down = jnp.stack(halve(down, "xl")).reshape(8, 448, LANES)
+    kept, got = halve(down, "zm")
+    acts = run(acts_kernel, (4, 2, 56, rows), (at, exchange(sums, PHASE)))
+    acts, got = lax.optimization_barrier((acts, got))
+    (kept0, got0), (kept1, got1) = halve(kept, "xl"), halve(got, "xl")
+    down = jnp.stack((kept0, kept1, got0, got1)).reshape(8, 448, LANES)
     down = jnp.stack((down, send(down, shift(core=1))), 1)
     down = down.transpose(2, 0, 1, 3).reshape(448, 2048)
-    acts = run(acts_kernel, (4, 2, 56, rows), (at, sums))
     acts = exchange(acts.reshape(4, 112, rows), FAR).reshape(448, rows)
     partials = lax.dot_general(
         acts, down, (((0,), (0,)), ((), ())), preferred_element_type=f32

time: 202 us -> 199 us (0.985)
  blocking collectives: 32.5 us -> 44.1 us
  waiting for transfers between devices: 57 us -> 49.7 us
  starting transfers between devices: 82.9 us -> 77.2 us
  other arithmetic: 5.86 us -> 2.94 us
    ppermute x10 -> x11, waiting for transfers between devices: 41.9 us -> 18.5 us  [send(): return lax.ppermute(value, AXES, route(move))]
    all_to_all x4, waiting for transfers between devices: 15.1 us -> 31.2 us  [exchange(): return lax.all_to_all(value, axes, 0, 0, tiled=True)]
    all_to_all x1, blocking collectives: 32.5 us -> 44.1 us  [exchange(): return lax.all_to_all(value, axes, 0, 0, tiled=True)]
    ppermute x10 -> x11, starting transfers between devices: 47.8 us -> 44 us  [send(): return lax.ppermute(value, AXES, route(move))]
    another operation x3 -> x1, other arithmetic: 2.82 us -> 0.12 us  [local(): down = jnp.stack((kept0, kept1, got0, got1)).reshape(8, 448, LANES)]
  transfers between devices with their start and end apart: 14 -> 15, of which waited for: 8 -> 8; matrix products, arithmetic and copies ran while one was open for 5% -> 5% of each run, Pallas kernels for 1% -> 1%
where the time goes in v8:
time: 199 us; the launch traced here: 198 us
  starting transfers between devices  77.2 us (39%)
  waiting for transfers between devices  49.7 us (25%)
  blocking collectives  44.1 us (22%)
  local copies, waits for them, and re-layouts  12.7 us (6%)
  Pallas kernels  8.39 us (4%)
  other arithmetic  2.94 us (1%)
  matrix products  2.79 us (1%)
    all_to_all x1, blocking collectives, exchange(): return lax.all_to_all(value, axes, 0, 0, tiled=True)  44.1 us
    ppermute x11, starting transfers between devices, send(): return lax.ppermute(value, AXES, route(move))  44 us
    all_to_all x4, starting transfers between devices, exchange(): return lax.all_to_all(value, axes, 0, 0, tiled=True)  33.3 us
    all_to_all x4, waiting for transfers between devices, exchange(): return lax.all_to_all(value, axes, 0, 0, tiled=True)  31.2 us
    ppermute x11, waiting for transfers between devices, send(): return lax.ppermute(value, AXES, route(move))  18.5 us
    pallas_call x4, Pallas kernels, run(): pl.pallas_call(kernel, out_shape=jax.ShapeDtypeStruct(out_shape, bf16), i...  8.39 us
    unnamed x12, local copies, waits for them, and re-layouts  4.38 us
  transfers between devices with their start and end apart: 15, of which 8 were waited for; matrix products, arithmetic and copies ran while one was open for 5% of the time, Pallas kernels for 1%

profile of v8, /device:TPU:1, one launch (start us, length us, event | category | flops | bytes accessed | tf_op | source)
XLA Modules:
  0.0 198.1 jit_solution(2695689478832269952)
XLA Ops:
  0.0 0.1 pad_add_fusion.at
  0.1 0.0 copy-start.1
  0.1 1.2 copy-done.1
  1.3 0.0 copy-start.2
  1.3 1.2 copy-done.2
  2.4 1.9 shard_map.55
  4.4 7.5 %all-to-all-start = ((bf16[8,112,1024]{2,1,0:T(8,128)(2,1)}), bf16[8,112,1024]{2,1,0:T(8,128)(2,1)S(1)}, u32[]{:S(2)}, u32[]{:S(2)}) async-start(bf16[8,112,1024]{2,1,0:T(8,128)(2,1)} %shard_map.55), calls=%async_computation | async-start | bytes 3670016 | tf_op jit(solution)/shard_map/all_to_all | solution.py:25
  11.8 1.2 reshape.47
  13.1 0.1 pad.4
  13.2 0.0 copy-start.4
  13.2 0.0 copy-start.5
  13.2 0.1 copy.15
  13.3 0.8 dynamic-slice_bitcast_fusion.2
  14.1 3.5 %collective-permute-start.2 = (bf16[2,2,448,128]{3,2,1,0:T(8,128)(2,1)}, bf16[2,2,448,128]{3,2,1,0:T(8,128)(2,1)S(1)}, u32[]{:S(2)}, u32[]{:S(2)}) collective-permute-start(bf16[2,2,448,128]{3,2,1,0:T(8,128)(2,1)} %get-tuple-element.20), channel_id=1, source_target_pairs={{0,2},{1,3},{2,0},{3,1},{4,6},{5,7},{6,4},{7,5},{8,10},{9,11},{10,... | collective-permute-start | bytes 1376264 | tf_op jit(solution)/shard_map/ppermute | solution.py:39
  17.7 0.0 copy-done.4
  17.7 0.0 copy-done.5
  17.8 15.7 %collective-permute-start.1 = (bf16[528,128]{1,0:T(8,128)(2,1)S(1)}, bf16[528,128]{1,0:T(8,128)(2,1)S(1)}, u32[]{:S(2)}, u32[]{:S(2)}) collective-permute-start(bf16[528,128]{1,0:T(8,128)(2,1)S(1)} %get-tuple-element.25), channel_id=1, source_target_pairs={{0,17},{1,16},{2,19},{3,18},{4,77},{5,76},{6,79},{7,78},{8,137},{9... | collective-permute-start | bytes 405512 | tf_op jit(solution)/shard_map/ppermute | solution.py:39
  33.4 0.7 collective-permute-start
  34.1 0.0 collective-permute-done.2
  34.1 0.0 copy-start.3
  34.1 0.8 copy-done.3
  34.9 1.1 pad_maximum_fusion
  36.0 2.5 %collective-permute-done.1 = bf16[528,128]{1,0:T(8,128)(2,1)S(1)} collective-permute-done((bf16[528,128]{1,0:T(8,128)(2,1)S(1)}, bf16[528,128]{1,0:T(8,128)(2,1)S(1)}, u32[]{:S(2)}, u32[]{:S(2)}) %collective-permute-start.1) | collective-permute-done | bytes 135200 | tf_op jit(solution)/shard_map/ppermute | solution.py:39
  38.5 0.0 collective-permute-done
  38.5 0.0 all-to-all-done.w_own
  38.5 2.2 %collective-permute-start.6 = (bf16[8,112,1024]{2,1,0:T(8,128)(2,1)S(1)}, bf16[8,112,1024]{2,1,0:T(8,128)(2,1)S(1)}, u32[]{:S(2)}, u32[]{:S(2)}) collective-permute-start(bf16[8,112,1024]{2,1,0:T(8,128)(2,1)S(1)} %all-to-all-done.w_own), channel_id=1, source_target_pairs={{0,1},{1,0},{2,3},{3,2},{4,5},{5,4},{6,7},{7,6},{8,9},{9,8},{10,11... | collective-permute-start | bytes 5505032 | tf_op jit(solution)/shard_map/ppermute | solution.py:39
  40.8 4.0 %collective-permute-start.5 = (bf16[2,528,128]{2,1,0:T(8,128)(2,1)S(1)}, bf16[2,528,128]{2,1,0:T(8,128)(2,1)S(1)}, u32[]{:S(2)}, u32[]{:S(2)}) collective-permute-start(bf16[2,528,128]{2,1,0:T(8,128)(2,1)S(1)} %pad_maximum_fusion.2.x0), channel_id=1, source_target_pairs={{0,34},{1,35},{2,32},{3,33},{4,38},{5,39},{6,36},{7,37},{8,42},{9,... | collective-permute-start | bytes 811016 | tf_op jit(solution)/shard_map/ppermute | solution.py:39
  44.7 2.8 %collective-permute-start.4 = (bf16[2,528,128]{2,1,0:T(8,128)(2,1)S(1)}, bf16[2,528,128]{2,1,0:T(8,128)(2,1)S(1)}, u32[]{:S(2)}, u32[]{:S(2)}) collective-permute-start(bf16[2,528,128]{2,1,0:T(8,128)(2,1)S(1)} %pad_maximum_fusion.2.x0), channel_id=1, source_target_pairs={{0,32},{1,33},{2,34},{3,35},{4,36},{5,37},{6,38},{7,39},{8,40},{9,... | collective-permute-start | bytes 811016 | tf_op jit(solution)/shard_map/ppermute | solution.py:39
  47.6 1.9 collective-permute-start.3
  49.5 8.3 %collective-permute-done.5.x3 = bf16[2,528,128]{2,1,0:T(8,128)(2,1)S(1)} collective-permute-done((bf16[2,528,128]{2,1,0:T(8,128)(2,1)S(1)}, bf16[2,528,128]{2,1,0:T(8,128)(2,1)S(1)}, u32[]{:S(2)}, u32[]{:S(2)}) %collective-permute-start.5) | collective-permute-done | bytes 270368 | tf_op jit(solution)/shard_map/ppermute | solution.py:39
  57.8 2.4 %collective-permute-done.4.x2 = bf16[2,528,128]{2,1,0:T(8,128)(2,1)S(1)} collective-permute-done((bf16[2,528,128]{2,1,0:T(8,128)(2,1)S(1)}, bf16[2,528,128]{2,1,0:T(8,128)(2,1)S(1)}, u32[]{:S(2)}, u32[]{:S(2)}) %collective-permute-start.4) | collective-permute-done | bytes 270368 | tf_op jit(solution)/shard_map/ppermute | solution.py:39
  60.1 3.3 %collective-permute-done.3.x1 = bf16[2,528,128]{2,1,0:T(8,128)(2,1)S(1)} collective-permute-done((bf16[2,528,128]{2,1,0:T(8,128)(2,1)S(1)}, bf16[2,528,128]{2,1,0:T(8,128)(2,1)S(1)}, u32[]{:S(2)}, u32[]{:S(2)}) %collective-permute-start.3) | collective-permute-done | bytes 270368 | tf_op jit(solution)/shard_map/ppermute | solution.py:39
  63.4 0.0 collective-permute-done.6.w_other
  63.4 3.3 %shard_map.56 = bf16[8,2,112,512]{3,2,1,0:T(8,128)(2,1)S(1)} custom-call(s32[3]{0:T(128)S(1)} %pad_add_fusion.at, bf16[2,528,128]{2,1,0:T(8,128)(2,1)S(1)} %pad_maximum_fusion.2.x0, bf16[2,528,128]{2,1,0:T(8,128)(2,1)S(1)} %collective-permute-done.3.x1, bf16[2,528,128]{2,1,0:T(8,128)(2,1)S(1)} %collective-permute-done.4.x2, ...), custom_call_target="tpu_custom_call" | custom-call | flops 1879048192 | bytes 6586380 | tf_op jit(solution)/shard_map/pallas_call | solution.py:135
  66.7 0.0 copy-start
  66.7 1.2 copy-done
  68.0 14.6 %all-to-all-start.1 = ((bf16[8,2,112,512]{3,2,1,0:T(8,128)(2,1)}), bf16[8,2,112,512]{3,2,1,0:T(8,128)(2,1)S(1)}, u32[]{:S(2)}, u32[]{:S(2)}) async-start(bf16[8,2,112,512]{3,2,1,0:T(8,128)(2,1)} %copy-done), calls=%async_computation.1 | async-start | bytes 3670016 | tf_op jit(solution)/shard_map/all_to_all | solution.py:25
  82.6 3.9 %collective-permute-start.7 = (bf16[2,2,448,128]{3,2,1,0:T(8,128)(2,1)S(1)}, bf16[2,2,448,128]{3,2,1,0:T(8,128)(2,1)}, u32[]{:S(2)}, u32[]{:S(2)}) collective-permute-start(bf16[2,2,448,128]{3,2,1,0:T(8,128)(2,1)S(1)} %dynamic-slice_bitcast_fusion), channel_id=1, source_target_pairs={{0,4},{1,5},{2,6},{3,7},{4,0},{5,1},{6,2},{7,3},{8,12},{9,13},{10,... | collective-permute-start | bytes 1376264 | tf_op jit(solution)/shard_map/ppermute | solution.py:39
  86.5 0.7 dynamic-slice_bitcast_fusion.5
  87.2 1.9 collective-permute-start.8
  89.1 18.4 %all-to-all-done.1.sums = bf16[8,2,112,512]{3,2,1,0:T(8,128)(2,1)S(1)} async-done(((bf16[8,2,112,512]{3,2,1,0:T(8,128)(2,1)}), bf16[8,2,112,512]{3,2,1,0:T(8,128)(2,1)S(1)}, u32[]{:S(2)}, u32[]{:S(2)}) %all-to-all-start.1) | async-done | bytes 1835040 | tf_op jit(solution)/shard_map/all_to_all | solution.py:25
  107.5 1.6 shard_map.57
  109.2 0.0 collective-permute-done.7
  109.2 1.1 constant_dynamic-slice_fusion
  110.3 2.3 %collective-permute-start.9 = (bf16[2,448,128]{2,1,0:T(8,128)(2,1)S(1)}, bf16[2,448,128]{2,1,0:T(8,128)(2,1)S(1)}, u32[]{:S(2)}, u32[]{:S(2)}) collective-permute-start(bf16[2,448,128]{2,1,0:T(8,128)(2,1)S(1)} %get-tuple-element.22), channel_id=1, source_target_pairs={{0,32},{1,33},{2,34},{3,35},{4,36},{5,37},{6,38},{7,39},{8,40},{9,... | collective-permute-start | bytes 688136 | tf_op jit(solution)/shard_map/ppermute | solution.py:39
  112.6 5.3 %all-to-all-start.2 = ((bf16[4,112,512]{2,1,0:T(8,128)(2,1)}), bf16[4,112,512]{2,1,0:T(8,128)(2,1)S(1)}, u32[]{:S(2)}, u32[]{:S(2)}) async-start(bf16[4,112,512]{2,1,0:T(8,128)(2,1)} %bitcast.16), calls=%async_computation.2 | async-start | bytes 917504 | tf_op jit(solution)/shard_map/all_to_all | solution.py:25
  117.9 0.0 collective-permute-done.8
  117.9 0.0 collective-permute-done.9
  117.9 0.1 pad_maximum_fusion.1
  118.0 5.1 %collective-permute-start.10 = (bf16[8,448,128]{2,1,0:T(8,128)(2,1)S(1)}, bf16[8,448,128]{2,1,0:T(8,128)(2,1)S(1)}, u32[]{:S(2)}, u32[]{:S(2)}) collective-permute-start(bf16[8,448,128]{2,1,0:T(8,128)(2,1)S(1)} %bitcast.45), channel_id=1, source_target_pairs={{0,1},{1,0},{2,3},{3,2},{4,5},{5,4},{6,7},{7,6},{8,9},{9,8},{10,11... | collective-permute-start | bytes 2752520 | tf_op jit(solution)/shard_map/ppermute | solution.py:39
  123.2 2.1 %collective-permute-done.10 = bf16[8,448,128]{2,1,0:T(8,128)(2,1)S(1)} collective-permute-done((bf16[8,448,128]{2,1,0:T(8,128)(2,1)S(1)}, bf16[8,448,128]{2,1,0:T(8,128)(2,1)S(1)}, u32[]{:S(2)}, u32[]{:S(2)}) %collective-permute-start.10) | collective-permute-done | bytes 917536 | tf_op jit(solution)/shard_map/ppermute | solution.py:39
  125.3 0.2 maximum_bitcast_fusion
  125.4 1.9 copy.16
  127.3 2.3 %reshape.53 = bf16[448,2048]{1,0:T(8,128)(2,1)} reshape(bf16[448,8,2,128]{3,2,1,0:T(2,128)(2,1)S(1)} %copy.16) | data formatting | bytes 3670016 | tf_op jit(solution)/shard_map/reshape | solution.py:193
  129.7 3.3 %all-to-all-done.2 = bf16[4,112,512]{2,1,0:T(8,128)(2,1)S(1)} async-done(((bf16[4,112,512]{2,1,0:T(8,128)(2,1)}), bf16[4,112,512]{2,1,0:T(8,128)(2,1)S(1)}, u32[]{:S(2)}, u32[]{:S(2)}) %all-to-all-start.2) | async-done | bytes 458784 | tf_op jit(solution)/shard_map/all_to_all | solution.py:25
  132.9 2.8 %convolution_convert_fusion = bf16[512,2048]{1,0:T(8,128)(2,1)S(1)} fusion(bf16[448,512]{1,0:T(8,128)(2,1)S(1)} %bitcast.55, bf16[448,2048]{1,0:T(8,128)(2,1)} %reshape.53), kind=kOutput, calls=%fused_computation | convolution fusion | flops 940572672 | bytes 4390912 | tf_op jit(solution)/shard_map/dot_general | solution.py:195
  135.7 44.1 %all_to_all.25.parts = bf16[8,64,2048]{2,1,0:T(8,128)(2,1)S(1)} all-to-all(bf16[8,64,2048]{2,1,0:T(8,128)(2,1)S(1)} %bitcast.49), channel_id=1, replica_groups=mesh['y'=4,'xh'=2,'xl'=2,'zh'=4,'zm'=2,'z0'=2,'core'=2] {'y','xh'}, dimensions={0} | all-to-all | bytes 4194304 | tf_op jit(solution)/shard_map/all_to_all | solution.py:25
  179.8 1.5 shard_map.58
  181.3 5.9 %all-to-all-start.4 = ((bf16[16,64,128]{2,1,0:T(8,128)(2,1)}), bf16[16,64,128]{2,1,0:T(8,128)(2,1)S(1)}, u32[]{:S(2)}, u32[]{:S(2)}) async-start(bf16[16,64,128]{2,1,0:T(8,128)(2,1)} %shard_map.58), calls=%async_computation.4 | async-start | bytes 524288 | tf_op jit(solution)/shard_map/all_to_all | solution.py:25
  187.2 9.5 %all-to-all-done.4 = bf16[16,64,128]{2,1,0:T(8,128)(2,1)S(1)} async-done(((bf16[16,64,128]{2,1,0:T(8,128)(2,1)}), bf16[16,64,128]{2,1,0:T(8,128)(2,1)S(1)}, u32[]{:S(2)}, u32[]{:S(2)}) %all-to-all-start.4) | async-done | bytes 262176 | tf_op jit(solution)/shard_map/all_to_all | solution.py:25
  196.7 1.4 add_convert_fusion
  (6 shorter events, 0.1 us)
Async XLA Ops:
  0.1 1.2 copy-start.1
  1.3 1.2 copy-start.2
  4.4 34.2 %all-to-all-start = ((bf16[8,112,1024]{2,1,0:T(8,128)(2,1)}), bf16[8,112,1024]{2,1,0:T(8,128)(2,1)S(1)}, u32[]{:S(2)}, u32[]{:S(2)}) async-start(bf16[8,112,1024]{2,1,0:T(8,128)(2,1)} %shard_map.55), calls=%async_computation | async-start | bytes 3670016 | tf_op jit(solution)/shard_map/all_to_all | solution.py:25
  13.2 4.5 %copy-start.4 = (bf16[1024,128]{1,0:T(8,128)(2,1)S(1)}, bf16[1024,128]{1,0:T(8,128)(2,1)}, u32[]{:S(2)}) copy-start(bf16[1024,128]{1,0:T(8,128)(2,1)} %param.5) | copy-start | bytes 786436
  13.2 4.5 %copy-start.5 = (bf16[128]{0:T(256)(128)(2,1)S(1)}, bf16[128]{0:T(256)(128)(2,1)}, u32[]{:S(2)}) copy-start(bf16[128]{0:T(256)(128)(2,1)} %param.6) | copy-start | bytes 772
  14.1 20.0 %collective-permute-start.2 = (bf16[2,2,448,128]{3,2,1,0:T(8,128)(2,1)}, bf16[2,2,448,128]{3,2,1,0:T(8,128)(2,1)S(1)}, u32[]{:S(2)}, u32[]{:S(2)}) collective-permute-start(bf16[2,2,448,128]{3,2,1,0:T(8,128)(2,1)} %get-tuple-element.20), channel_id=1, source_target_pairs={{0,2},{1,3},{2,0},{3,1},{4,6},{5,7},{6,4},{7,5},{8,10},{9,11},{10,... | collective-permute-start | bytes 1376264 | tf_op jit(solution)/shard_map/ppermute | solution.py:39
  17.8 20.8 %collective-permute-start.1 = (bf16[528,128]{1,0:T(8,128)(2,1)S(1)}, bf16[528,128]{1,0:T(8,128)(2,1)S(1)}, u32[]{:S(2)}, u32[]{:S(2)}) collective-permute-start(bf16[528,128]{1,0:T(8,128)(2,1)S(1)} %get-tuple-element.25), channel_id=1, source_target_pairs={{0,17},{1,16},{2,19},{3,18},{4,77},{5,76},{6,79},{7,78},{8,137},{9... | collective-permute-start | bytes 405512 | tf_op jit(solution)/shard_map/ppermute | solution.py:39
  33.4 5.1 %collective-permute-start = (bf16[528,128]{1,0:T(8,128)(2,1)S(1)}, bf16[528,128]{1,0:T(8,128)(2,1)S(1)}, u32[]{:S(2)}, u32[]{:S(2)}) collective-permute-start(bf16[528,128]{1,0:T(8,128)(2,1)S(1)} %get-tuple-element.26), channel_id=1, source_target_pairs={{0,0},{1,1},{2,2},{3,3},{4,92},{5,93},{6,94},{7,95},{8,152},{9,153... | collective-permute-start | bytes 405512 | tf_op jit(solution)/shard_map/ppermute | solution.py:39
  34.1 0.8 copy-start.3
  38.5 24.9 %collective-permute-start.6 = (bf16[8,112,1024]{2,1,0:T(8,128)(2,1)S(1)}, bf16[8,112,1024]{2,1,0:T(8,128)(2,1)S(1)}, u32[]{:S(2)}, u32[]{:S(2)}) collective-permute-start(bf16[8,112,1024]{2,1,0:T(8,128)(2,1)S(1)} %all-to-all-done.w_own), channel_id=1, source_target_pairs={{0,1},{1,0},{2,3},{3,2},{4,5},{5,4},{6,7},{7,6},{8,9},{9,8},{10,11... | collective-permute-start | bytes 5505032 | tf_op jit(solution)/shard_map/ppermute | solution.py:39
  40.8 17.0 %collective-permute-start.5 = (bf16[2,528,128]{2,1,0:T(8,128)(2,1)S(1)}, bf16[2,528,128]{2,1,0:T(8,128)(2,1)S(1)}, u32[]{:S(2)}, u32[]{:S(2)}) collective-permute-start(bf16[2,528,128]{2,1,0:T(8,128)(2,1)S(1)} %pad_maximum_fusion.2.x0), channel_id=1, source_target_pairs={{0,34},{1,35},{2,32},{3,33},{4,38},{5,39},{6,36},{7,37},{8,42},{9,... | collective-permute-start | bytes 811016 | tf_op jit(solution)/shard_map/ppermute | solution.py:39
  44.7 15.4 %collective-permute-start.4 = (bf16[2,528,128]{2,1,0:T(8,128)(2,1)S(1)}, bf16[2,528,128]{2,1,0:T(8,128)(2,1)S(1)}, u32[]{:S(2)}, u32[]{:S(2)}) collective-permute-start(bf16[2,528,128]{2,1,0:T(8,128)(2,1)S(1)} %pad_maximum_fusion.2.x0), channel_id=1, source_target_pairs={{0,32},{1,33},{2,34},{3,35},{4,36},{5,37},{6,38},{7,39},{8,40},{9,... | collective-permute-start | bytes 811016 | tf_op jit(solution)/shard_map/ppermute | solution.py:39
  47.6 15.8 %collective-permute-start.3 = (bf16[2,528,128]{2,1,0:T(8,128)(2,1)S(1)}, bf16[2,528,128]{2,1,0:T(8,128)(2,1)S(1)}, u32[]{:S(2)}, u32[]{:S(2)}) collective-permute-start(bf16[2,528,128]{2,1,0:T(8,128)(2,1)S(1)} %pad_maximum_fusion.2.x0), channel_id=1, source_target_pairs={{0,2},{1,3},{2,0},{3,1},{4,6},{5,7},{6,4},{7,5},{8,10},{9,11},{10,... | collective-permute-start | bytes 811016 | tf_op jit(solution)/shard_map/ppermute | solution.py:39
  66.7 1.3 copy-start
  68.0 39.6 %all-to-all-start.1 = ((bf16[8,2,112,512]{3,2,1,0:T(8,128)(2,1)}), bf16[8,2,112,512]{3,2,1,0:T(8,128)(2,1)S(1)}, u32[]{:S(2)}, u32[]{:S(2)}) async-start(bf16[8,2,112,512]{3,2,1,0:T(8,128)(2,1)} %copy-done), calls=%async_computation.1 | async-start | bytes 3670016 | tf_op jit(solution)/shard_map/all_to_all | solution.py:25
  82.6 26.6 %collective-permute-start.7 = (bf16[2,2,448,128]{3,2,1,0:T(8,128)(2,1)S(1)}, bf16[2,2,448,128]{3,2,1,0:T(8,128)(2,1)}, u32[]{:S(2)}, u32[]{:S(2)}) collective-permute-start(bf16[2,2,448,128]{3,2,1,0:T(8,128)(2,1)S(1)} %dynamic-slice_bitcast_fusion), channel_id=1, source_target_pairs={{0,4},{1,5},{2,6},{3,7},{4,0},{5,1},{6,2},{7,3},{8,12},{9,13},{10,... | collective-permute-start | bytes 1376264 | tf_op jit(solution)/shard_map/ppermute | solution.py:39
  87.2 30.7 %collective-permute-start.8 = (bf16[2,448,128]{2,1,0:T(8,128)(2,1)}, bf16[2,448,128]{2,1,0:T(8,128)(2,1)S(1)}, u32[]{:S(2)}, u32[]{:S(2)}) collective-permute-start(bf16[2,448,128]{2,1,0:T(8,128)(2,1)} %get-tuple-element.18), channel_id=1, source_target_pairs={{0,32},{1,33},{2,34},{3,35},{4,36},{5,37},{6,38},{7,39},{8,40},{9,... | collective-permute-start | bytes 688136 | tf_op jit(solution)/shard_map/ppermute | solution.py:39
  110.3 7.6 %collective-permute-start.9 = (bf16[2,448,128]{2,1,0:T(8,128)(2,1)S(1)}, bf16[2,448,128]{2,1,0:T(8,128)(2,1)S(1)}, u32[]{:S(2)}, u32[]{:S(2)}) collective-permute-start(bf16[2,448,128]{2,1,0:T(8,128)(2,1)S(1)} %get-tuple-element.22), channel_id=1, source_target_pairs={{0,32},{1,33},{2,34},{3,35},{4,36},{5,37},{6,38},{7,39},{8,40},{9,... | collective-permute-start | bytes 688136 | tf_op jit(solution)/shard_map/ppermute | solution.py:39
  112.6 20.4 %all-to-all-start.2 = ((bf16[4,112,512]{2,1,0:T(8,128)(2,1)}), bf16[4,112,512]{2,1,0:T(8,128)(2,1)S(1)}, u32[]{:S(2)}, u32[]{:S(2)}) async-start(bf16[4,112,512]{2,1,0:T(8,128)(2,1)} %bitcast.16), calls=%async_computation.2 | async-start | bytes 917504 | tf_op jit(solution)/shard_map/all_to_all | solution.py:25
  118.0 7.2 %collective-permute-start.10 = (bf16[8,448,128]{2,1,0:T(8,128)(2,1)S(1)}, bf16[8,448,128]{2,1,0:T(8,128)(2,1)S(1)}, u32[]{:S(2)}, u32[]{:S(2)}) collective-permute-start(bf16[8,448,128]{2,1,0:T(8,128)(2,1)S(1)} %bitcast.45), channel_id=1, source_target_pairs={{0,1},{1,0},{2,3},{3,2},{4,5},{5,4},{6,7},{7,6},{8,9},{9,8},{10,11... | collective-permute-start | bytes 2752520 | tf_op jit(solution)/shard_map/ppermute | solution.py:39
  181.3 15.4 %all-to-all-start.4 = ((bf16[16,64,128]{2,1,0:T(8,128)(2,1)}), bf16[16,64,128]{2,1,0:T(8,128)(2,1)S(1)}, u32[]{:S(2)}, u32[]{:S(2)}) async-start(bf16[16,64,128]{2,1,0:T(8,128)(2,1)} %shard_map.58), calls=%async_computation.4 | async-start | bytes 524288 | tf_op jit(solution)/shard_map/all_to_all | solution.py:25

commit v9 on v8

--- a/solution.py
+++ b/solution.py
@@ -57,14 +57,25 @@
     return move
 
 
-def cut_kernel(at, gate, up, out):
-    del at
+def cut_kernel(gate, up, out):
     zero = jnp.zeros((56 - gate.shape[0], 512), f32)
-    for group in range(8):
-        for side in (0, 1):
-            start = side * FEAT // 2 + group * 512
-            parts = (gate[:, start : start + 512].astype(f32), zero, up[:, start : start + 512].astype(f32), zero)
-            out[group, :, side * 512 : side * 512 + 512] = jnp.concatenate(parts).astype(bf16)
+    for group in range(4):
+        columns = slice(group * 512, group * 512 + 512)
+        parts = (gate[:, columns].astype(f32), zero, up[:, columns].astype(f32), zero)
+        out[group] = jnp.concatenate(parts).astype(bf16)
+
+
+def cut(gate, up):
+    units = gate.shape[0]
+    return pl.pallas_call(
+        cut_kernel,
+        grid=(4,),
+        out_shape=jax.ShapeDtypeStruct((8, 112, 1024), bf16),
+        in_specs=[pl.BlockSpec((units, 2048), lambda i: (0, i))] * 2,
+        out_specs=pl.BlockSpec((4, 112, 512), lambda i: (i % 2, 0, i // 2)),
+        compiler_params=pltpu.CompilerParams(vmem_limit_bytes=60 * 2**20),
+        cost_estimate=pl.CostEstimate(flops=0, bytes_accessed=8 * units * FEAT, transcendentals=0),
+    )(gate, up)
 
 
 def sums_kernel(at, x0, x1, x2, x3, w_own, w_other, out, scaled):
@@ -112,13 +123,15 @@
     row = lax.broadcasted_iota(jnp.int32, (8, rows), 0)
     squares = jnp.where((row >= 4) & (row < 7), own[48:56], 0.0)
     inv_rms = lax.rsqrt(jnp.sum(squares, 0, keepdims=True) / FEAT + EPS)
-    unit = lax.broadcasted_iota(jnp.int32, (56, rows), 0)
-    for side, total in enumerate((own, other)):
-        gate = total[:56] * inv_rms
-        acts = gate / (1.0 + jnp.exp(-gate)) * (total[56:] * inv_rms)
-        acts = jnp.where(unit < 52, acts, 0.0).astype(bf16)
-        for copy in range(4):
-            out[copy, jnp.bitwise_xor(at[0], side)] = acts
+    acts = []
+    for total in (own, other):
+        gate = total[:52] * inv_rms
+        acts.append(gate / (1.0 + jnp.exp(-gate)) * (total[56:108] * inv_rms))
+    swapped = at[0] == 1
+    acts = (jnp.where(swapped, acts[1], acts[0]), jnp.where(swapped, acts[0], acts[1]))
+    acts = jnp.concatenate(acts).astype(bf16)
+    for copy in range(4):
+        out[copy] = acts
 
 
 def place_kernel(at, parts, out):
@@ -130,7 +143,7 @@
         out[jnp.bitwise_xor(at[2], piece)] = total[:, column : column + LANES].astype(bf16)
 
 
-def run(kernel, out_shape, operands, scratch=(), flops=0):
+def run(kernel, out_shape, operands, scratch=(), flops=0, vmem=32):
     moved = sum(o.size * o.dtype.itemsize for o in operands) + int(np.prod(out_shape)) * 2
     return pl.pallas_call(
         kernel,
@@ -139,7 +152,7 @@
         + [pl.BlockSpec(memory_space=pltpu.VMEM)] * (len(operands) - 1),
         out_specs=pl.BlockSpec(memory_space=pltpu.VMEM),
         scratch_shapes=list(scratch),
-        compiler_params=pltpu.CompilerParams(vmem_limit_bytes=40 * 2**20),
+        compiler_params=pltpu.CompilerParams(vmem_limit_bytes=vmem * 2**20),
         cost_estimate=pl.CostEstimate(flops=flops, bytes_accessed=moved, transcendentals=0),
     )(*operands)
 
@@ -165,11 +178,11 @@
         )
         return kept, send(sent, shift(**{axis: 1}))
 
-    down = jnp.pad(down_weight.reshape(64, units, LANES), ((0, 0), (0, 56 - units), (0, 0)))
-    down = down.reshape(2, 4, 2, 2, 112, LANES).transpose(3, 2, 0, 1, 4, 5).reshape(2, 2, 2, 448, LANES)
+    down = down_weight.reshape(2, 4, 2, 2, 2 * units, LANES)
+    down = down.transpose(3, 2, 0, 1, 4, 5).reshape(2, 2, 2, 8 * units, LANES)
     down = jnp.stack(halve(down, "z0"), 2)
 
-    own_w = exchange(run(cut_kernel, (8, 112, 1024), (at, gate_weight, up_weight)), PHASE)
+    own_w = exchange(cut(gate_weight, up_weight), PHASE)
     first = send(half(core), spread(0, 0))
     second = send(half(1 - core), spread(4, 1))
     first, second, own_w, down = lax.optimization_barrier((first, second, own_w, down))
@@ -183,15 +196,16 @@
         (at, *blocks, own_w, other_w),
         (pltpu.VMEM((rows, 1024), bf16),),
         flops=2 * 1792 * 1024 * rows,
+        vmem=60,
     )
     kept, got = halve(down, "zm")
-    acts = run(acts_kernel, (4, 2, 56, rows), (at, exchange(sums, PHASE)))
+    acts = run(acts_kernel, (4, 2 * units, rows), (at, exchange(sums, PHASE)))
     acts, got = lax.optimization_barrier((acts, got))
     (kept0, got0), (kept1, got1) = halve(kept, "xl"), halve(got, "xl")
-    down = jnp.stack((kept0, kept1, got0, got1)).reshape(8, 448, LANES)
+    down = jnp.stack((kept0, kept1, got0, got1)).reshape(8, 8 * units, LANES)
     down = jnp.stack((down, send(down, shift(core=1))), 1)
-    down = down.transpose(2, 0, 1, 3).reshape(448, 2048)
-    acts = exchange(acts.reshape(4, 112, rows), FAR).reshape(448, rows)
+    down = down.transpose(2, 0, 1, 3).reshape(8 * units, 2048)
+    acts = exchange(acts, FAR).reshape(8 * units, rows)
     partials = lax.dot_general(
         acts, down, (((0,), (0,)), ((), ())), preferred_element_type=f32
     ).astype(bf16)

time: 199 us -> 197 us (0.990)
  blocking collectives: 44.1 us -> 34.1 us
  local copies, waits for them, and re-layouts: 12.7 us -> 6.01 us
  starting transfers between devices: 77.2 us -> 83.1 us
  Pallas kernels: 8.39 us -> 13.4 us
  waiting for transfers between devices: 49.7 us -> 54.3 us
    all_to_all x1, blocking collectives: 44.1 us -> 34.1 us  [exchange(): return lax.all_to_all(value, axes, 0, 0, tiled=True)]
    all_to_all x4, starting transfers between devices: 33.3 us -> 39 us  [exchange(): return lax.all_to_all(value, axes, 0, 0, tiled=True)]
    pallas_call x0 -> x1, Pallas kernels: none -> 3.85 us  [cut(): pl.pallas_call(cut_kernel, grid=(4,), out_shape=jax.ShapeDtypeStruct((8,...]
    all_to_all x4, waiting for transfers between devices: 31.2 us -> 34.9 us  [exchange(): return lax.all_to_all(value, axes, 0, 0, tiled=True)]
    unnamed x12 -> x16, local copies, waits for them, and re-layouts: 4.38 us -> 0.72 us
    pallas_call x4 -> x3, Pallas kernels: 8.39 us -> 9.55 us  [run(): pl.pallas_call(kernel, out_shape=jax.ShapeDtypeStruct(out_shape, bf16), i...]
  transfers between devices with their start and end apart: 15 -> 15, of which waited for: 8 -> 8; matrix products, arithmetic and copies ran while one was open for 5% -> 3% of each run, Pallas kernels for 1% -> 1%
where the time goes in v9:
time: 197 us; the launch traced here: 196 us
  starting transfers between devices  83.1 us (42%)
  waiting for transfers between devices  54.3 us (28%)
  blocking collectives  34.1 us (17%)
  Pallas kernels  13.4 us (7%)
  local copies, waits for them, and re-layouts  6.01 us (3%)
  matrix products  2.73 us (1%)
  other arithmetic  2.42 us (1%)
    ppermute x11, starting transfers between devices, send(): return lax.ppermute(value, AXES, route(move))  44.2 us
    all_to_all x4, starting transfers between devices, exchange(): return lax.all_to_all(value, axes, 0, 0, tiled=True)  39 us
    all_to_all x4, waiting for transfers between devices, exchange(): return lax.all_to_all(value, axes, 0, 0, tiled=True)  34.9 us
    all_to_all x1, blocking collectives, exchange(): return lax.all_to_all(value, axes, 0, 0, tiled=True)  34.1 us
    ppermute x11, waiting for transfers between devices, send(): return lax.ppermute(value, AXES, route(move))  19.4 us
    pallas_call x3, Pallas kernels, run(): pl.pallas_call(kernel, out_shape=jax.ShapeDtypeStruct(out_shape, bf16), i...  9.55 us
  transfers between devices with their start and end apart: 15, of which 8 were waited for; matrix products, arithmetic and copies ran while one was open for 3% of the time, Pallas kernels for 1%

profile of v9, /device:TPU:1, one launch (start us, length us, event | category | flops | bytes accessed | tf_op | source)
XLA Modules:
  0.0 196.4 jit_solution(4672178379194720103)
XLA Ops:
  0.0 3.8 %shard_map.55 = bf16[8,112,1024]{2,1,0:T(8,128)(2,1)} custom-call(bf16[52,8192]{1,0:T(8,128)(2,1)} %gate.1, bf16[52,8192]{1,0:T(8,128)(2,1)} %up.1), custom_call_target="tpu_custom_call" | custom-call | bytes 3407872 | tf_op jit(solution)/shard_map/pallas_call | solution.py:70
  3.8 0.0 copy-start.1
  3.8 7.6 %all-to-all-start = ((bf16[8,112,1024]{2,1,0:T(8,128)(2,1)}), bf16[8,112,1024]{2,1,0:T(8,128)(2,1)}, u32[]{:S(2)}, u32[]{:S(2)}) async-start(bf16[8,112,1024]{2,1,0:T(8,128)(2,1)} %shard_map.55), calls=%async_computation | async-start | bytes 3670016 | tf_op jit(solution)/shard_map/all_to_all | solution.py:25
  11.5 0.0 copy-start.2
  11.5 0.0 copy-done.1
  11.5 0.0 copy-start.4
  11.5 0.1 copy.14
  11.6 0.1 dynamic-slice_bitcast_fusion.2
  11.6 3.5 %collective-permute-start.2 = (bf16[2,2,416,128]{3,2,1,0:T(8,128)(2,1)S(1)}, bf16[2,2,416,128]{3,2,1,0:T(8,128)(2,1)S(1)}, u32[]{:S(2)}, u32[]{:S(2)}) collective-permute-start(bf16[2,2,416,128]{3,2,1,0:T(8,128)(2,1)S(1)} %get-tuple-element.20), channel_id=1, source_target_pairs={{0,2},{1,3},{2,0},{3,1},{4,6},{5,7},{6,4},{7,5},{8,10},{9,11},{10,... | collective-permute-start | bytes 1277960 | tf_op jit(solution)/shard_map/ppermute | solution.py:39
  15.2 0.0 copy-done.2
  15.2 0.0 copy-done.4
  15.3 15.7 %collective-permute-start.1 = (bf16[528,128]{1,0:T(8,128)(2,1)S(1)}, bf16[528,128]{1,0:T(8,128)(2,1)S(1)}, u32[]{:S(2)}, u32[]{:S(2)}) collective-permute-start(bf16[528,128]{1,0:T(8,128)(2,1)S(1)} %get-tuple-element.25), channel_id=1, source_target_pairs={{0,17},{1,16},{2,19},{3,18},{4,77},{5,76},{6,79},{7,78},{8,137},{9... | collective-permute-start | bytes 405512 | tf_op jit(solution)/shard_map/ppermute | solution.py:39
  31.0 0.7 collective-permute-start
  31.6 0.0 collective-permute-done.2
  31.7 0.1 pad_maximum_fusion
  31.7 6.7 %collective-permute-done.1 = bf16[528,128]{1,0:T(8,128)(2,1)S(1)} collective-permute-done((bf16[528,128]{1,0:T(8,128)(2,1)S(1)}, bf16[528,128]{1,0:T(8,128)(2,1)S(1)}, u32[]{:S(2)}, u32[]{:S(2)}) %collective-permute-start.1) | collective-permute-done | bytes 135200 | tf_op jit(solution)/shard_map/ppermute | solution.py:39
  38.4 0.0 collective-permute-done
  38.4 0.0 all-to-all-done.w_own
  38.4 2.4 %collective-permute-start.6 = (bf16[8,112,1024]{2,1,0:T(8,128)(2,1)}, bf16[8,112,1024]{2,1,0:T(8,128)(2,1)}, u32[]{:S(2)}, u32[]{:S(2)}) collective-permute-start(bf16[8,112,1024]{2,1,0:T(8,128)(2,1)} %all-to-all-done.w_own), channel_id=1, source_target_pairs={{0,1},{1,0},{2,3},{3,2},{4,5},{5,4},{6,7},{7,6},{8,9},{9,8},{10,11... | collective-permute-start | bytes 5505032 | tf_op jit(solution)/shard_map/ppermute | solution.py:39
  40.9 0.0 copy-start.3
  40.9 3.6 %collective-permute-start.5 = (bf16[2,528,128]{2,1,0:T(8,128)(2,1)S(1)}, bf16[2,528,128]{2,1,0:T(8,128)(2,1)S(1)}, u32[]{:S(2)}, u32[]{:S(2)}) collective-permute-start(bf16[2,528,128]{2,1,0:T(8,128)(2,1)S(1)} %pad_maximum_fusion.2.x0), channel_id=1, source_target_pairs={{0,34},{1,35},{2,32},{3,33},{4,38},{5,39},{6,36},{7,37},{8,42},{9,... | collective-permute-start | bytes 811016 | tf_op jit(solution)/shard_map/ppermute | solution.py:39
  44.5 2.8 %collective-permute-start.4 = (bf16[2,528,128]{2,1,0:T(8,128)(2,1)S(1)}, bf16[2,528,128]{2,1,0:T(8,128)(2,1)S(1)}, u32[]{:S(2)}, u32[]{:S(2)}) collective-permute-start(bf16[2,528,128]{2,1,0:T(8,128)(2,1)S(1)} %pad_maximum_fusion.2.x0), channel_id=1, source_target_pairs={{0,32},{1,33},{2,34},{3,35},{4,36},{5,37},{6,38},{7,39},{8,40},{9,... | collective-permute-start | bytes 811016 | tf_op jit(solution)/shard_map/ppermute | solution.py:39
  47.3 2.2 %collective-permute-start.3 = (bf16[2,528,128]{2,1,0:T(8,128)(2,1)S(1)}, bf16[2,528,128]{2,1,0:T(8,128)(2,1)S(1)}, u32[]{:S(2)}, u32[]{:S(2)}) collective-permute-start(bf16[2,528,128]{2,1,0:T(8,128)(2,1)S(1)} %pad_maximum_fusion.2.x0), channel_id=1, source_target_pairs={{0,2},{1,3},{2,0},{3,1},{4,6},{5,7},{6,4},{7,5},{8,10},{9,11},{10,... | collective-permute-start | bytes 811016 | tf_op jit(solution)/shard_map/ppermute | solution.py:39
  49.5 0.6 pad_add_fusion.at
  50.1 4.9 %collective-permute-done.5.x3 = bf16[2,528,128]{2,1,0:T(8,128)(2,1)S(1)} collective-permute-done((bf16[2,528,128]{2,1,0:T(8,128)(2,1)S(1)}, bf16[2,528,128]{2,1,0:T(8,128)(2,1)S(1)}, u32[]{:S(2)}, u32[]{:S(2)}) %collective-permute-start.5) | collective-permute-done | bytes 270368 | tf_op jit(solution)/shard_map/ppermute | solution.py:39
  55.0 0.0 copy-start.5
  55.0 5.2 %collective-permute-done.4.x2 = bf16[2,528,128]{2,1,0:T(8,128)(2,1)S(1)} collective-permute-done((bf16[2,528,128]{2,1,0:T(8,128)(2,1)S(1)}, bf16[2,528,128]{2,1,0:T(8,128)(2,1)S(1)}, u32[]{:S(2)}, u32[]{:S(2)}) %collective-permute-start.4) | collective-permute-done | bytes 270368 | tf_op jit(solution)/shard_map/ppermute | solution.py:39
  60.2 0.0 copy-start.6
  60.2 0.6 collective-permute-done.3.x1
  60.8 0.0 copy-start.7
  60.8 0.0 collective-permute-done.6.w_other
  60.8 0.0 copy-done.3
  60.8 0.0 copy-done.5
  60.8 0.1 copy-done.6
  60.9 0.6 copy-done.7
  61.5 6.4 %shard_map.56 = bf16[8,2,112,512]{3,2,1,0:T(8,128)(2,1)} custom-call(s32[3]{0:T(128)} %pad_add_fusion.at, bf16[2,528,128]{2,1,0:T(8,128)(2,1)} %copy-done.3, bf16[2,528,128]{2,1,0:T(8,128)(2,1)} %copy-done.7, bf16[2,528,128]{2,1,0:T(8,128)(2,1)} %copy-done.6, bf16[2,528,128]{2,1,0:T(8,128)(2,1)} %copy-done.5, bf16[8,112,1024]{2,1,0:T(8,128)(2,1)} %all-to-all-done.w_own, ...), custom_call_target="tpu_custom_call" | custom-call | flops 1879048192 | bytes 6586380 | tf_op jit(solution)/shard_map/pallas_call | solution.py:148
  67.9 0.0 copy-start
  67.9 14.3 %all-to-all-start.1 = ((bf16[8,2,112,512]{3,2,1,0:T(8,128)(2,1)}), bf16[8,2,112,512]{3,2,1,0:T(8,128)(2,1)S(1)}, u32[]{:S(2)}, u32[]{:S(2)}) async-start(bf16[8,2,112,512]{3,2,1,0:T(8,128)(2,1)} %shard_map.56), calls=%async_computation.1 | async-start | bytes 3670016 | tf_op jit(solution)/shard_map/all_to_all | solution.py:25
  82.3 3.6 %collective-permute-start.7 = (bf16[2,2,416,128]{3,2,1,0:T(8,128)(2,1)S(1)}, bf16[2,2,416,128]{3,2,1,0:T(8,128)(2,1)}, u32[]{:S(2)}, u32[]{:S(2)}) collective-permute-start(bf16[2,2,416,128]{3,2,1,0:T(8,128)(2,1)S(1)} %dynamic-slice_bitcast_fusion), channel_id=1, source_target_pairs={{0,4},{1,5},{2,6},{3,7},{4,0},{5,1},{6,2},{7,3},{8,12},{9,13},{10,... | collective-permute-start | bytes 1277960 | tf_op jit(solution)/shard_map/ppermute | solution.py:39
  86.0 2.2 %collective-permute-start.8 = (bf16[2,416,128]{2,1,0:T(8,128)(2,1)S(1)}, bf16[2,416,128]{2,1,0:T(8,128)(2,1)S(1)}, u32[]{:S(2)}, u32[]{:S(2)}) collective-permute-start(bf16[2,416,128]{2,1,0:T(8,128)(2,1)S(1)} %get-tuple-element.18), channel_id=1, source_target_pairs={{0,32},{1,33},{2,34},{3,35},{4,36},{5,37},{6,38},{7,39},{8,40},{9,... | collective-permute-start | bytes 638984 | tf_op jit(solution)/shard_map/ppermute | solution.py:39
  88.1 19.1 %all-to-all-done.1.sums = bf16[8,2,112,512]{3,2,1,0:T(8,128)(2,1)S(1)} async-done(((bf16[8,2,112,512]{3,2,1,0:T(8,128)(2,1)}), bf16[8,2,112,512]{3,2,1,0:T(8,128)(2,1)S(1)}, u32[]{:S(2)}, u32[]{:S(2)}) %all-to-all-start.1) | async-done | bytes 1835040 | tf_op jit(solution)/shard_map/all_to_all | solution.py:25
  107.3 0.0 copy-done
  107.3 1.6 shard_map.57
  108.9 0.0 collective-permute-done.7
  108.9 1.1 constant_dynamic-slice_fusion
  109.9 2.2 %collective-permute-start.9 = (bf16[2,416,128]{2,1,0:T(8,128)(2,1)S(1)}, bf16[2,416,128]{2,1,0:T(8,128)(2,1)S(1)}, u32[]{:S(2)}, u32[]{:S(2)}) collective-permute-start(bf16[2,416,128]{2,1,0:T(8,128)(2,1)S(1)} %get-tuple-element.22), channel_id=1, source_target_pairs={{0,32},{1,33},{2,34},{3,35},{4,36},{5,37},{6,38},{7,39},{8,40},{9,... | collective-permute-start | bytes 638984 | tf_op jit(solution)/shard_map/ppermute | solution.py:39
  112.2 7.0 %all-to-all-start.2 = ((bf16[4,104,512]{2,1,0:T(8,128)(2,1)}), bf16[4,104,512]{2,1,0:T(8,128)(2,1)S(1)}, u32[]{:S(2)}, u32[]{:S(2)}) async-start(bf16[4,104,512]{2,1,0:T(8,128)(2,1)} %shard_map.57), calls=%async_computation.2 | async-start | bytes 851968 | tf_op jit(solution)/shard_map/all_to_all | solution.py:25
  119.2 0.0 collective-permute-done.8
  119.2 0.0 collective-permute-done.9
  119.2 0.1 pad_maximum_fusion.1
  119.3 5.3 %collective-permute-start.10 = (bf16[8,416,128]{2,1,0:T(8,128)(2,1)S(1)}, bf16[8,416,128]{2,1,0:T(8,128)(2,1)S(1)}, u32[]{:S(2)}, u32[]{:S(2)}) collective-permute-start(bf16[8,416,128]{2,1,0:T(8,128)(2,1)S(1)} %bitcast.45), channel_id=1, source_target_pairs={{0,1},{1,0},{2,3},{3,2},{4,5},{5,4},{6,7},{7,6},{8,9},{9,8},{10,11... | collective-permute-start | bytes 2555912 | tf_op jit(solution)/shard_map/ppermute | solution.py:39
  124.7 2.0 %collective-permute-done.10 = bf16[8,416,128]{2,1,0:T(8,128)(2,1)S(1)} collective-permute-done((bf16[8,416,128]{2,1,0:T(8,128)(2,1)S(1)}, bf16[8,416,128]{2,1,0:T(8,128)(2,1)S(1)}, u32[]{:S(2)}, u32[]{:S(2)}) %collective-permute-start.10) | collective-permute-done | bytes 852000 | tf_op jit(solution)/shard_map/ppermute | solution.py:39
  126.6 0.2 maximum_bitcast_fusion
  126.8 1.8 copy.15
  128.6 2.2 %reshape.45 = bf16[416,2048]{1,0:T(8,128)(2,1)} reshape(bf16[416,8,2,128]{3,2,1,0:T(2,128)(2,1)S(1)} %copy.15) | data formatting | bytes 3407872 | tf_op jit(solution)/shard_map/reshape | solution.py:207
  130.8 6.3 %all-to-all-done.2 = bf16[4,104,512]{2,1,0:T(8,128)(2,1)S(1)} async-done(((bf16[4,104,512]{2,1,0:T(8,128)(2,1)}), bf16[4,104,512]{2,1,0:T(8,128)(2,1)S(1)}, u32[]{:S(2)}, u32[]{:S(2)}) %all-to-all-start.2) | async-done | bytes 426016 | tf_op jit(solution)/shard_map/all_to_all | solution.py:25
  137.1 2.7 %convolution_convert_fusion = bf16[512,2048]{1,0:T(8,128)(2,1)S(1)} fusion(bf16[416,512]{1,0:T(8,128)(2,1)S(1)} %bitcast.53, bf16[416,2048]{1,0:T(8,128)(2,1)} %reshape.45), kind=kOutput, calls=%fused_computation | convolution fusion | flops 873463808 | bytes 4227072 | tf_op jit(solution)/shard_map/dot_general | solution.py:209
  139.8 34.1 %all_to_all.25.parts = bf16[8,64,2048]{2,1,0:T(8,128)(2,1)S(1)} all-to-all(bf16[8,64,2048]{2,1,0:T(8,128)(2,1)S(1)} %bitcast.47), channel_id=1, replica_groups=mesh['y'=4,'xh'=2,'xl'=2,'zh'=4,'zm'=2,'z0'=2,'core'=2] {'y','xh'}, dimensions={0} | all-to-all | bytes 4194304 | tf_op jit(solution)/shard_map/all_to_all | solution.py:25
  173.9 1.5 shard_map.58
  175.4 10.0 %all-to-all-start.4 = ((bf16[16,64,128]{2,1,0:T(8,128)(2,1)}), bf16[16,64,128]{2,1,0:T(8,128)(2,1)S(1)}, u32[]{:S(2)}, u32[]{:S(2)}) async-start(bf16[16,64,128]{2,1,0:T(8,128)(2,1)} %shard_map.58), calls=%async_computation.4 | async-start | bytes 524288 | tf_op jit(solution)/shard_map/all_to_all | solution.py:25
  185.4 9.5 %all-to-all-done.4 = bf16[16,64,128]{2,1,0:T(8,128)(2,1)S(1)} async-done(((bf16[16,64,128]{2,1,0:T(8,128)(2,1)}), bf16[16,64,128]{2,1,0:T(8,128)(2,1)S(1)}, u32[]{:S(2)}, u32[]{:S(2)}) %all-to-all-start.4) | async-done | bytes 262176 | tf_op jit(solution)/shard_map/all_to_all | solution.py:25
  195.0 1.4 add_convert_fusion
  (7 shorter events, 0.2 us)
Async XLA Ops:
  3.8 7.6 %copy-start.1 = (bf16[3328,128]{1,0:T(8,128)(2,1)S(1)}, bf16[3328,128]{1,0:T(8,128)(2,1)}, u32[]{:S(2)}) copy-start(bf16[3328,128]{1,0:T(8,128)(2,1)} %param.9) | copy-start | bytes 2555908
  3.8 34.6 %all-to-all-start = ((bf16[8,112,1024]{2,1,0:T(8,128)(2,1)}), bf16[8,112,1024]{2,1,0:T(8,128)(2,1)}, u32[]{:S(2)}, u32[]{:S(2)}) async-start(bf16[8,112,1024]{2,1,0:T(8,128)(2,1)} %shard_map.55), calls=%async_computation | async-start | bytes 3670016 | tf_op jit(solution)/shard_map/all_to_all | solution.py:25
  11.5 3.7 %copy-start.2 = (bf16[1024,128]{1,0:T(8,128)(2,1)S(1)}, bf16[1024,128]{1,0:T(8,128)(2,1)}, u32[]{:S(2)}) copy-start(bf16[1024,128]{1,0:T(8,128)(2,1)} %param.5) | copy-start | bytes 786436
  11.5 3.8 %copy-start.4 = (bf16[128]{0:T(256)(128)(2,1)S(1)}, bf16[128]{0:T(256)(128)(2,1)}, u32[]{:S(2)}) copy-start(bf16[128]{0:T(256)(128)(2,1)} %param.6) | copy-start | bytes 772
  11.6 20.0 %collective-permute-start.2 = (bf16[2,2,416,128]{3,2,1,0:T(8,128)(2,1)S(1)}, bf16[2,2,416,128]{3,2,1,0:T(8,128)(2,1)S(1)}, u32[]{:S(2)}, u32[]{:S(2)}) collective-permute-start(bf16[2,2,416,128]{3,2,1,0:T(8,128)(2,1)S(1)} %get-tuple-element.20), channel_id=1, source_target_pairs={{0,2},{1,3},{2,0},{3,1},{4,6},{5,7},{6,4},{7,5},{8,10},{9,11},{10,... | collective-permute-start | bytes 1277960 | tf_op jit(solution)/shard_map/ppermute | solution.py:39
  15.3 23.1 %collective-permute-start.1 = (bf16[528,128]{1,0:T(8,128)(2,1)S(1)}, bf16[528,128]{1,0:T(8,128)(2,1)S(1)}, u32[]{:S(2)}, u32[]{:S(2)}) collective-permute-start(bf16[528,128]{1,0:T(8,128)(2,1)S(1)} %get-tuple-element.25), channel_id=1, source_target_pairs={{0,17},{1,16},{2,19},{3,18},{4,77},{5,76},{6,79},{7,78},{8,137},{9... | collective-permute-start | bytes 405512 | tf_op jit(solution)/shard_map/ppermute | solution.py:39
  31.0 7.5 %collective-permute-start = (bf16[528,128]{1,0:T(8,128)(2,1)S(1)}, bf16[528,128]{1,0:T(8,128)(2,1)S(1)}, u32[]{:S(2)}, u32[]{:S(2)}) collective-permute-start(bf16[528,128]{1,0:T(8,128)(2,1)S(1)} %get-tuple-element.26), channel_id=1, source_target_pairs={{0,0},{1,1},{2,2},{3,3},{4,92},{5,93},{6,94},{7,95},{8,152},{9,153... | collective-permute-start | bytes 405512 | tf_op jit(solution)/shard_map/ppermute | solution.py:39
  38.4 22.4 %collective-permute-start.6 = (bf16[8,112,1024]{2,1,0:T(8,128)(2,1)}, bf16[8,112,1024]{2,1,0:T(8,128)(2,1)}, u32[]{:S(2)}, u32[]{:S(2)}) collective-permute-start(bf16[8,112,1024]{2,1,0:T(8,128)(2,1)} %all-to-all-done.w_own), channel_id=1, source_target_pairs={{0,1},{1,0},{2,3},{3,2},{4,5},{5,4},{6,7},{7,6},{8,9},{9,8},{10,11... | collective-permute-start | bytes 5505032 | tf_op jit(solution)/shard_map/ppermute | solution.py:39
  40.9 19.9 %copy-start.3 = (bf16[2,528,128]{2,1,0:T(8,128)(2,1)}, bf16[2,528,128]{2,1,0:T(8,128)(2,1)S(1)}, u32[]{:S(2)}) copy-start(bf16[2,528,128]{2,1,0:T(8,128)(2,1)S(1)} %pad_maximum_fusion.2.x0) | copy-start | bytes 811012
  40.9 14.1 %collective-permute-start.5 = (bf16[2,528,128]{2,1,0:T(8,128)(2,1)S(1)}, bf16[2,528,128]{2,1,0:T(8,128)(2,1)S(1)}, u32[]{:S(2)}, u32[]{:S(2)}) collective-permute-start(bf16[2,528,128]{2,1,0:T(8,128)(2,1)S(1)} %pad_maximum_fusion.2.x0), channel_id=1, source_target_pairs={{0,34},{1,35},{2,32},{3,33},{4,38},{5,39},{6,36},{7,37},{8,42},{9,... | collective-permute-start | bytes 811016 | tf_op jit(solution)/shard_map/ppermute | solution.py:39
  44.5 15.7 %collective-permute-start.4 = (bf16[2,528,128]{2,1,0:T(8,128)(2,1)S(1)}, bf16[2,528,128]{2,1,0:T(8,128)(2,1)S(1)}, u32[]{:S(2)}, u32[]{:S(2)}) collective-permute-start(bf16[2,528,128]{2,1,0:T(8,128)(2,1)S(1)} %pad_maximum_fusion.2.x0), channel_id=1, source_target_pairs={{0,32},{1,33},{2,34},{3,35},{4,36},{5,37},{6,38},{7,39},{8,40},{9,... | collective-permute-start | bytes 811016 | tf_op jit(solution)/shard_map/ppermute | solution.py:39
  47.3 13.5 %collective-permute-start.3 = (bf16[2,528,128]{2,1,0:T(8,128)(2,1)S(1)}, bf16[2,528,128]{2,1,0:T(8,128)(2,1)S(1)}, u32[]{:S(2)}, u32[]{:S(2)}) collective-permute-start(bf16[2,528,128]{2,1,0:T(8,128)(2,1)S(1)} %pad_maximum_fusion.2.x0), channel_id=1, source_target_pairs={{0,2},{1,3},{2,0},{3,1},{4,6},{5,7},{6,4},{7,5},{8,10},{9,11},{10,... | collective-permute-start | bytes 811016 | tf_op jit(solution)/shard_map/ppermute | solution.py:39
  55.0 5.8 %copy-start.5 = (bf16[2,528,128]{2,1,0:T(8,128)(2,1)}, bf16[2,528,128]{2,1,0:T(8,128)(2,1)S(1)}, u32[]{:S(2)}) copy-start(bf16[2,528,128]{2,1,0:T(8,128)(2,1)S(1)} %collective-permute-done.5.x3) | copy-start | bytes 811012
  60.2 0.7 copy-start.6
  60.8 0.7 copy-start.7
  67.9 39.3 %copy-start = (s32[3]{0:T(128)S(1)}, s32[3]{0:T(128)}, u32[]{:S(2)}) copy-start(s32[3]{0:T(128)} %pad_add_fusion.at) | copy-start | bytes 40
  67.9 39.3 %all-to-all-start.1 = ((bf16[8,2,112,512]{3,2,1,0:T(8,128)(2,1)}), bf16[8,2,112,512]{3,2,1,0:T(8,128)(2,1)S(1)}, u32[]{:S(2)}, u32[]{:S(2)}) async-start(bf16[8,2,112,512]{3,2,1,0:T(8,128)(2,1)} %shard_map.56), calls=%async_computation.1 | async-start | bytes 3670016 | tf_op jit(solution)/shard_map/all_to_all | solution.py:25
  82.3 26.6 %collective-permute-start.7 = (bf16[2,2,416,128]{3,2,1,0:T(8,128)(2,1)S(1)}, bf16[2,2,416,128]{3,2,1,0:T(8,128)(2,1)}, u32[]{:S(2)}, u32[]{:S(2)}) collective-permute-start(bf16[2,2,416,128]{3,2,1,0:T(8,128)(2,1)S(1)} %dynamic-slice_bitcast_fusion), channel_id=1, source_target_pairs={{0,4},{1,5},{2,6},{3,7},{4,0},{5,1},{6,2},{7,3},{8,12},{9,13},{10,... | collective-permute-start | bytes 1277960 | tf_op jit(solution)/shard_map/ppermute | solution.py:39
  86.0 33.2 %collective-permute-start.8 = (bf16[2,416,128]{2,1,0:T(8,128)(2,1)S(1)}, bf16[2,416,128]{2,1,0:T(8,128)(2,1)S(1)}, u32[]{:S(2)}, u32[]{:S(2)}) collective-permute-start(bf16[2,416,128]{2,1,0:T(8,128)(2,1)S(1)} %get-tuple-element.18), channel_id=1, source_target_pairs={{0,32},{1,33},{2,34},{3,35},{4,36},{5,37},{6,38},{7,39},{8,40},{9,... | collective-permute-start | bytes 638984 | tf_op jit(solution)/shard_map/ppermute | solution.py:39
  109.9 9.3 %collective-permute-start.9 = (bf16[2,416,128]{2,1,0:T(8,128)(2,1)S(1)}, bf16[2,416,128]{2,1,0:T(8,128)(2,1)S(1)}, u32[]{:S(2)}, u32[]{:S(2)}) collective-permute-start(bf16[2,416,128]{2,1,0:T(8,128)(2,1)S(1)} %get-tuple-element.22), channel_id=1, source_target_pairs={{0,32},{1,33},{2,34},{3,35},{4,36},{5,37},{6,38},{7,39},{8,40},{9,... | collective-permute-start | bytes 638984 | tf_op jit(solution)/shard_map/ppermute | solution.py:39
  112.2 24.9 %all-to-all-start.2 = ((bf16[4,104,512]{2,1,0:T(8,128)(2,1)}), bf16[4,104,512]{2,1,0:T(8,128)(2,1)S(1)}, u32[]{:S(2)}, u32[]{:S(2)}) async-start(bf16[4,104,512]{2,1,0:T(8,128)(2,1)} %shard_map.57), calls=%async_computation.2 | async-start | bytes 851968 | tf_op jit(solution)/shard_map/all_to_all | solution.py:25
  119.3 7.3 %collective-permute-start.10 = (bf16[8,416,128]{2,1,0:T(8,128)(2,1)S(1)}, bf16[8,416,128]{2,1,0:T(8,128)(2,1)S(1)}, u32[]{:S(2)}, u32[]{:S(2)}) collective-permute-start(bf16[8,416,128]{2,1,0:T(8,128)(2,1)S(1)} %bitcast.45), channel_id=1, source_target_pairs={{0,1},{1,0},{2,3},{3,2},{4,5},{5,4},{6,7},{7,6},{8,9},{9,8},{10,11... | collective-permute-start | bytes 2555912 | tf_op jit(solution)/shard_map/ppermute | solution.py:39
  175.4 19.5 %all-to-all-start.4 = ((bf16[16,64,128]{2,1,0:T(8,128)(2,1)}), bf16[16,64,128]{2,1,0:T(8,128)(2,1)S(1)}, u32[]{:S(2)}, u32[]{:S(2)}) async-start(bf16[16,64,128]{2,1,0:T(8,128)(2,1)} %shard_map.58), calls=%async_computation.4 | async-start | bytes 524288 | tf_op jit(solution)/shard_map/all_to_all | solution.py:25

commit v10 on v9

--- a/solution.py
+++ b/solution.py
@@ -196,13 +196,19 @@
         (at, *blocks, own_w, other_w),
         (pltpu.VMEM((rows, 1024), bf16),),
         flops=2 * 1792 * 1024 * rows,
-        vmem=60,
+        vmem=40,
     )
-    kept, got = halve(down, "zm")
+    zm, xl = lax.axis_index("zm"), lax.axis_index("xl")
+
+    def piece(xl_off, zm_off):
+        part = lax.dynamic_index_in_dim(down, jnp.bitwise_xor(zm, zm_off), 0, keepdims=False)
+        part = lax.dynamic_index_in_dim(part, jnp.bitwise_xor(xl, xl_off), 0, keepdims=False)
+        return send(part, shift(xl=xl_off, zm=zm_off)) if xl_off or zm_off else part
+
+    pieces = [piece(xl_off, zm_off) for xl_off in (0, 1) for zm_off in (0, 1)]
     acts = run(acts_kernel, (4, 2 * units, rows), (at, exchange(sums, PHASE)))
-    acts, got = lax.optimization_barrier((acts, got))
-    (kept0, got0), (kept1, got1) = halve(kept, "xl"), halve(got, "xl")
-    down = jnp.stack((kept0, kept1, got0, got1)).reshape(8, 8 * units, LANES)
+    acts, *pieces = lax.optimization_barrier((acts, *pieces))
+    down = jnp.stack(pieces).reshape(8, 8 * units, LANES)
     down = jnp.stack((down, send(down, shift(core=1))), 1)
     down = down.transpose(2, 0, 1, 3).reshape(8 * units, 2048)
     acts = exchange(acts, FAR).reshape(8 * units, rows)

time: 197 us -> 201 us (1.020)
  waiting for transfers between devices: 54.3 us -> 58.8 us
  Pallas kernels: 13.4 us -> 11.3 us
    all_to_all x4, waiting for transfers between devices: 34.9 us -> 41.8 us  [exchange(): return lax.all_to_all(value, axes, 0, 0, tiled=True)]
    ppermute x11, waiting for transfers between devices: 19.4 us -> 16.9 us  [send(): return lax.ppermute(value, AXES, route(move))]
    pallas_call x3, Pallas kernels: 9.55 us -> 7.42 us  [run(): pl.pallas_call(kernel, out_shape=jax.ShapeDtypeStruct(out_shape, bf16), i...]
  transfers between devices with their start and end apart: 15 -> 15, of which waited for: 8 -> 7; matrix products, arithmetic and copies ran while one was open for 3% -> 3% of each run, Pallas kernels for 1% -> 1%
where the time goes in v10:
time: 201 us; the launch traced here: 200 us
  starting transfers between devices  84.8 us (42%)
  waiting for transfers between devices  58.8 us (29%)
  blocking collectives  33 us (16%)
  Pallas kernels  11.3 us (6%)
  local copies, waits for them, and re-layouts  5.54 us (3%)
  other arithmetic  3.71 us (2%)
  matrix products  2.3 us (1%)
    ppermute x11, starting transfers between devices, send(): return lax.ppermute(value, AXES, route(move))  45.7 us
    all_to_all x4, waiting for transfers between devices, exchange(): return lax.all_to_all(value, axes, 0, 0, tiled=True)  41.8 us
    all_to_all x4, starting transfers between devices, exchange(): return lax.all_to_all(value, axes, 0, 0, tiled=True)  39.1 us
    all_to_all x1, blocking collectives, exchange(): return lax.all_to_all(value, axes, 0, 0, tiled=True)  33 us
    ppermute x11, waiting for transfers between devices, send(): return lax.ppermute(value, AXES, route(move))  16.9 us
    pallas_call x3, Pallas kernels, run(): pl.pallas_call(kernel, out_shape=jax.ShapeDtypeStruct(out_shape, bf16), i...  7.42 us
  transfers between devices with their start and end apart: 15, of which 7 were waited for; matrix products, arithmetic and copies ran while one was open for 3% of the time, Pallas kernels for 1%

profile of v10, /device:TPU:1, one launch (start us, length us, event | category | flops | bytes accessed | tf_op | source)
XLA Modules:
  0.0 199.7 jit_solution(4626227030612451451)
XLA Ops:
  0.0 3.8 %shard_map.55 = bf16[8,112,1024]{2,1,0:T(8,128)(2,1)} custom-call(bf16[52,8192]{1,0:T(8,128)(2,1)} %gate.1, bf16[52,8192]{1,0:T(8,128)(2,1)} %up.1), custom_call_target="tpu_custom_call" | custom-call | bytes 3407872 | tf_op jit(solution)/shard_map/pallas_call | solution.py:70
  3.8 0.0 copy-start.2
  3.9 7.6 %all-to-all-start = ((bf16[8,112,1024]{2,1,0:T(8,128)(2,1)}), bf16[8,112,1024]{2,1,0:T(8,128)(2,1)S(1)}, u32[]{:S(2)}, u32[]{:S(2)}) async-start(bf16[8,112,1024]{2,1,0:T(8,128)(2,1)} %shard_map.55), calls=%async_computation | async-start | bytes 3670016 | tf_op jit(solution)/shard_map/all_to_all | solution.py:25
  11.5 0.0 copy-done.2
  11.5 0.0 copy-start.3
  11.5 0.1 copy.12
  11.6 0.1 dynamic-slice_bitcast_fusion.1
  11.6 3.5 %collective-permute-start.2 = (bf16[2,2,416,128]{3,2,1,0:T(8,128)(2,1)S(1)}, bf16[2,2,416,128]{3,2,1,0:T(8,128)(2,1)S(1)}, u32[]{:S(2)}, u32[]{:S(2)}) collective-permute-start(bf16[2,2,416,128]{3,2,1,0:T(8,128)(2,1)S(1)} %get-tuple-element.28), channel_id=1, source_target_pairs={{0,2},{1,3},{2,0},{3,1},{4,6},{5,7},{6,4},{7,5},{8,10},{9,11},{10,... | collective-permute-start | bytes 1277960 | tf_op jit(solution)/shard_map/ppermute | solution.py:39
  15.2 1.0 constant_dynamic-slice_fusion
  16.2 0.0 copy-done.3
  16.2 15.7 %collective-permute-start.1 = (bf16[528,128]{1,0:T(8,128)(2,1)S(1)}, bf16[528,128]{1,0:T(8,128)(2,1)S(1)}, u32[]{:S(2)}, u32[]{:S(2)}) collective-permute-start(bf16[528,128]{1,0:T(8,128)(2,1)S(1)} %get-tuple-element.31), channel_id=1, source_target_pairs={{0,17},{1,16},{2,19},{3,18},{4,77},{5,76},{6,79},{7,78},{8,137},{9... | collective-permute-start | bytes 405512 | tf_op jit(solution)/shard_map/ppermute | solution.py:39
  31.9 1.3 collective-permute-start
  33.2 0.0 collective-permute-done.2
  33.2 1.0 pad_maximum_fusion
  34.2 3.9 %collective-permute-done.1 = bf16[528,128]{1,0:T(8,128)(2,1)S(1)} collective-permute-done((bf16[528,128]{1,0:T(8,128)(2,1)S(1)}, bf16[528,128]{1,0:T(8,128)(2,1)S(1)}, u32[]{:S(2)}, u32[]{:S(2)}) %collective-permute-start.1) | collective-permute-done | bytes 135200 | tf_op jit(solution)/shard_map/ppermute | solution.py:39
  38.1 0.0 collective-permute-done
  38.1 0.0 all-to-all-done.w_own
  38.2 2.2 %collective-permute-start.6 = (bf16[8,112,1024]{2,1,0:T(8,128)(2,1)S(1)}, bf16[8,112,1024]{2,1,0:T(8,128)(2,1)}, u32[]{:S(2)}, u32[]{:S(2)}) collective-permute-start(bf16[8,112,1024]{2,1,0:T(8,128)(2,1)S(1)} %all-to-all-done.w_own), channel_id=1, source_target_pairs={{0,1},{1,0},{2,3},{3,2},{4,5},{5,4},{6,7},{7,6},{8,9},{9,8},{10,11... | collective-permute-start | bytes 5505032 | tf_op jit(solution)/shard_map/ppermute | solution.py:39
  40.3 0.9 pad_maximum_fusion.2.x0
  41.3 4.0 %collective-permute-start.5 = (bf16[2,528,128]{2,1,0:T(8,128)(2,1)S(1)}, bf16[2,528,128]{2,1,0:T(8,128)(2,1)S(1)}, u32[]{:S(2)}, u32[]{:S(2)}) collective-permute-start(bf16[2,528,128]{2,1,0:T(8,128)(2,1)S(1)} %pad_maximum_fusion.2.x0), channel_id=1, source_target_pairs={{0,34},{1,35},{2,32},{3,33},{4,38},{5,39},{6,36},{7,37},{8,42},{9,... | collective-permute-start | bytes 811016 | tf_op jit(solution)/shard_map/ppermute | solution.py:39
  45.3 2.8 %collective-permute-start.4 = (bf16[2,528,128]{2,1,0:T(8,128)(2,1)S(1)}, bf16[2,528,128]{2,1,0:T(8,128)(2,1)S(1)}, u32[]{:S(2)}, u32[]{:S(2)}) collective-permute-start(bf16[2,528,128]{2,1,0:T(8,128)(2,1)S(1)} %pad_maximum_fusion.2.x0), channel_id=1, source_target_pairs={{0,32},{1,33},{2,34},{3,35},{4,36},{5,37},{6,38},{7,39},{8,40},{9,... | collective-permute-start | bytes 811016 | tf_op jit(solution)/shard_map/ppermute | solution.py:39
  48.1 1.9 collective-permute-start.3
  50.0 0.1 pad_add_fusion.at
  50.1 5.3 %collective-permute-done.5.x3 = bf16[2,528,128]{2,1,0:T(8,128)(2,1)S(1)} collective-permute-done((bf16[2,528,128]{2,1,0:T(8,128)(2,1)S(1)}, bf16[2,528,128]{2,1,0:T(8,128)(2,1)S(1)}, u32[]{:S(2)}, u32[]{:S(2)}) %collective-permute-start.5) | collective-permute-done | bytes 270368 | tf_op jit(solution)/shard_map/ppermute | solution.py:39
  55.4 5.7 %collective-permute-done.4.x2 = bf16[2,528,128]{2,1,0:T(8,128)(2,1)S(1)} collective-permute-done((bf16[2,528,128]{2,1,0:T(8,128)(2,1)S(1)}, bf16[2,528,128]{2,1,0:T(8,128)(2,1)S(1)}, u32[]{:S(2)}, u32[]{:S(2)}) %collective-permute-start.4) | collective-permute-done | bytes 270368 | tf_op jit(solution)/shard_map/ppermute | solution.py:39
  61.1 0.0 collective-permute-done.3.x1
  61.1 0.0 collective-permute-done.6.w_other
  61.1 4.3 %shard_map.56 = bf16[8,2,112,512]{3,2,1,0:T(8,128)(2,1)S(1)} custom-call(s32[3]{0:T(128)S(1)} %pad_add_fusion.at, bf16[2,528,128]{2,1,0:T(8,128)(2,1)S(1)} %pad_maximum_fusion.2.x0, bf16[2,528,128]{2,1,0:T(8,128)(2,1)S(1)} %collective-permute-done.3.x1, bf16[2,528,128]{2,1,0:T(8,128)(2,1)S(1)} %collective-permute-done.4.x2, ...), custom_call_target="tpu_custom_call" | custom-call | flops 1879048192 | bytes 6586380 | tf_op jit(solution)/shard_map/pallas_call | solution.py:148
  65.4 0.0 copy-start
  65.4 1.3 copy-done
  66.7 0.0 copy-start.1
  66.7 14.9 %all-to-all-start.1 = ((bf16[8,2,112,512]{3,2,1,0:T(8,128)(2,1)}), bf16[8,2,112,512]{3,2,1,0:T(8,128)(2,1)S(1)}, u32[]{:S(2)}, u32[]{:S(2)}) async-start(bf16[8,2,112,512]{3,2,1,0:T(8,128)(2,1)} %copy-done), calls=%async_computation.1 | async-start | bytes 3670016 | tf_op jit(solution)/shard_map/all_to_all | solution.py:25
  81.6 0.0 copy-done.1
  81.6 0.1 dynamic-slice_bitcast_fusion.2
  81.7 3.9 %collective-permute-start.9 = (bf16[2,416,128]{2,1,0:T(8,128)(2,1)S(1)}, bf16[2,416,128]{2,1,0:T(8,128)(2,1)S(1)}, u32[]{:S(2)}, u32[]{:S(2)}) collective-permute-start(bf16[2,416,128]{2,1,0:T(8,128)(2,1)S(1)} %get-tuple-element.23), channel_id=1, source_target_pairs={{0,36},{1,37},{2,38},{3,39},{4,32},{5,33},{6,34},{7,35},{8,44},{9,... | collective-permute-start | bytes 638984 | tf_op jit(solution)/shard_map/ppermute | solution.py:39
  85.6 3.1 %collective-permute-start.8 = (bf16[2,416,128]{2,1,0:T(8,128)(2,1)S(1)}, bf16[2,416,128]{2,1,0:T(8,128)(2,1)S(1)}, u32[]{:S(2)}, u32[]{:S(2)}) collective-permute-start(bf16[2,416,128]{2,1,0:T(8,128)(2,1)S(1)} %get-tuple-element.24), channel_id=1, source_target_pairs={{0,32},{1,33},{2,34},{3,35},{4,36},{5,37},{6,38},{7,39},{8,40},{9,... | collective-permute-start | bytes 638984 | tf_op jit(solution)/shard_map/ppermute | solution.py:39
  88.7 2.3 %collective-permute-start.7 = (bf16[2,416,128]{2,1,0:T(8,128)(2,1)S(1)}, bf16[2,416,128]{2,1,0:T(8,128)(2,1)S(1)}, u32[]{:S(2)}, u32[]{:S(2)}) collective-permute-start(bf16[2,416,128]{2,1,0:T(8,128)(2,1)S(1)} %get-tuple-element.25), channel_id=1, source_target_pairs={{0,4},{1,5},{2,6},{3,7},{4,0},{5,1},{6,2},{7,3},{8,12},{9,13},{10,... | collective-permute-start | bytes 638984 | tf_op jit(solution)/shard_map/ppermute | solution.py:39
  91.0 20.2 %all-to-all-done.1.sums = bf16[8,2,112,512]{3,2,1,0:T(8,128)(2,1)S(1)} async-done(((bf16[8,2,112,512]{3,2,1,0:T(8,128)(2,1)}), bf16[8,2,112,512]{3,2,1,0:T(8,128)(2,1)S(1)}, u32[]{:S(2)}, u32[]{:S(2)}) %all-to-all-start.1) | async-done | bytes 1835040 | tf_op jit(solution)/shard_map/all_to_all | solution.py:25
  111.1 1.6 shard_map.57
  112.8 0.0 collective-permute-done.9
  112.8 0.0 collective-permute-done.8
  112.8 0.0 collective-permute-done.7
  112.8 7.8 %all-to-all-start.2 = ((bf16[4,104,512]{2,1,0:T(8,128)(2,1)}), bf16[4,104,512]{2,1,0:T(8,128)(2,1)}, u32[]{:S(2)}, u32[]{:S(2)}) async-start(bf16[4,104,512]{2,1,0:T(8,128)(2,1)} %shard_map.57), calls=%async_computation.2 | async-start | bytes 851968 | tf_op jit(solution)/shard_map/all_to_all | solution.py:25
  120.5 0.1 pad_maximum_fusion.1
  120.6 5.1 %collective-permute-start.10 = (bf16[8,416,128]{2,1,0:T(8,128)(2,1)S(1)}, bf16[8,416,128]{2,1,0:T(8,128)(2,1)S(1)}, u32[]{:S(2)}, u32[]{:S(2)}) collective-permute-start(bf16[8,416,128]{2,1,0:T(8,128)(2,1)S(1)} %bitcast.47), channel_id=1, source_target_pairs={{0,1},{1,0},{2,3},{3,2},{4,5},{5,4},{6,7},{7,6},{8,9},{9,8},{10,11... | collective-permute-start | bytes 2555912 | tf_op jit(solution)/shard_map/ppermute | solution.py:39
  125.7 2.0 collective-permute-done.10
  127.7 0.2 maximum_bitcast_fusion
  127.9 1.8 copy.13
  129.6 1.3 reshape.50
  130.9 12.2 %all-to-all-done.2 = bf16[4,104,512]{2,1,0:T(8,128)(2,1)} async-done(((bf16[4,104,512]{2,1,0:T(8,128)(2,1)}), bf16[4,104,512]{2,1,0:T(8,128)(2,1)}, u32[]{:S(2)}, u32[]{:S(2)}) %all-to-all-start.2) | async-done | bytes 426016 | tf_op jit(solution)/shard_map/all_to_all | solution.py:25
  143.1 2.3 %convolution_convert_fusion = bf16[512,2048]{1,0:T(8,128)(2,1)S(1)} fusion(bf16[416,512]{1,0:T(8,128)(2,1)} %bitcast.18, bf16[416,2048]{1,0:T(8,128)(2,1)S(1)} %reshape.50), kind=kOutput, calls=%fused_computation | convolution fusion | flops 873463808 | bytes 4227072 | tf_op jit(solution)/shard_map/dot_general | solution.py:215
  145.4 33.0 %all_to_all.25.parts = bf16[8,64,2048]{2,1,0:T(8,128)(2,1)S(1)} all-to-all(bf16[8,64,2048]{2,1,0:T(8,128)(2,1)S(1)} %bitcast.49), channel_id=1, replica_groups=mesh['y'=4,'xh'=2,'xl'=2,'zh'=4,'zm'=2,'z0'=2,'core'=2] {'y','xh'}, dimensions={0} | all-to-all | bytes 4194304 | tf_op jit(solution)/shard_map/all_to_all | solution.py:25
  178.4 1.5 shard_map.58
  179.9 8.8 %all-to-all-start.4 = ((bf16[16,64,128]{2,1,0:T(8,128)(2,1)}), bf16[16,64,128]{2,1,0:T(8,128)(2,1)S(1)}, u32[]{:S(2)}, u32[]{:S(2)}) async-start(bf16[16,64,128]{2,1,0:T(8,128)(2,1)} %shard_map.58), calls=%async_computation.4 | async-start | bytes 524288 | tf_op jit(solution)/shard_map/all_to_all | solution.py:25
  188.7 9.5 %all-to-all-done.4 = bf16[16,64,128]{2,1,0:T(8,128)(2,1)S(1)} async-done(((bf16[16,64,128]{2,1,0:T(8,128)(2,1)}), bf16[16,64,128]{2,1,0:T(8,128)(2,1)S(1)}, u32[]{:S(2)}, u32[]{:S(2)}) %all-to-all-start.4) | async-done | bytes 262176 | tf_op jit(solution)/shard_map/all_to_all | solution.py:25
  198.3 1.4 add_convert_fusion
  (3 shorter events, 0.1 us)
Async XLA Ops:
  3.8 7.6 %copy-start.2 = (bf16[3328,128]{1,0:T(8,128)(2,1)S(1)}, bf16[3328,128]{1,0:T(8,128)(2,1)}, u32[]{:S(2)}) copy-start(bf16[3328,128]{1,0:T(8,128)(2,1)} %param.9) | copy-start | bytes 2555908
  3.9 34.3 %all-to-all-start = ((bf16[8,112,1024]{2,1,0:T(8,128)(2,1)}), bf16[8,112,1024]{2,1,0:T(8,128)(2,1)S(1)}, u32[]{:S(2)}, u32[]{:S(2)}) async-start(bf16[8,112,1024]{2,1,0:T(8,128)(2,1)} %shard_map.55), calls=%async_computation | async-start | bytes 3670016 | tf_op jit(solution)/shard_map/all_to_all | solution.py:25
  11.5 4.7 %copy-start.3 = (bf16[128]{0:T(256)(128)(2,1)S(1)}, bf16[128]{0:T(256)(128)(2,1)}, u32[]{:S(2)}) copy-start(bf16[128]{0:T(256)(128)(2,1)} %param.6) | copy-start | bytes 772
  11.6 21.6 %collective-permute-start.2 = (bf16[2,2,416,128]{3,2,1,0:T(8,128)(2,1)S(1)}, bf16[2,2,416,128]{3,2,1,0:T(8,128)(2,1)S(1)}, u32[]{:S(2)}, u32[]{:S(2)}) collective-permute-start(bf16[2,2,416,128]{3,2,1,0:T(8,128)(2,1)S(1)} %get-tuple-element.28), channel_id=1, source_target_pairs={{0,2},{1,3},{2,0},{3,1},{4,6},{5,7},{6,4},{7,5},{8,10},{9,11},{10,... | collective-permute-start | bytes 1277960 | tf_op jit(solution)/shard_map/ppermute | solution.py:39
  16.2 21.9 %collective-permute-start.1 = (bf16[528,128]{1,0:T(8,128)(2,1)S(1)}, bf16[528,128]{1,0:T(8,128)(2,1)S(1)}, u32[]{:S(2)}, u32[]{:S(2)}) collective-permute-start(bf16[528,128]{1,0:T(8,128)(2,1)S(1)} %get-tuple-element.31), channel_id=1, source_target_pairs={{0,17},{1,16},{2,19},{3,18},{4,77},{5,76},{6,79},{7,78},{8,137},{9... | collective-permute-start | bytes 405512 | tf_op jit(solution)/shard_map/ppermute | solution.py:39
  31.9 6.2 %collective-permute-start = (bf16[528,128]{1,0:T(8,128)(2,1)S(1)}, bf16[528,128]{1,0:T(8,128)(2,1)}, u32[]{:S(2)}, u32[]{:S(2)}) collective-permute-start(bf16[528,128]{1,0:T(8,128)(2,1)S(1)} %get-tuple-element.32), channel_id=1, source_target_pairs={{0,0},{1,1},{2,2},{3,3},{4,92},{5,93},{6,94},{7,95},{8,152},{9,153... | collective-permute-start | bytes 405512 | tf_op jit(solution)/shard_map/ppermute | solution.py:39
  38.2 23.0 %collective-permute-start.6 = (bf16[8,112,1024]{2,1,0:T(8,128)(2,1)S(1)}, bf16[8,112,1024]{2,1,0:T(8,128)(2,1)}, u32[]{:S(2)}, u32[]{:S(2)}) collective-permute-start(bf16[8,112,1024]{2,1,0:T(8,128)(2,1)S(1)} %all-to-all-done.w_own), channel_id=1, source_target_pairs={{0,1},{1,0},{2,3},{3,2},{4,5},{5,4},{6,7},{7,6},{8,9},{9,8},{10,11... | collective-permute-start | bytes 5505032 | tf_op jit(solution)/shard_map/ppermute | solution.py:39
  41.3 14.1 %collective-permute-start.5 = (bf16[2,528,128]{2,1,0:T(8,128)(2,1)S(1)}, bf16[2,528,128]{2,1,0:T(8,128)(2,1)S(1)}, u32[]{:S(2)}, u32[]{:S(2)}) collective-permute-start(bf16[2,528,128]{2,1,0:T(8,128)(2,1)S(1)} %pad_maximum_fusion.2.x0), channel_id=1, source_target_pairs={{0,34},{1,35},{2,32},{3,33},{4,38},{5,39},{6,36},{7,37},{8,42},{9,... | collective-permute-start | bytes 811016 | tf_op jit(solution)/shard_map/ppermute | solution.py:39
  45.3 15.8 %collective-permute-start.4 = (bf16[2,528,128]{2,1,0:T(8,128)(2,1)S(1)}, bf16[2,528,128]{2,1,0:T(8,128)(2,1)S(1)}, u32[]{:S(2)}, u32[]{:S(2)}) collective-permute-start(bf16[2,528,128]{2,1,0:T(8,128)(2,1)S(1)} %pad_maximum_fusion.2.x0), channel_id=1, source_target_pairs={{0,32},{1,33},{2,34},{3,35},{4,36},{5,37},{6,38},{7,39},{8,40},{9,... | collective-permute-start | bytes 811016 | tf_op jit(solution)/shard_map/ppermute | solution.py:39
  48.1 13.1 %collective-permute-start.3 = (bf16[2,528,128]{2,1,0:T(8,128)(2,1)S(1)}, bf16[2,528,128]{2,1,0:T(8,128)(2,1)S(1)}, u32[]{:S(2)}, u32[]{:S(2)}) collective-permute-start(bf16[2,528,128]{2,1,0:T(8,128)(2,1)S(1)} %pad_maximum_fusion.2.x0), channel_id=1, source_target_pairs={{0,2},{1,3},{2,0},{3,1},{4,6},{5,7},{6,4},{7,5},{8,10},{9,11},{10,... | collective-permute-start | bytes 811016 | tf_op jit(solution)/shard_map/ppermute | solution.py:39
  65.4 1.3 copy-start
  66.7 14.9 %copy-start.1 = (bf16[2,2,2,416,128]{4,3,2,1,0:T(8,128)(2,1)S(1)}, bf16[2,2,2,416,128]{4,3,2,1,0:T(8,128)(2,1)}, u32[]{:S(2)}) copy-start(bf16[2,2,2,416,128]{4,3,2,1,0:T(8,128)(2,1)} %pad_maximum_fusion) | copy-start | bytes 2555908
  66.7 44.5 %all-to-all-start.1 = ((bf16[8,2,112,512]{3,2,1,0:T(8,128)(2,1)}), bf16[8,2,112,512]{3,2,1,0:T(8,128)(2,1)S(1)}, u32[]{:S(2)}, u32[]{:S(2)}) async-start(bf16[8,2,112,512]{3,2,1,0:T(8,128)(2,1)} %copy-done), calls=%async_computation.1 | async-start | bytes 3670016 | tf_op jit(solution)/shard_map/all_to_all | solution.py:25
  81.7 31.1 %collective-permute-start.9 = (bf16[2,416,128]{2,1,0:T(8,128)(2,1)S(1)}, bf16[2,416,128]{2,1,0:T(8,128)(2,1)S(1)}, u32[]{:S(2)}, u32[]{:S(2)}) collective-permute-start(bf16[2,416,128]{2,1,0:T(8,128)(2,1)S(1)} %get-tuple-element.23), channel_id=1, source_target_pairs={{0,36},{1,37},{2,38},{3,39},{4,32},{5,33},{6,34},{7,35},{8,44},{9,... | collective-permute-start | bytes 638984 | tf_op jit(solution)/shard_map/ppermute | solution.py:39
  85.6 27.2 %collective-permute-start.8 = (bf16[2,416,128]{2,1,0:T(8,128)(2,1)S(1)}, bf16[2,416,128]{2,1,0:T(8,128)(2,1)S(1)}, u32[]{:S(2)}, u32[]{:S(2)}) collective-permute-start(bf16[2,416,128]{2,1,0:T(8,128)(2,1)S(1)} %get-tuple-element.24), channel_id=1, source_target_pairs={{0,32},{1,33},{2,34},{3,35},{4,36},{5,37},{6,38},{7,39},{8,40},{9,... | collective-permute-start | bytes 638984 | tf_op jit(solution)/shard_map/ppermute | solution.py:39
  88.7 24.1 %collective-permute-start.7 = (bf16[2,416,128]{2,1,0:T(8,128)(2,1)S(1)}, bf16[2,416,128]{2,1,0:T(8,128)(2,1)S(1)}, u32[]{:S(2)}, u32[]{:S(2)}) collective-permute-start(bf16[2,416,128]{2,1,0:T(8,128)(2,1)S(1)} %get-tuple-element.25), channel_id=1, source_target_pairs={{0,4},{1,5},{2,6},{3,7},{4,0},{5,1},{6,2},{7,3},{8,12},{9,13},{10,... | collective-permute-start | bytes 638984 | tf_op jit(solution)/shard_map/ppermute | solution.py:39
  112.8 30.3 %all-to-all-start.2 = ((bf16[4,104,512]{2,1,0:T(8,128)(2,1)}), bf16[4,104,512]{2,1,0:T(8,128)(2,1)}, u32[]{:S(2)}, u32[]{:S(2)}) async-start(bf16[4,104,512]{2,1,0:T(8,128)(2,1)} %shard_map.57), calls=%async_computation.2 | async-start | bytes 851968 | tf_op jit(solution)/shard_map/all_to_all | solution.py:25
  120.6 7.0 %collective-permute-start.10 = (bf16[8,416,128]{2,1,0:T(8,128)(2,1)S(1)}, bf16[8,416,128]{2,1,0:T(8,128)(2,1)S(1)}, u32[]{:S(2)}, u32[]{:S(2)}) collective-permute-start(bf16[8,416,128]{2,1,0:T(8,128)(2,1)S(1)} %bitcast.47), channel_id=1, source_target_pairs={{0,1},{1,0},{2,3},{3,2},{4,5},{5,4},{6,7},{7,6},{8,9},{9,8},{10,11... | collective-permute-start | bytes 2555912 | tf_op jit(solution)/shard_map/ppermute | solution.py:39
  179.9 18.3 %all-to-all-start.4 = ((bf16[16,64,128]{2,1,0:T(8,128)(2,1)}), bf16[16,64,128]{2,1,0:T(8,128)(2,1)S(1)}, u32[]{:S(2)}, u32[]{:S(2)}) async-start(bf16[16,64,128]{2,1,0:T(8,128)(2,1)} %shard_map.58), calls=%async_computation.4 | async-start | bytes 524288 | tf_op jit(solution)/shard_map/all_to_all | solution.py:25

commit v11 on v10

--- a/solution.py
+++ b/solution.py
@@ -202,12 +202,14 @@
 
     def piece(xl_off, zm_off):
         part = lax.dynamic_index_in_dim(down, jnp.bitwise_xor(zm, zm_off), 0, keepdims=False)
-        part = lax.dynamic_index_in_dim(part, jnp.bitwise_xor(xl, xl_off), 0, keepdims=False)
-        return send(part, shift(xl=xl_off, zm=zm_off)) if xl_off or zm_off else part
-
-    pieces = [piece(xl_off, zm_off) for xl_off in (0, 1) for zm_off in (0, 1)]
-    acts = run(acts_kernel, (4, 2 * units, rows), (at, exchange(sums, PHASE)))
-    acts, *pieces = lax.optimization_barrier((acts, *pieces))
+        return lax.dynamic_index_in_dim(part, jnp.bitwise_xor(xl, xl_off), 0, keepdims=False)
+
+    onward = send(piece(1, 1), shift(zm=1))
+    across = send(piece(0, 1), shift(zm=1))
+    sums, onward = lax.optimization_barrier((exchange(sums, PHASE), onward))
+    acts = run(acts_kernel, (4, 2 * units, rows), (at, sums))
+    acts, across = lax.optimization_barrier((acts, across))
+    pieces = (piece(0, 0), across, send(piece(1, 0), shift(xl=1)), send(onward, shift(xl=1)))
     down = jnp.stack(pieces).reshape(8, 8 * units, LANES)
     down = jnp.stack((down, send(down, shift(core=1))), 1)
     down = down.transpose(2, 0, 1, 3).reshape(8 * units, 2048)

time: 201 us -> 197 us (0.980)
  waiting for transfers between devices: 58.8 us -> 47.7 us
  starting transfers between devices: 84.8 us -> 89.9 us
  blocking collectives: 33 us -> 35.2 us
    all_to_all x4, waiting for transfers between devices: 41.8 us -> 20.8 us  [exchange(): return lax.all_to_all(value, axes, 0, 0, tiled=True)]
    ppermute x11 -> x12, waiting for transfers between devices: 16.9 us -> 26.8 us  [send(): return lax.ppermute(value, AXES, route(move))]
    all_to_all x4, starting transfers between devices: 39.1 us -> 42.5 us  [exchange(): return lax.all_to_all(value, axes, 0, 0, tiled=True)]
    all_to_all x1, blocking collectives: 33 us -> 35.2 us  [exchange(): return lax.all_to_all(value, axes, 0, 0, tiled=True)]
    ppermute x11 -> x12, starting transfers between devices: 45.7 us -> 47.3 us  [send(): return lax.ppermute(value, AXES, route(move))]
  transfers between devices with their start and end apart: 15 -> 16, of which waited for: 7 -> 8; matrix products, arithmetic and copies ran while one was open for 3% -> 3% of each run, Pallas kernels for 1% -> 1%
where the time goes in v11:
time: 197 us; the launch traced here: 196 us
  starting transfers between devices  89.9 us (46%)
  waiting for transfers between devices  47.7 us (24%)
  blocking collectives  35.2 us (18%)
  Pallas kernels  11.3 us (6%)
  local copies, waits for them, and re-layouts  5.53 us (3%)
  other arithmetic  3.71 us (2%)
  matrix products  2.3 us (1%)
    ppermute x12, starting transfers between devices, send(): return lax.ppermute(value, AXES, route(move))  47.3 us
    all_to_all x4, starting transfers between devices, exchange(): return lax.all_to_all(value, axes, 0, 0, tiled=True)  42.5 us
    all_to_all x1, blocking collectives, exchange(): return lax.all_to_all(value, axes, 0, 0, tiled=True)  35.2 us
    ppermute x12, waiting for transfers between devices, send(): return lax.ppermute(value, AXES, route(move))  26.8 us
    all_to_all x4, waiting for transfers between devices, exchange(): return lax.all_to_all(value, axes, 0, 0, tiled=True)  20.8 us
    pallas_call x3, Pallas kernels, run(): pl.pallas_call(kernel, out_shape=jax.ShapeDtypeStruct(out_shape, bf16), i...  7.41 us
  transfers between devices with their start and end apart: 16, of which 8 were waited for; matrix products, arithmetic and copies ran while one was open for 3% of the time, Pallas kernels for 1%

profile of v11, /device:TPU:1, one launch (start us, length us, event | category | flops | bytes accessed | tf_op | source)
XLA Modules:
  0.0 195.8 jit_solution(8044374956487166978)
XLA Ops:
  0.0 3.9 %shard_map.55 = bf16[8,112,1024]{2,1,0:T(8,128)(2,1)} custom-call(bf16[52,8192]{1,0:T(8,128)(2,1)} %gate.1, bf16[52,8192]{1,0:T(8,128)(2,1)} %up.1), custom_call_target="tpu_custom_call" | custom-call | bytes 3407872 | tf_op jit(solution)/shard_map/pallas_call | solution.py:70
  3.9 0.0 copy-start.2
  3.9 7.6 %all-to-all-start = ((bf16[8,112,1024]{2,1,0:T(8,128)(2,1)}), bf16[8,112,1024]{2,1,0:T(8,128)(2,1)S(1)}, u32[]{:S(2)}, u32[]{:S(2)}) async-start(bf16[8,112,1024]{2,1,0:T(8,128)(2,1)} %shard_map.55), calls=%async_computation | async-start | bytes 3670016 | tf_op jit(solution)/shard_map/all_to_all | solution.py:25
  11.5 0.0 copy-done.2
  11.5 0.0 copy-start.3
  11.5 0.1 copy.12
  11.6 0.1 dynamic-slice_bitcast_fusion.1
  11.6 3.5 %collective-permute-start.2 = (bf16[2,2,416,128]{3,2,1,0:T(8,128)(2,1)S(1)}, bf16[2,2,416,128]{3,2,1,0:T(8,128)(2,1)S(1)}, u32[]{:S(2)}, u32[]{:S(2)}) collective-permute-start(bf16[2,2,416,128]{3,2,1,0:T(8,128)(2,1)S(1)} %get-tuple-element.26), channel_id=1, source_target_pairs={{0,2},{1,3},{2,0},{3,1},{4,6},{5,7},{6,4},{7,5},{8,10},{9,11},{10,... | collective-permute-start | bytes 1277960 | tf_op jit(solution)/shard_map/ppermute | solution.py:39
  15.2 1.0 constant_dynamic-slice_fusion
  16.2 0.0 copy-done.3
  16.3 15.7 %collective-permute-start.1 = (bf16[528,128]{1,0:T(8,128)(2,1)S(1)}, bf16[528,128]{1,0:T(8,128)(2,1)S(1)}, u32[]{:S(2)}, u32[]{:S(2)}) collective-permute-start(bf16[528,128]{1,0:T(8,128)(2,1)S(1)} %get-tuple-element.29), channel_id=1, source_target_pairs={{0,17},{1,16},{2,19},{3,18},{4,77},{5,76},{6,79},{7,78},{8,137},{9... | collective-permute-start | bytes 405512 | tf_op jit(solution)/shard_map/ppermute | solution.py:39
  31.9 1.3 collective-permute-start
  33.2 0.0 collective-permute-done.2
  33.2 1.0 pad_maximum_fusion
  34.2 3.9 %collective-permute-done.1 = bf16[528,128]{1,0:T(8,128)(2,1)S(1)} collective-permute-done((bf16[528,128]{1,0:T(8,128)(2,1)S(1)}, bf16[528,128]{1,0:T(8,128)(2,1)S(1)}, u32[]{:S(2)}, u32[]{:S(2)}) %collective-permute-start.1) | collective-permute-done | bytes 135200 | tf_op jit(solution)/shard_map/ppermute | solution.py:39
  38.2 0.0 collective-permute-done
  38.2 0.0 all-to-all-done.w_own
  38.2 2.2 %collective-permute-start.6 = (bf16[8,112,1024]{2,1,0:T(8,128)(2,1)S(1)}, bf16[8,112,1024]{2,1,0:T(8,128)(2,1)}, u32[]{:S(2)}, u32[]{:S(2)}) collective-permute-start(bf16[8,112,1024]{2,1,0:T(8,128)(2,1)S(1)} %all-to-all-done.w_own), channel_id=1, source_target_pairs={{0,1},{1,0},{2,3},{3,2},{4,5},{5,4},{6,7},{7,6},{8,9},{9,8},{10,11... | collective-permute-start | bytes 5505032 | tf_op jit(solution)/shard_map/ppermute | solution.py:39
  40.4 0.9 pad_maximum_fusion.2.x0
  41.3 4.0 %collective-permute-start.5 = (bf16[2,528,128]{2,1,0:T(8,128)(2,1)S(1)}, bf16[2,528,128]{2,1,0:T(8,128)(2,1)S(1)}, u32[]{:S(2)}, u32[]{:S(2)}) collective-permute-start(bf16[2,528,128]{2,1,0:T(8,128)(2,1)S(1)} %pad_maximum_fusion.2.x0), channel_id=1, source_target_pairs={{0,34},{1,35},{2,32},{3,33},{4,38},{5,39},{6,36},{7,37},{8,42},{9,... | collective-permute-start | bytes 811016 | tf_op jit(solution)/shard_map/ppermute | solution.py:39
  45.3 2.8 %collective-permute-start.4 = (bf16[2,528,128]{2,1,0:T(8,128)(2,1)S(1)}, bf16[2,528,128]{2,1,0:T(8,128)(2,1)S(1)}, u32[]{:S(2)}, u32[]{:S(2)}) collective-permute-start(bf16[2,528,128]{2,1,0:T(8,128)(2,1)S(1)} %pad_maximum_fusion.2.x0), channel_id=1, source_target_pairs={{0,32},{1,33},{2,34},{3,35},{4,36},{5,37},{6,38},{7,39},{8,40},{9,... | collective-permute-start | bytes 811016 | tf_op jit(solution)/shard_map/ppermute | solution.py:39
  48.1 1.9 collective-permute-start.3
  50.0 0.1 pad_add_fusion.at
  50.1 5.3 %collective-permute-done.5.x3 = bf16[2,528,128]{2,1,0:T(8,128)(2,1)S(1)} collective-permute-done((bf16[2,528,128]{2,1,0:T(8,128)(2,1)S(1)}, bf16[2,528,128]{2,1,0:T(8,128)(2,1)S(1)}, u32[]{:S(2)}, u32[]{:S(2)}) %collective-permute-start.5) | collective-permute-done | bytes 270368 | tf_op jit(solution)/shard_map/ppermute | solution.py:39
  55.4 5.7 %collective-permute-done.4.x2 = bf16[2,528,128]{2,1,0:T(8,128)(2,1)S(1)} collective-permute-done((bf16[2,528,128]{2,1,0:T(8,128)(2,1)S(1)}, bf16[2,528,128]{2,1,0:T(8,128)(2,1)S(1)}, u32[]{:S(2)}, u32[]{:S(2)}) %collective-permute-start.4) | collective-permute-done | bytes 270368 | tf_op jit(solution)/shard_map/ppermute | solution.py:39
  61.1 0.0 collective-permute-done.3.x1
  61.1 0.0 collective-permute-done.6.w_other
  61.1 4.3 %shard_map.56 = bf16[8,2,112,512]{3,2,1,0:T(8,128)(2,1)S(1)} custom-call(s32[3]{0:T(128)S(1)} %pad_add_fusion.at, bf16[2,528,128]{2,1,0:T(8,128)(2,1)S(1)} %pad_maximum_fusion.2.x0, bf16[2,528,128]{2,1,0:T(8,128)(2,1)S(1)} %collective-permute-done.3.x1, bf16[2,528,128]{2,1,0:T(8,128)(2,1)S(1)} %collective-permute-done.4.x2, ...), custom_call_target="tpu_custom_call" | custom-call | flops 1879048192 | bytes 6586380 | tf_op jit(solution)/shard_map/pallas_call | solution.py:148
  65.4 0.0 copy-start
  65.4 1.3 copy-done
  66.7 0.0 copy-start.1
  66.7 14.9 %all-to-all-start.1 = ((bf16[8,2,112,512]{3,2,1,0:T(8,128)(2,1)}), bf16[8,2,112,512]{3,2,1,0:T(8,128)(2,1)S(1)}, u32[]{:S(2)}, u32[]{:S(2)}) async-start(bf16[8,2,112,512]{3,2,1,0:T(8,128)(2,1)} %copy-done), calls=%async_computation.1 | async-start | bytes 3670016 | tf_op jit(solution)/shard_map/all_to_all | solution.py:25
  81.6 0.0 copy-done.1
  81.6 0.1 dynamic-slice_bitcast_fusion.3
  81.7 3.9 %collective-permute-start.7 = (bf16[2,416,128]{2,1,0:T(8,128)(2,1)S(1)}, bf16[2,416,128]{2,1,0:T(8,128)(2,1)S(1)}, u32[]{:S(2)}, u32[]{:S(2)}) collective-permute-start(bf16[2,416,128]{2,1,0:T(8,128)(2,1)S(1)} %get-tuple-element.24), channel_id=1, source_target_pairs={{0,4},{1,5},{2,6},{3,7},{4,0},{5,1},{6,2},{7,3},{8,12},{9,13},{10,... | collective-permute-start | bytes 638984 | tf_op jit(solution)/shard_map/ppermute | solution.py:39
  85.6 2.3 %collective-permute-start.8 = (bf16[2,416,128]{2,1,0:T(8,128)(2,1)S(1)}, bf16[2,416,128]{2,1,0:T(8,128)(2,1)S(1)}, u32[]{:S(2)}, u32[]{:S(2)}) collective-permute-start(bf16[2,416,128]{2,1,0:T(8,128)(2,1)S(1)} %get-tuple-element.23), channel_id=1, source_target_pairs={{0,4},{1,5},{2,6},{3,7},{4,0},{5,1},{6,2},{7,3},{8,12},{9,13},{10,... | collective-permute-start | bytes 638984 | tf_op jit(solution)/shard_map/ppermute | solution.py:39
  87.9 2.2 %collective-permute-start.9 = (bf16[2,416,128]{2,1,0:T(8,128)(2,1)S(1)}, bf16[2,416,128]{2,1,0:T(8,128)(2,1)S(1)}, u32[]{:S(2)}, u32[]{:S(2)}) collective-permute-start(bf16[2,416,128]{2,1,0:T(8,128)(2,1)S(1)} %get-tuple-element.22), channel_id=1, source_target_pairs={{0,32},{1,33},{2,34},{3,35},{4,36},{5,37},{6,38},{7,39},{8,40},{9,... | collective-permute-start | bytes 638984 | tf_op jit(solution)/shard_map/ppermute | solution.py:39
  90.1 9.9 %collective-permute-done.7 = bf16[2,416,128]{2,1,0:T(8,128)(2,1)S(1)} collective-permute-done((bf16[2,416,128]{2,1,0:T(8,128)(2,1)S(1)}, bf16[2,416,128]{2,1,0:T(8,128)(2,1)S(1)}, u32[]{:S(2)}, u32[]{:S(2)}) %collective-permute-start.7) | collective-permute-done | bytes 213024 | tf_op jit(solution)/shard_map/ppermute | solution.py:39
  100.0 6.6 %all-to-all-done.1.sums = bf16[8,2,112,512]{3,2,1,0:T(8,128)(2,1)S(1)} async-done(((bf16[8,2,112,512]{3,2,1,0:T(8,128)(2,1)}), bf16[8,2,112,512]{3,2,1,0:T(8,128)(2,1)S(1)}, u32[]{:S(2)}, u32[]{:S(2)}) %all-to-all-start.1) | async-done | bytes 1835040 | tf_op jit(solution)/shard_map/all_to_all | solution.py:25
  106.6 2.2 %collective-permute-start.10 = (bf16[2,416,128]{2,1,0:T(8,128)(2,1)S(1)}, bf16[2,416,128]{2,1,0:T(8,128)(2,1)S(1)}, u32[]{:S(2)}, u32[]{:S(2)}) collective-permute-start(bf16[2,416,128]{2,1,0:T(8,128)(2,1)S(1)} %collective-permute-done.7), channel_id=1, source_target_pairs={{0,32},{1,33},{2,34},{3,35},{4,36},{5,37},{6,38},{7,39},{8,40},{9,... | collective-permute-start | bytes 638984 | tf_op jit(solution)/shard_map/ppermute | solution.py:39
  108.8 1.6 shard_map.57
  110.4 0.0 collective-permute-done.8
  110.4 7.8 %all-to-all-start.2 = ((bf16[4,104,512]{2,1,0:T(8,128)(2,1)}), bf16[4,104,512]{2,1,0:T(8,128)(2,1)}, u32[]{:S(2)}, u32[]{:S(2)}) async-start(bf16[4,104,512]{2,1,0:T(8,128)(2,1)} %shard_map.57), calls=%async_computation.2 | async-start | bytes 851968 | tf_op jit(solution)/shard_map/all_to_all | solution.py:25
  118.2 0.0 collective-permute-done.9
  118.2 0.0 collective-permute-done.10
  118.2 0.1 pad_maximum_fusion.1
  118.3 5.3 %collective-permute-start.11 = (bf16[8,416,128]{2,1,0:T(8,128)(2,1)S(1)}, bf16[8,416,128]{2,1,0:T(8,128)(2,1)S(1)}, u32[]{:S(2)}, u32[]{:S(2)}) collective-permute-start(bf16[8,416,128]{2,1,0:T(8,128)(2,1)S(1)} %bitcast.46), channel_id=1, source_target_pairs={{0,1},{1,0},{2,3},{3,2},{4,5},{5,4},{6,7},{7,6},{8,9},{9,8},{10,11... | collective-permute-start | bytes 2555912 | tf_op jit(solution)/shard_map/ppermute | solution.py:39
  123.7 2.0 %collective-permute-done.11 = bf16[8,416,128]{2,1,0:T(8,128)(2,1)S(1)} collective-permute-done((bf16[8,416,128]{2,1,0:T(8,128)(2,1)S(1)}, bf16[8,416,128]{2,1,0:T(8,128)(2,1)S(1)}, u32[]{:S(2)}, u32[]{:S(2)}) %collective-permute-start.11) | collective-permute-done | bytes 852000 | tf_op jit(solution)/shard_map/ppermute | solution.py:39
  125.7 0.2 maximum_bitcast_fusion
  125.8 1.8 copy.13
  127.6 1.3 reshape.49
  128.9 4.7 %all-to-all-done.2 = bf16[4,104,512]{2,1,0:T(8,128)(2,1)} async-done(((bf16[4,104,512]{2,1,0:T(8,128)(2,1)}), bf16[4,104,512]{2,1,0:T(8,128)(2,1)}, u32[]{:S(2)}, u32[]{:S(2)}) %all-to-all-start.2) | async-done | bytes 426016 | tf_op jit(solution)/shard_map/all_to_all | solution.py:25
  133.6 2.3 %convolution_convert_fusion = bf16[512,2048]{1,0:T(8,128)(2,1)S(1)} fusion(bf16[416,512]{1,0:T(8,128)(2,1)} %bitcast.16, bf16[416,2048]{1,0:T(8,128)(2,1)S(1)} %reshape.49), kind=kOutput, calls=%fused_computation | convolution fusion | flops 873463808 | bytes 4227072 | tf_op jit(solution)/shard_map/dot_general | solution.py:217
  135.9 35.2 %all_to_all.25.parts = bf16[8,64,2048]{2,1,0:T(8,128)(2,1)S(1)} all-to-all(bf16[8,64,2048]{2,1,0:T(8,128)(2,1)S(1)} %bitcast.48), channel_id=1, replica_groups=mesh['y'=4,'xh'=2,'xl'=2,'zh'=4,'zm'=2,'z0'=2,'core'=2] {'y','xh'}, dimensions={0} | all-to-all | bytes 4194304 | tf_op jit(solution)/shard_map/all_to_all | solution.py:25
  171.1 1.5 shard_map.58
  172.6 12.2 %all-to-all-start.4 = ((bf16[16,64,128]{2,1,0:T(8,128)(2,1)}), bf16[16,64,128]{2,1,0:T(8,128)(2,1)S(1)}, u32[]{:S(2)}, u32[]{:S(2)}) async-start(bf16[16,64,128]{2,1,0:T(8,128)(2,1)} %shard_map.58), calls=%async_computation.4 | async-start | bytes 524288 | tf_op jit(solution)/shard_map/all_to_all | solution.py:25
  184.8 9.5 %all-to-all-done.4 = bf16[16,64,128]{2,1,0:T(8,128)(2,1)S(1)} async-done(((bf16[16,64,128]{2,1,0:T(8,128)(2,1)}), bf16[16,64,128]{2,1,0:T(8,128)(2,1)S(1)}, u32[]{:S(2)}, u32[]{:S(2)}) %all-to-all-start.4) | async-done | bytes 262176 | tf_op jit(solution)/shard_map/all_to_all | solution.py:25
  194.4 1.4 add_convert_fusion
  (3 shorter events, 0.1 us)
Async XLA Ops:
  3.9 7.6 %copy-start.2 = (bf16[3328,128]{1,0:T(8,128)(2,1)S(1)}, bf16[3328,128]{1,0:T(8,128)(2,1)}, u32[]{:S(2)}) copy-start(bf16[3328,128]{1,0:T(8,128)(2,1)} %param.9) | copy-start | bytes 2555908
  3.9 34.3 %all-to-all-start = ((bf16[8,112,1024]{2,1,0:T(8,128)(2,1)}), bf16[8,112,1024]{2,1,0:T(8,128)(2,1)S(1)}, u32[]{:S(2)}, u32[]{:S(2)}) async-start(bf16[8,112,1024]{2,1,0:T(8,128)(2,1)} %shard_map.55), calls=%async_computation | async-start | bytes 3670016 | tf_op jit(solution)/shard_map/all_to_all | solution.py:25
  11.5 4.7 %copy-start.3 = (bf16[128]{0:T(256)(128)(2,1)S(1)}, bf16[128]{0:T(256)(128)(2,1)}, u32[]{:S(2)}) copy-start(bf16[128]{0:T(256)(128)(2,1)} %param.6) | copy-start | bytes 772
  11.6 21.6 %collective-permute-start.2 = (bf16[2,2,416,128]{3,2,1,0:T(8,128)(2,1)S(1)}, bf16[2,2,416,128]{3,2,1,0:T(8,128)(2,1)S(1)}, u32[]{:S(2)}, u32[]{:S(2)}) collective-permute-start(bf16[2,2,416,128]{3,2,1,0:T(8,128)(2,1)S(1)} %get-tuple-element.26), channel_id=1, source_target_pairs={{0,2},{1,3},{2,0},{3,1},{4,6},{5,7},{6,4},{7,5},{8,10},{9,11},{10,... | collective-permute-start | bytes 1277960 | tf_op jit(solution)/shard_map/ppermute | solution.py:39
  16.3 21.9 %collective-permute-start.1 = (bf16[528,128]{1,0:T(8,128)(2,1)S(1)}, bf16[528,128]{1,0:T(8,128)(2,1)S(1)}, u32[]{:S(2)}, u32[]{:S(2)}) collective-permute-start(bf16[528,128]{1,0:T(8,128)(2,1)S(1)} %get-tuple-element.29), channel_id=1, source_target_pairs={{0,17},{1,16},{2,19},{3,18},{4,77},{5,76},{6,79},{7,78},{8,137},{9... | collective-permute-start | bytes 405512 | tf_op jit(solution)/shard_map/ppermute | solution.py:39
  31.9 6.2 %collective-permute-start = (bf16[528,128]{1,0:T(8,128)(2,1)S(1)}, bf16[528,128]{1,0:T(8,128)(2,1)}, u32[]{:S(2)}, u32[]{:S(2)}) collective-permute-start(bf16[528,128]{1,0:T(8,128)(2,1)S(1)} %get-tuple-element.30), channel_id=1, source_target_pairs={{0,0},{1,1},{2,2},{3,3},{4,92},{5,93},{6,94},{7,95},{8,152},{9,153... | collective-permute-start | bytes 405512 | tf_op jit(solution)/shard_map/ppermute | solution.py:39
  38.2 23.0 %collective-permute-start.6 = (bf16[8,112,1024]{2,1,0:T(8,128)(2,1)S(1)}, bf16[8,112,1024]{2,1,0:T(8,128)(2,1)}, u32[]{:S(2)}, u32[]{:S(2)}) collective-permute-start(bf16[8,112,1024]{2,1,0:T(8,128)(2,1)S(1)} %all-to-all-done.w_own), channel_id=1, source_target_pairs={{0,1},{1,0},{2,3},{3,2},{4,5},{5,4},{6,7},{7,6},{8,9},{9,8},{10,11... | collective-permute-start | bytes 5505032 | tf_op jit(solution)/shard_map/ppermute | solution.py:39
  41.3 14.1 %collective-permute-start.5 = (bf16[2,528,128]{2,1,0:T(8,128)(2,1)S(1)}, bf16[2,528,128]{2,1,0:T(8,128)(2,1)S(1)}, u32[]{:S(2)}, u32[]{:S(2)}) collective-permute-start(bf16[2,528,128]{2,1,0:T(8,128)(2,1)S(1)} %pad_maximum_fusion.2.x0), channel_id=1, source_target_pairs={{0,34},{1,35},{2,32},{3,33},{4,38},{5,39},{6,36},{7,37},{8,42},{9,... | collective-permute-start | bytes 811016 | tf_op jit(solution)/shard_map/ppermute | solution.py:39
  45.3 15.8 %collective-permute-start.4 = (bf16[2,528,128]{2,1,0:T(8,128)(2,1)S(1)}, bf16[2,528,128]{2,1,0:T(8,128)(2,1)S(1)}, u32[]{:S(2)}, u32[]{:S(2)}) collective-permute-start(bf16[2,528,128]{2,1,0:T(8,128)(2,1)S(1)} %pad_maximum_fusion.2.x0), channel_id=1, source_target_pairs={{0,32},{1,33},{2,34},{3,35},{4,36},{5,37},{6,38},{7,39},{8,40},{9,... | collective-permute-start | bytes 811016 | tf_op jit(solution)/shard_map/ppermute | solution.py:39
  48.1 13.1 %collective-permute-start.3 = (bf16[2,528,128]{2,1,0:T(8,128)(2,1)S(1)}, bf16[2,528,128]{2,1,0:T(8,128)(2,1)S(1)}, u32[]{:S(2)}, u32[]{:S(2)}) collective-permute-start(bf16[2,528,128]{2,1,0:T(8,128)(2,1)S(1)} %pad_maximum_fusion.2.x0), channel_id=1, source_target_pairs={{0,2},{1,3},{2,0},{3,1},{4,6},{5,7},{6,4},{7,5},{8,10},{9,11},{10,... | collective-permute-start | bytes 811016 | tf_op jit(solution)/shard_map/ppermute | solution.py:39
  65.4 1.3 copy-start
  66.7 14.9 %copy-start.1 = (bf16[2,2,2,416,128]{4,3,2,1,0:T(8,128)(2,1)S(1)}, bf16[2,2,2,416,128]{4,3,2,1,0:T(8,128)(2,1)}, u32[]{:S(2)}) copy-start(bf16[2,2,2,416,128]{4,3,2,1,0:T(8,128)(2,1)} %pad_maximum_fusion) | copy-start | bytes 2555908
  66.7 39.9 %all-to-all-start.1 = ((bf16[8,2,112,512]{3,2,1,0:T(8,128)(2,1)}), bf16[8,2,112,512]{3,2,1,0:T(8,128)(2,1)S(1)}, u32[]{:S(2)}, u32[]{:S(2)}) async-start(bf16[8,2,112,512]{3,2,1,0:T(8,128)(2,1)} %copy-done), calls=%async_computation.1 | async-start | bytes 3670016 | tf_op jit(solution)/shard_map/all_to_all | solution.py:25
  81.7 18.3 %collective-permute-start.7 = (bf16[2,416,128]{2,1,0:T(8,128)(2,1)S(1)}, bf16[2,416,128]{2,1,0:T(8,128)(2,1)S(1)}, u32[]{:S(2)}, u32[]{:S(2)}) collective-permute-start(bf16[2,416,128]{2,1,0:T(8,128)(2,1)S(1)} %get-tuple-element.24), channel_id=1, source_target_pairs={{0,4},{1,5},{2,6},{3,7},{4,0},{5,1},{6,2},{7,3},{8,12},{9,13},{10,... | collective-permute-start | bytes 638984 | tf_op jit(solution)/shard_map/ppermute | solution.py:39
  85.6 24.9 %collective-permute-start.8 = (bf16[2,416,128]{2,1,0:T(8,128)(2,1)S(1)}, bf16[2,416,128]{2,1,0:T(8,128)(2,1)S(1)}, u32[]{:S(2)}, u32[]{:S(2)}) collective-permute-start(bf16[2,416,128]{2,1,0:T(8,128)(2,1)S(1)} %get-tuple-element.23), channel_id=1, source_target_pairs={{0,4},{1,5},{2,6},{3,7},{4,0},{5,1},{6,2},{7,3},{8,12},{9,13},{10,... | collective-permute-start | bytes 638984 | tf_op jit(solution)/shard_map/ppermute | solution.py:39
  87.9 30.3 %collective-permute-start.9 = (bf16[2,416,128]{2,1,0:T(8,128)(2,1)S(1)}, bf16[2,416,128]{2,1,0:T(8,128)(2,1)S(1)}, u32[]{:S(2)}, u32[]{:S(2)}) collective-permute-start(bf16[2,416,128]{2,1,0:T(8,128)(2,1)S(1)} %get-tuple-element.22), channel_id=1, source_target_pairs={{0,32},{1,33},{2,34},{3,35},{4,36},{5,37},{6,38},{7,39},{8,40},{9,... | collective-permute-start | bytes 638984 | tf_op jit(solution)/shard_map/ppermute | solution.py:39
  106.6 11.6 %collective-permute-start.10 = (bf16[2,416,128]{2,1,0:T(8,128)(2,1)S(1)}, bf16[2,416,128]{2,1,0:T(8,128)(2,1)S(1)}, u32[]{:S(2)}, u32[]{:S(2)}) collective-permute-start(bf16[2,416,128]{2,1,0:T(8,128)(2,1)S(1)} %collective-permute-done.7), channel_id=1, source_target_pairs={{0,32},{1,33},{2,34},{3,35},{4,36},{5,37},{6,38},{7,39},{8,40},{9,... | collective-permute-start | bytes 638984 | tf_op jit(solution)/shard_map/ppermute | solution.py:39
  110.4 23.2 %all-to-all-start.2 = ((bf16[4,104,512]{2,1,0:T(8,128)(2,1)}), bf16[4,104,512]{2,1,0:T(8,128)(2,1)}, u32[]{:S(2)}, u32[]{:S(2)}) async-start(bf16[4,104,512]{2,1,0:T(8,128)(2,1)} %shard_map.57), calls=%async_computation.2 | async-start | bytes 851968 | tf_op jit(solution)/shard_map/all_to_all | solution.py:25
  118.3 7.3 %collective-permute-start.11 = (bf16[8,416,128]{2,1,0:T(8,128)(2,1)S(1)}, bf16[8,416,128]{2,1,0:T(8,128)(2,1)S(1)}, u32[]{:S(2)}, u32[]{:S(2)}) collective-permute-start(bf16[8,416,128]{2,1,0:T(8,128)(2,1)S(1)} %bitcast.46), channel_id=1, source_target_pairs={{0,1},{1,0},{2,3},{3,2},{4,5},{5,4},{6,7},{7,6},{8,9},{9,8},{10,11... | collective-permute-start | bytes 2555912 | tf_op jit(solution)/shard_map/ppermute | solution.py:39
  172.6 21.7 %all-to-all-start.4 = ((bf16[16,64,128]{2,1,0:T(8,128)(2,1)}), bf16[16,64,128]{2,1,0:T(8,128)(2,1)S(1)}, u32[]{:S(2)}, u32[]{:S(2)}) async-start(bf16[16,64,128]{2,1,0:T(8,128)(2,1)} %shard_map.58), calls=%async_computation.4 | async-start | bytes 524288 | tf_op jit(solution)/shard_map/all_to_all | solution.py:25

commit v12 on v11

--- a/solution.py
+++ b/solution.py
@@ -59,7 +59,7 @@
 
 def cut_kernel(gate, up, out):
     zero = jnp.zeros((56 - gate.shape[0], 512), f32)
-    for group in range(4):
+    for group in range(8):
         columns = slice(group * 512, group * 512 + 512)
         parts = (gate[:, columns].astype(f32), zero, up[:, columns].astype(f32), zero)
         out[group] = jnp.concatenate(parts).astype(bf16)
@@ -69,10 +69,10 @@
     units = gate.shape[0]
     return pl.pallas_call(
         cut_kernel,
-        grid=(4,),
+        grid=(2,),
         out_shape=jax.ShapeDtypeStruct((8, 112, 1024), bf16),
-        in_specs=[pl.BlockSpec((units, 2048), lambda i: (0, i))] * 2,
-        out_specs=pl.BlockSpec((4, 112, 512), lambda i: (i % 2, 0, i // 2)),
+        in_specs=[pl.BlockSpec((units, 4096), lambda i: (0, i))] * 2,
+        out_specs=pl.BlockSpec((8, 112, 512), lambda i: (0, 0, i)),
         compiler_params=pltpu.CompilerParams(vmem_limit_bytes=60 * 2**20),
         cost_estimate=pl.CostEstimate(flops=0, bytes_accessed=8 * units * FEAT, transcendentals=0),
     )(gate, up)
@@ -171,23 +171,18 @@
         part = lax.dynamic_slice_in_dim(halves, index, 1, 1).reshape(rows, LANES)
         return jnp.concatenate((part, gain))
 
-    def halve(value, axis):
-        place = lax.axis_index(axis)
-        kept, sent = (
-            lax.dynamic_index_in_dim(value, i, 0, keepdims=False) for i in (place, 1 - place)
-        )
-        return kept, send(sent, shift(**{axis: 1}))
-
     down = down_weight.reshape(2, 4, 2, 2, 2 * units, LANES)
     down = down.transpose(3, 2, 0, 1, 4, 5).reshape(2, 2, 2, 8 * units, LANES)
-    down = jnp.stack(halve(down, "z0"), 2)
+    z0 = lax.axis_index("z0")
+    kept, sent = (lax.dynamic_index_in_dim(down, i, 0, keepdims=False) for i in (z0, 1 - z0))
+    got = send(sent, shift(z0=1))
 
     own_w = exchange(cut(gate_weight, up_weight), PHASE)
     first = send(half(core), spread(0, 0))
     second = send(half(1 - core), spread(4, 1))
-    first, second, own_w, down = lax.optimization_barrier((first, second, own_w, down))
+    held, own_w, kept, got = lax.optimization_barrier((jnp.stack((first, second)), own_w, kept, got))
     other_w = send(own_w, shift(core=1))
-    held = jnp.stack((first, second))
+    down = jnp.stack((kept, got), 2)
     blocks = [held] + [send(held, shift(xl=i, z0=j)) for i, j in ((0, 1), (1, 0), (1, 1))]
 
     sums = run(

time: 197 us -> 194 us (0.985)
  starting transfers between devices: 89.9 us -> 103 us
  blocking collectives: 35.2 us -> 25 us
  waiting for transfers between devices: 47.7 us -> 44.3 us
    all_to_all x1, blocking collectives: 35.2 us -> 25 us  [exchange(): return lax.all_to_all(value, axes, 0, 0, tiled=True)]
    all_to_all x4, starting transfers between devices: 42.5 us -> 50.5 us  [exchange(): return lax.all_to_all(value, axes, 0, 0, tiled=True)]
    ppermute x12, starting transfers between devices: 47.3 us -> 52.1 us  [send(): return lax.ppermute(value, AXES, route(move))]
    ppermute x12, waiting for transfers between devices: 26.8 us -> 24.3 us  [send(): return lax.ppermute(value, AXES, route(move))]
where the time goes in v12:
time: 194 us; the launch traced here: 193 us
  starting transfers between devices  103 us (53%)
  waiting for transfers between devices  44.3 us (23%)
  blocking collectives  25 us (13%)
  Pallas kernels  9.94 us (5%)
  local copies, waits for them, and re-layouts  6.95 us (4%)
  matrix products  2.3 us (1%)
    ppermute x12, starting transfers between devices, send(): return lax.ppermute(value, AXES, route(move))  52.1 us
    all_to_all x4, starting transfers between devices, exchange(): return lax.all_to_all(value, axes, 0, 0, tiled=True)  50.5 us
    all_to_all x1, blocking collectives, exchange(): return lax.all_to_all(value, axes, 0, 0, tiled=True)  25 us
    ppermute x12, waiting for transfers between devices, send(): return lax.ppermute(value, AXES, route(move))  24.3 us
    all_to_all x4, waiting for transfers between devices, exchange(): return lax.all_to_all(value, axes, 0, 0, tiled=True)  20 us
    pallas_call x3, Pallas kernels, run(): pl.pallas_call(kernel, out_shape=jax.ShapeDtypeStruct(out_shape, bf16), i...  7.43 us
  transfers between devices with their start and end apart: 16, of which 8 were waited for; matrix products, arithmetic and copies ran while one was open for 3% of the time, Pallas kernels for 1%

profile of v12, /device:TPU:1, one launch (start us, length us, event | category | flops | bytes accessed | tf_op | source)
XLA Modules:
  0.0 193.3 jit_solution(17867469375472488392)
XLA Ops:
  0.0 2.5 %shard_map.55 = bf16[8,112,1024]{2,1,0:T(8,128)(2,1)} custom-call(bf16[52,8192]{1,0:T(8,128)(2,1)} %gate.1, bf16[52,8192]{1,0:T(8,128)(2,1)} %up.1), custom_call_target="tpu_custom_call" | custom-call | bytes 3407872 | tf_op jit(solution)/shard_map/pallas_call | solution.py:70
  2.5 0.0 copy-start.1
  2.5 7.6 %all-to-all-start = ((bf16[8,112,1024]{2,1,0:T(8,128)(2,1)}), bf16[8,112,1024]{2,1,0:T(8,128)(2,1)S(1)}, u32[]{:S(2)}, u32[]{:S(2)}) async-start(bf16[8,112,1024]{2,1,0:T(8,128)(2,1)} %shard_map.55), calls=%async_computation | async-start | bytes 3670016 | tf_op jit(solution)/shard_map/all_to_all | solution.py:25
  10.1 0.0 copy-done.1
  10.1 0.0 copy-start.4
  10.1 0.1 copy.12
  10.2 0.8 dynamic-slice_bitcast_fusion
  11.0 3.5 %collective-permute-start.2 = (bf16[2,2,416,128]{3,2,1,0:T(8,128)(2,1)}, bf16[2,2,416,128]{3,2,1,0:T(8,128)(2,1)S(1)}, u32[]{:S(2)}, u32[]{:S(2)}) collective-permute-start(bf16[2,2,416,128]{3,2,1,0:T(8,128)(2,1)} %get-tuple-element.25), channel_id=1, source_target_pairs={{0,2},{1,3},{2,0},{3,1},{4,6},{5,7},{6,4},{7,5},{8,10},{9,11},{10,... | collective-permute-start | bytes 1277960 | tf_op jit(solution)/shard_map/ppermute | solution.py:39
  14.6 1.0 constant_dynamic-slice_fusion.1
  15.6 0.0 copy-done.4
  15.6 0.7 collective-permute-start
  16.3 20.4 %collective-permute-start.1 = (bf16[528,128]{1,0:T(8,128)(2,1)S(1)}, bf16[528,128]{1,0:T(8,128)(2,1)S(1)}, u32[]{:S(2)}, u32[]{:S(2)}) collective-permute-start(bf16[528,128]{1,0:T(8,128)(2,1)S(1)} %get-tuple-element.30), channel_id=1, source_target_pairs={{0,17},{1,16},{2,19},{3,18},{4,77},{5,76},{6,79},{7,78},{8,137},{9... | collective-permute-start | bytes 405512 | tf_op jit(solution)/shard_map/ppermute | solution.py:39
  36.7 0.0 collective-permute-done
  36.8 4.6 %collective-permute-done.1 = bf16[528,128]{1,0:T(8,128)(2,1)S(1)} collective-permute-done((bf16[528,128]{1,0:T(8,128)(2,1)S(1)}, bf16[528,128]{1,0:T(8,128)(2,1)S(1)}, u32[]{:S(2)}, u32[]{:S(2)}) %collective-permute-start.1) | collective-permute-done | bytes 135200 | tf_op jit(solution)/shard_map/ppermute | solution.py:39
  41.4 0.0 collective-permute-done.2
  41.4 0.0 copy-start.2
  41.4 0.0 all-to-all-done.w_own
  41.5 0.7 copy-done.2
  42.2 2.0 %collective-permute-start.6 = (bf16[8,112,1024]{2,1,0:T(8,128)(2,1)S(1)}, bf16[8,112,1024]{2,1,0:T(8,128)(2,1)}, u32[]{:S(2)}, u32[]{:S(2)}) collective-permute-start(bf16[8,112,1024]{2,1,0:T(8,128)(2,1)S(1)} %all-to-all-done.w_own), channel_id=1, source_target_pairs={{0,1},{1,0},{2,3},{3,2},{4,5},{5,4},{6,7},{7,6},{8,9},{9,8},{10,11... | collective-permute-start | bytes 5505032 | tf_op jit(solution)/shard_map/ppermute | solution.py:39
  44.2 3.8 %collective-permute-start.5 = (bf16[2,528,128]{2,1,0:T(8,128)(2,1)S(1)}, bf16[2,528,128]{2,1,0:T(8,128)(2,1)S(1)}, u32[]{:S(2)}, u32[]{:S(2)}) collective-permute-start(bf16[2,528,128]{2,1,0:T(8,128)(2,1)S(1)} %pad_maximum_fusion.1.x0), channel_id=1, source_target_pairs={{0,34},{1,35},{2,32},{3,33},{4,38},{5,39},{6,36},{7,37},{8,42},{9,... | collective-permute-start | bytes 811016 | tf_op jit(solution)/shard_map/ppermute | solution.py:39
  48.1 3.1 %collective-permute-start.4 = (bf16[2,528,128]{2,1,0:T(8,128)(2,1)S(1)}, bf16[2,528,128]{2,1,0:T(8,128)(2,1)S(1)}, u32[]{:S(2)}, u32[]{:S(2)}) collective-permute-start(bf16[2,528,128]{2,1,0:T(8,128)(2,1)S(1)} %pad_maximum_fusion.1.x0), channel_id=1, source_target_pairs={{0,32},{1,33},{2,34},{3,35},{4,36},{5,37},{6,38},{7,39},{8,40},{9,... | collective-permute-start | bytes 811016 | tf_op jit(solution)/shard_map/ppermute | solution.py:39
  51.1 1.9 collective-permute-start.3
  53.1 0.1 pad_add_fusion.at
  53.2 1.6 collective-permute-done.5.x3
  54.8 6.4 %collective-permute-done.4.x2 = bf16[2,528,128]{2,1,0:T(8,128)(2,1)S(1)} collective-permute-done((bf16[2,528,128]{2,1,0:T(8,128)(2,1)S(1)}, bf16[2,528,128]{2,1,0:T(8,128)(2,1)S(1)}, u32[]{:S(2)}, u32[]{:S(2)}) %collective-permute-start.4) | collective-permute-done | bytes 270368 | tf_op jit(solution)/shard_map/ppermute | solution.py:39
  61.2 0.0 collective-permute-done.3.x1
  61.2 0.0 collective-permute-done.6.w_other
  61.2 4.3 %shard_map.56 = bf16[8,2,112,512]{3,2,1,0:T(8,128)(2,1)S(1)} custom-call(s32[3]{0:T(128)S(1)} %pad_add_fusion.at, bf16[2,528,128]{2,1,0:T(8,128)(2,1)S(1)} %pad_maximum_fusion.1.x0, bf16[2,528,128]{2,1,0:T(8,128)(2,1)S(1)} %collective-permute-done.3.x1, bf16[2,528,128]{2,1,0:T(8,128)(2,1)S(1)} %collective-permute-done.4.x2, ...), custom_call_target="tpu_custom_call" | custom-call | flops 1879048192 | bytes 6586380 | tf_op jit(solution)/shard_map/pallas_call | solution.py:148
  65.5 0.0 copy-start
  65.5 1.2 copy-done
  66.8 0.0 copy-start.3
  66.8 14.3 %all-to-all-start.1 = ((bf16[8,2,112,512]{3,2,1,0:T(8,128)(2,1)}), bf16[8,2,112,512]{3,2,1,0:T(8,128)(2,1)S(1)}, u32[]{:S(2)}, u32[]{:S(2)}) async-start(bf16[8,2,112,512]{3,2,1,0:T(8,128)(2,1)} %copy-done), calls=%async_computation.1 | async-start | bytes 3670016 | tf_op jit(solution)/shard_map/all_to_all | solution.py:25
  81.1 0.0 copy-done.3
  81.1 0.1 fusion.7
  81.2 4.9 %collective-permute-start.7 = (bf16[2,416,128]{2,1,0:T(8,128)(2,1)S(1)}, bf16[2,416,128]{2,1,0:T(8,128)(2,1)S(1)}, u32[]{:S(2)}, u32[]{:S(2)}) collective-permute-start(bf16[2,416,128]{2,1,0:T(8,128)(2,1)S(1)} %get-tuple-element.22), channel_id=1, source_target_pairs={{0,4},{1,5},{2,6},{3,7},{4,0},{5,1},{6,2},{7,3},{8,12},{9,13},{10,... | collective-permute-start | bytes 638984 | tf_op jit(solution)/shard_map/ppermute | solution.py:39
  86.0 1.9 collective-permute-start.8
  88.0 2.4 %collective-permute-start.9 = (bf16[2,416,128]{2,1,0:T(8,128)(2,1)S(1)}, bf16[2,416,128]{2,1,0:T(8,128)(2,1)S(1)}, u32[]{:S(2)}, u32[]{:S(2)}) collective-permute-start(bf16[2,416,128]{2,1,0:T(8,128)(2,1)S(1)} %get-tuple-element.24), channel_id=1, source_target_pairs={{0,32},{1,33},{2,34},{3,35},{4,36},{5,37},{6,38},{7,39},{8,40},{9,... | collective-permute-start | bytes 638984 | tf_op jit(solution)/shard_map/ppermute | solution.py:39
  90.4 9.6 %collective-permute-done.7 = bf16[2,416,128]{2,1,0:T(8,128)(2,1)S(1)} collective-permute-done((bf16[2,416,128]{2,1,0:T(8,128)(2,1)S(1)}, bf16[2,416,128]{2,1,0:T(8,128)(2,1)S(1)}, u32[]{:S(2)}, u32[]{:S(2)}) %collective-permute-start.7) | collective-permute-done | bytes 213024 | tf_op jit(solution)/shard_map/ppermute | solution.py:39
  100.0 6.0 %all-to-all-done.1.sums = bf16[8,2,112,512]{3,2,1,0:T(8,128)(2,1)S(1)} async-done(((bf16[8,2,112,512]{3,2,1,0:T(8,128)(2,1)}), bf16[8,2,112,512]{3,2,1,0:T(8,128)(2,1)S(1)}, u32[]{:S(2)}, u32[]{:S(2)}) %all-to-all-start.1) | async-done | bytes 1835040 | tf_op jit(solution)/shard_map/all_to_all | solution.py:25
  106.0 2.2 %collective-permute-start.10 = (bf16[2,416,128]{2,1,0:T(8,128)(2,1)S(1)}, bf16[2,416,128]{2,1,0:T(8,128)(2,1)S(1)}, u32[]{:S(2)}, u32[]{:S(2)}) collective-permute-start(bf16[2,416,128]{2,1,0:T(8,128)(2,1)S(1)} %collective-permute-done.7), channel_id=1, source_target_pairs={{0,32},{1,33},{2,34},{3,35},{4,36},{5,37},{6,38},{7,39},{8,40},{9,... | collective-permute-start | bytes 638984 | tf_op jit(solution)/shard_map/ppermute | solution.py:39
  108.3 1.6 shard_map.57
  109.9 0.0 collective-permute-done.8
  109.9 4.5 %all-to-all-start.2 = ((bf16[4,104,512]{2,1,0:T(8,128)(2,1)}), bf16[4,104,512]{2,1,0:T(8,128)(2,1)}, u32[]{:S(2)}, u32[]{:S(2)}) async-start(bf16[4,104,512]{2,1,0:T(8,128)(2,1)} %shard_map.57), calls=%async_computation.2 | async-start | bytes 851968 | tf_op jit(solution)/shard_map/all_to_all | solution.py:25
  114.4 0.0 collective-permute-done.9
  114.4 0.0 collective-permute-done.10
  114.4 0.1 pad_maximum_fusion
  114.5 5.2 %collective-permute-start.11 = (bf16[8,416,128]{2,1,0:T(8,128)(2,1)S(1)}, bf16[8,416,128]{2,1,0:T(8,128)(2,1)S(1)}, u32[]{:S(2)}, u32[]{:S(2)}) collective-permute-start(bf16[8,416,128]{2,1,0:T(8,128)(2,1)S(1)} %bitcast.47), channel_id=1, source_target_pairs={{0,1},{1,0},{2,3},{3,2},{4,5},{5,4},{6,7},{7,6},{8,9},{9,8},{10,11... | collective-permute-start | bytes 2555912 | tf_op jit(solution)/shard_map/ppermute | solution.py:39
  119.7 2.0 %collective-permute-done.11 = bf16[8,416,128]{2,1,0:T(8,128)(2,1)S(1)} collective-permute-done((bf16[8,416,128]{2,1,0:T(8,128)(2,1)S(1)}, bf16[8,416,128]{2,1,0:T(8,128)(2,1)S(1)}, u32[]{:S(2)}, u32[]{:S(2)}) %collective-permute-start.11) | collective-permute-done | bytes 852000 | tf_op jit(solution)/shard_map/ppermute | solution.py:39
  121.7 0.2 maximum_bitcast_fusion
  121.9 1.8 copy.13
  123.6 1.3 reshape.48
  124.9 4.5 %all-to-all-done.2 = bf16[4,104,512]{2,1,0:T(8,128)(2,1)} async-done(((bf16[4,104,512]{2,1,0:T(8,128)(2,1)}), bf16[4,104,512]{2,1,0:T(8,128)(2,1)}, u32[]{:S(2)}, u32[]{:S(2)}) %all-to-all-start.2) | async-done | bytes 426016 | tf_op jit(solution)/shard_map/all_to_all | solution.py:25
  129.4 2.3 %convolution_convert_fusion = bf16[512,2048]{1,0:T(8,128)(2,1)S(1)} fusion(bf16[416,512]{1,0:T(8,128)(2,1)} %bitcast.17, bf16[416,2048]{1,0:T(8,128)(2,1)S(1)} %reshape.48), kind=kOutput, calls=%fused_computation | convolution fusion | flops 873463808 | bytes 4227072 | tf_op jit(solution)/shard_map/dot_general | solution.py:212
  131.7 25.0 %all_to_all.25.parts = bf16[8,64,2048]{2,1,0:T(8,128)(2,1)S(1)} all-to-all(bf16[8,64,2048]{2,1,0:T(8,128)(2,1)S(1)} %bitcast.49), channel_id=1, replica_groups=mesh['y'=4,'xh'=2,'xl'=2,'zh'=4,'zm'=2,'z0'=2,'core'=2] {'y','xh'}, dimensions={0} | all-to-all | bytes 4194304 | tf_op jit(solution)/shard_map/all_to_all | solution.py:25
  156.7 1.5 shard_map.58
  158.2 24.2 %all-to-all-start.4 = ((bf16[16,64,128]{2,1,0:T(8,128)(2,1)}), bf16[16,64,128]{2,1,0:T(8,128)(2,1)S(1)}, u32[]{:S(2)}, u32[]{:S(2)}) async-start(bf16[16,64,128]{2,1,0:T(8,128)(2,1)} %shard_map.58), calls=%async_computation.4 | async-start | bytes 524288 | tf_op jit(solution)/shard_map/all_to_all | solution.py:25
  182.4 9.5 %all-to-all-done.4 = bf16[16,64,128]{2,1,0:T(8,128)(2,1)S(1)} async-done(((bf16[16,64,128]{2,1,0:T(8,128)(2,1)}), bf16[16,64,128]{2,1,0:T(8,128)(2,1)S(1)}, u32[]{:S(2)}, u32[]{:S(2)}) %all-to-all-start.4) | async-done | bytes 262176 | tf_op jit(solution)/shard_map/all_to_all | solution.py:25
  191.9 1.4 add_convert_fusion
  (4 shorter events, 0.1 us)
Async XLA Ops:
  2.5 7.6 %copy-start.1 = (bf16[3328,128]{1,0:T(8,128)(2,1)S(1)}, bf16[3328,128]{1,0:T(8,128)(2,1)}, u32[]{:S(2)}) copy-start(bf16[3328,128]{1,0:T(8,128)(2,1)} %param.9) | copy-start | bytes 2555908
  2.5 38.9 %all-to-all-start = ((bf16[8,112,1024]{2,1,0:T(8,128)(2,1)}), bf16[8,112,1024]{2,1,0:T(8,128)(2,1)S(1)}, u32[]{:S(2)}, u32[]{:S(2)}) async-start(bf16[8,112,1024]{2,1,0:T(8,128)(2,1)} %shard_map.55), calls=%async_computation | async-start | bytes 3670016 | tf_op jit(solution)/shard_map/all_to_all | solution.py:25
  10.1 5.5 %copy-start.4 = (bf16[128]{0:T(256)(128)(2,1)S(1)}, bf16[128]{0:T(256)(128)(2,1)}, u32[]{:S(2)}) copy-start(bf16[128]{0:T(256)(128)(2,1)} %param.6) | copy-start | bytes 772
  11.0 30.4 %collective-permute-start.2 = (bf16[2,2,416,128]{3,2,1,0:T(8,128)(2,1)}, bf16[2,2,416,128]{3,2,1,0:T(8,128)(2,1)S(1)}, u32[]{:S(2)}, u32[]{:S(2)}) collective-permute-start(bf16[2,2,416,128]{3,2,1,0:T(8,128)(2,1)} %get-tuple-element.25), channel_id=1, source_target_pairs={{0,2},{1,3},{2,0},{3,1},{4,6},{5,7},{6,4},{7,5},{8,10},{9,11},{10,... | collective-permute-start | bytes 1277960 | tf_op jit(solution)/shard_map/ppermute | solution.py:39
  15.6 21.1 %collective-permute-start = (bf16[528,128]{1,0:T(8,128)(2,1)S(1)}, bf16[528,128]{1,0:T(8,128)(2,1)S(1)}, u32[]{:S(2)}, u32[]{:S(2)}) collective-permute-start(bf16[528,128]{1,0:T(8,128)(2,1)S(1)} %get-tuple-element.29), channel_id=1, source_target_pairs={{0,0},{1,1},{2,2},{3,3},{4,92},{5,93},{6,94},{7,95},{8,152},{9,153... | collective-permute-start | bytes 405512 | tf_op jit(solution)/shard_map/ppermute | solution.py:39
  16.3 25.1 %collective-permute-start.1 = (bf16[528,128]{1,0:T(8,128)(2,1)S(1)}, bf16[528,128]{1,0:T(8,128)(2,1)S(1)}, u32[]{:S(2)}, u32[]{:S(2)}) collective-permute-start(bf16[528,128]{1,0:T(8,128)(2,1)S(1)} %get-tuple-element.30), channel_id=1, source_target_pairs={{0,17},{1,16},{2,19},{3,18},{4,77},{5,76},{6,79},{7,78},{8,137},{9... | collective-permute-start | bytes 405512 | tf_op jit(solution)/shard_map/ppermute | solution.py:39
  41.4 0.8 copy-start.2
  42.2 19.1 %collective-permute-start.6 = (bf16[8,112,1024]{2,1,0:T(8,128)(2,1)S(1)}, bf16[8,112,1024]{2,1,0:T(8,128)(2,1)}, u32[]{:S(2)}, u32[]{:S(2)}) collective-permute-start(bf16[8,112,1024]{2,1,0:T(8,128)(2,1)S(1)} %all-to-all-done.w_own), channel_id=1, source_target_pairs={{0,1},{1,0},{2,3},{3,2},{4,5},{5,4},{6,7},{7,6},{8,9},{9,8},{10,11... | collective-permute-start | bytes 5505032 | tf_op jit(solution)/shard_map/ppermute | solution.py:39
  44.2 10.5 %collective-permute-start.5 = (bf16[2,528,128]{2,1,0:T(8,128)(2,1)S(1)}, bf16[2,528,128]{2,1,0:T(8,128)(2,1)S(1)}, u32[]{:S(2)}, u32[]{:S(2)}) collective-permute-start(bf16[2,528,128]{2,1,0:T(8,128)(2,1)S(1)} %pad_maximum_fusion.1.x0), channel_id=1, source_target_pairs={{0,34},{1,35},{2,32},{3,33},{4,38},{5,39},{6,36},{7,37},{8,42},{9,... | collective-permute-start | bytes 811016 | tf_op jit(solution)/shard_map/ppermute | solution.py:39
  48.1 13.2 %collective-permute-start.4 = (bf16[2,528,128]{2,1,0:T(8,128)(2,1)S(1)}, bf16[2,528,128]{2,1,0:T(8,128)(2,1)S(1)}, u32[]{:S(2)}, u32[]{:S(2)}) collective-permute-start(bf16[2,528,128]{2,1,0:T(8,128)(2,1)S(1)} %pad_maximum_fusion.1.x0), channel_id=1, source_target_pairs={{0,32},{1,33},{2,34},{3,35},{4,36},{5,37},{6,38},{7,39},{8,40},{9,... | collective-permute-start | bytes 811016 | tf_op jit(solution)/shard_map/ppermute | solution.py:39
  51.1 10.1 %collective-permute-start.3 = (bf16[2,528,128]{2,1,0:T(8,128)(2,1)S(1)}, bf16[2,528,128]{2,1,0:T(8,128)(2,1)S(1)}, u32[]{:S(2)}, u32[]{:S(2)}) collective-permute-start(bf16[2,528,128]{2,1,0:T(8,128)(2,1)S(1)} %pad_maximum_fusion.1.x0), channel_id=1, source_target_pairs={{0,2},{1,3},{2,0},{3,1},{4,6},{5,7},{6,4},{7,5},{8,10},{9,11},{10,... | collective-permute-start | bytes 811016 | tf_op jit(solution)/shard_map/ppermute | solution.py:39
  65.5 1.3 copy-start
  66.8 14.3 %copy-start.3 = (bf16[2,2,416,128]{3,2,1,0:T(8,128)(2,1)S(1)}, bf16[2,2,416,128]{3,2,1,0:T(8,128)(2,1)}, u32[]{:S(2)}) copy-start(bf16[2,2,416,128]{3,2,1,0:T(8,128)(2,1)} %copy-done.2) | copy-start | bytes 1277956
  66.8 39.2 %all-to-all-start.1 = ((bf16[8,2,112,512]{3,2,1,0:T(8,128)(2,1)}), bf16[8,2,112,512]{3,2,1,0:T(8,128)(2,1)S(1)}, u32[]{:S(2)}, u32[]{:S(2)}) async-start(bf16[8,2,112,512]{3,2,1,0:T(8,128)(2,1)} %copy-done), calls=%async_computation.1 | async-start | bytes 3670016 | tf_op jit(solution)/shard_map/all_to_all | solution.py:25
  81.2 18.9 %collective-permute-start.7 = (bf16[2,416,128]{2,1,0:T(8,128)(2,1)S(1)}, bf16[2,416,128]{2,1,0:T(8,128)(2,1)S(1)}, u32[]{:S(2)}, u32[]{:S(2)}) collective-permute-start(bf16[2,416,128]{2,1,0:T(8,128)(2,1)S(1)} %get-tuple-element.22), channel_id=1, source_target_pairs={{0,4},{1,5},{2,6},{3,7},{4,0},{5,1},{6,2},{7,3},{8,12},{9,13},{10,... | collective-permute-start | bytes 638984 | tf_op jit(solution)/shard_map/ppermute | solution.py:39
  86.0 23.8 %collective-permute-start.8 = (bf16[2,416,128]{2,1,0:T(8,128)(2,1)S(1)}, bf16[2,416,128]{2,1,0:T(8,128)(2,1)S(1)}, u32[]{:S(2)}, u32[]{:S(2)}) collective-permute-start(bf16[2,416,128]{2,1,0:T(8,128)(2,1)S(1)} %get-tuple-element.23), channel_id=1, source_target_pairs={{0,4},{1,5},{2,6},{3,7},{4,0},{5,1},{6,2},{7,3},{8,12},{9,13},{10,... | collective-permute-start | bytes 638984 | tf_op jit(solution)/shard_map/ppermute | solution.py:39
  88.0 26.4 %collective-permute-start.9 = (bf16[2,416,128]{2,1,0:T(8,128)(2,1)S(1)}, bf16[2,416,128]{2,1,0:T(8,128)(2,1)S(1)}, u32[]{:S(2)}, u32[]{:S(2)}) collective-permute-start(bf16[2,416,128]{2,1,0:T(8,128)(2,1)S(1)} %get-tuple-element.24), channel_id=1, source_target_pairs={{0,32},{1,33},{2,34},{3,35},{4,36},{5,37},{6,38},{7,39},{8,40},{9,... | collective-permute-start | bytes 638984 | tf_op jit(solution)/shard_map/ppermute | solution.py:39
  106.0 8.3 %collective-permute-start.10 = (bf16[2,416,128]{2,1,0:T(8,128)(2,1)S(1)}, bf16[2,416,128]{2,1,0:T(8,128)(2,1)S(1)}, u32[]{:S(2)}, u32[]{:S(2)}) collective-permute-start(bf16[2,416,128]{2,1,0:T(8,128)(2,1)S(1)} %collective-permute-done.7), channel_id=1, source_target_pairs={{0,32},{1,33},{2,34},{3,35},{4,36},{5,37},{6,38},{7,39},{8,40},{9,... | collective-permute-start | bytes 638984 | tf_op jit(solution)/shard_map/ppermute | solution.py:39
  109.9 19.5 %all-to-all-start.2 = ((bf16[4,104,512]{2,1,0:T(8,128)(2,1)}), bf16[4,104,512]{2,1,0:T(8,128)(2,1)}, u32[]{:S(2)}, u32[]{:S(2)}) async-start(bf16[4,104,512]{2,1,0:T(8,128)(2,1)} %shard_map.57), calls=%async_computation.2 | async-start | bytes 851968 | tf_op jit(solution)/shard_map/all_to_all | solution.py:25
  114.5 7.2 %collective-permute-start.11 = (bf16[8,416,128]{2,1,0:T(8,128)(2,1)S(1)}, bf16[8,416,128]{2,1,0:T(8,128)(2,1)S(1)}, u32[]{:S(2)}, u32[]{:S(2)}) collective-permute-start(bf16[8,416,128]{2,1,0:T(8,128)(2,1)S(1)} %bitcast.47), channel_id=1, source_target_pairs={{0,1},{1,0},{2,3},{3,2},{4,5},{5,4},{6,7},{7,6},{8,9},{9,8},{10,11... | collective-permute-start | bytes 2555912 | tf_op jit(solution)/shard_map/ppermute | solution.py:39
  158.2 33.7 %all-to-all-start.4 = ((bf16[16,64,128]{2,1,0:T(8,128)(2,1)}), bf16[16,64,128]{2,1,0:T(8,128)(2,1)S(1)}, u32[]{:S(2)}, u32[]{:S(2)}) async-start(bf16[16,64,128]{2,1,0:T(8,128)(2,1)} %shard_map.58), calls=%async_computation.4 | async-start | bytes 524288 | tf_op jit(solution)/shard_map/all_to_all | solution.py:25

commit v13 on v12

--- a/solution.py
+++ b/solution.py
@@ -191,7 +191,7 @@
         (at, *blocks, own_w, other_w),
         (pltpu.VMEM((rows, 1024), bf16),),
         flops=2 * 1792 * 1024 * rows,
-        vmem=40,
+        vmem=54,
     )
     zm, xl = lax.axis_index("zm"), lax.axis_index("xl")
 

time: 194 us -> 194 us (level)
  local copies, waits for them, and re-layouts: 6.95 us -> 4.22 us
  Pallas kernels: 9.94 us -> 12.1 us
    pallas_call x3, Pallas kernels: 7.43 us -> 9.58 us  [run(): pl.pallas_call(kernel, out_shape=jax.ShapeDtypeStruct(out_shape, bf16), i...]
    unnamed x10, local copies, waits for them, and re-layouts: 2 us -> 0.02 us
where the time goes in v13:
time: 194 us
  starting transfers between devices  102 us (53%)
  waiting for transfers between devices  43.8 us (23%)
  blocking collectives  25.7 us (13%)
  Pallas kernels  12.1 us (6%)
  local copies, waits for them, and re-layouts  4.22 us (2%)
  other arithmetic  3.2 us (2%)
  matrix products  2.3 us (1%)
    ppermute x12, starting transfers between devices, send(): return lax.ppermute(value, AXES, route(move))  52.1 us
    all_to_all x4, starting transfers between devices, exchange(): return lax.all_to_all(value, axes, 0, 0, tiled=True)  49.9 us
    all_to_all x1, blocking collectives, exchange(): return lax.all_to_all(value, axes, 0, 0, tiled=True)  25.7 us
    ppermute x12, waiting for transfers between devices, send(): return lax.ppermute(value, AXES, route(move))  23.6 us
    all_to_all x4, waiting for transfers between devices, exchange(): return lax.all_to_all(value, axes, 0, 0, tiled=True)  20.2 us
    pallas_call x3, Pallas kernels, run(): pl.pallas_call(kernel, out_shape=jax.ShapeDtypeStruct(out_shape, bf16), i...  9.58 us
  transfers between devices with their start and end apart: 16, of which 8 were waited for; matrix products, arithmetic and copies ran while one was open for 3% of the time, Pallas kernels for 1%

profile of v13, /device:TPU:1, one launch (start us, length us, event | category | flops | bytes accessed | tf_op | source)
XLA Modules:
  0.0 193.5 jit_solution(11299266049488068880)
XLA Ops:
  0.0 2.5 %shard_map.55 = bf16[8,112,1024]{2,1,0:T(8,128)(2,1)} custom-call(bf16[52,8192]{1,0:T(8,128)(2,1)} %gate.1, bf16[52,8192]{1,0:T(8,128)(2,1)} %up.1), custom_call_target="tpu_custom_call" | custom-call | bytes 3407872 | tf_op jit(solution)/shard_map/pallas_call | solution.py:70
  2.5 0.0 copy-start.2
  2.5 7.6 %all-to-all-start = ((bf16[8,112,1024]{2,1,0:T(8,128)(2,1)}), bf16[8,112,1024]{2,1,0:T(8,128)(2,1)S(1)}, u32[]{:S(2)}, u32[]{:S(2)}) async-start(bf16[8,112,1024]{2,1,0:T(8,128)(2,1)} %shard_map.55), calls=%async_computation | async-start | bytes 3670016 | tf_op jit(solution)/shard_map/all_to_all | solution.py:25
  10.1 0.0 copy-done.2
  10.1 0.0 copy-start.3
  10.1 0.1 copy.12
  10.2 0.1 dynamic-slice_bitcast_fusion
  10.3 3.5 %collective-permute-start.2 = (bf16[2,2,416,128]{3,2,1,0:T(8,128)(2,1)S(1)}, bf16[2,2,416,128]{3,2,1,0:T(8,128)(2,1)S(1)}, u32[]{:S(2)}, u32[]{:S(2)}) collective-permute-start(bf16[2,2,416,128]{3,2,1,0:T(8,128)(2,1)S(1)} %get-tuple-element.25), channel_id=1, source_target_pairs={{0,2},{1,3},{2,0},{3,1},{4,6},{5,7},{6,4},{7,5},{8,10},{9,11},{10,... | collective-permute-start | bytes 1277960 | tf_op jit(solution)/shard_map/ppermute | solution.py:39
  13.9 1.0 constant_dynamic-slice_fusion.1
  14.9 0.0 copy-done.3
  14.9 0.7 collective-permute-start
  15.6 20.4 %collective-permute-start.1 = (bf16[528,128]{1,0:T(8,128)(2,1)S(1)}, bf16[528,128]{1,0:T(8,128)(2,1)S(1)}, u32[]{:S(2)}, u32[]{:S(2)}) collective-permute-start(bf16[528,128]{1,0:T(8,128)(2,1)S(1)} %get-tuple-element.30), channel_id=1, source_target_pairs={{0,17},{1,16},{2,19},{3,18},{4,77},{5,76},{6,79},{7,78},{8,137},{9... | collective-permute-start | bytes 405512 | tf_op jit(solution)/shard_map/ppermute | solution.py:39
  36.0 0.0 collective-permute-done
  36.0 4.4 %collective-permute-done.1 = bf16[528,128]{1,0:T(8,128)(2,1)S(1)} collective-permute-done((bf16[528,128]{1,0:T(8,128)(2,1)S(1)}, bf16[528,128]{1,0:T(8,128)(2,1)S(1)}, u32[]{:S(2)}, u32[]{:S(2)}) %collective-permute-start.1) | collective-permute-done | bytes 135200 | tf_op jit(solution)/shard_map/ppermute | solution.py:39
  40.4 0.7 pad_maximum_fusion.1.x0
  41.2 0.0 collective-permute-done.2
  41.2 0.0 all-to-all-done.w_own
  41.2 0.0 copy-start.1
  41.2 2.1 %collective-permute-start.6 = (bf16[8,112,1024]{2,1,0:T(8,128)(2,1)S(1)}, bf16[8,112,1024]{2,1,0:T(8,128)(2,1)}, u32[]{:S(2)}, u32[]{:S(2)}) collective-permute-start(bf16[8,112,1024]{2,1,0:T(8,128)(2,1)S(1)} %all-to-all-done.w_own), channel_id=1, source_target_pairs={{0,1},{1,0},{2,3},{3,2},{4,5},{5,4},{6,7},{7,6},{8,9},{9,8},{10,11... | collective-permute-start | bytes 5505032 | tf_op jit(solution)/shard_map/ppermute | solution.py:39
  43.3 4.0 %collective-permute-start.5 = (bf16[2,528,128]{2,1,0:T(8,128)(2,1)}, bf16[2,528,128]{2,1,0:T(8,128)(2,1)S(1)}, u32[]{:S(2)}, u32[]{:S(2)}) collective-permute-start(bf16[2,528,128]{2,1,0:T(8,128)(2,1)} %pad_maximum_fusion.1.x0), channel_id=1, source_target_pairs={{0,34},{1,35},{2,32},{3,33},{4,38},{5,39},{6,36},{7,37},{8,42},{9,... | collective-permute-start | bytes 811016 | tf_op jit(solution)/shard_map/ppermute | solution.py:39
  47.3 3.1 %collective-permute-start.4 = (bf16[2,528,128]{2,1,0:T(8,128)(2,1)}, bf16[2,528,128]{2,1,0:T(8,128)(2,1)}, u32[]{:S(2)}, u32[]{:S(2)}) collective-permute-start(bf16[2,528,128]{2,1,0:T(8,128)(2,1)} %pad_maximum_fusion.1.x0), channel_id=1, source_target_pairs={{0,32},{1,33},{2,34},{3,35},{4,36},{5,37},{6,38},{7,39},{8,40},{9,... | collective-permute-start | bytes 811016 | tf_op jit(solution)/shard_map/ppermute | solution.py:39
  50.4 1.9 collective-permute-start.3
  52.3 0.7 pad_add_fusion.at
  53.0 1.0 collective-permute-done.5.x3
  54.0 0.0 copy-start.4
  54.0 6.5 %collective-permute-done.4.x2 = bf16[2,528,128]{2,1,0:T(8,128)(2,1)} collective-permute-done((bf16[2,528,128]{2,1,0:T(8,128)(2,1)}, bf16[2,528,128]{2,1,0:T(8,128)(2,1)}, u32[]{:S(2)}, u32[]{:S(2)}) %collective-permute-start.4) | collective-permute-done | bytes 270368 | tf_op jit(solution)/shard_map/ppermute | solution.py:39
  60.6 0.0 collective-permute-done.3.x1
  60.6 0.0 collective-permute-done.6.w_other
  60.6 0.0 copy-done.1
  60.6 0.0 copy-done.4
  60.6 6.4 %shard_map.56 = bf16[8,2,112,512]{3,2,1,0:T(8,128)(2,1)} custom-call(s32[3]{0:T(128)} %pad_add_fusion.at, bf16[2,528,128]{2,1,0:T(8,128)(2,1)} %pad_maximum_fusion.1.x0, bf16[2,528,128]{2,1,0:T(8,128)(2,1)} %collective-permute-done.3.x1, bf16[2,528,128]{2,1,0:T(8,128)(2,1)} %collective-permute-done.4.x2, bf16[2,528,128]{2,1,0:T(8,128)(2,1)} %copy-done.4, ...), custom_call_target="tpu_custom_call" | custom-call | flops 1879048192 | bytes 6586380 | tf_op jit(solution)/shard_map/pallas_call | solution.py:148
  67.0 0.0 copy-start
  67.0 14.5 %all-to-all-start.1 = ((bf16[8,2,112,512]{3,2,1,0:T(8,128)(2,1)}), bf16[8,2,112,512]{3,2,1,0:T(8,128)(2,1)S(1)}, u32[]{:S(2)}, u32[]{:S(2)}) async-start(bf16[8,2,112,512]{3,2,1,0:T(8,128)(2,1)} %shard_map.56), calls=%async_computation.1 | async-start | bytes 3670016 | tf_op jit(solution)/shard_map/all_to_all | solution.py:25
  81.5 0.1 fusion.7
  81.6 4.9 %collective-permute-start.7 = (bf16[2,416,128]{2,1,0:T(8,128)(2,1)S(1)}, bf16[2,416,128]{2,1,0:T(8,128)(2,1)S(1)}, u32[]{:S(2)}, u32[]{:S(2)}) collective-permute-start(bf16[2,416,128]{2,1,0:T(8,128)(2,1)S(1)} %get-tuple-element.22), channel_id=1, source_target_pairs={{0,4},{1,5},{2,6},{3,7},{4,0},{5,1},{6,2},{7,3},{8,12},{9,13},{10,... | collective-permute-start | bytes 638984 | tf_op jit(solution)/shard_map/ppermute | solution.py:39
  86.5 1.9 collective-permute-start.8
  88.4 2.4 %collective-permute-start.9 = (bf16[2,416,128]{2,1,0:T(8,128)(2,1)S(1)}, bf16[2,416,128]{2,1,0:T(8,128)(2,1)S(1)}, u32[]{:S(2)}, u32[]{:S(2)}) collective-permute-start(bf16[2,416,128]{2,1,0:T(8,128)(2,1)S(1)} %get-tuple-element.24), channel_id=1, source_target_pairs={{0,32},{1,33},{2,34},{3,35},{4,36},{5,37},{6,38},{7,39},{8,40},{9,... | collective-permute-start | bytes 638984 | tf_op jit(solution)/shard_map/ppermute | solution.py:39
  90.8 9.6 %collective-permute-done.7 = bf16[2,416,128]{2,1,0:T(8,128)(2,1)S(1)} collective-permute-done((bf16[2,416,128]{2,1,0:T(8,128)(2,1)S(1)}, bf16[2,416,128]{2,1,0:T(8,128)(2,1)S(1)}, u32[]{:S(2)}, u32[]{:S(2)}) %collective-permute-start.7) | collective-permute-done | bytes 213024 | tf_op jit(solution)/shard_map/ppermute | solution.py:39
  100.5 6.0 %all-to-all-done.1.sums = bf16[8,2,112,512]{3,2,1,0:T(8,128)(2,1)S(1)} async-done(((bf16[8,2,112,512]{3,2,1,0:T(8,128)(2,1)}), bf16[8,2,112,512]{3,2,1,0:T(8,128)(2,1)S(1)}, u32[]{:S(2)}, u32[]{:S(2)}) %all-to-all-start.1) | async-done | bytes 1835040 | tf_op jit(solution)/shard_map/all_to_all | solution.py:25
  106.5 2.2 %collective-permute-start.10 = (bf16[2,416,128]{2,1,0:T(8,128)(2,1)S(1)}, bf16[2,416,128]{2,1,0:T(8,128)(2,1)S(1)}, u32[]{:S(2)}, u32[]{:S(2)}) collective-permute-start(bf16[2,416,128]{2,1,0:T(8,128)(2,1)S(1)} %collective-permute-done.7), channel_id=1, source_target_pairs={{0,32},{1,33},{2,34},{3,35},{4,36},{5,37},{6,38},{7,39},{8,40},{9,... | collective-permute-start | bytes 638984 | tf_op jit(solution)/shard_map/ppermute | solution.py:39
  108.7 0.0 copy-done
  108.7 1.6 shard_map.57
  110.3 0.0 collective-permute-done.8
  110.3 4.8 %all-to-all-start.2 = ((bf16[4,104,512]{2,1,0:T(8,128)(2,1)}), bf16[4,104,512]{2,1,0:T(8,128)(2,1)}, u32[]{:S(2)}, u32[]{:S(2)}) async-start(bf16[4,104,512]{2,1,0:T(8,128)(2,1)} %shard_map.57), calls=%async_computation.2 | async-start | bytes 851968 | tf_op jit(solution)/shard_map/all_to_all | solution.py:25
  115.1 0.0 collective-permute-done.9
  115.1 0.0 collective-permute-done.10
  115.1 0.1 pad_maximum_fusion
  115.2 5.0 %collective-permute-start.11 = (bf16[8,416,128]{2,1,0:T(8,128)(2,1)S(1)}, bf16[8,416,128]{2,1,0:T(8,128)(2,1)S(1)}, u32[]{:S(2)}, u32[]{:S(2)}) collective-permute-start(bf16[8,416,128]{2,1,0:T(8,128)(2,1)S(1)} %bitcast.47), channel_id=1, source_target_pairs={{0,1},{1,0},{2,3},{3,2},{4,5},{5,4},{6,7},{7,6},{8,9},{9,8},{10,11... | collective-permute-start | bytes 2555912 | tf_op jit(solution)/shard_map/ppermute | solution.py:39
  120.2 2.0 %collective-permute-done.11 = bf16[8,416,128]{2,1,0:T(8,128)(2,1)S(1)} collective-permute-done((bf16[8,416,128]{2,1,0:T(8,128)(2,1)S(1)}, bf16[8,416,128]{2,1,0:T(8,128)(2,1)S(1)}, u32[]{:S(2)}, u32[]{:S(2)}) %collective-permute-start.11) | collective-permute-done | bytes 852000 | tf_op jit(solution)/shard_map/ppermute | solution.py:39
  122.2 0.2 maximum_bitcast_fusion
  122.4 1.8 copy.13
  124.1 1.3 reshape.48
  125.4 4.6 %all-to-all-done.2 = bf16[4,104,512]{2,1,0:T(8,128)(2,1)} async-done(((bf16[4,104,512]{2,1,0:T(8,128)(2,1)}), bf16[4,104,512]{2,1,0:T(8,128)(2,1)}, u32[]{:S(2)}, u32[]{:S(2)}) %all-to-all-start.2) | async-done | bytes 426016 | tf_op jit(solution)/shard_map/all_to_all | solution.py:25
  130.1 2.3 %convolution_convert_fusion = bf16[512,2048]{1,0:T(8,128)(2,1)S(1)} fusion(bf16[416,512]{1,0:T(8,128)(2,1)} %bitcast.17, bf16[416,2048]{1,0:T(8,128)(2,1)S(1)} %reshape.48), kind=kOutput, calls=%fused_computation | convolution fusion | flops 873463808 | bytes 4227072 | tf_op jit(solution)/shard_map/dot_general | solution.py:212
  132.4 25.7 %all_to_all.25.parts = bf16[8,64,2048]{2,1,0:T(8,128)(2,1)S(1)} all-to-all(bf16[8,64,2048]{2,1,0:T(8,128)(2,1)S(1)} %bitcast.49), channel_id=1, replica_groups=mesh['y'=4,'xh'=2,'xl'=2,'zh'=4,'zm'=2,'z0'=2,'core'=2] {'y','xh'}, dimensions={0} | all-to-all | bytes 4194304 | tf_op jit(solution)/shard_map/all_to_all | solution.py:25
  158.0 1.5 shard_map.58
  159.6 23.0 %all-to-all-start.4 = ((bf16[16,64,128]{2,1,0:T(8,128)(2,1)}), bf16[16,64,128]{2,1,0:T(8,128)(2,1)S(1)}, u32[]{:S(2)}, u32[]{:S(2)}) async-start(bf16[16,64,128]{2,1,0:T(8,128)(2,1)} %shard_map.58), calls=%async_computation.4 | async-start | bytes 524288 | tf_op jit(solution)/shard_map/all_to_all | solution.py:25
  182.6 9.5 %all-to-all-done.4 = bf16[16,64,128]{2,1,0:T(8,128)(2,1)S(1)} async-done(((bf16[16,64,128]{2,1,0:T(8,128)(2,1)}), bf16[16,64,128]{2,1,0:T(8,128)(2,1)S(1)}, u32[]{:S(2)}, u32[]{:S(2)}) %all-to-all-start.4) | async-done | bytes 262176 | tf_op jit(solution)/shard_map/all_to_all | solution.py:25
  192.1 1.4 add_convert_fusion
  (3 shorter events, 0.1 us)
Async XLA Ops:
  2.5 7.6 %copy-start.2 = (bf16[3328,128]{1,0:T(8,128)(2,1)S(1)}, bf16[3328,128]{1,0:T(8,128)(2,1)}, u32[]{:S(2)}) copy-start(bf16[3328,128]{1,0:T(8,128)(2,1)} %param.9) | copy-start | bytes 2555908
  2.5 38.7 %all-to-all-start = ((bf16[8,112,1024]{2,1,0:T(8,128)(2,1)}), bf16[8,112,1024]{2,1,0:T(8,128)(2,1)S(1)}, u32[]{:S(2)}, u32[]{:S(2)}) async-start(bf16[8,112,1024]{2,1,0:T(8,128)(2,1)} %shard_map.55), calls=%async_computation | async-start | bytes 3670016 | tf_op jit(solution)/shard_map/all_to_all | solution.py:25
  10.1 4.7 %copy-start.3 = (bf16[128]{0:T(256)(128)(2,1)S(1)}, bf16[128]{0:T(256)(128)(2,1)}, u32[]{:S(2)}) copy-start(bf16[128]{0:T(256)(128)(2,1)} %param.6) | copy-start | bytes 772
  10.3 30.9 %collective-permute-start.2 = (bf16[2,2,416,128]{3,2,1,0:T(8,128)(2,1)S(1)}, bf16[2,2,416,128]{3,2,1,0:T(8,128)(2,1)S(1)}, u32[]{:S(2)}, u32[]{:S(2)}) collective-permute-start(bf16[2,2,416,128]{3,2,1,0:T(8,128)(2,1)S(1)} %get-tuple-element.25), channel_id=1, source_target_pairs={{0,2},{1,3},{2,0},{3,1},{4,6},{5,7},{6,4},{7,5},{8,10},{9,11},{10,... | collective-permute-start | bytes 1277960 | tf_op jit(solution)/shard_map/ppermute | solution.py:39
  14.9 21.1 %collective-permute-start = (bf16[528,128]{1,0:T(8,128)(2,1)S(1)}, bf16[528,128]{1,0:T(8,128)(2,1)S(1)}, u32[]{:S(2)}, u32[]{:S(2)}) collective-permute-start(bf16[528,128]{1,0:T(8,128)(2,1)S(1)} %get-tuple-element.29), channel_id=1, source_target_pairs={{0,0},{1,1},{2,2},{3,3},{4,92},{5,93},{6,94},{7,95},{8,152},{9,153... | collective-permute-start | bytes 405512 | tf_op jit(solution)/shard_map/ppermute | solution.py:39
  15.6 24.9 %collective-permute-start.1 = (bf16[528,128]{1,0:T(8,128)(2,1)S(1)}, bf16[528,128]{1,0:T(8,128)(2,1)S(1)}, u32[]{:S(2)}, u32[]{:S(2)}) collective-permute-start(bf16[528,128]{1,0:T(8,128)(2,1)S(1)} %get-tuple-element.30), channel_id=1, source_target_pairs={{0,17},{1,16},{2,19},{3,18},{4,77},{5,76},{6,79},{7,78},{8,137},{9... | collective-permute-start | bytes 405512 | tf_op jit(solution)/shard_map/ppermute | solution.py:39
  41.2 19.4 %copy-start.1 = (bf16[8,112,1024]{2,1,0:T(8,128)(2,1)}, bf16[8,112,1024]{2,1,0:T(8,128)(2,1)S(1)}, u32[]{:S(2)}) copy-start(bf16[8,112,1024]{2,1,0:T(8,128)(2,1)S(1)} %all-to-all-done.w_own) | copy-start | bytes 5505028
  41.2 19.4 %collective-permute-start.6 = (bf16[8,112,1024]{2,1,0:T(8,128)(2,1)S(1)}, bf16[8,112,1024]{2,1,0:T(8,128)(2,1)}, u32[]{:S(2)}, u32[]{:S(2)}) collective-permute-start(bf16[8,112,1024]{2,1,0:T(8,128)(2,1)S(1)} %all-to-all-done.w_own), channel_id=1, source_target_pairs={{0,1},{1,0},{2,3},{3,2},{4,5},{5,4},{6,7},{7,6},{8,9},{9,8},{10,11... | collective-permute-start | bytes 5505032 | tf_op jit(solution)/shard_map/ppermute | solution.py:39
  43.3 10.8 %collective-permute-start.5 = (bf16[2,528,128]{2,1,0:T(8,128)(2,1)}, bf16[2,528,128]{2,1,0:T(8,128)(2,1)S(1)}, u32[]{:S(2)}, u32[]{:S(2)}) collective-permute-start(bf16[2,528,128]{2,1,0:T(8,128)(2,1)} %pad_maximum_fusion.1.x0), channel_id=1, source_target_pairs={{0,34},{1,35},{2,32},{3,33},{4,38},{5,39},{6,36},{7,37},{8,42},{9,... | collective-permute-start | bytes 811016 | tf_op jit(solution)/shard_map/ppermute | solution.py:39
  47.3 13.3 %collective-permute-start.4 = (bf16[2,528,128]{2,1,0:T(8,128)(2,1)}, bf16[2,528,128]{2,1,0:T(8,128)(2,1)}, u32[]{:S(2)}, u32[]{:S(2)}) collective-permute-start(bf16[2,528,128]{2,1,0:T(8,128)(2,1)} %pad_maximum_fusion.1.x0), channel_id=1, source_target_pairs={{0,32},{1,33},{2,34},{3,35},{4,36},{5,37},{6,38},{7,39},{8,40},{9,... | collective-permute-start | bytes 811016 | tf_op jit(solution)/shard_map/ppermute | solution.py:39
  50.4 10.2 %collective-permute-start.3 = (bf16[2,528,128]{2,1,0:T(8,128)(2,1)}, bf16[2,528,128]{2,1,0:T(8,128)(2,1)}, u32[]{:S(2)}, u32[]{:S(2)}) collective-permute-start(bf16[2,528,128]{2,1,0:T(8,128)(2,1)} %pad_maximum_fusion.1.x0), channel_id=1, source_target_pairs={{0,2},{1,3},{2,0},{3,1},{4,6},{5,7},{6,4},{7,5},{8,10},{9,11},{10,... | collective-permute-start | bytes 811016 | tf_op jit(solution)/shard_map/ppermute | solution.py:39
  54.0 6.6 %copy-start.4 = (bf16[2,528,128]{2,1,0:T(8,128)(2,1)}, bf16[2,528,128]{2,1,0:T(8,128)(2,1)S(1)}, u32[]{:S(2)}) copy-start(bf16[2,528,128]{2,1,0:T(8,128)(2,1)S(1)} %collective-permute-done.5.x3) | copy-start | bytes 811012
  67.0 41.6 %copy-start = (s32[3]{0:T(128)S(1)}, s32[3]{0:T(128)}, u32[]{:S(2)}) copy-start(s32[3]{0:T(128)} %pad_add_fusion.at) | copy-start | bytes 40
  67.0 39.4 %all-to-all-start.1 = ((bf16[8,2,112,512]{3,2,1,0:T(8,128)(2,1)}), bf16[8,2,112,512]{3,2,1,0:T(8,128)(2,1)S(1)}, u32[]{:S(2)}, u32[]{:S(2)}) async-start(bf16[8,2,112,512]{3,2,1,0:T(8,128)(2,1)} %shard_map.56), calls=%async_computation.1 | async-start | bytes 3670016 | tf_op jit(solution)/shard_map/all_to_all | solution.py:25
  81.6 18.9 %collective-permute-start.7 = (bf16[2,416,128]{2,1,0:T(8,128)(2,1)S(1)}, bf16[2,416,128]{2,1,0:T(8,128)(2,1)S(1)}, u32[]{:S(2)}, u32[]{:S(2)}) collective-permute-start(bf16[2,416,128]{2,1,0:T(8,128)(2,1)S(1)} %get-tuple-element.22), channel_id=1, source_target_pairs={{0,4},{1,5},{2,6},{3,7},{4,0},{5,1},{6,2},{7,3},{8,12},{9,13},{10,... | collective-permute-start | bytes 638984 | tf_op jit(solution)/shard_map/ppermute | solution.py:39
  86.5 23.8 %collective-permute-start.8 = (bf16[2,416,128]{2,1,0:T(8,128)(2,1)S(1)}, bf16[2,416,128]{2,1,0:T(8,128)(2,1)S(1)}, u32[]{:S(2)}, u32[]{:S(2)}) collective-permute-start(bf16[2,416,128]{2,1,0:T(8,128)(2,1)S(1)} %get-tuple-element.23), channel_id=1, source_target_pairs={{0,4},{1,5},{2,6},{3,7},{4,0},{5,1},{6,2},{7,3},{8,12},{9,13},{10,... | collective-permute-start | bytes 638984 | tf_op jit(solution)/shard_map/ppermute | solution.py:39
  88.4 26.7 %collective-permute-start.9 = (bf16[2,416,128]{2,1,0:T(8,128)(2,1)S(1)}, bf16[2,416,128]{2,1,0:T(8,128)(2,1)S(1)}, u32[]{:S(2)}, u32[]{:S(2)}) collective-permute-start(bf16[2,416,128]{2,1,0:T(8,128)(2,1)S(1)} %get-tuple-element.24), channel_id=1, source_target_pairs={{0,32},{1,33},{2,34},{3,35},{4,36},{5,37},{6,38},{7,39},{8,40},{9,... | collective-permute-start | bytes 638984 | tf_op jit(solution)/shard_map/ppermute | solution.py:39
  106.5 8.6 %collective-permute-start.10 = (bf16[2,416,128]{2,1,0:T(8,128)(2,1)S(1)}, bf16[2,416,128]{2,1,0:T(8,128)(2,1)S(1)}, u32[]{:S(2)}, u32[]{:S(2)}) collective-permute-start(bf16[2,416,128]{2,1,0:T(8,128)(2,1)S(1)} %collective-permute-done.7), channel_id=1, source_target_pairs={{0,32},{1,33},{2,34},{3,35},{4,36},{5,37},{6,38},{7,39},{8,40},{9,... | collective-permute-start | bytes 638984 | tf_op jit(solution)/shard_map/ppermute | solution.py:39
  110.3 19.8 %all-to-all-start.2 = ((bf16[4,104,512]{2,1,0:T(8,128)(2,1)}), bf16[4,104,512]{2,1,0:T(8,128)(2,1)}, u32[]{:S(2)}, u32[]{:S(2)}) async-start(bf16[4,104,512]{2,1,0:T(8,128)(2,1)} %shard_map.57), calls=%async_computation.2 | async-start | bytes 851968 | tf_op jit(solution)/shard_map/all_to_all | solution.py:25
  115.2 7.0 %collective-permute-start.11 = (bf16[8,416,128]{2,1,0:T(8,128)(2,1)S(1)}, bf16[8,416,128]{2,1,0:T(8,128)(2,1)S(1)}, u32[]{:S(2)}, u32[]{:S(2)}) collective-permute-start(bf16[8,416,128]{2,1,0:T(8,128)(2,1)S(1)} %bitcast.47), channel_id=1, source_target_pairs={{0,1},{1,0},{2,3},{3,2},{4,5},{5,4},{6,7},{7,6},{8,9},{9,8},{10,11... | collective-permute-start | bytes 2555912 | tf_op jit(solution)/shard_map/ppermute | solution.py:39
  159.6 32.5 %all-to-all-start.4 = ((bf16[16,64,128]{2,1,0:T(8,128)(2,1)}), bf16[16,64,128]{2,1,0:T(8,128)(2,1)S(1)}, u32[]{:S(2)}, u32[]{:S(2)}) async-start(bf16[16,64,128]{2,1,0:T(8,128)(2,1)} %shard_map.58), calls=%async_computation.4 | async-start | bytes 524288 | tf_op jit(solution)/shard_map/all_to_all | solution.py:25

commit v14 on v12

--- a/solution.py
+++ b/solution.py
@@ -180,7 +180,9 @@
     own_w = exchange(cut(gate_weight, up_weight), PHASE)
     first = send(half(core), spread(0, 0))
     second = send(half(1 - core), spread(4, 1))
-    held, own_w, kept, got = lax.optimization_barrier((jnp.stack((first, second)), own_w, kept, got))
+    residual = lax.dynamic_slice_in_dim(layer_input, phase * (rows // 4), rows // 4, 0)
+    held = jnp.stack((first, second))
+    held, own_w, kept, got, residual = lax.optimization_barrier((held, own_w, kept, got, residual))
     other_w = send(own_w, shift(core=1))
     down = jnp.stack((kept, got), 2)
     blocks = [held] + [send(held, shift(xl=i, z0=j)) for i, j in ((0, 1), (1, 0), (1, 1))]
@@ -216,7 +218,6 @@
     partials = run(place_kernel, (16, rows // 8, LANES), (at, partials))
     partials = exchange(partials, (*BLOCK, "core")).astype(f32)
     ffn_out = jnp.sum(partials.reshape(8, rows // 4, LANES), 0)
-    residual = lax.dynamic_slice_in_dim(layer_input, phase * (rows // 4), rows // 4, 0)
     return (residual.astype(f32) + ffn_out).astype(bf16)
 
 

time: 194 us -> 193 us (level)
  blocking collectives: 25 us -> 58.5 us
  starting transfers between devices: 103 us -> 78.5 us
  waiting for transfers between devices: 44.3 us -> 33.4 us
    all_to_all x1 -> x2, blocking collectives: 25 us -> 58.5 us  [exchange(): return lax.all_to_all(value, axes, 0, 0, tiled=True)]
    all_to_all x4 -> x3, starting transfers between devices: 50.5 us -> 26.4 us  [exchange(): return lax.all_to_all(value, axes, 0, 0, tiled=True)]
    all_to_all x4 -> x3, waiting for transfers between devices: 20 us -> 10.5 us  [exchange(): return lax.all_to_all(value, axes, 0, 0, tiled=True)]
  transfers between devices with their start and end apart: 16 -> 15, of which waited for: 8 -> 7; matrix products, arithmetic and copies ran while one was open for 3% -> 4% of each run, Pallas kernels for 1% -> 1%
where the time goes in v14:
time: 193 us; the launch traced here: 192 us
  starting transfers between devices  78.5 us (41%)
  blocking collectives  58.5 us (30%)
  waiting for transfers between devices  33.4 us (17%)
  Pallas kernels  9.22 us (5%)
  local copies, waits for them, and re-layouts  8.35 us (4%)
  matrix products  2.28 us (1%)
    all_to_all x2, blocking collectives, exchange(): return lax.all_to_all(value, axes, 0, 0, tiled=True)  58.5 us
    ppermute x12, starting transfers between devices, send(): return lax.ppermute(value, AXES, route(move))  52.2 us
    all_to_all x3, starting transfers between devices, exchange(): return lax.all_to_all(value, axes, 0, 0, tiled=True)  26.4 us
    ppermute x12, waiting for transfers between devices, send(): return lax.ppermute(value, AXES, route(move))  22.9 us
    all_to_all x3, waiting for transfers between devices, exchange(): return lax.all_to_all(value, axes, 0, 0, tiled=True)  10.5 us
    pallas_call x3, Pallas kernels, run(): pl.pallas_call(kernel, out_shape=jax.ShapeDtypeStruct(out_shape, bf16), i...  6.71 us
  transfers between devices with their start and end apart: 15, of which 7 were waited for; matrix products, arithmetic and copies ran while one was open for 4% of the time, Pallas kernels for 1%

profile of v14, /device:TPU:1, one launch (start us, length us, event | category | flops | bytes accessed | tf_op | source)
XLA Modules:
  0.0 191.7 jit_solution(16597124002781855368)
XLA Ops:
  0.0 2.5 %shard_map.55 = bf16[8,112,1024]{2,1,0:T(8,128)(2,1)} custom-call(bf16[52,8192]{1,0:T(8,128)(2,1)} %gate.1, bf16[52,8192]{1,0:T(8,128)(2,1)} %up.1), custom_call_target="tpu_custom_call" | custom-call | bytes 3407872 | tf_op jit(solution)/shard_map/pallas_call | solution.py:70
  2.5 0.0 copy-start.1
  2.5 7.6 %all-to-all-start = ((bf16[8,112,1024]{2,1,0:T(8,128)(2,1)}), bf16[8,112,1024]{2,1,0:T(8,128)(2,1)S(1)}, u32[]{:S(2)}, u32[]{:S(2)}) async-start(bf16[8,112,1024]{2,1,0:T(8,128)(2,1)} %shard_map.55), calls=%async_computation | async-start | bytes 3670016 | tf_op jit(solution)/shard_map/all_to_all | solution.py:25
  10.1 0.0 copy-done.1
  10.1 0.0 copy-start.5
  10.1 0.1 copy.12
  10.2 0.8 dynamic-slice_bitcast_fusion
  11.1 3.5 %collective-permute-start.2 = (bf16[2,2,416,128]{3,2,1,0:T(8,128)(2,1)}, bf16[2,2,416,128]{3,2,1,0:T(8,128)(2,1)S(1)}, u32[]{:S(2)}, u32[]{:S(2)}) collective-permute-start(bf16[2,2,416,128]{3,2,1,0:T(8,128)(2,1)} %get-tuple-element.27), channel_id=1, source_target_pairs={{0,2},{1,3},{2,0},{3,1},{4,6},{5,7},{6,4},{7,5},{8,10},{9,11},{10,... | collective-permute-start | bytes 1277960 | tf_op jit(solution)/shard_map/ppermute | solution.py:39
  14.6 1.0 constant_dynamic-slice_fusion.2
  15.6 0.0 copy-done.5
  15.6 0.7 collective-permute-start
  16.3 20.4 %collective-permute-start.1 = (bf16[528,128]{1,0:T(8,128)(2,1)S(1)}, bf16[528,128]{1,0:T(8,128)(2,1)S(1)}, u32[]{:S(2)}, u32[]{:S(2)}) collective-permute-start(bf16[528,128]{1,0:T(8,128)(2,1)S(1)} %get-tuple-element.32), channel_id=1, source_target_pairs={{0,17},{1,16},{2,19},{3,18},{4,77},{5,76},{6,79},{7,78},{8,137},{9... | collective-permute-start | bytes 405512 | tf_op jit(solution)/shard_map/ppermute | solution.py:39
  36.8 1.4 constant_dynamic-slice_fusion
  38.1 0.0 collective-permute-done
  38.1 3.3 %collective-permute-done.1 = bf16[528,128]{1,0:T(8,128)(2,1)S(1)} collective-permute-done((bf16[528,128]{1,0:T(8,128)(2,1)S(1)}, bf16[528,128]{1,0:T(8,128)(2,1)S(1)}, u32[]{:S(2)}, u32[]{:S(2)}) %collective-permute-start.1) | collective-permute-done | bytes 135200 | tf_op jit(solution)/shard_map/ppermute | solution.py:39
  41.4 0.0 collective-permute-done.2
  41.4 0.0 copy-start.2
  41.4 0.0 all-to-all-done.w_own
  41.5 0.7 copy-done.2
  42.2 2.0 %collective-permute-start.6 = (bf16[8,112,1024]{2,1,0:T(8,128)(2,1)S(1)}, bf16[8,112,1024]{2,1,0:T(8,128)(2,1)}, u32[]{:S(2)}, u32[]{:S(2)}) collective-permute-start(bf16[8,112,1024]{2,1,0:T(8,128)(2,1)S(1)} %all-to-all-done.w_own), channel_id=1, source_target_pairs={{0,1},{1,0},{2,3},{3,2},{4,5},{5,4},{6,7},{7,6},{8,9},{9,8},{10,11... | collective-permute-start | bytes 5505032 | tf_op jit(solution)/shard_map/ppermute | solution.py:39
  44.3 3.8 %collective-permute-start.5 = (bf16[2,528,128]{2,1,0:T(8,128)(2,1)S(1)}, bf16[2,528,128]{2,1,0:T(8,128)(2,1)S(1)}, u32[]{:S(2)}, u32[]{:S(2)}) collective-permute-start(bf16[2,528,128]{2,1,0:T(8,128)(2,1)S(1)} %pad_maximum_fusion.1.x0), channel_id=1, source_target_pairs={{0,34},{1,35},{2,32},{3,33},{4,38},{5,39},{6,36},{7,37},{8,42},{9,... | collective-permute-start | bytes 811016 | tf_op jit(solution)/shard_map/ppermute | solution.py:39
  48.1 3.1 %collective-permute-start.4 = (bf16[2,528,128]{2,1,0:T(8,128)(2,1)S(1)}, bf16[2,528,128]{2,1,0:T(8,128)(2,1)S(1)}, u32[]{:S(2)}, u32[]{:S(2)}) collective-permute-start(bf16[2,528,128]{2,1,0:T(8,128)(2,1)S(1)} %pad_maximum_fusion.1.x0), channel_id=1, source_target_pairs={{0,32},{1,33},{2,34},{3,35},{4,36},{5,37},{6,38},{7,39},{8,40},{9,... | collective-permute-start | bytes 811016 | tf_op jit(solution)/shard_map/ppermute | solution.py:39
  51.2 1.9 %collective-permute-start.3 = (bf16[2,528,128]{2,1,0:T(8,128)(2,1)S(1)}, bf16[2,528,128]{2,1,0:T(8,128)(2,1)S(1)}, u32[]{:S(2)}, u32[]{:S(2)}) collective-permute-start(bf16[2,528,128]{2,1,0:T(8,128)(2,1)S(1)} %pad_maximum_fusion.1.x0), channel_id=1, source_target_pairs={{0,2},{1,3},{2,0},{3,1},{4,6},{5,7},{6,4},{7,5},{8,10},{9,11},{10,... | collective-permute-start | bytes 811016 | tf_op jit(solution)/shard_map/ppermute | solution.py:39
  53.1 0.1 pad_add_fusion.at
  53.2 1.6 collective-permute-done.5.x3
  54.8 6.4 %collective-permute-done.4.x2 = bf16[2,528,128]{2,1,0:T(8,128)(2,1)S(1)} collective-permute-done((bf16[2,528,128]{2,1,0:T(8,128)(2,1)S(1)}, bf16[2,528,128]{2,1,0:T(8,128)(2,1)S(1)}, u32[]{:S(2)}, u32[]{:S(2)}) %collective-permute-start.4) | collective-permute-done | bytes 270368 | tf_op jit(solution)/shard_map/ppermute | solution.py:39
  61.2 0.0 collective-permute-done.3.x1
  61.3 0.0 collective-permute-done.6.w_other
  61.3 4.3 %shard_map.56 = bf16[8,2,112,512]{3,2,1,0:T(8,128)(2,1)S(1)} custom-call(s32[3]{0:T(128)S(1)} %pad_add_fusion.at, bf16[2,528,128]{2,1,0:T(8,128)(2,1)S(1)} %pad_maximum_fusion.1.x0, bf16[2,528,128]{2,1,0:T(8,128)(2,1)S(1)} %collective-permute-done.3.x1, bf16[2,528,128]{2,1,0:T(8,128)(2,1)S(1)} %collective-permute-done.4.x2, ...), custom_call_target="tpu_custom_call" | custom-call | flops 1879048192 | bytes 6586380 | tf_op jit(solution)/shard_map/pallas_call | solution.py:148
  65.5 0.0 copy-start
  65.6 1.3 copy-done
  66.8 0.0 copy-start.3
  66.8 14.3 %all-to-all-start.1 = ((bf16[8,2,112,512]{3,2,1,0:T(8,128)(2,1)}), bf16[8,2,112,512]{3,2,1,0:T(8,128)(2,1)S(1)}, u32[]{:S(2)}, u32[]{:S(2)}) async-start(bf16[8,2,112,512]{3,2,1,0:T(8,128)(2,1)} %copy-done), calls=%async_computation.1 | async-start | bytes 3670016 | tf_op jit(solution)/shard_map/all_to_all | solution.py:25
  81.1 0.0 copy-done.3
  81.1 0.1 fusion.7
  81.2 4.9 %collective-permute-start.7 = (bf16[2,416,128]{2,1,0:T(8,128)(2,1)S(1)}, bf16[2,416,128]{2,1,0:T(8,128)(2,1)S(1)}, u32[]{:S(2)}, u32[]{:S(2)}) collective-permute-start(bf16[2,416,128]{2,1,0:T(8,128)(2,1)S(1)} %get-tuple-element.24), channel_id=1, source_target_pairs={{0,4},{1,5},{2,6},{3,7},{4,0},{5,1},{6,2},{7,3},{8,12},{9,13},{10,... | collective-permute-start | bytes 638984 | tf_op jit(solution)/shard_map/ppermute | solution.py:39
  86.1 1.9 %collective-permute-start.8 = (bf16[2,416,128]{2,1,0:T(8,128)(2,1)S(1)}, bf16[2,416,128]{2,1,0:T(8,128)(2,1)S(1)}, u32[]{:S(2)}, u32[]{:S(2)}) collective-permute-start(bf16[2,416,128]{2,1,0:T(8,128)(2,1)S(1)} %get-tuple-element.25), channel_id=1, source_target_pairs={{0,4},{1,5},{2,6},{3,7},{4,0},{5,1},{6,2},{7,3},{8,12},{9,13},{10,... | collective-permute-start | bytes 638984 | tf_op jit(solution)/shard_map/ppermute | solution.py:39
  88.0 2.4 %collective-permute-start.9 = (bf16[2,416,128]{2,1,0:T(8,128)(2,1)S(1)}, bf16[2,416,128]{2,1,0:T(8,128)(2,1)S(1)}, u32[]{:S(2)}, u32[]{:S(2)}) collective-permute-start(bf16[2,416,128]{2,1,0:T(8,128)(2,1)S(1)} %get-tuple-element.26), channel_id=1, source_target_pairs={{0,32},{1,33},{2,34},{3,35},{4,36},{5,37},{6,38},{7,39},{8,40},{9,... | collective-permute-start | bytes 638984 | tf_op jit(solution)/shard_map/ppermute | solution.py:39
  90.4 9.6 %collective-permute-done.7 = bf16[2,416,128]{2,1,0:T(8,128)(2,1)S(1)} collective-permute-done((bf16[2,416,128]{2,1,0:T(8,128)(2,1)S(1)}, bf16[2,416,128]{2,1,0:T(8,128)(2,1)S(1)}, u32[]{:S(2)}, u32[]{:S(2)}) %collective-permute-start.7) | collective-permute-done | bytes 213024 | tf_op jit(solution)/shard_map/ppermute | solution.py:39
  100.0 6.0 %all-to-all-done.1.sums = bf16[8,2,112,512]{3,2,1,0:T(8,128)(2,1)S(1)} async-done(((bf16[8,2,112,512]{3,2,1,0:T(8,128)(2,1)}), bf16[8,2,112,512]{3,2,1,0:T(8,128)(2,1)S(1)}, u32[]{:S(2)}, u32[]{:S(2)}) %all-to-all-start.1) | async-done | bytes 1835040 | tf_op jit(solution)/shard_map/all_to_all | solution.py:25
  106.0 2.2 %collective-permute-start.10 = (bf16[2,416,128]{2,1,0:T(8,128)(2,1)S(1)}, bf16[2,416,128]{2,1,0:T(8,128)(2,1)S(1)}, u32[]{:S(2)}, u32[]{:S(2)}) collective-permute-start(bf16[2,416,128]{2,1,0:T(8,128)(2,1)S(1)} %collective-permute-done.7), channel_id=1, source_target_pairs={{0,32},{1,33},{2,34},{3,35},{4,36},{5,37},{6,38},{7,39},{8,40},{9,... | collective-permute-start | bytes 638984 | tf_op jit(solution)/shard_map/ppermute | solution.py:39
  108.3 1.6 shard_map.57
  109.9 0.0 collective-permute-done.8
  109.9 4.5 %all-to-all-start.2 = ((bf16[4,104,512]{2,1,0:T(8,128)(2,1)}), bf16[4,104,512]{2,1,0:T(8,128)(2,1)}, u32[]{:S(2)}, u32[]{:S(2)}) async-start(bf16[4,104,512]{2,1,0:T(8,128)(2,1)} %shard_map.57), calls=%async_computation.2 | async-start | bytes 851968 | tf_op jit(solution)/shard_map/all_to_all | solution.py:25
  114.4 0.0 collective-permute-done.9
  114.4 0.0 collective-permute-done.10
  114.4 0.1 pad_maximum_fusion
  114.5 5.2 %collective-permute-start.11 = (bf16[8,416,128]{2,1,0:T(8,128)(2,1)S(1)}, bf16[8,416,128]{2,1,0:T(8,128)(2,1)S(1)}, u32[]{:S(2)}, u32[]{:S(2)}) collective-permute-start(bf16[8,416,128]{2,1,0:T(8,128)(2,1)S(1)} %bitcast.47), channel_id=1, source_target_pairs={{0,1},{1,0},{2,3},{3,2},{4,5},{5,4},{6,7},{7,6},{8,9},{9,8},{10,11... | collective-permute-start | bytes 2555912 | tf_op jit(solution)/shard_map/ppermute | solution.py:39
  119.7 2.0 %collective-permute-done.11 = bf16[8,416,128]{2,1,0:T(8,128)(2,1)S(1)} collective-permute-done((bf16[8,416,128]{2,1,0:T(8,128)(2,1)S(1)}, bf16[8,416,128]{2,1,0:T(8,128)(2,1)S(1)}, u32[]{:S(2)}, u32[]{:S(2)}) %collective-permute-start.11) | collective-permute-done | bytes 852000 | tf_op jit(solution)/shard_map/ppermute | solution.py:39
  121.7 0.2 maximum_bitcast_fusion
  121.9 1.8 copy.13
  123.6 1.3 reshape.48
  124.9 4.5 %all-to-all-done.2 = bf16[4,104,512]{2,1,0:T(8,128)(2,1)} async-done(((bf16[4,104,512]{2,1,0:T(8,128)(2,1)}), bf16[4,104,512]{2,1,0:T(8,128)(2,1)}, u32[]{:S(2)}, u32[]{:S(2)}) %all-to-all-start.2) | async-done | bytes 426016 | tf_op jit(solution)/shard_map/all_to_all | solution.py:25
  129.4 2.3 %convolution_convert_fusion = bf16[512,2048]{1,0:T(8,128)(2,1)S(1)} fusion(bf16[416,512]{1,0:T(8,128)(2,1)} %bitcast.17, bf16[416,2048]{1,0:T(8,128)(2,1)S(1)} %reshape.48), kind=kOutput, calls=%fused_computation | convolution fusion | flops 873463808 | bytes 4227072 | tf_op jit(solution)/shard_map/dot_general | solution.py:214
  131.7 25.0 %all_to_all.25.parts = bf16[8,64,2048]{2,1,0:T(8,128)(2,1)S(1)} all-to-all(bf16[8,64,2048]{2,1,0:T(8,128)(2,1)S(1)} %bitcast.49), channel_id=1, replica_groups=mesh['y'=4,'xh'=2,'xl'=2,'zh'=4,'zm'=2,'z0'=2,'core'=2] {'y','xh'}, dimensions={0} | all-to-all | bytes 4194304 | tf_op jit(solution)/shard_map/all_to_all | solution.py:25
  156.7 0.0 copy-start.4
  156.7 0.8 shard_map.58
  157.5 33.4 %all_to_all.26 = bf16[16,64,128]{2,1,0:T(8,128)(2,1)S(1)} all-to-all(bf16[16,64,128]{2,1,0:T(8,128)(2,1)S(1)} %shard_map.58), channel_id=1, replica_groups=mesh['y'=4,'xh'=2,'xl'=2,'zh'=4,'zm'=2,'z0'=2,'core'=2] {'xl','zm','z0',..., dimensions={0} | all-to-all | bytes 524288 | tf_op jit(solution)/shard_map/all_to_all | solution.py:25
  191.0 0.0 copy-done.4
  191.0 0.6 add_convert_fusion
  (4 shorter events, 0.1 us)
Async XLA Ops:
  2.5 7.6 %copy-start.1 = (bf16[3328,128]{1,0:T(8,128)(2,1)S(1)}, bf16[3328,128]{1,0:T(8,128)(2,1)}, u32[]{:S(2)}) copy-start(bf16[3328,128]{1,0:T(8,128)(2,1)} %param.9) | copy-start | bytes 2555908
  2.5 38.9 %all-to-all-start = ((bf16[8,112,1024]{2,1,0:T(8,128)(2,1)}), bf16[8,112,1024]{2,1,0:T(8,128)(2,1)S(1)}, u32[]{:S(2)}, u32[]{:S(2)}) async-start(bf16[8,112,1024]{2,1,0:T(8,128)(2,1)} %shard_map.55), calls=%async_computation | async-start | bytes 3670016 | tf_op jit(solution)/shard_map/all_to_all | solution.py:25
  10.1 5.5 %copy-start.5 = (bf16[128]{0:T(256)(128)(2,1)S(1)}, bf16[128]{0:T(256)(128)(2,1)}, u32[]{:S(2)}) copy-start(bf16[128]{0:T(256)(128)(2,1)} %param.6) | copy-start | bytes 772
  11.1 30.4 %collective-permute-start.2 = (bf16[2,2,416,128]{3,2,1,0:T(8,128)(2,1)}, bf16[2,2,416,128]{3,2,1,0:T(8,128)(2,1)S(1)}, u32[]{:S(2)}, u32[]{:S(2)}) collective-permute-start(bf16[2,2,416,128]{3,2,1,0:T(8,128)(2,1)} %get-tuple-element.27), channel_id=1, source_target_pairs={{0,2},{1,3},{2,0},{3,1},{4,6},{5,7},{6,4},{7,5},{8,10},{9,11},{10,... | collective-permute-start | bytes 1277960 | tf_op jit(solution)/shard_map/ppermute | solution.py:39
  15.6 22.5 %collective-permute-start = (bf16[528,128]{1,0:T(8,128)(2,1)S(1)}, bf16[528,128]{1,0:T(8,128)(2,1)S(1)}, u32[]{:S(2)}, u32[]{:S(2)}) collective-permute-start(bf16[528,128]{1,0:T(8,128)(2,1)S(1)} %get-tuple-element.31), channel_id=1, source_target_pairs={{0,0},{1,1},{2,2},{3,3},{4,92},{5,93},{6,94},{7,95},{8,152},{9,153... | collective-permute-start | bytes 405512 | tf_op jit(solution)/shard_map/ppermute | solution.py:39
  16.3 25.1 %collective-permute-start.1 = (bf16[528,128]{1,0:T(8,128)(2,1)S(1)}, bf16[528,128]{1,0:T(8,128)(2,1)S(1)}, u32[]{:S(2)}, u32[]{:S(2)}) collective-permute-start(bf16[528,128]{1,0:T(8,128)(2,1)S(1)} %get-tuple-element.32), channel_id=1, source_target_pairs={{0,17},{1,16},{2,19},{3,18},{4,77},{5,76},{6,79},{7,78},{8,137},{9... | collective-permute-start | bytes 405512 | tf_op jit(solution)/shard_map/ppermute | solution.py:39
  41.4 0.8 copy-start.2
  42.2 19.1 %collective-permute-start.6 = (bf16[8,112,1024]{2,1,0:T(8,128)(2,1)S(1)}, bf16[8,112,1024]{2,1,0:T(8,128)(2,1)}, u32[]{:S(2)}, u32[]{:S(2)}) collective-permute-start(bf16[8,112,1024]{2,1,0:T(8,128)(2,1)S(1)} %all-to-all-done.w_own), channel_id=1, source_target_pairs={{0,1},{1,0},{2,3},{3,2},{4,5},{5,4},{6,7},{7,6},{8,9},{9,8},{10,11... | collective-permute-start | bytes 5505032 | tf_op jit(solution)/shard_map/ppermute | solution.py:39
  44.3 10.5 %collective-permute-start.5 = (bf16[2,528,128]{2,1,0:T(8,128)(2,1)S(1)}, bf16[2,528,128]{2,1,0:T(8,128)(2,1)S(1)}, u32[]{:S(2)}, u32[]{:S(2)}) collective-permute-start(bf16[2,528,128]{2,1,0:T(8,128)(2,1)S(1)} %pad_maximum_fusion.1.x0), channel_id=1, source_target_pairs={{0,34},{1,35},{2,32},{3,33},{4,38},{5,39},{6,36},{7,37},{8,42},{9,... | collective-permute-start | bytes 811016 | tf_op jit(solution)/shard_map/ppermute | solution.py:39
  48.1 13.2 %collective-permute-start.4 = (bf16[2,528,128]{2,1,0:T(8,128)(2,1)S(1)}, bf16[2,528,128]{2,1,0:T(8,128)(2,1)S(1)}, u32[]{:S(2)}, u32[]{:S(2)}) collective-permute-start(bf16[2,528,128]{2,1,0:T(8,128)(2,1)S(1)} %pad_maximum_fusion.1.x0), channel_id=1, source_target_pairs={{0,32},{1,33},{2,34},{3,35},{4,36},{5,37},{6,38},{7,39},{8,40},{9,... | collective-permute-start | bytes 811016 | tf_op jit(solution)/shard_map/ppermute | solution.py:39
  51.2 10.1 %collective-permute-start.3 = (bf16[2,528,128]{2,1,0:T(8,128)(2,1)S(1)}, bf16[2,528,128]{2,1,0:T(8,128)(2,1)S(1)}, u32[]{:S(2)}, u32[]{:S(2)}) collective-permute-start(bf16[2,528,128]{2,1,0:T(8,128)(2,1)S(1)} %pad_maximum_fusion.1.x0), channel_id=1, source_target_pairs={{0,2},{1,3},{2,0},{3,1},{4,6},{5,7},{6,4},{7,5},{8,10},{9,11},{10,... | collective-permute-start | bytes 811016 | tf_op jit(solution)/shard_map/ppermute | solution.py:39
  65.5 1.3 copy-start
  66.8 14.3 %copy-start.3 = (bf16[2,2,416,128]{3,2,1,0:T(8,128)(2,1)S(1)}, bf16[2,2,416,128]{3,2,1,0:T(8,128)(2,1)}, u32[]{:S(2)}) copy-start(bf16[2,2,416,128]{3,2,1,0:T(8,128)(2,1)} %copy-done.2) | copy-start | bytes 1277956
  66.8 39.2 %all-to-all-start.1 = ((bf16[8,2,112,512]{3,2,1,0:T(8,128)(2,1)}), bf16[8,2,112,512]{3,2,1,0:T(8,128)(2,1)S(1)}, u32[]{:S(2)}, u32[]{:S(2)}) async-start(bf16[8,2,112,512]{3,2,1,0:T(8,128)(2,1)} %copy-done), calls=%async_computation.1 | async-start | bytes 3670016 | tf_op jit(solution)/shard_map/all_to_all | solution.py:25
  81.2 18.9 %collective-permute-start.7 = (bf16[2,416,128]{2,1,0:T(8,128)(2,1)S(1)}, bf16[2,416,128]{2,1,0:T(8,128)(2,1)S(1)}, u32[]{:S(2)}, u32[]{:S(2)}) collective-permute-start(bf16[2,416,128]{2,1,0:T(8,128)(2,1)S(1)} %get-tuple-element.24), channel_id=1, source_target_pairs={{0,4},{1,5},{2,6},{3,7},{4,0},{5,1},{6,2},{7,3},{8,12},{9,13},{10,... | collective-permute-start | bytes 638984 | tf_op jit(solution)/shard_map/ppermute | solution.py:39
  86.1 23.8 %collective-permute-start.8 = (bf16[2,416,128]{2,1,0:T(8,128)(2,1)S(1)}, bf16[2,416,128]{2,1,0:T(8,128)(2,1)S(1)}, u32[]{:S(2)}, u32[]{:S(2)}) collective-permute-start(bf16[2,416,128]{2,1,0:T(8,128)(2,1)S(1)} %get-tuple-element.25), channel_id=1, source_target_pairs={{0,4},{1,5},{2,6},{3,7},{4,0},{5,1},{6,2},{7,3},{8,12},{9,13},{10,... | collective-permute-start | bytes 638984 | tf_op jit(solution)/shard_map/ppermute | solution.py:39
  88.0 26.4 %collective-permute-start.9 = (bf16[2,416,128]{2,1,0:T(8,128)(2,1)S(1)}, bf16[2,416,128]{2,1,0:T(8,128)(2,1)S(1)}, u32[]{:S(2)}, u32[]{:S(2)}) collective-permute-start(bf16[2,416,128]{2,1,0:T(8,128)(2,1)S(1)} %get-tuple-element.26), channel_id=1, source_target_pairs={{0,32},{1,33},{2,34},{3,35},{4,36},{5,37},{6,38},{7,39},{8,40},{9,... | collective-permute-start | bytes 638984 | tf_op jit(solution)/shard_map/ppermute | solution.py:39
  106.0 8.3 %collective-permute-start.10 = (bf16[2,416,128]{2,1,0:T(8,128)(2,1)S(1)}, bf16[2,416,128]{2,1,0:T(8,128)(2,1)S(1)}, u32[]{:S(2)}, u32[]{:S(2)}) collective-permute-start(bf16[2,416,128]{2,1,0:T(8,128)(2,1)S(1)} %collective-permute-done.7), channel_id=1, source_target_pairs={{0,32},{1,33},{2,34},{3,35},{4,36},{5,37},{6,38},{7,39},{8,40},{9,... | collective-permute-start | bytes 638984 | tf_op jit(solution)/shard_map/ppermute | solution.py:39
  109.9 19.5 %all-to-all-start.2 = ((bf16[4,104,512]{2,1,0:T(8,128)(2,1)}), bf16[4,104,512]{2,1,0:T(8,128)(2,1)}, u32[]{:S(2)}, u32[]{:S(2)}) async-start(bf16[4,104,512]{2,1,0:T(8,128)(2,1)} %shard_map.57), calls=%async_computation.2 | async-start | bytes 851968 | tf_op jit(solution)/shard_map/all_to_all | solution.py:25
  114.5 7.2 %collective-permute-start.11 = (bf16[8,416,128]{2,1,0:T(8,128)(2,1)S(1)}, bf16[8,416,128]{2,1,0:T(8,128)(2,1)S(1)}, u32[]{:S(2)}, u32[]{:S(2)}) collective-permute-start(bf16[8,416,128]{2,1,0:T(8,128)(2,1)S(1)} %bitcast.47), channel_id=1, source_target_pairs={{0,1},{1,0},{2,3},{3,2},{4,5},{5,4},{6,7},{7,6},{8,9},{9,8},{10,11... | collective-permute-start | bytes 2555912 | tf_op jit(solution)/shard_map/ppermute | solution.py:39
  156.7 34.3 %copy-start.4 = (bf16[128,128]{1,0:T(8,128)(2,1)S(1)}, bf16[128,128]{1,0:T(8,128)(2,1)}, u32[]{:S(2)}) copy-start(bf16[128,128]{1,0:T(8,128)(2,1)} %constant_dynamic-slice_fusion) | copy-start | bytes 98308
